TPU v7x, 32 devices: a whole 2x2x4 slice. The times are simulated.
32 devices in a mesh: expert: 4 (over z), context: 2 (over y), dp: 4 (over x, core).
Axes of the slice: x: 2, y: 2, z: 4, core: 2. Of those that a mesh axis runs over, the one named last changes fastest.
Arguments:
- hidden_in: bfloat16 [2, 16, 2048, 768], P(None, ('expert', 'dp'), 'context'), may hold values from -6 to 6
- segments: int32 [2, 16, 2048], P(None, ('expert', 'dp')), may hold values from 0 to 4, as said below
- routes: int32 [2, 16, 2048, 2], P(None, ('expert', 'dp'), 'context'), may hold values from 0 to 11, all different within a row; in each aligned block of 1024 rows (0 to 1023, 1024 to 2047, ..., all dimensions but the last counted through in order) at most 256 rows name the same one
- prev_logits: float32 [2, 16, 2048, 12], P(None, ('expert', 'dp'), 'context'), may hold values from -4 to 4
- out_grad: bfloat16 [2, 16, 2048, 768], P(None, ('expert', 'dp'), 'context'), may hold values from -6 to 6
- norm_attn: bfloat16 [2, 768], P(None, ('context', 'dp')), may hold values from 0.5 to 1.5
- w_query: bfloat16 [2, 768, 768], P(None, ('context', 'dp')), may hold values from -0.3125 to 0.3125
- w_key: bfloat16 [2, 768, 768], P(None, ('context', 'dp')), may hold values from -0.3125 to 0.3125
- w_value: bfloat16 [2, 768, 768], P(None, ('context', 'dp')), may hold values from -0.21875 to 0.21875
- w_out: bfloat16 [2, 768, 768], P(None, ('context', 'dp')), may hold values from -1.75 to 1.75
- norm_moe: bfloat16 [2, 768], P(None, ('context', 'dp')), may hold values from 0.5 to 1.5
- w_router: bfloat16 [2, 768, 12], P(None, ('context', 'dp')), may hold values from -0.109375 to 0.109375
- w_res: bfloat16 [2, 12, 12], replicated, may hold values from -1.75 to 1.75
- w_const: bfloat16 [2, 2, 768, 2], P(None, None, ('context', 'dp')), may hold values from -0.21875 to 0.21875
- const_vec: bfloat16 [2, 2, 768], P(None, None, ('context', 'dp')), may hold values from -5 to 5
- w_gate: bfloat16 [2, 8, 768, 2048], P(None, 'expert', ('context', 'dp')), may hold values from -0.21875 to 0.21875
- w_up: bfloat16 [2, 8, 768, 2048], P(None, 'expert', ('context', 'dp')), may hold values from -0.21875 to 0.21875
- w_down: bfloat16 [2, 8, 2048, 768], P(None, 'expert', ('context', 'dp')), may hold values from -0.125 to 0.125
Outputs:
- hidden_out: bfloat16 [2, 16, 2048, 768], P(None, ('expert', 'dp'), 'context')
- hidden_grad: bfloat16 [2, 16, 2048, 768], P(None, ('expert', 'dp'), 'context')
- norm_attn_grad: float32 [2, 768], P(None, ('context', 'dp'))
- query_grad: float32 [2, 768, 768], P(None, ('context', 'dp'))
- key_grad: float32 [2, 768, 768], P(None, ('context', 'dp'))
- value_grad: float32 [2, 768, 768], P(None, ('context', 'dp'))
- proj_out_grad: float32 [2, 768, 768], P(None, ('context', 'dp'))
- norm_moe_grad: float32 [2, 768], P(None, ('context', 'dp'))
- router_grad: float32 [2, 768, 12], P(None, ('context', 'dp'))
- gate_res_grad: float32 [2, 12, 12], replicated
- const_grad: float32 [2, 2, 768, 2], P(None, None, ('context', 'dp'))
- vector_grad: float32 [2, 2, 768], P(None, None, ('context', 'dp'))
- gate_grad: float32 [2, 8, 768, 2048], P(None, 'expert', ('context', 'dp'))
- up_grad: float32 [2, 8, 768, 2048], P(None, 'expert', ('context', 'dp'))
- down_grad: float32 [2, 8, 2048, 768], P(None, 'expert', ('context', 'dp'))
Inputs may be any that keep to these rules, and one draw needn't show every extreme that they name: `routes`: each token names 2 different experts; numbers below 8 are feed-forward experts, 8 the zero expert, 9 the copy expert, the rest constant experts; within each aligned block of 1024 positions of a sequence no number is named more than 256 times, a bound that some block reaches. `segments`: document numbers never fall along a sequence.
All inputs are finite; a program needn't handle non-finite values.
Results may differ from a plain program's by a relative error of at most 0.028.
Values may be sent and summed in bfloat16 or wider, within the bound.
No kernel may reach another device: no remote copies, remote signals or barrier semaphores. Data moves between devices by JAX's collectives and lax.ppermute only.
A program may use at most 1.125 GiB of HBM per device.

v0:
```python
import jax
import jax.numpy as jnp
from jax import lax
from jax.sharding import PartitionSpec as P

HEADS = 12
EXPERTS = 8
TOP = 2
WINDOW = 1024
ROUTED = 12


norm_eps = 1e-05
masked = -1000000000.0
highest = lax.Precision.HIGHEST


def passed_along(block, axis, distance):
    devices = range(lax.axis_size(axis))
    route = [(i - distance, i) for i in devices if i - distance in devices]
    return lax.ppermute(block, axis, route)


def rms_norm(rows_in, gain_vec):
    return (
        rows_in
        * lax.rsqrt(jnp.mean(rows_in * rows_in, axis=-1, keepdims=True) + norm_eps)
        * gain_vec
    )


def mixture(
    normed, normed_low, earlier, router_w, residual_w, const_w, const_v, expert_rows, chosen_onehot
):
    logits = jnp.dot(normed_low, router_w, precision=highest) + jnp.dot(
        earlier, residual_w, precision=highest
    )
    chosen = jnp.sum(chosen_onehot * logits[:, None, :], axis=-1)
    gate_vals = jax.nn.softmax(chosen, axis=-1)
    mix_weights = jax.nn.softmax(
        jnp.einsum("td,jdk->tjk", normed_low, const_w, precision=highest), axis=-1
    )
    constant = (
        mix_weights[:, :, 0:1] * normed[:, None, :] + mix_weights[:, :, 1:2] * const_v[None, :, :]
    )
    copied = chosen_onehot[:, :, EXPERTS + 1 : EXPERTS + 2] * normed[:, None, :]
    outputs = (
        expert_rows
        + copied
        + jnp.einsum(
            "tkj,tjd->tkd", chosen_onehot[:, :, EXPERTS + 2 :], constant, precision=highest
        )
    )
    return (jnp.sum(gate_vals[:, :, None] * outputs, axis=1), logits)


def matmul_f32(left_op, right_op):
    return jnp.dot(left_op, right_op, preferred_element_type=jnp.float32)


def fetch_layer(local_params, current_layer_index):
    (
        attn_gain,
        query_w,
        key_w,
        value_w,
        out_w,
        moe_gain,
        router_w,
        const_w,
        const_v,
        gate_w,
        up_w,
        down_w,
    ) = local_params
    return (
        lax.all_gather(attn_gain[current_layer_index], ("context", "dp"), axis=0, tiled=True),
        lax.all_gather(query_w[current_layer_index], ("context", "dp"), axis=0, tiled=True),
        lax.all_gather(key_w[current_layer_index], ("context", "dp"), axis=0, tiled=True),
        lax.all_gather(value_w[current_layer_index], ("context", "dp"), axis=0, tiled=True),
        lax.all_gather(out_w[current_layer_index], ("context", "dp"), axis=0, tiled=True),
        lax.all_gather(moe_gain[current_layer_index], ("context", "dp"), axis=0, tiled=True),
        lax.all_gather(router_w[current_layer_index], ("context", "dp"), axis=0, tiled=True),
        lax.all_gather(const_w[current_layer_index], ("context", "dp"), axis=1, tiled=True),
        lax.all_gather(const_v[current_layer_index], ("context", "dp"), axis=1, tiled=True),
        lax.all_gather(gate_w[current_layer_index], ("context", "dp"), axis=1, tiled=True),
        lax.all_gather(up_w[current_layer_index], ("context", "dp"), axis=1, tiled=True),
        lax.all_gather(down_w[current_layer_index], ("context", "dp"), axis=1, tiled=True),
    )


def layer_reducer(layer_grads):
    (
        g_attn_gain,
        g_query,
        g_key,
        g_value,
        g_out,
        g_moe_gain,
        g_router,
        g_const,
        g_vector,
        g_gate,
        g_up,
        g_down,
        g_residual,
    ) = layer_grads
    shards = (
        lax.psum_scatter(
            g_attn_gain.astype(jnp.bfloat16), ("context", "dp"), scatter_dimension=0, tiled=True
        ).astype(jnp.float32),
        lax.psum_scatter(
            g_query.astype(jnp.bfloat16), ("context", "dp"), scatter_dimension=0, tiled=True
        ).astype(jnp.float32),
        lax.psum_scatter(
            g_key.astype(jnp.bfloat16), ("context", "dp"), scatter_dimension=0, tiled=True
        ).astype(jnp.float32),
        lax.psum_scatter(
            g_value.astype(jnp.bfloat16), ("context", "dp"), scatter_dimension=0, tiled=True
        ).astype(jnp.float32),
        lax.psum_scatter(
            g_out.astype(jnp.bfloat16), ("context", "dp"), scatter_dimension=0, tiled=True
        ).astype(jnp.float32),
        lax.psum_scatter(
            g_moe_gain.astype(jnp.bfloat16), ("context", "dp"), scatter_dimension=0, tiled=True
        ).astype(jnp.float32),
        lax.psum_scatter(
            g_router.astype(jnp.bfloat16), ("context", "dp"), scatter_dimension=0, tiled=True
        ).astype(jnp.float32),
        lax.psum_scatter(
            g_const.astype(jnp.bfloat16), ("context", "dp"), scatter_dimension=1, tiled=True
        ).astype(jnp.float32),
        lax.psum_scatter(
            g_vector.astype(jnp.bfloat16), ("context", "dp"), scatter_dimension=1, tiled=True
        ).astype(jnp.float32),
        lax.psum_scatter(
            g_gate.astype(jnp.bfloat16), ("context", "dp"), scatter_dimension=1, tiled=True
        ).astype(jnp.float32),
        lax.psum_scatter(
            g_up.astype(jnp.bfloat16), ("context", "dp"), scatter_dimension=1, tiled=True
        ).astype(jnp.float32),
        lax.psum_scatter(
            g_down.astype(jnp.bfloat16), ("context", "dp"), scatter_dimension=1, tiled=True
        ).astype(jnp.float32),
    )
    dense_part = (
        lax.psum(shards[0].astype(jnp.bfloat16), "expert").astype(jnp.float32),
        lax.psum(shards[1].astype(jnp.bfloat16), "expert").astype(jnp.float32),
        lax.psum(shards[2].astype(jnp.bfloat16), "expert").astype(jnp.float32),
        lax.psum(shards[3].astype(jnp.bfloat16), "expert").astype(jnp.float32),
        lax.psum(shards[4].astype(jnp.bfloat16), "expert").astype(jnp.float32),
        lax.psum(shards[5].astype(jnp.bfloat16), "expert").astype(jnp.float32),
        lax.psum(shards[6].astype(jnp.bfloat16), "expert").astype(jnp.float32),
        lax.psum(shards[7].astype(jnp.bfloat16), "expert").astype(jnp.float32),
        lax.psum(shards[8].astype(jnp.bfloat16), "expert").astype(jnp.float32),
    )
    residual_total = lax.psum(g_residual, ("expert", "context", "dp"))
    return tuple(dense_part) + (shards[9], shards[10], shards[11], residual_total)


def routing_tables(route_ids, capacity, expert_groups):
    block_len = route_ids.shape[0]
    flat = route_ids.reshape(-1)
    onehot = (flat[:, None] == jnp.arange(ROUTED, dtype=jnp.int32)[None, :]).astype(jnp.int32)
    slot_rank = jnp.sum((jnp.cumsum(onehot, axis=0) - onehot) * onehot, axis=1)
    per_dev = EXPERTS // expert_groups
    slot_index = flat % per_dev * expert_groups * capacity + flat // per_dev * capacity + slot_rank
    route_table = (
        slot_index[None, :] == jnp.arange(EXPERTS * capacity, dtype=jnp.int32)[:, None]
    ) & (flat < EXPERTS)[None, :]
    return route_table.astype(jnp.bfloat16).reshape(EXPERTS * capacity, block_len, TOP)


def window_mask(seg_full, block_start, block_len, hop_count):
    query_place = block_start + jnp.arange(block_len, dtype=jnp.int32)
    key_place = (
        block_start
        - hop_count * block_len
        + jnp.arange((hop_count + 1) * block_len, dtype=jnp.int32)
    )
    seg_query = lax.dynamic_slice_in_dim(seg_full, block_start, block_len, 0)
    seg_key = jnp.take(seg_full, jnp.clip(key_place, 0, seg_full.shape[0] - 1))
    allowed = (key_place[None, :] >= 0) & (key_place[None, :] <= query_place[:, None])
    return (
        allowed
        & (query_place[:, None] - key_place[None, :] < WINDOW)
        & (seg_query[:, None] == seg_key[None, :])
    )


def head_views(query_low, all_kv):
    block_len, model_width = query_low.shape
    span = all_kv.shape[1]
    head_dim = model_width // HEADS
    query_heads = query_low.reshape(block_len, HEADS, head_dim)
    key_heads = all_kv[0].reshape(span, HEADS, head_dim)
    value_heads = all_kv[1].reshape(span, HEADS, head_dim)
    return (query_heads, key_heads, value_heads, head_dim ** (-0.5))


def attention_forward(query_low, all_kv, window_ok):
    block_len, model_width = query_low.shape
    query_heads, key_heads, value_heads, scale_factor = head_views(query_low, all_kv)
    scores = (
        jnp.einsum("qhd,khd->hqk", query_heads, key_heads, preferred_element_type=jnp.float32)
        * scale_factor
    )
    scores = jnp.where(window_ok[None], scores, masked)
    row_max = jnp.max(scores, axis=-1, keepdims=True)
    exponent = jnp.exp(scores - row_max)
    row_sum = jnp.sum(exponent, axis=-1, keepdims=True)
    prob_low = (exponent / row_sum).astype(jnp.bfloat16)
    out_heads = jnp.einsum(
        "hqk,khd->qhd", prob_low, value_heads, preferred_element_type=jnp.float32
    )
    return (out_heads.reshape(block_len, model_width).astype(jnp.bfloat16), row_max, row_sum)


def attention_backward(query_low, all_kv, window_ok, row_max, row_sum, grad_att):
    block_len, model_width = query_low.shape
    span = all_kv.shape[1]
    query_heads, key_heads, value_heads, scale_factor = head_views(query_low, all_kv)
    scores = (
        jnp.einsum("qhd,khd->hqk", query_heads, key_heads, preferred_element_type=jnp.float32)
        * scale_factor
    )
    scores = jnp.where(window_ok[None], scores, masked)
    prob_f32 = jnp.exp(scores - row_max) / row_sum
    prob_low = prob_f32.astype(jnp.bfloat16)
    grad_heads = grad_att.reshape(block_len, HEADS, model_width // HEADS)
    grad_probs = jnp.einsum(
        "qhd,khd->hqk", grad_heads, value_heads, preferred_element_type=jnp.float32
    )
    row_delta = jnp.sum(prob_f32 * grad_probs, axis=-1, keepdims=True)
    grad_scores = (prob_f32 * (grad_probs - row_delta)).astype(jnp.bfloat16)
    grad_query = (
        jnp.einsum("hqk,khd->qhd", grad_scores, key_heads, preferred_element_type=jnp.float32)
        * scale_factor
    )
    grad_key = (
        jnp.einsum("hqk,qhd->khd", grad_scores, query_heads, preferred_element_type=jnp.float32)
        * scale_factor
    )
    grad_value = jnp.einsum(
        "hqk,qhd->khd", prob_low, grad_heads, preferred_element_type=jnp.float32
    )
    grad_kv = jnp.stack(
        [grad_key.reshape(span, model_width), grad_value.reshape(span, model_width)]
    )
    return (grad_query.reshape(block_len, model_width), grad_kv)


def layer_forward(
    hidden, earlier, layer_w, route_table, chosen_onehot, window_ok, hop_count, expert_groups
):
    (
        attn_gain,
        query_w,
        key_w,
        value_w,
        out_w,
        moe_gain,
        router_w,
        const_w,
        const_v,
        gate_w,
        up_w,
        down_w,
        residual_w,
    ) = layer_w
    block_len, model_width = hidden.shape
    capacity = route_table.shape[0] // EXPERTS
    per_dev = EXPERTS // expert_groups
    normed_attn = rms_norm(hidden, attn_gain.astype(jnp.float32)).astype(jnp.bfloat16)
    query_low = matmul_f32(normed_attn, query_w).astype(jnp.bfloat16)
    key_val = jnp.stack([matmul_f32(normed_attn, key_w), matmul_f32(normed_attn, value_w)]).astype(
        jnp.bfloat16
    )
    pieces = []
    for hop_index in range(hop_count, 0, -1):
        pieces.append(passed_along(key_val, "context", hop_index))
    all_kv = jnp.concatenate(pieces + [key_val], axis=1)
    attended, row_max, row_sum = attention_forward(query_low, all_kv, window_ok)
    mid_rows = hidden + matmul_f32(attended, out_w)
    normed = rms_norm(mid_rows, moe_gain.astype(jnp.float32))
    normed_low = normed.astype(jnp.bfloat16)
    send_rows = jnp.einsum(
        "stk,td->sd", route_table, normed_low, preferred_element_type=jnp.float32
    ).astype(jnp.bfloat16)
    arrived = lax.all_to_all(
        send_rows.reshape(per_dev, expert_groups, capacity, model_width),
        "expert",
        split_axis=1,
        concat_axis=1,
        tiled=True,
    )
    inputs = arrived.reshape(per_dev, expert_groups * capacity, model_width)
    gate_pre = jnp.einsum("jrd,jdf->jrf", inputs, gate_w, preferred_element_type=jnp.float32)
    up_pre = jnp.einsum("jrd,jdf->jrf", inputs, up_w, preferred_element_type=jnp.float32)
    activated = (jax.nn.silu(gate_pre) * up_pre).astype(jnp.bfloat16)
    produced = jnp.einsum(
        "jrf,jfd->jrd", activated, down_w, preferred_element_type=jnp.float32
    ).astype(jnp.bfloat16)
    returned = lax.all_to_all(
        produced.reshape(per_dev, expert_groups, capacity, model_width),
        "expert",
        split_axis=1,
        concat_axis=1,
        tiled=True,
    )
    expert_rows = jnp.einsum(
        "stk,sd->tkd",
        route_table,
        returned.reshape(-1, model_width),
        preferred_element_type=jnp.float32,
    )
    mixed_out, logits = mixture(
        normed,
        normed_low.astype(jnp.float32),
        earlier,
        router_w.astype(jnp.float32),
        residual_w,
        const_w.astype(jnp.float32),
        const_v.astype(jnp.float32),
        expert_rows,
        chosen_onehot,
    )
    kept_state = (
        hidden,
        normed_attn,
        query_low,
        all_kv,
        attended,
        row_max,
        row_sum,
        mid_rows,
        normed,
        normed_low,
        earlier,
        expert_rows,
        inputs,
        gate_pre,
        up_pre,
        activated,
    )
    return (mid_rows + mixed_out, logits, kept_state)


def layer_backward(
    kept_state,
    layer_w,
    grad_out,
    grad_logits,
    route_table,
    chosen_onehot,
    window_ok,
    hop_count,
    expert_groups,
):
    (
        attn_gain,
        query_w,
        key_w,
        value_w,
        out_w,
        moe_gain,
        router_w,
        const_w,
        const_v,
        gate_w,
        up_w,
        down_w,
        residual_w,
    ) = layer_w
    (
        hidden,
        normed_attn,
        query_low,
        all_kv,
        attended,
        row_max,
        row_sum,
        mid_rows,
        normed,
        normed_low,
        earlier,
        expert_rows,
        inputs,
        gate_pre,
        up_pre,
        activated,
    ) = kept_state
    block_len, model_width = hidden.shape
    capacity = route_table.shape[0] // EXPERTS
    per_dev, rows_dev, unused_width = inputs.shape

    def mix_local(norm_full, norm_lowf, prior, router_f, residual_f, const_f, vector_f, rows_f):
        return mixture(
            norm_full,
            norm_lowf,
            prior,
            router_f,
            residual_f,
            const_f,
            vector_f,
            rows_f,
            chosen_onehot,
        )

    unused_out, mix_pull = jax.vjp(
        mix_local,
        normed,
        normed_low.astype(jnp.float32),
        earlier,
        router_w.astype(jnp.float32),
        residual_w,
        const_w.astype(jnp.float32),
        const_v.astype(jnp.float32),
        expert_rows,
    )
    d_full, d_low, d_prior, d_router, d_residual, d_const, d_vector, d_rows = mix_pull(
        (grad_out, grad_logits)
    )
    grad_send = jnp.einsum(
        "stk,tkd->sd", route_table, d_rows.astype(jnp.bfloat16), preferred_element_type=jnp.float32
    ).astype(jnp.bfloat16)
    grad_prod = lax.all_to_all(
        grad_send.reshape(per_dev, expert_groups, capacity, model_width),
        "expert",
        split_axis=1,
        concat_axis=1,
        tiled=True,
    ).reshape(per_dev, rows_dev, model_width)
    grad_act = jnp.einsum("jrd,jfd->jrf", grad_prod, down_w, preferred_element_type=jnp.float32)
    g_down = jnp.einsum("jrf,jrd->jfd", activated, grad_prod, preferred_element_type=jnp.float32)
    sigmoid_val = jax.nn.sigmoid(gate_pre)
    swish_val = gate_pre * sigmoid_val
    grad_gate = (grad_act * up_pre * sigmoid_val * (1.0 + gate_pre * (1.0 - sigmoid_val))).astype(
        jnp.bfloat16
    )
    grad_up = (grad_act * swish_val).astype(jnp.bfloat16)
    g_gate = jnp.einsum("jrd,jrf->jdf", inputs, grad_gate, preferred_element_type=jnp.float32)
    g_up = jnp.einsum("jrd,jrf->jdf", inputs, grad_up, preferred_element_type=jnp.float32)
    grad_in = jnp.einsum("jrf,jdf->jrd", grad_gate, gate_w, preferred_element_type=jnp.float32)
    grad_in = (
        grad_in + jnp.einsum("jrf,jdf->jrd", grad_up, up_w, preferred_element_type=jnp.float32)
    ).astype(jnp.bfloat16)
    back_rows = lax.all_to_all(
        grad_in.reshape(per_dev, expert_groups, capacity, model_width),
        "expert",
        split_axis=1,
        concat_axis=1,
        tiled=True,
    )
    grad_normed = (
        d_full
        + d_low
        + jnp.einsum(
            "stk,sd->td",
            route_table,
            back_rows.reshape(-1, model_width),
            preferred_element_type=jnp.float32,
        )
    )
    unused_norm, moe_pull = jax.vjp(rms_norm, mid_rows, moe_gain.astype(jnp.float32))
    d_mid, g_moe_gain = moe_pull(grad_normed)
    grad_mid = grad_out + d_mid
    g_out = jnp.dot(attended.astype(jnp.float32).T, grad_mid, precision=highest)
    grad_att = jnp.dot(grad_mid, out_w.astype(jnp.float32).T, precision=highest).astype(
        jnp.bfloat16
    )
    grad_query, grad_kv = attention_backward(
        query_low, all_kv, window_ok, row_max, row_sum, grad_att
    )
    own_grad = grad_kv[:, hop_count * block_len :]
    for hop_index in range(1, hop_count + 1):
        piece_start = (hop_count - hop_index) * block_len
        own_grad = own_grad + passed_along(
            grad_kv[:, piece_start : piece_start + block_len].astype(jnp.bfloat16),
            "context",
            -hop_index,
        ).astype(jnp.float32)
    grad_kv_low = own_grad.astype(jnp.bfloat16)
    grad_query_low = grad_query.astype(jnp.bfloat16)
    g_query = matmul_f32(normed_attn.T, grad_query_low)
    g_key = matmul_f32(normed_attn.T, grad_kv_low[0])
    g_value = matmul_f32(normed_attn.T, grad_kv_low[1])
    grad_attn_in = (
        matmul_f32(grad_query_low, query_w.T)
        + matmul_f32(grad_kv_low[0], key_w.T)
        + matmul_f32(grad_kv_low[1], value_w.T)
    )
    unused_attn, attn_pull = jax.vjp(rms_norm, hidden, attn_gain.astype(jnp.float32))
    d_hidden, g_attn_gain = attn_pull(grad_attn_in)
    layer_grads = (
        g_attn_gain,
        g_query,
        g_key,
        g_value,
        g_out,
        g_moe_gain,
        d_router,
        d_const,
        d_vector,
        g_gate,
        g_up,
        g_down,
        d_residual,
    )
    return (grad_mid + d_hidden, d_prior, layer_grads)


def per_device(
    hidden_in,
    segments,
    routes,
    prev_logits,
    out_grad,
    norm_attn,
    w_query,
    w_key,
    w_value,
    w_out,
    norm_moe,
    w_router,
    w_res,
    w_const,
    const_vec,
    w_gate,
    w_up,
    w_down,
):
    micro_count = hidden_in.shape[0]
    block_len = hidden_in.shape[2]
    expert_groups = lax.axis_size("expert")
    ctx_count = lax.axis_size("context")
    hop_count = min((WINDOW + block_len - 2) // block_len, ctx_count - 1)
    capacity = block_len // 4
    block_start = lax.axis_index("context") * block_len
    count_of_layers = norm_attn.shape[0]
    local_params = (
        norm_attn,
        w_query,
        w_key,
        w_value,
        w_out,
        norm_moe,
        w_router,
        w_const,
        const_vec,
        w_gate,
        w_up,
        w_down,
    )
    residual_f = w_res.astype(jnp.float32)
    fetched = [
        fetch_layer(local_params, current_layer_index)
        for current_layer_index in range(count_of_layers)
    ]
    grand_totals = None
    results = []
    grads_in = []
    for micro_index in range(micro_count):
        hidden = hidden_in[micro_index, 0].astype(jnp.float32)
        earlier = prev_logits[micro_index, 0]
        route_ids = routes[micro_index, 0]
        route_table = routing_tables(route_ids, capacity, expert_groups)
        chosen_onehot = (
            route_ids[:, :, None] == jnp.arange(ROUTED, dtype=jnp.int32)[None, None, :]
        ).astype(jnp.float32)
        window_ok = window_mask(segments[micro_index, 0], block_start, block_len, hop_count)
        saved_layers = []
        weight_sets = []
        for current_layer_index in range(count_of_layers):
            layer_w = tuple(fetched[current_layer_index]) + (residual_f[current_layer_index],)
            weight_sets.append(layer_w)
            hidden, earlier, kept_state = layer_forward(
                hidden,
                earlier,
                layer_w,
                route_table,
                chosen_onehot,
                window_ok,
                hop_count,
                expert_groups,
            )
            saved_layers.append(kept_state)
        results.append(hidden.astype(jnp.bfloat16))
        grad_hidden = out_grad[micro_index, 0].astype(jnp.float32)
        grad_logits = jnp.zeros_like(earlier)
        layerwise_values = [None] * count_of_layers
        for current_layer_index in range(count_of_layers - 1, -1, -1):
            grad_hidden, grad_logits, layerwise_values[current_layer_index] = layer_backward(
                saved_layers[current_layer_index],
                weight_sets[current_layer_index],
                grad_hidden,
                grad_logits,
                route_table,
                chosen_onehot,
                window_ok,
                hop_count,
                expert_groups,
            )
        grads_in.append(grad_hidden.astype(jnp.bfloat16))
        summand_terms = [
            layer_reducer(layerwise_values[current_layer_index])
            for current_layer_index in range(count_of_layers)
        ]
        if grand_totals is None:
            grand_totals = summand_terms
        else:
            grand_totals = [
                tuple(
                    (
                        running_total + summand_term
                        for running_total, summand_term in zip(
                            grand_totals[current_layer_index], summand_terms[current_layer_index]
                        )
                    )
                )
                for current_layer_index in range(count_of_layers)
            ]
    stacked = tuple(
        (
            jnp.stack(
                [
                    grand_totals[current_layer_index][slot_pos]
                    for current_layer_index in range(count_of_layers)
                ]
            )
            for slot_pos in range(13)
        )
    )
    hidden_out = jnp.stack(results)[:, None]
    hidden_grad = jnp.stack(grads_in)[:, None]
    return (
        hidden_out,
        hidden_grad,
        stacked[0],
        stacked[1],
        stacked[2],
        stacked[3],
        stacked[4],
        stacked[5],
        stacked[6],
        stacked[12],
        stacked[7],
        stacked[8],
        stacked[9],
        stacked[10],
        stacked[11],
    )


def solution(mesh):
    placed = (
        P(None, ("expert", "dp"), "context", None),
        P(None, ("expert", "dp"), None),
        P(None, ("expert", "dp"), "context", None),
        P(None, ("expert", "dp"), "context", None),
        P(None, ("expert", "dp"), "context", None),
        P(None, ("context", "dp")),
        P(None, ("context", "dp"), None),
        P(None, ("context", "dp"), None),
        P(None, ("context", "dp"), None),
        P(None, ("context", "dp"), None),
        P(None, ("context", "dp")),
        P(None, ("context", "dp"), None),
        P(),
        P(None, None, ("context", "dp"), None),
        P(None, None, ("context", "dp")),
        P(None, "expert", ("context", "dp"), None),
        P(None, "expert", ("context", "dp"), None),
        P(None, "expert", ("context", "dp"), None),
    )
    return jax.shard_map(
        per_device,
        mesh=mesh,
        in_specs=placed,
        out_specs=(
            P(None, ("expert", "dp"), "context", None),
            P(None, ("expert", "dp"), "context", None),
            P(None, ("context", "dp")),
            P(None, ("context", "dp"), None),
            P(None, ("context", "dp"), None),
            P(None, ("context", "dp"), None),
            P(None, ("context", "dp"), None),
            P(None, ("context", "dp")),
            P(None, ("context", "dp"), None),
            P(),
            P(None, None, ("context", "dp"), None),
            P(None, None, ("context", "dp")),
            P(None, "expert", ("context", "dp"), None),
            P(None, "expert", ("context", "dp"), None),
            P(None, "expert", ("context", "dp"), None),
        ),
        check_vma=False,
    )
```

profile of v0, /device:TPU:2, one launch (start us, length us, event | category | flops | bytes accessed | tf_op | source)
XLA Modules:
  0.0 4349.5 jit_solution(644427712082936349)
XLA Ops:
  126.3 73.6 %collective-permute-done = bf16[2,1024,768]{2,1,0:T(8,128)(2,1)} collective-permute-done((bf16[2,1024,768]{2,1,0:T(8,128)(2,1)}, bf16[2,1024,768]{2,1,0:T(8,128)(2,1)}, u32[]{:S(2)}, u32[]{:S(2)}) %collective-permute-start) | collective-permute-done | bytes 3145760 | tf_op jit(solution)/shard_map/ppermute | solution.py:21
  212.5 90.3 %collective-permute-done.2 = bf16[2,1024,768]{2,1,0:T(8,128)(2,1)} collective-permute-done((bf16[2,1024,768]{2,1,0:T(8,128)(2,1)}, bf16[2,1024,768]{2,1,0:T(8,128)(2,1)}, u32[]{:S(2)}, u32[]{:S(2)}) %collective-permute-start.2) | collective-permute-done | bytes 3145760 | tf_op jit(solution)/shard_map/ppermute | solution.py:21
  315.9 43.1 fusion.471
  359.0 35.2 fusion.245
  394.2 41.4 fusion.470
  435.6 34.7 fusion.251
  494.8 68.0 %all-to-all-done = bf16[2,4,256,768]{3,2,0,1:T(8,128)(2,1)} async-done(((bf16[2,4,256,768]{3,2,0,1:T(8,128)(2,1)}), bf16[2,4,256,768]{3,2,0,1:T(8,128)(2,1)}, u32[]{:S(2)}, u32[]{:S(2)}) %all-to-all-start) | async-done | bytes 3145760 | tf_op jit(solution)/shard_map/all_to_all | solution.py:290
  580.0 17.8 multiply_convert_fusion.15
  675.1 18.4 fusion.478
  747.9 97.4 %all-gather.18 = bf16[1,768,12]{2,0,1:T(2,128)(2,1)S(1)} all-gather(bf16[1,96,12]{2,0,1:T(2,128)(2,1)S(1)} %copy.1240), channel_id=20, replica_groups=mesh['expert'=4,'context'=2,'dp'=4] {'context','dp'}, dimensions={1}, use_global_device_ids=true | all-gather | bytes 20736 | tf_op jit(solution)/shard_map/all_gather | solution.py:83
  884.9 42.6 fusion.473
  927.5 35.1 fusion.248
  1041.5 16.7 all-to-all-done.8
  1063.3 17.7 multiply_convert_fusion.13
  1098.1 35.5 all-to-all-done.2
  1162.3 26.1 multiply_convert_fusion.11
  1300.7 18.4 fusion.479
  1344.9 16.8 multiply_reduce_fusion.23
  1384.8 64.7 %multiply_reduce_fusion.3 = (f32[12,1024]{1,0:T(8,128)S(1)}, f32[12,1024,2048]{2,1,0:T(8,128)}) fusion(f32[12,1024,2048]{2,1,0:T(8,128)} %get-tuple-element.331, f32[12,1024]{1,0:T(8,128)S(1)} %copy-done.282, bf16[1024,12,64]{0,2,1:T(8,128)(2,1)} %bitcast.1110, bf16[2048,12,64]{0,2,1:T(8,128)(2,1)S(1)} %bitcast.1023), kind=kOutput, calls=%fused_computation.17 | convolution fusion | flops 3296710656 | bytes 206143488 | tf_op jit(solution)/shard_map/qhd,khd->hqk/dot_general | solution.py:231
  1449.5 78.2 %multiply_convert_fusion.3 = bf16[12,1024,2048]{2,1,0:T(8,128)(2,1)} fusion(f32[12,1024,2048]{2,1,0:T(8,128)} %get-tuple-element.338, f32[12,1024]{1,0:T(8,128)S(1)} %get-tuple-element.337, f32[12,1024,2048]{2,1,0:T(8,128)} %get-tuple-element.331, f32[12,1024]{1,0:T(8,128)S(1)} %copy-done.282), kind=kLoop, calls=%fused_computation.16 | loop fusion | flops 100663296 | bytes 251756544 | tf_op jit(solution)/shard_map/convert_element_type | solution.py:235
  1527.7 32.4 fusion.32
  1560.2 20.9 convolution_multiply_fusion.3
  1595.7 22.2 multiply_convert_fusion.27
  1619.3 36.3 collective-permute-done.4
  1683.0 17.6 fusion.484
  1730.5 18.4 fusion.480
  1792.0 55.8 %collective-permute-done.3 = bf16[2,1024,768]{2,1,0:T(8,128)(2,1)} collective-permute-done((bf16[2,1024,768]{2,1,0:T(8,128)(2,1)}, bf16[2,1024,768]{2,1,0:T(8,128)(2,1)}, u32[]{:S(2)}, u32[]{:S(2)}) %collective-permute-start.3) | collective-permute-done | bytes 3145760 | tf_op jit(solution)/shard_map/ppermute | solution.py:21
  1860.7 42.6 fusion.476
  1903.2 35.1 fusion.254
  1969.1 60.5 %all-to-all-done.12 = bf16[2,4,256,768]{3,2,0,1:T(8,128)(2,1)} async-done(((bf16[2,4,256,768]{3,2,0,1:T(8,128)(2,1)}), bf16[2,4,256,768]{3,2,0,1:T(8,128)(2,1)}, u32[]{:S(2)}, u32[]{:S(2)}) %all-to-all-start.12) | async-done | bytes 3145760 | tf_op jit(solution)/shard_map/all_to_all | solution.py:427
  2058.7 45.7 %all-to-all-done.6 = bf16[2,4,256,768]{3,2,0,1:T(8,128)(2,1)} async-done(((bf16[2,4,256,768]{3,2,0,1:T(8,128)(2,1)}), bf16[2,4,256,768]{3,2,0,1:T(8,128)(2,1)}, u32[]{:S(2)}, u32[]{:S(2)}) %all-to-all-start.6) | async-done | bytes 3145760 | tf_op jit(solution)/shard_map/all_to_all | solution.py:290
  2130.1 25.9 multiply_convert_fusion.7
  2267.5 18.4 fusion.481
  2345.2 34.8 fusion.24
  2380.0 64.7 %multiply_reduce_fusion.1 = (f32[12,1024]{1,0:T(8,128)S(1)}, f32[12,1024,2048]{2,1,0:T(8,128)}) fusion(f32[12,1024,2048]{2,1,0:T(8,128)} %get-tuple-element.347, f32[12,1024]{1,0:T(8,128)S(1)} %copy-done.280, bf16[1024,12,64]{0,2,1:T(8,128)(2,1)} %bitcast.1113, bf16[2048,12,64]{0,2,1:T(8,128)(2,1)S(1)} %bitcast.1019), kind=kOutput, calls=%fused_computation.13 | convolution fusion | flops 3296710656 | bytes 206143488 | tf_op jit(solution)/shard_map/qhd,khd->hqk/dot_general | solution.py:231
  2444.8 77.9 %multiply_convert_fusion.1 = bf16[12,1024,2048]{2,1,0:T(8,128)(2,1)} fusion(f32[12,1024,2048]{2,1,0:T(8,128)} %get-tuple-element.354, f32[12,1024]{1,0:T(8,128)S(1)} %get-tuple-element.353, f32[12,1024,2048]{2,1,0:T(8,128)} %get-tuple-element.347, f32[12,1024]{1,0:T(8,128)S(1)} %copy-done.280), kind=kLoop, calls=%fused_computation.12 | loop fusion | flops 100663296 | bytes 251756544 | tf_op jit(solution)/shard_map/convert_element_type | solution.py:235
  2522.7 18.8 convolution_multiply_fusion.1
  2551.6 22.5 multiply_convert_fusion.25
  2575.6 42.4 collective-permute-done.6
  2645.6 17.5 fusion.488
  2805.4 56.4 %all-to-all-done.10 = bf16[2,4,256,768]{3,2,0,1:T(8,128)(2,1)} async-done(((bf16[2,4,256,768]{3,2,0,1:T(8,128)(2,1)}), bf16[2,4,256,768]{3,2,0,1:T(8,128)(2,1)}, u32[]{:S(2)}, u32[]{:S(2)}) %all-to-all-start.10) | async-done | bytes 3145760 | tf_op jit(solution)/shard_map/all_to_all | solution.py:427
  2879.6 25.8 multiply_convert_fusion.9
  2959.0 24.9 multiply_convert_fusion.5
  3056.6 44.5 %all-to-all-done.15 = bf16[2,4,256,768]{3,2,0,1:T(8,128)(2,1)S(1)} async-done(((bf16[2,4,256,768]{3,2,0,1:T(8,128)(2,1)}), bf16[2,4,256,768]{3,2,0,1:T(8,128)(2,1)S(1)}, u32[]{:S(2)}, u32[]{:S(2)}) %all-to-all-start.15) | async-done | bytes 3145760 | tf_op jit(solution)/shard_map/all_to_all | solution.py:448
  3128.8 38.2 fusion.28
  3167.0 68.5 %multiply_reduce_fusion = (f32[12,1024]{1,0:T(8,128)}, f32[12,1024,2048]{2,1,0:T(8,128)}) fusion(f32[12,1024,2048]{2,1,0:T(8,128)} %get-tuple-element.317, f32[12,1024]{1,0:T(8,128)S(1)} %copy-done.275, bf16[1024,12,64]{0,2,1:T(8,128)(2,1)} %bitcast.1117, bf16[2048,12,64]{0,2,1:T(8,128)(2,1)} %bitcast.999), kind=kOutput, calls=%fused_computation.11 | convolution fusion | flops 3296710656 | bytes 206143488 | tf_op jit(solution)/shard_map/qhd,khd->hqk/dot_general | solution.py:231
  3242.1 65.9 %multiply_reduce_fusion.2 = (f32[12,1024]{1,0:T(8,128)S(1)}, f32[12,1024,2048]{2,1,0:T(8,128)}) fusion(f32[12,1024,2048]{2,1,0:T(8,128)} %get-tuple-element.319, f32[12,1024]{1,0:T(8,128)S(1)} %copy-done.278, bf16[1024,12,64]{0,2,1:T(8,128)(2,1)} %bitcast.1114, bf16[2048,12,64]{0,2,1:T(8,128)(2,1)} %bitcast.997), kind=kOutput, calls=%fused_computation.15 | convolution fusion | flops 3296710656 | bytes 206143488 | tf_op jit(solution)/shard_map/qhd,khd->hqk/dot_general | solution.py:231
  3308.0 35.7 fusion.36
  3348.7 80.0 %multiply_convert_fusion.2 = bf16[12,1024,2048]{2,1,0:T(8,128)(2,1)} fusion(f32[12,1024,2048]{2,1,0:T(8,128)} %get-tuple-element.358, f32[12,1024]{1,0:T(8,128)S(1)} %get-tuple-element.357, f32[12,1024,2048]{2,1,0:T(8,128)} %get-tuple-element.319, f32[12,1024]{1,0:T(8,128)S(1)} %copy-done.278), kind=kLoop, calls=%fused_computation.14 | loop fusion | flops 100663296 | bytes 251756544 | tf_op jit(solution)/shard_map/convert_element_type | solution.py:235
  3428.7 19.4 convolution_multiply_fusion.2
  3459.3 22.5 multiply_convert_fusion.26
  3484.4 79.2 %multiply_convert_fusion = bf16[12,1024,2048]{2,1,0:T(8,128)(2,1)} fusion(f32[12,1024,2048]{2,1,0:T(8,128)} %get-tuple-element.360, f32[12,1024]{1,0:T(8,128)S(1)} %copy-done.283, f32[12,1024,2048]{2,1,0:T(8,128)} %get-tuple-element.317, f32[12,1024]{1,0:T(8,128)S(1)} %copy-done.276), kind=kLoop, calls=%fused_computation.10 | loop fusion | flops 100663296 | bytes 251756544 | tf_op jit(solution)/shard_map/convert_element_type | solution.py:235
  3563.7 23.6 multiply_convert_fusion.24
  3591.2 18.9 convolution_multiply_fusion
  3629.8 65.5 %collective-permute-done.7 = bf16[2,1024,768]{1,2,0:T(8,128)(2,1)} collective-permute-done((bf16[2,1024,768]{1,2,0:T(8,128)(2,1)}, bf16[2,1024,768]{1,2,0:T(8,128)(2,1)}, u32[]{:S(2)}, u32[]{:S(2)}) %collective-permute-start.7) | collective-permute-done | bytes 3145760 | tf_op jit(solution)/shard_map/ppermute | solution.py:21
  3802.0 39.0 all-reduce.20
  3873.2 20.5 all-reduce.21
  3894.3 18.8 all-reduce.23
  3916.5 52.2 %reduce-scatter.115.cloned.1.call-done = bf16[2,256,768]{2,1,0:T(8,128)(2,1)} async-done(((bf16[2,2048,768]{2,1,0:T(8,128)(2,1)}), bf16[2,256,768]{2,1,0:T(8,128)(2,1)}) %reduce-scatter.115.cloned.1.call-update) | async-done | bytes 786448 | tf_op jit(solution)/shard_map/reduce_scatter | solution.py:142
  3972.3 61.4 %reduce-scatter.105.cloned.1.call-done = bf16[2,96,2048]{2,1,0:T(8,128)(2,1)} async-done(((bf16[2,768,2048]{2,1,0:T(8,128)(2,1)}), bf16[2,96,2048]{2,1,0:T(8,128)(2,1)}) %reduce-scatter.105.cloned.1.call-update) | async-done | bytes 786448 | tf_op jit(solution)/shard_map/reduce_scatter | solution.py:139
  4033.7 65.6 %reduce-scatter.107.cloned.1.call-done = bf16[2,96,2048]{2,1,0:T(8,128)(2,1)} async-done(((bf16[2,768,2048]{2,1,0:T(8,128)(2,1)}), bf16[2,96,2048]{2,1,0:T(8,128)(2,1)}) %reduce-scatter.107.cloned.1.call-update) | async-done | bytes 786448 | tf_op jit(solution)/shard_map/reduce_scatter | solution.py:139
  4102.8 61.5 %reduce-scatter.97.cloned.1.call-done = bf16[2,96,2048]{2,1,0:T(8,128)(2,1)} async-done(((bf16[2,768,2048]{2,1,0:T(8,128)(2,1)}), bf16[2,96,2048]{2,1,0:T(8,128)(2,1)}) %reduce-scatter.97.cloned.1.call-update) | async-done | bytes 786448 | tf_op jit(solution)/shard_map/reduce_scatter | solution.py:136
  4164.3 65.5 %reduce-scatter.99.cloned.1.call-done = bf16[2,96,2048]{2,1,0:T(8,128)(2,1)} async-done(((bf16[2,768,2048]{2,1,0:T(8,128)(2,1)}), bf16[2,96,2048]{2,1,0:T(8,128)(2,1)}) %reduce-scatter.99.cloned.1.call-update) | async-done | bytes 786448 | tf_op jit(solution)/shard_map/reduce_scatter | solution.py:136
  4233.3 101.3 %all-reduce.27.cloned.1.call-done = (bf16[96,768]{1,0:T(8,128)(2,1)}, bf16[96,768]{1,0:T(8,128)(2,1)}, bf16[96,768]{1,0:T(8,128)(2,1)}, bf16[96,768]{1,0:T(8,128...) async-done(((bf16[96,768]{1,0:T(8,128)(2,1)}, ...) | async-done | bytes 2359312 | tf_op jit(solution)/shard_map/psum | solution.py:148
  (1548 shorter events, 1590.4 us)
Async XLA Ops:
  7.2 83.6 %all-gather.41.cloned.1.call-start = ((), (), s32[]{:S(2)}) async-start(), calls=%async_computation.85 | async-start | bytes 1327104 | tf_op jit(solution)/shard_map/all_gather | solution.py:80
  9.1 85.7 %all-gather.39.cloned.1.call-start = ((), (), s32[]{:S(2)}) async-start(), calls=%async_computation.84 | async-start | bytes 1327104 | tf_op jit(solution)/shard_map/all_gather | solution.py:79
  11.0 108.5 %all-gather.43.cloned.1.call-start = ((), (), s32[]{:S(2)}) async-start(), calls=%async_computation.86 | async-start | bytes 1327104 | tf_op jit(solution)/shard_map/all_gather | solution.py:78
  12.8 457.6 %all-gather.45.cloned.1.call-start = ((), (), s32[]{:S(2)}) async-start(), calls=%async_computation.87 | async-start | bytes 1327104 | tf_op jit(solution)/shard_map/all_gather | solution.py:81
  14.6 552.0 %all-gather.47.cloned.1.call-start = ((), (), s32[]{:S(2)}) async-start(), calls=%async_computation.88 | async-start | bytes 7077888 | tf_op jit(solution)/shard_map/all_gather | solution.py:86
  16.0 564.0 %all-gather.49.cloned.1.call-start = ((), (), s32[]{:S(2)}) async-start(), calls=%async_computation.89 | async-start | bytes 7077888 | tf_op jit(solution)/shard_map/all_gather | solution.py:87
  17.4 580.5 %all-gather.51.cloned.1.call-start = ((), (), s32[]{:S(2)}) async-start(), calls=%async_computation.90 | async-start | bytes 7077888 | tf_op jit(solution)/shard_map/all_gather | solution.py:88
  19.2 715.5 %all-gather.55.cloned.1.call-start = ((), (), s32[]{:S(2)}) async-start(), calls=%async_computation.92 | async-start | bytes 1327104 | tf_op jit(solution)/shard_map/all_gather | solution.py:80
  20.0 718.0 %all-gather.53.cloned.1.call-start = ((), (), s32[]{:S(2)}) async-start(), calls=%async_computation.91 | async-start | bytes 1327104 | tf_op jit(solution)/shard_map/all_gather | solution.py:79
  99.9 100.0 %collective-permute-start = (bf16[2,1024,768]{2,1,0:T(8,128)(2,1)}, bf16[2,1024,768]{2,1,0:T(8,128)(2,1)}, u32[]{:S(2)}, u32[]{:S(2)}) collective-permute-start(bf16[2,1024,768]{2,1,0:T(8,128)(2,1)} %pad_maximum_fusion.4), channel_id=1, source_target_pairs={{0,4},{1,5},{2,6},{3,7},{8,12},{9,13},{10,14},{11,15},{16,20},{17,... | collective-permute-start | bytes 9437192 | tf_op jit(solution)/shard_map/ppermute | solution.py:21
  109.8 192.9 %collective-permute-start.2 = (bf16[2,1024,768]{2,1,0:T(8,128)(2,1)}, bf16[2,1024,768]{2,1,0:T(8,128)(2,1)}, u32[]{:S(2)}, u32[]{:S(2)}) collective-permute-start(bf16[2,1024,768]{2,1,0:T(8,128)(2,1)} %pad_maximum_fusion.6), channel_id=1, source_target_pairs={{0,4},{1,5},{2,6},{3,7},{8,12},{9,13},{10,14},{11,15},{16,20},{17,... | collective-permute-start | bytes 9437192 | tf_op jit(solution)/shard_map/ppermute | solution.py:21
  492.9 375.1 %all-gather.57.cloned.1.call-start = ((), (), s32[]{:S(2)}) async-start(), calls=%async_computation.93 | async-start | bytes 1327104 | tf_op jit(solution)/shard_map/all_gather | solution.py:78
  493.5 469.2 %all-gather.59.cloned.1.call-start = ((), (), s32[]{:S(2)}) async-start(), calls=%async_computation.94 | async-start | bytes 1327104 | tf_op jit(solution)/shard_map/all_gather | solution.py:81
  494.2 641.5 %all-gather.63.cloned.1.call-start = ((), (), s32[]{:S(2)}) async-start(), calls=%async_computation.96 | async-start | bytes 7077888 | tf_op jit(solution)/shard_map/all_gather | solution.py:87
  610.7 95.0 %all-to-all-start.1 = ((bf16[2,4,256,768]{3,2,0,1:T(8,128)(2,1)}), bf16[2,4,256,768]{3,2,0,1:T(8,128)(2,1)}, u32[]{:S(2)}, u32[]{:S(2)}) async-start(bf16[2,4,256,768]{3,2,0,1:T(8,128)(2,1)} %copy.974), calls=%async_computation.1 | async-start | bytes 6291456 | tf_op jit(solution)/shard_map/all_to_all | solution.py:304
  615.5 533.7 %all-gather.65.cloned.1.call-start = ((), (), s32[]{:S(2)}) async-start(), calls=%async_computation.97 | async-start | bytes 7077888 | tf_op jit(solution)/shard_map/all_gather | solution.py:88
  742.8 129.6 %collective-permute-start.1 = (bf16[2,1024,768]{2,1,0:T(8,128)(2,1)}, bf16[2,1024,768]{2,1,0:T(8,128)(2,1)}, u32[]{:S(2)}, u32[]{:S(2)}) collective-permute-start(bf16[2,1024,768]{2,1,0:T(8,128)(2,1)} %pad_maximum_fusion.5), channel_id=1, source_target_pairs={{0,4},{1,5},{2,6},{3,7},{8,12},{9,13},{10,14},{11,15},{16,20},{17,... | collective-permute-start | bytes 9437192 | tf_op jit(solution)/shard_map/ppermute | solution.py:21
  861.9 120.2 %all-to-all-start.4 = ((bf16[2,4,256,768]{3,2,0,1:T(8,128)(2,1)}), bf16[2,4,256,768]{3,2,0,1:T(8,128)(2,1)}, u32[]{:S(2)}, u32[]{:S(2)}) async-start(bf16[2,4,256,768]{3,2,0,1:T(8,128)(2,1)} %copy.1011), calls=%async_computation.4 | async-start | bytes 6291456 | tf_op jit(solution)/shard_map/all_to_all | solution.py:290
  987.3 175.0 %all-gather.61.cloned.1.call-start = ((), (), s32[]{:S(2)}) async-start(), calls=%async_computation.95 | async-start | bytes 7077888 | tf_op jit(solution)/shard_map/all_gather | solution.py:86
  1277.2 84.7 %all-to-all-start.9 = ((bf16[2,4,256,768]{3,2,0,1:T(8,128)(2,1)}), bf16[2,4,256,768]{3,2,0,1:T(8,128)(2,1)S(1)}, u32[]{:S(2)}, u32[]{:S(2)}) async-start(bf16[2,4,256,768]{3,2,0,1:T(8,128)(2,1)} %copy.1042), calls=%async_computation.9 | async-start | bytes 6291456 | tf_op jit(solution)/shard_map/all_to_all | solution.py:448
  1361.9 224.8 %all-to-all-start.5 = ((bf16[2,4,256,768]{3,2,0,1:T(8,128)(2,1)}), bf16[2,4,256,768]{3,2,0,1:T(8,128)(2,1)}, u32[]{:S(2)}, u32[]{:S(2)}) async-start(bf16[2,4,256,768]{3,2,0,1:T(8,128)(2,1)} %copy.1013), calls=%async_computation.5 | async-start | bytes 6291456 | tf_op jit(solution)/shard_map/all_to_all | solution.py:304
  2034.3 1736.9 %reduce-scatter.141.cloned.1.call-start = ((), (), s32[]{:S(2)}) async-start(), calls=%async_computation.108 | async-start | bytes 221184
  2036.5 1735.6 %reduce-scatter.133.cloned.1.call-start = ((), (), s32[]{:S(2)}) async-start(), calls=%async_computation.104 | async-start | bytes 221184
  2041.1 1745.5 %reduce-scatter.125.cloned.1.call-start = ((), (), s32[]{:S(2)}) async-start(), calls=%async_computation.100 | async-start | bytes 221184
  2043.7 1743.9 %reduce-scatter.137.cloned.1.call-start = ((), (), s32[]{:S(2)}) async-start(), calls=%async_computation.106 | async-start | bytes 221184
  2044.8 1743.7 %reduce-scatter.129.cloned.1.call-start = ((), (), s32[]{:S(2)}) async-start(), calls=%async_computation.102 | async-start | bytes 221184
  2050.8 1738.7 %reduce-scatter.121.cloned.1.call-start = ((), (), s32[]{:S(2)}) async-start(), calls=%async_computation.98 | async-start | bytes 221184
  2243.0 83.6 %all-to-all-start.13 = ((bf16[2,4,256,768]{3,2,0,1:T(8,128)(2,1)}), bf16[2,4,256,768]{3,2,0,1:T(8,128)(2,1)}, u32[]{:S(2)}, u32[]{:S(2)}) async-start(bf16[2,4,256,768]{3,2,0,1:T(8,128)(2,1)} %copy.1077), calls=%async_computation.13 | async-start | bytes 6291456 | tf_op jit(solution)/shard_map/all_to_all | solution.py:448
  2247.6 1542.6 %reduce-scatter.143.cloned.1.call-start = ((), (), s32[]{:S(2)}) async-start(), calls=%async_computation.109 | async-start | bytes 221184
  2297.0 1494.1 %reduce-scatter.135.cloned.1.call-start = ((), (), s32[]{:S(2)}) async-start(), calls=%async_computation.105 | async-start | bytes 221184
  2549.3 1251.6 %reduce-scatter.127.cloned.1.call-start = ((), (), s32[]{:S(2)}) async-start(), calls=%async_computation.101 | async-start | bytes 221184
  2551.5 1290.1 %reduce-scatter.139.cloned.1.call-start = ((), (), s32[]{:S(2)}) async-start(), calls=%async_computation.107 | async-start | bytes 221184
  2683.5 1159.0 %reduce-scatter.131.cloned.1.call-start = ((), (), s32[]{:S(2)}) async-start(), calls=%async_computation.103 | async-start | bytes 221184
  2685.1 1158.3 %reduce-scatter.123.cloned.1.call-start = ((), (), s32[]{:S(2)}) async-start(), calls=%async_computation.99 | async-start | bytes 221184
  2687.3 1156.9 %reduce-scatter.117.cloned.1.call-start = ((), (), s32[]{:S(2)}) async-start(), calls=%async_computation.82 | async-start | bytes 7077888 | tf_op jit(solution)/shard_map/reduce_scatter | solution.py:142
  2699.7 1144.5 %reduce-scatter.119.cloned.1.call-start = ((), (), s32[]{:S(2)}) async-start(), calls=%async_computation.83 | async-start | bytes 7077888 | tf_op jit(solution)/shard_map/reduce_scatter | solution.py:142
  2716.7 1130.2 %reduce-scatter.109.cloned.1.call-start = ((), (), s32[]{:S(2)}) async-start(), calls=%async_computation.78 | async-start | bytes 7077888 | tf_op jit(solution)/shard_map/reduce_scatter | solution.py:139
  2730.7 1116.3 %reduce-scatter.111.cloned.1.call-start = ((), (), s32[]{:S(2)}) async-start(), calls=%async_computation.79 | async-start | bytes 7077888 | tf_op jit(solution)/shard_map/reduce_scatter | solution.py:139
  2743.7 1106.0 %reduce-scatter.101.cloned.1.call-start = ((), (), s32[]{:S(2)}) async-start(), calls=%async_computation.74 | async-start | bytes 7077888 | tf_op jit(solution)/shard_map/reduce_scatter | solution.py:136
  2755.9 1093.8 %reduce-scatter.103.cloned.1.call-start = ((), (), s32[]{:S(2)}) async-start(), calls=%async_computation.75 | async-start | bytes 7077888 | tf_op jit(solution)/shard_map/reduce_scatter | solution.py:136
  2769.8 1145.1 %reduce-scatter.93.cloned.1.call-start = ((), (), s32[]{:S(2)}) async-start(), calls=%async_computation.70 | async-start | bytes 1327104 | tf_op jit(solution)/shard_map/reduce_scatter | solution.py:121
  2792.4 1122.5 %reduce-scatter.69.cloned.1.call-start = ((), (), s32[]{:S(2)}) async-start(), calls=%async_computation.58 | async-start | bytes 1327104 | tf_op jit(solution)/shard_map/reduce_scatter | solution.py:112
  2796.9 1118.0 %reduce-scatter.77.cloned.1.call-start = ((), (), s32[]{:S(2)}) async-start(), calls=%async_computation.62 | async-start | bytes 1327104 | tf_op jit(solution)/shard_map/reduce_scatter | solution.py:115
  2800.9 1114.1 %reduce-scatter.85.cloned.1.call-start = ((), (), s32[]{:S(2)}) async-start(), calls=%async_computation.66 | async-start | bytes 1327104 | tf_op jit(solution)/shard_map/reduce_scatter | solution.py:118
  2879.6 1035.5 %reduce-scatter.95.cloned.1.call-start = ((), (), s32[]{:S(2)}) async-start(), calls=%async_computation.71 | async-start | bytes 1327104 | tf_op jit(solution)/shard_map/reduce_scatter | solution.py:121
  3030.9 884.1 %reduce-scatter.71.cloned.1.call-start = ((), (), s32[]{:S(2)}) async-start(), calls=%async_computation.59 | async-start | bytes 1327104 | tf_op jit(solution)/shard_map/reduce_scatter | solution.py:112
  3035.4 879.6 %reduce-scatter.79.cloned.1.call-start = ((), (), s32[]{:S(2)}) async-start(), calls=%async_computation.63 | async-start | bytes 1327104 | tf_op jit(solution)/shard_map/reduce_scatter | solution.py:115
  3040.3 874.8 %reduce-scatter.87.cloned.1.call-start = ((), (), s32[]{:S(2)}) async-start(), calls=%async_computation.67 | async-start | bytes 1327104 | tf_op jit(solution)/shard_map/reduce_scatter | solution.py:118
  3053.4 861.7 %reduce-scatter.89.cloned.1.call-start = ((), (), s32[]{:S(2)}) async-start(), calls=%async_computation.68 | async-start | bytes 1327104 | tf_op jit(solution)/shard_map/reduce_scatter | solution.py:121
  3348.7 566.5 %reduce-scatter.91.cloned.1.call-start = ((), (), s32[]{:S(2)}) async-start(), calls=%async_computation.69 | async-start | bytes 1327104 | tf_op jit(solution)/shard_map/reduce_scatter | solution.py:121
  3452.8 165.2 %collective-permute-start.5 = (bf16[2,1024,768]{1,2,0:T(8,128)(2,1)}, bf16[2,1024,768]{1,2,0:T(8,128)(2,1)}, u32[]{:S(2)}, u32[]{:S(2)}) collective-permute-start(bf16[2,1024,768]{1,2,0:T(8,128)(2,1)} %fusion.107), channel_id=1, source_target_pairs={{4,0},{5,1},{6,2},{7,3},{12,8},{13,9},{14,10},{15,11},{20,16},{21,... | collective-permute-start | bytes 9437192 | tf_op jit(solution)/shard_map/ppermute | solution.py:21
  3459.3 455.9 %reduce-scatter.65.cloned.1.call-start = ((), (), s32[]{:S(2)}) async-start(), calls=%async_computation.56 | async-start | bytes 1327104 | tf_op jit(solution)/shard_map/reduce_scatter | solution.py:112
  3484.4 430.8 %reduce-scatter.67.cloned.1.call-start = ((), (), s32[]{:S(2)}) async-start(), calls=%async_computation.57 | async-start | bytes 1327104 | tf_op jit(solution)/shard_map/reduce_scatter | solution.py:112
  3591.2 324.0 %reduce-scatter.81.cloned.1.call-start = ((), (), s32[]{:S(2)}) async-start(), calls=%async_computation.64 | async-start | bytes 1327104 | tf_op jit(solution)/shard_map/reduce_scatter | solution.py:118
  3625.7 289.5 %reduce-scatter.73.cloned.1.call-start = ((), (), s32[]{:S(2)}) async-start(), calls=%async_computation.60 | async-start | bytes 1327104 | tf_op jit(solution)/shard_map/reduce_scatter | solution.py:115
  3629.8 285.5 %reduce-scatter.83.cloned.1.call-start = ((), (), s32[]{:S(2)}) async-start(), calls=%async_computation.65 | async-start | bytes 1327104 | tf_op jit(solution)/shard_map/reduce_scatter | solution.py:118
  3703.8 211.5 %reduce-scatter.75.cloned.1.call-start = ((), (), s32[]{:S(2)}) async-start(), calls=%async_computation.61 | async-start | bytes 1327104 | tf_op jit(solution)/shard_map/reduce_scatter | solution.py:115
  3707.8 208.7 %reduce-scatter.113.cloned.1.call-start = ((), (), s32[]{:S(2)}) async-start(), calls=%async_computation.80 | async-start | bytes 7077888 | tf_op jit(solution)/shard_map/reduce_scatter | solution.py:142
  3720.1 248.6 %reduce-scatter.115.cloned.1.call-start = ((), (), s32[]{:S(2)}) async-start(), calls=%async_computation.81 | async-start | bytes 7077888 | tf_op jit(solution)/shard_map/reduce_scatter | solution.py:142
  3732.2 301.5 %reduce-scatter.105.cloned.1.call-start = ((), (), s32[]{:S(2)}) async-start(), calls=%async_computation.76 | async-start | bytes 7077888 | tf_op jit(solution)/shard_map/reduce_scatter | solution.py:139
  3744.9 354.4 %reduce-scatter.107.cloned.1.call-start = ((), (), s32[]{:S(2)}) async-start(), calls=%async_computation.77 | async-start | bytes 7077888 | tf_op jit(solution)/shard_map/reduce_scatter | solution.py:139
  3758.0 406.3 %reduce-scatter.97.cloned.1.call-start = ((), (), s32[]{:S(2)}) async-start(), calls=%async_computation.72 | async-start | bytes 7077888 | tf_op jit(solution)/shard_map/reduce_scatter | solution.py:136
  3770.6 459.3 %reduce-scatter.99.cloned.1.call-start = ((), (), s32[]{:S(2)}) async-start(), calls=%async_computation.73 | async-start | bytes 7077888 | tf_op jit(solution)/shard_map/reduce_scatter | solution.py:136
  3785.6 549.0 %all-reduce.27.cloned.1.call-start = ((), (), s32[]{:S(2)}) async-start(), calls=%async_computation.110 | async-start | bytes 4718592 | tf_op jit(solution)/shard_map/psum | solution.py:148
  (435 other events, 7935.2 us)
Sparse Core Ops, SparseCore 0:
  10.5 25.3 all-gather.40
  38.3 24.2 all-gather.38
  64.5 24.1 all-gather.42
  90.4 24.0 all-gather.44
  116.3 70.6 all-gather.46
  188.7 71.0 all-gather.48
  261.7 57.7 all-gather.50
  321.9 26.1 all-gather.54
  350.6 24.0 all-gather.52
  495.3 28.2 all-gather.56
  525.4 24.0 all-gather.58
  551.3 45.5 all-gather.62
  747.3 67.7 all-gather.64
  989.7 48.2 all-gather.60
  2037.9 35.8 reduce-scatter.140
  2076.9 33.5 reduce-scatter.132
  2113.9 33.4 reduce-scatter.124
  2150.6 33.4 reduce-scatter.136
  2187.2 33.5 reduce-scatter.128
  2224.5 33.5 reduce-scatter.120
  2297.2 35.8 reduce-scatter.142
  2549.4 37.6 reduce-scatter.134
  2590.7 33.4 reduce-scatter.126
  2683.6 33.6 reduce-scatter.138
  2720.3 33.5 reduce-scatter.130
  2757.6 33.5 reduce-scatter.122
  2794.4 61.7 reduce-scatter.116
  2859.9 61.7 reduce-scatter.118
  2925.1 61.7 reduce-scatter.108
  2990.4 61.7 reduce-scatter.110
  3055.6 61.7 reduce-scatter.100
  3121.1 61.7 reduce-scatter.102
  3186.0 36.7 reduce-scatter.92
  3226.3 36.7 reduce-scatter.68
  3266.4 36.7 reduce-scatter.76
  3306.6 36.7 reduce-scatter.84
  3346.4 36.7 reduce-scatter.94
  3386.8 36.7 reduce-scatter.70
  3426.7 38.4 reduce-scatter.78
  3468.7 41.6 reduce-scatter.86
  3513.6 36.7 reduce-scatter.88
  3554.0 36.7 reduce-scatter.90
  3593.9 38.5 reduce-scatter.64
  3636.0 41.5 reduce-scatter.66
  3680.7 36.7 reduce-scatter.80
  3720.9 36.7 reduce-scatter.72
  3760.7 36.7 reduce-scatter.82
  3800.9 36.8 reduce-scatter.74
  3841.0 62.1 reduce-scatter.112
  3907.0 61.7 reduce-scatter.114
  3972.0 61.7 reduce-scatter.104
  4037.5 61.7 reduce-scatter.106
  4102.5 61.7 reduce-scatter.96
  4168.1 61.7 reduce-scatter.98
  4233.4 101.2 all-reduce.26
where the time goes:
time: 4370 us; the launch traced here: 4350 us
  matrix products  1860 us (43%)
  waiting for transfers between devices  1140 us (26%)
  other arithmetic  523 us (12%)
  local copies, waits for them, and re-layouts  472 us (11%)
  blocking collectives  236 us (5%)
  starting transfers between devices  97 us (2%)
    ppermute x8, waiting for transfers between devices, passed_along(): return lax.ppermute(block, axis, route)  364 us
    convert_element_type x4, other arithmetic, attention_backward(): grad_scores = (prob_f32 * (grad_probs - row_delta)).astype(jnp.bfloat16)  315 us
    dot_general x4, matrix products, attention_backward(): jnp.einsum('qhd,khd->hqk', grad_heads, value_heads, preferred_element_typ...  264 us
    sub x4, matrix products, attention_forward(): exponent = jnp.exp(scores - row_max)  170 us
    all_to_all x4, waiting for transfers between devices, layer_forward(): lax.all_to_all(send_rows.reshape(per_dev, expert_groups, capacity, model_...  149 us
    all_to_all x4, waiting for transfers between devices, layer_backward(): lax.all_to_all(grad_send.reshape(per_dev, expert_groups, capacity, model_...  145 us
    dot_general x4, matrix products, attention_backward(): jnp.einsum('hqk,qhd->khd', prob_low, grad_heads, preferred_element_type=j...  141 us
    dot_general x8, matrix products, mixture(): jnp.einsum('tkj,tjd->tkd', chosen_onehot[:, :, EXPERTS + 2:], constant, p...  141 us
  transfers between devices with their start and end apart: 79, of which 23 were waited for; matrix products, arithmetic and copies ran while one was open for 58% of the time, Pallas kernels for 0%

commit v1 on v0

v1 whole, which is shorter than its diff:
```python
import functools

import jax
import jax.numpy as jnp
from jax import lax
from jax.experimental import pallas as pl
from jax.experimental.pallas import tpu as pltpu
from jax.sharding import PartitionSpec as P

HEADS = 12
HEAD_DIM = 64
EXPERTS = 8
TOP = 2
WINDOW = 1024
ROUTED = 12
LANES = 128
MIB = 1 << 20

norm_eps = 1e-05
masked = -1000000000.0
highest = lax.Precision.HIGHEST
f32 = jnp.float32
bf16 = jnp.bfloat16
SHARDED = ("context", "dp")


ANY_SPEC = pl.BlockSpec(memory_space=pl.ANY)


def dot_on(left_op, right_op, left_dim, right_dim):
    return lax.dot_general(
        left_op,
        right_op,
        (((left_dim,), (right_dim,)), ((), ())),
        preferred_element_type=f32,
    )


def rows_of(values, picks):
    count = 8 if len(picks) <= 8 else 16
    row = lax.broadcasted_iota(jnp.int32, (count, LANES), 0)
    lane = lax.broadcasted_iota(jnp.int32, (count, LANES), 1)
    pick = jnp.zeros((count, LANES), f32)
    for index, source in enumerate(picks):
        pick = jnp.where((row == index) & (lane == source), 1.0, pick)
    return lax.dot_general(
        pick, values, (((1,), (1,)), ((), ())), precision=highest, preferred_element_type=f32
    )


def join_spans(buffer_ref, earlier_ref, own_ref):
    buffer_ref[:WINDOW, :] = earlier_ref[...]
    buffer_ref[WINDOW:, :] = own_ref[...]


def attention_forward_kernel(
    rows, keys, blocks, q_ref, ko_ref, vo_ref, kp_ref, vp_ref, sq_ref, sk_ref, *rest
):
    out_ref, lse_rows_ref, lse_ref, bias_ref, k_ref, v_ref = rest[-6:]
    pair = pl.program_id(0)

    @pl.when(pair == 0)
    def _():
        lse_ref[...] = jnp.zeros_like(lse_ref)
        rel = lax.broadcasted_iota(jnp.int32, (rows, keys), 1) - lax.broadcasted_iota(
            jnp.int32, (rows, keys), 0
        )
        inside = (rel > 0) & (rel <= WINDOW)
        for block in range(blocks):
            first = block * rows
            same = sq_ref[first : first + rows, :] == sk_ref[:, first : first + keys]
            bias_ref[block] = jnp.where(inside & same, 0.0, masked)

    join_spans(k_ref, kp_ref, ko_ref)
    join_spans(v_ref, vp_ref, vo_ref)
    lane = lax.broadcasted_iota(jnp.int32, (rows, LANES), 1)
    low = lane < HEAD_DIM
    for block in range(blocks):
        own = slice(block * rows, (block + 1) * rows)
        span = slice(block * rows, block * rows + keys)
        query = q_ref[own, :] * (HEAD_DIM ** -0.5)
        key = k_ref[span, :]
        value = v_ref[span, :]
        heads_out = []
        for half in range(2):
            mine = low if half == 0 else ~low
            scores = (
                dot_on(jnp.where(mine, query, jnp.zeros_like(query)), key, 1, 1) + bias_ref[block]
            )
            row_max = jnp.max(scores, axis=1, keepdims=True)
            exponent = jnp.exp(scores - row_max)
            row_sum = jnp.sum(exponent, axis=1, keepdims=True)
            heads_out.append(dot_on(exponent.astype(bf16), value, 1, 0) * (1.0 / row_sum))
            lse_ref[own, :] = jnp.where(
                lane == 2 * pair + half, row_max + jnp.log(row_sum), lse_ref[own, :]
            )
        out_ref[own, :] = jnp.where(low, heads_out[0], heads_out[1]).astype(bf16)

    @pl.when(pair == pl.num_programs(0) - 1)
    def _():
        lse_rows_ref[...] = rows_of(lse_ref[...], range(HEADS))


def attention_forward(qkv, kv_earlier, seg_query, seg_key, after):
    length = qkv.shape[0]
    width = qkv.shape[1] // 3
    pairs = width // LANES
    rows = min(256, length)
    keys = rows + WINDOW
    blocks = length // rows
    span = WINDOW + length

    def column(count, offset):
        return pl.BlockSpec((count, LANES), lambda p: (0, offset + p))

    return pl.pallas_call(
        functools.partial(attention_forward_kernel, rows, keys, blocks),
        grid=(pairs,),
        in_specs=[
            column(length, 0),
            column(length, pairs),
            column(length, 2 * pairs),
            column(WINDOW, 0),
            column(WINDOW, pairs),
            pl.BlockSpec((length, 1), lambda p: (0, 0)),
            pl.BlockSpec((1, span), lambda p: (0, 0)),
        ]
        + [ANY_SPEC] * len(after),
        out_specs=[column(length, 0), pl.BlockSpec((16, length), lambda p: (0, 0))],
        out_shape=[
            jax.ShapeDtypeStruct((length, width), bf16),
            jax.ShapeDtypeStruct((16, length), f32),
        ],
        scratch_shapes=[
            pltpu.VMEM((length, LANES), f32),
            pltpu.VMEM((blocks, rows, keys), f32),
            pltpu.VMEM((span, LANES), bf16),
            pltpu.VMEM((span, LANES), bf16),
        ],
        compiler_params=pltpu.CompilerParams(vmem_limit_bytes=40 * MIB),
        cost_estimate=pl.CostEstimate(
            flops=4 * length * keys * width * 4, bytes_accessed=12 * length * width,
            transcendentals=length * keys * HEADS,
        ),
        name="attention_forward",
    )(qkv, qkv, qkv, kv_earlier, kv_earlier, seg_query, seg_key, *after)


def attention_backward_kernel(
    rows, keys, blocks, q_ref, ko_ref, vo_ref, kp_ref, vp_ref, do_ref, out_ref, lse_ref,
    sq_ref, sk_ref, *rest
):
    dq_ref, dk_ref, dv_ref, bias_ref, k_ref, v_ref, dk_sum, dv_sum = rest[-8:]
    pair = pl.program_id(0)

    @pl.when(pair == 0)
    def _():
        rel = lax.broadcasted_iota(jnp.int32, (keys, rows), 0) - lax.broadcasted_iota(
            jnp.int32, (keys, rows), 1
        )
        inside = (rel > 0) & (rel <= WINDOW)
        for block in range(blocks):
            first = block * rows
            same = sk_ref[first : first + keys, :] == sq_ref[:, first : first + rows]
            bias_ref[block] = jnp.where(inside & same, 0.0, masked)

    join_spans(k_ref, kp_ref, ko_ref)
    join_spans(v_ref, vp_ref, vo_ref)
    dk_sum[...] = jnp.zeros_like(dk_sum)
    dv_sum[...] = jnp.zeros_like(dv_sum)
    low = lax.broadcasted_iota(jnp.int32, (rows, LANES), 1) < HEAD_DIM
    ones = jnp.ones((8, LANES), bf16)
    for block in range(blocks):
        own = slice(block * rows, (block + 1) * rows)
        span = slice(block * rows, block * rows + keys)
        query = q_ref[own, :] * (HEAD_DIM ** -0.5)
        grad = do_ref[own, :]
        key = k_ref[span, :]
        value = v_ref[span, :]
        product = grad.astype(f32) * out_ref[own, :].astype(f32)
        heads_dq = []
        for half in range(2):
            mine = low if half == 0 else ~low
            query_h = jnp.where(mine, query, jnp.zeros_like(query))
            grad_h = jnp.where(mine, grad, jnp.zeros_like(grad))
            product_h = jnp.where(mine, product, 0.0)
            coarse = product_h.astype(bf16)
            fine = (product_h - coarse.astype(f32)).astype(bf16)
            delta = (dot_on(ones, coarse, 1, 1) + dot_on(ones, fine, 1, 1))[0:1, :]
            scores = dot_on(key, query_h, 1, 1) + bias_ref[block]
            probs = jnp.exp(scores - lse_ref[pl.ds(2 * pair + half, 1), own])
            d_probs = dot_on(value, grad_h, 1, 1)
            d_scores = (probs * (d_probs - delta)).astype(bf16)
            dv_sum[span, :] += dot_on(probs.astype(bf16), grad_h, 1, 0)
            dk_sum[span, :] += dot_on(d_scores, query_h, 1, 0)
            heads_dq.append(dot_on(d_scores, key, 0, 0))
        dq_ref[own, :] = (
            jnp.where(low, heads_dq[0], heads_dq[1]) * (HEAD_DIM ** -0.5)
        ).astype(bf16)
    dk_ref[...] = dk_sum[...].astype(bf16)
    dv_ref[...] = dv_sum[...].astype(bf16)


def attention_backward(qkv, kv_earlier, grad_att, attended, lse, seg_query, seg_key, after):
    length = qkv.shape[0]
    width = qkv.shape[1] // 3
    pairs = width // LANES
    rows = min(256, length)
    keys = rows + WINDOW
    blocks = length // rows
    span = WINDOW + length

    def column(count, offset):
        return pl.BlockSpec((count, LANES), lambda p: (0, offset + p))

    return pl.pallas_call(
        functools.partial(attention_backward_kernel, rows, keys, blocks),
        grid=(pairs,),
        in_specs=[
            column(length, 0),
            column(length, pairs),
            column(length, 2 * pairs),
            column(WINDOW, 0),
            column(WINDOW, pairs),
            column(length, 0),
            column(length, 0),
            pl.BlockSpec((16, length), lambda p: (0, 0)),
            pl.BlockSpec((1, length), lambda p: (0, 0)),
            pl.BlockSpec((span, 1), lambda p: (0, 0)),
        ]
        + [ANY_SPEC] * len(after),
        out_specs=[column(length, 0), column(span, 0), column(span, 0)],
        out_shape=[
            jax.ShapeDtypeStruct((length, width), bf16),
            jax.ShapeDtypeStruct((span, width), bf16),
            jax.ShapeDtypeStruct((span, width), bf16),
        ],
        scratch_shapes=[
            pltpu.VMEM((blocks, keys, rows), f32),
            pltpu.VMEM((span, LANES), bf16),
            pltpu.VMEM((span, LANES), bf16),
            pltpu.VMEM((span, LANES), f32),
            pltpu.VMEM((span, LANES), f32),
        ],
        compiler_params=pltpu.CompilerParams(vmem_limit_bytes=48 * MIB),
        cost_estimate=pl.CostEstimate(
            flops=10 * length * keys * width * 4, bytes_accessed=24 * length * width,
            transcendentals=length * keys * HEADS,
        ),
        name="attention_backward",
    )(
        qkv, qkv, qkv, kv_earlier, kv_earlier, grad_att, attended, lse, seg_query, seg_key, *after
    )


def sigmoid(values):
    return 1.0 / (1.0 + jnp.exp(-values))


def experts_forward_kernel(
    chunks, x_ref, gate_w_ref, up_w_ref, down_w_ref, *rest
):
    out_ref, gate_ref, up_ref, total_ref = rest[-4:]
    chunk = pl.program_id(1)
    rows_in = x_ref[0]
    gate_pre = dot_on(rows_in, gate_w_ref[0], 1, 0)
    up_pre = dot_on(rows_in, up_w_ref[0], 1, 0)
    activated = (gate_pre * sigmoid(gate_pre) * up_pre).astype(bf16)
    gate_ref[0] = gate_pre.astype(bf16)
    up_ref[0] = up_pre.astype(bf16)
    part = dot_on(activated, down_w_ref[0], 1, 0)

    @pl.when(chunk == 0)
    def _():
        total_ref[...] = part

    @pl.when(chunk > 0)
    def _():
        total_ref[...] += part

    @pl.when(chunk == chunks - 1)
    def _():
        out_ref[0] = total_ref[...].astype(bf16)


def experts_forward(rows_in, gate_up_w, down_w, after):
    count, rows, _ = rows_in.shape
    width, hidden = gate_up_w.shape[1:]
    chunk = hidden
    chunks = hidden // chunk
    return pl.pallas_call(
        functools.partial(experts_forward_kernel, chunks),
        grid=(count, chunks),
        in_specs=[
            pl.BlockSpec((1, rows, width), lambda j, f: (j, 0, 0)),
            pl.BlockSpec((1, width, chunk), lambda j, f: (j, 0, f)),
            pl.BlockSpec((1, width, chunk), lambda j, f: (count + j, 0, f)),
            pl.BlockSpec((1, chunk, width), lambda j, f: (j, f, 0)),
        ]
        + [ANY_SPEC] * len(after),
        out_specs=[
            pl.BlockSpec((1, rows, width), lambda j, f: (j, 0, 0)),
            pl.BlockSpec((1, rows, chunk), lambda j, f: (j, 0, f)),
            pl.BlockSpec((1, rows, chunk), lambda j, f: (j, 0, f)),
        ],
        out_shape=[
            jax.ShapeDtypeStruct((count, rows, width), bf16),
            jax.ShapeDtypeStruct((count, rows, hidden), bf16),
            jax.ShapeDtypeStruct((count, rows, hidden), bf16),
        ],
        scratch_shapes=[pltpu.VMEM((rows, width), f32)],
        compiler_params=pltpu.CompilerParams(vmem_limit_bytes=48 * MIB),
        cost_estimate=pl.CostEstimate(
            flops=6 * count * rows * width * hidden,
            bytes_accessed=6 * count * width * hidden + 4 * count * rows * (width + hidden),
            transcendentals=count * rows * hidden,
        ),
        name="experts_forward",
    )(rows_in, gate_up_w, gate_up_w, down_w, *after)


def experts_backward_kernel(chunks, has_gate, has_sums, *refs):
    x_ref, dy_ref, gate_ref, up_ref, gate_w_ref, up_w_ref, down_w_ref = refs[:7]
    given = refs[7:]
    dx_ref, gate_up_grad_ref, down_grad_ref, total_ref, scaled_ref = refs[-5:]
    chunk = pl.program_id(1)
    rows_in = x_ref[0]
    if has_gate:
        share_ref, given = given[0], given[1:]

        @pl.when(chunk == 0)
        def _():
            share = share_ref[0].astype(f32)
            share = share[:, 0:1] + share[:, 1:2]
            scaled_ref[...] = (dy_ref[0].astype(f32) * share).astype(bf16)

        d_out = scaled_ref[...]
    else:
        d_out = dy_ref[0]
    gate_pre = gate_ref[0].astype(f32)
    up_pre = up_ref[0].astype(f32)
    share = sigmoid(gate_pre)
    swish = gate_pre * share
    activated = (swish * up_pre).astype(bf16)
    d_act = dot_on(d_out, down_w_ref[0], 1, 1)
    d_gate = (d_act * up_pre * (share * (1.0 + gate_pre * (1.0 - share)))).astype(bf16)
    d_up = (d_act * swish).astype(bf16)
    part = dot_on(d_gate, gate_w_ref[0], 1, 1) + dot_on(d_up, up_w_ref[0], 1, 1)
    gate_grad = dot_on(rows_in, d_gate, 0, 0)
    up_grad = dot_on(rows_in, d_up, 0, 0)
    down_grad = dot_on(activated, d_out, 0, 0)
    if has_sums:
        gate_up_sum_ref, down_sum_ref = given[:2]
        gate_grad += gate_up_sum_ref[0, 0].astype(f32)
        up_grad += gate_up_sum_ref[1, 0].astype(f32)
        down_grad += down_sum_ref[0].astype(f32)
    gate_up_grad_ref[0, 0] = gate_grad.astype(bf16)
    gate_up_grad_ref[1, 0] = up_grad.astype(bf16)
    down_grad_ref[0] = down_grad.astype(bf16)

    @pl.when(chunk == 0)
    def _():
        total_ref[...] = part

    @pl.when(chunk > 0)
    def _():
        total_ref[...] += part

    @pl.when(chunk == chunks - 1)
    def _():
        dx_ref[0] = total_ref[...].astype(bf16)


def experts_backward(rows_in, d_out, gate_pre, up_pre, gate_up_w, down_w, has_gate, sums, after):
    count, rows, _ = rows_in.shape
    width, hidden = gate_up_w.shape[1:]
    chunk = min(512, hidden)
    chunks = hidden // chunk
    row_spec = pl.BlockSpec((1, rows, width), lambda j, f: (j, 0, 0))
    hidden_spec = pl.BlockSpec((1, rows, chunk), lambda j, f: (j, 0, f))
    wide_spec = pl.BlockSpec((1, width, chunk), lambda j, f: (j, 0, f))
    up_spec = pl.BlockSpec((1, width, chunk), lambda j, f: (count + j, 0, f))
    tall_spec = pl.BlockSpec((1, chunk, width), lambda j, f: (j, f, 0))
    both_spec = pl.BlockSpec((2, 1, width, chunk), lambda j, f: (0, j, 0, f))
    operands = [rows_in, d_out, gate_pre, up_pre, gate_up_w, gate_up_w, down_w]
    specs = [row_spec, row_spec, hidden_spec, hidden_spec, wide_spec, up_spec, tall_spec]
    if has_gate:
        operands.append(rows_in)
        specs.append(pl.BlockSpec((1, rows, LANES), lambda j, f: (j, 0, width // LANES)))
    if sums is not None:
        operands.extend(sums)
        specs.extend([both_spec, tall_spec])
    return pl.pallas_call(
        functools.partial(experts_backward_kernel, chunks, has_gate, sums is not None),
        grid=(count, chunks),
        in_specs=specs + [ANY_SPEC] * len(after),
        out_specs=[row_spec, both_spec, tall_spec],
        out_shape=[
            jax.ShapeDtypeStruct((count, rows, width), bf16),
            jax.ShapeDtypeStruct((2, count, width, hidden), bf16),
            jax.ShapeDtypeStruct((count, hidden, width), bf16),
        ],
        scratch_shapes=[pltpu.VMEM((rows, width), f32), pltpu.VMEM((rows, width), bf16)],
        compiler_params=pltpu.CompilerParams(vmem_limit_bytes=56 * MIB),
        cost_estimate=pl.CostEstimate(
            flops=12 * count * rows * width * hidden,
            bytes_accessed=12 * count * width * hidden + 4 * count * rows * (width + hidden),
            transcendentals=count * rows * hidden,
        ),
        name="experts_backward",
    )(*operands, *after)


def passed_along(block, axis, distance):
    devices = range(lax.axis_size(axis))
    route = [(i - distance, i) for i in devices if i - distance in devices]
    return lax.ppermute(block, axis, route)


def earlier_rows(block, hop_count):
    pieces = [passed_along(block, "context", hop) for hop in range(hop_count, 0, -1)]
    missing = WINDOW - hop_count * block.shape[-2]
    if missing > 0:
        shape = block.shape[:-2] + (missing, block.shape[-1])
        pieces = [jnp.zeros(shape, block.dtype)] + pieces
    rows = pieces[0] if len(pieces) == 1 else jnp.concatenate(pieces, axis=-2)
    return rows[..., rows.shape[-2] - WINDOW :, :]


def returned_rows(block, length, hop_count):
    total = None
    for hop in range(1, hop_count + 1):
        first = WINDOW - hop * length
        part = block[max(first, 0) : first + length]
        if first < 0:
            part = jnp.concatenate([jnp.zeros((-first, block.shape[1]), block.dtype), part])
        part = passed_along(part, "context", -hop).astype(f32)
        total = part if total is None else total + part
    return total


def exchange(rows, groups, capacity):
    return lax.all_to_all(
        rows.reshape((EXPERTS // groups, groups, capacity) + rows.shape[1:]),
        "expert",
        split_axis=1,
        concat_axis=1,
        tiled=True,
    )


GATE, OF_NORMED, NORMED_SHARE, VECTOR_SHARE, MIX, SCALE, CHOSEN = 0, 2, 4, 5, 7, 9, 10
VECTOR_ROW, ATTN_GAIN_ROW, MOE_GAIN_ROW = 0, 2, 3


def inverse_rms(rows):
    return lax.rsqrt(jnp.mean(rows * rows, axis=-1, keepdims=True) + norm_eps)


def lane_iota(rows):
    return lax.broadcasted_iota(jnp.int32, (rows, LANES), 1)


def placed_on_lanes(rows, values):
    lane = lane_iota(rows)
    total = jnp.zeros((rows, LANES), f32)
    for index, value in values.items():
        total = jnp.where(lane == index, value, total)
    return total


def routing_kernel(groups, capacity, routes_ref, columns_ref, rows_ref):
    length = routes_ref.shape[1]
    lane = lane_iota(length)
    per_dev = EXPERTS // groups
    base = jnp.full((length, LANES), -1.0, f32)
    for e in range(EXPERTS):
        base = jnp.where(lane == e, float(e % per_dev * groups * capacity + e // per_dev * capacity), base)
    onehots = [(lane == routes_ref[0, :, k : k + 1]).astype(f32) for k in range(TOP)]
    counts = (onehots[0] + onehots[1]).astype(bf16)
    earlier = lax.broadcasted_iota(jnp.int32, (length, length), 0) > lax.broadcasted_iota(
        jnp.int32, (length, length), 1
    )
    rank = dot_on(jnp.where(earlier, 1.0, 0.0).astype(bf16), counts, 1, 0)
    place = base + jnp.where(lane < EXPERTS, rank, 0.0)
    slots = placed_on_lanes(
        length,
        {k: jnp.sum(onehots[k] * place, axis=1, keepdims=True) for k in range(TOP)},
    )
    columns_ref[0] = slots.astype(jnp.int32)
    rows_ref[0] = jnp.round(rows_of(slots, range(TOP))).astype(jnp.int32)


def routing_slots(routes, groups, capacity):
    count, length, _ = routes.shape
    return pl.pallas_call(
        functools.partial(routing_kernel, groups, capacity),
        grid=(count,),
        in_specs=[pl.BlockSpec((1, length, TOP), lambda m: (m, 0, 0))],
        out_specs=[
            pl.BlockSpec((1, length, LANES), lambda m: (m, 0, 0)),
            pl.BlockSpec((1, 8, length), lambda m: (m, 0, 0)),
        ],
        out_shape=[
            jax.ShapeDtypeStruct((count, length, LANES), jnp.int32),
            jax.ShapeDtypeStruct((count, 8, length), jnp.int32),
        ],
        compiler_params=pltpu.CompilerParams(vmem_limit_bytes=32 * MIB),
        cost_estimate=pl.CostEstimate(
            flops=2 * count * length * length * LANES, bytes_accessed=count * length * 1024,
            transcendentals=0,
        ),
        name="routing",
    )(routes)


def dispatch_kernel(mode, rows_ref, slots_ref, gates_ref, *rest):
    out_ref = rest[-1]
    count, length = out_ref.shape[0], rows_ref.shape[0]
    width = rows_ref.shape[1]
    slot = pl.program_id(0) * count + lax.broadcasted_iota(jnp.int32, (count, length), 0)
    hits = [slot == slots_ref[k : k + 1, :] for k in range(TOP)]
    table = jnp.where(hits[0] | hits[1], 1.0, 0.0).astype(bf16)
    found = dot_on(table, rows_ref[...].astype(bf16), 1, 0)
    if mode == "plain":
        out_ref[...] = found.astype(bf16)
        return
    gate = jnp.sum(
        jnp.where(hits[0], gates_ref[0:1, :], 0.0) + jnp.where(hits[1], gates_ref[1:2, :], 0.0),
        axis=1,
        keepdims=True,
    )
    if mode == "scaled":
        out_ref[...] = (found * gate).astype(bf16)
        return
    out_ref[:, :width] = found.astype(bf16)
    coarse = gate.astype(bf16).astype(f32)
    out_ref[:, width:] = placed_on_lanes(count, {0: coarse, 1: gate - coarse}).astype(bf16)


def dispatch(rows, slot_rows, gate_rows, mode, slots, after=()):
    length, width = rows.shape
    count = min(256, slots)
    out_width = width + LANES if mode == "with gate" else width
    return pl.pallas_call(
        functools.partial(dispatch_kernel, mode),
        grid=(slots // count,),
        in_specs=[
            pl.BlockSpec((length, width), lambda s: (0, 0)),
            pl.BlockSpec((8, length), lambda s: (0, 0)),
            pl.BlockSpec((8, length), lambda s: (0, 0)),
        ]
        + [ANY_SPEC] * len(after),
        out_specs=pl.BlockSpec((count, out_width), lambda s: (s, 0)),
        out_shape=jax.ShapeDtypeStruct((slots, out_width), bf16),
        compiler_params=pltpu.CompilerParams(vmem_limit_bytes=24 * MIB),
        cost_estimate=pl.CostEstimate(
            flops=2 * slots * length * out_width,
            bytes_accessed=2 * (slots + length) * width, transcendentals=0,
        ),
        name="dispatch",
    )(rows, slot_rows, gate_rows, *after)


def attention_output_kernel(
    hidden_ref, attended_ref, out_w_ref, small_w_ref, vectors_ref, prior_ref, residual_ref,
    routes_ref, mid_ref, low_ref, logits_ref, scalars_ref, gates_ref,
):
    rows = hidden_ref.shape[0]
    mid = hidden_ref[...] + dot_on(attended_ref[...], out_w_ref[...], 1, 0)
    mid_ref[...] = mid
    scale = inverse_rms(mid)
    low = (mid * scale * vectors_ref[MOE_GAIN_ROW : MOE_GAIN_ROW + 1, :]).astype(bf16)
    low_ref[...] = low
    logits = dot_on(low, small_w_ref[...], 1, 0) + jnp.dot(
        prior_ref[...], residual_ref[...], precision=highest
    )
    logits_ref[...] = logits
    lane = lane_iota(rows)
    onehots = [lane == routes_ref[:, k : k + 1] for k in range(TOP)]

    def lane_sum(values):
        return jnp.sum(values, axis=1, keepdims=True)

    difference = lane_sum(jnp.where(onehots[0], logits, jnp.where(onehots[1], -logits, 0.0)))
    gates = (sigmoid(difference), sigmoid(-difference))
    chosen = [
        [jnp.where(routes_ref[:, k : k + 1] == EXPERTS + 2 + j, 1.0, 0.0) for j in range(2)]
        for k in range(TOP)
    ]
    alphas = []
    for j in range(2):
        at = ROUTED + 2 * j
        gap = lane_sum(jnp.where(lane == at, logits, jnp.where(lane == at + 1, -logits, 0.0)))
        alphas.append((sigmoid(gap), sigmoid(-gap)))
    of_normed = [
        jnp.where(routes_ref[:, k : k + 1] == EXPERTS + 1, 1.0, 0.0)
        + chosen[k][0] * alphas[0][0]
        + chosen[k][1] * alphas[1][0]
        for k in range(TOP)
    ]
    vector_gate = [gates[0] * chosen[0][j] + gates[1] * chosen[1][j] for j in range(2)]
    values = {
        GATE: gates[0], GATE + 1: gates[1],
        OF_NORMED: of_normed[0], OF_NORMED + 1: of_normed[1],
        NORMED_SHARE: gates[0] * of_normed[0] + gates[1] * of_normed[1],
        SCALE: scale,
    }
    for j in range(2):
        values[VECTOR_SHARE + j] = vector_gate[j] * alphas[j][1]
        values[MIX + j] = vector_gate[j] * alphas[j][0] * alphas[j][1]
        for k in range(TOP):
            values[CHOSEN + 2 * k + j] = chosen[k][j] * alphas[j][1]
    scalars = placed_on_lanes(rows, values)
    scalars_ref[...] = scalars
    gates_ref[...] = rows_of(scalars, (GATE, GATE + 1))


def attention_output(hidden, attended, weights, prior, routes):
    length, width = hidden.shape
    rows = min(256, length)
    wide = pl.BlockSpec((rows, width), lambda t: (t, 0))
    lanes = pl.BlockSpec((rows, LANES), lambda t: (t, 0))
    return pl.pallas_call(
        attention_output_kernel,
        grid=(length // rows,),
        in_specs=[
            wide,
            wide,
            pl.BlockSpec((width, width), lambda t: (0, 3)),
            pl.BlockSpec((width, LANES), lambda t: (0, 4 * width // LANES)),
            pl.BlockSpec((8, width), lambda t: (0, 0)),
            lanes,
            pl.BlockSpec((LANES, LANES), lambda t: (0, 0)),
            pl.BlockSpec((rows, TOP), lambda t: (t, 0)),
        ],
        out_specs=[wide, wide, lanes, lanes, pl.BlockSpec((8, rows), lambda t: (0, t))],
        out_shape=[
            jax.ShapeDtypeStruct((length, width), f32),
            jax.ShapeDtypeStruct((length, width), bf16),
            jax.ShapeDtypeStruct((length, LANES), f32),
            jax.ShapeDtypeStruct((length, LANES), f32),
            jax.ShapeDtypeStruct((8, length), f32),
        ],
        compiler_params=pltpu.CompilerParams(vmem_limit_bytes=24 * MIB),
        cost_estimate=pl.CostEstimate(
            flops=2 * length * width * (width + LANES), bytes_accessed=14 * length * width,
            transcendentals=length,
        ),
        name="attention_output",
    )(
        hidden, attended, weights["dense"], weights["dense"], weights["vectors"], prior,
        weights["residual"], routes,
    )


def selection(columns, slots, which):
    slot = lax.broadcasted_iota(jnp.int32, (columns.shape[0], slots), 1)
    hit = slot == columns[:, which[0] : which[0] + 1]
    for k in which[1:]:
        hit = hit | (slot == columns[:, k : k + 1])
    return jnp.where(hit, 1.0, 0.0).astype(bf16)


def combine_kernel(
    last, back_ref, columns_ref, mid_ref, scalars_ref, vectors_ref, next_ref, *out_refs
):
    columns, scalars = columns_ref[...], scalars_ref[...]
    slots = back_ref.shape[0]
    mid = mid_ref[...]
    normed = mid * scalars[:, SCALE : SCALE + 1] * vectors_ref[MOE_GAIN_ROW : MOE_GAIN_ROW + 1, :]
    total = mid + scalars[:, NORMED_SHARE : NORMED_SHARE + 1] * normed
    for j in range(2):
        row = vectors_ref[VECTOR_ROW + j : VECTOR_ROW + j + 1, :]
        total += scalars[:, VECTOR_SHARE + j : VECTOR_SHARE + j + 1] * row
    for k in range(TOP):
        branch = dot_on(selection(columns, slots, (k,)), back_ref[...], 1, 0)
        out_refs[k][...] = branch.astype(bf16)
        total += scalars[:, GATE + k : GATE + k + 1] * branch
    if last:
        out_refs[TOP][...] = total.astype(bf16)
    else:
        out_refs[TOP][...] = total
        out_refs[TOP + 1][...] = (
            total * inverse_rms(total) * next_ref[ATTN_GAIN_ROW : ATTN_GAIN_ROW + 1, :]
        ).astype(bf16)


def combine(back, columns, mid, scalars, vectors, next_vectors):
    last = next_vectors is None
    length, width = mid.shape
    slots = back.shape[0]
    rows = min(256, length)
    wide = pl.BlockSpec((rows, width), lambda t: (t, 0))
    lanes = pl.BlockSpec((rows, LANES), lambda t: (t, 0))
    vector_spec = pl.BlockSpec((8, width), lambda t: (0, 0))
    low = jax.ShapeDtypeStruct((length, width), bf16)
    return pl.pallas_call(
        functools.partial(combine_kernel, last),
        grid=(length // rows,),
        in_specs=[
            pl.BlockSpec((slots, width), lambda t: (0, 0)), lanes, wide, lanes, vector_spec,
            vector_spec,
        ],
        out_specs=[wide] * (TOP + 1 if last else TOP + 2),
        out_shape=[low, low, low]
        if last
        else [low, low, jax.ShapeDtypeStruct((length, width), f32), low],
        compiler_params=pltpu.CompilerParams(vmem_limit_bytes=24 * MIB),
        cost_estimate=pl.CostEstimate(
            flops=4 * slots * length * width, bytes_accessed=(2 * slots + 14 * length) * width,
            transcendentals=0,
        ),
        name="combine",
    )(back, columns, mid, scalars, vectors, vectors if last else next_vectors)


def token_backward_kernel(
    has_prior, back_ref, columns_ref, grad_ref, mid_ref, scalars_ref, branch0_ref, branch1_ref,
    low_ref, prior_ref, attended_ref, routes_ref, out_w_ref, small_w_ref, vectors_ref,
    residual_ref, *rest
):
    d_mid_ref, d_att_ref, d_prior_ref, g_out_ref, g_small_ref, g_residual_ref, g_gain_ref = (
        rest[-7:]
    )
    step = pl.program_id(0)
    rows = mid_ref.shape[0]
    columns, scalars = columns_ref[...], scalars_ref[...]
    grad = grad_ref[...].astype(f32)
    mid = mid_ref[...]
    gain = vectors_ref[MOE_GAIN_ROW : MOE_GAIN_ROW + 1, :]
    scale = scalars[:, SCALE : SCALE + 1]
    unit = mid * scale
    lane = lane_iota(rows)

    def scalar(index):
        return scalars[:, index : index + 1]

    def row_sum(values):
        return jnp.sum(values, axis=1, keepdims=True)

    along = row_sum(grad * (unit * gain))
    along_vector = [
        row_sum(grad * vectors_ref[VECTOR_ROW + j : VECTOR_ROW + j + 1, :]) for j in range(2)
    ]
    d_gate = []
    for k, branch_ref in enumerate((branch0_ref, branch1_ref)):
        value = row_sum(grad * branch_ref[...].astype(f32)) + scalar(OF_NORMED + k) * along
        for j in range(2):
            value += scalar(CHOSEN + 2 * k + j) * along_vector[j]
        d_gate.append(value)
    d_choice = scalar(GATE) * scalar(GATE + 1) * (d_gate[0] - d_gate[1])
    d_small = jnp.where(
        lane == routes_ref[:, 0:1], d_choice, jnp.where(lane == routes_ref[:, 1:2], -d_choice, 0.0)
    )
    if has_prior:
        d_small += jnp.where(lane < ROUTED, rest[0][...], 0.0)
    d_logits = d_small
    for j in range(2):
        value = scalar(MIX + j) * (along - along_vector[j])
        at = ROUTED + 2 * j
        d_small = jnp.where(lane == at, value, jnp.where(lane == at + 1, -value, d_small))
    d_small_low = d_small.astype(bf16)
    d_prior_ref[...] = lax.dot_general(
        d_logits, residual_ref[...], (((1,), (1,)), ((), ())), precision=highest
    )
    vector_shares = placed_on_lanes(
        rows, {ROUTED + 4 + j: scalar(VECTOR_SHARE + j) for j in range(2)}
    ).astype(bf16)
    g_small = dot_on(low_ref[...], d_small_low, 0, 0) + dot_on(
        grad.astype(bf16), vector_shares, 0, 0
    )
    g_residual = lax.dot_general(
        prior_ref[...], d_logits, (((0,), (0,)), ((), ())), precision=highest
    )
    d_normed = (
        dot_on(selection(columns, back_ref.shape[0], (0, 1)), back_ref[...], 1, 0)
        + scalar(NORMED_SHARE) * grad
        + dot_on(d_small_low, small_w_ref[...], 1, 1)
    )
    g_gain = jnp.sum(d_normed * unit, axis=0, keepdims=True)
    d_unit = d_normed * gain
    d_mid = grad + (d_unit - unit * jnp.mean(d_unit * unit, axis=-1, keepdims=True)) * scale
    d_mid_ref[...] = d_mid
    d_mid_low = d_mid.astype(bf16)
    d_att_ref[...] = dot_on(d_mid_low, out_w_ref[...], 1, 1).astype(bf16)
    g_out = dot_on(attended_ref[...], d_mid_low, 0, 0)

    @pl.when(step == 0)
    def _():
        g_out_ref[...] = g_out
        g_small_ref[...] = g_small
        g_residual_ref[...] = g_residual
        g_gain_ref[...] = jnp.broadcast_to(g_gain, g_gain_ref.shape)

    @pl.when(step > 0)
    def _():
        g_out_ref[...] += g_out
        g_small_ref[...] += g_small
        g_residual_ref[...] += g_residual
        g_gain_ref[...] += jnp.broadcast_to(g_gain, g_gain_ref.shape)


def token_backward(back, kept, grad, weights, columns, routes, d_prior, after):
    length, width = grad.shape
    slots = back.shape[0]
    rows = min(256, length)
    wide = pl.BlockSpec((rows, width), lambda t: (t, 0))
    lanes = pl.BlockSpec((rows, LANES), lambda t: (t, 0))

    def fixed(*shape, at=0):
        return pl.BlockSpec(shape, lambda t: (0, at))

    operands = [
        back, columns, grad, kept["mid"], kept["scalars"], kept["branch"][0], kept["branch"][1],
        kept["low"], kept["prior"], kept["attended"], routes, weights["dense"], weights["dense"],
        weights["vectors"], weights["residual"],
    ]
    specs = [
        fixed(slots, width), lanes, wide, wide, lanes, wide, wide, wide, lanes, wide,
        pl.BlockSpec((rows, TOP), lambda t: (t, 0)), fixed(width, width, at=3),
        fixed(width, LANES, at=4 * width // LANES), fixed(8, width), fixed(LANES, LANES),
    ]
    if d_prior is not None:
        operands.append(d_prior)
        specs.append(lanes)
    return pl.pallas_call(
        functools.partial(token_backward_kernel, d_prior is not None),
        grid=(length // rows,),
        in_specs=specs + [ANY_SPEC] * len(after),
        out_specs=[
            wide, wide, lanes, fixed(width, width), fixed(width, LANES), fixed(LANES, LANES),
            fixed(8, width),
        ],
        out_shape=[
            jax.ShapeDtypeStruct((length, width), f32),
            jax.ShapeDtypeStruct((length, width), bf16),
            jax.ShapeDtypeStruct((length, LANES), f32),
            jax.ShapeDtypeStruct((width, width), f32),
            jax.ShapeDtypeStruct((width, LANES), f32),
            jax.ShapeDtypeStruct((LANES, LANES), f32),
            jax.ShapeDtypeStruct((8, width), f32),
        ],
        compiler_params=pltpu.CompilerParams(vmem_limit_bytes=48 * MIB),
        cost_estimate=pl.CostEstimate(
            flops=2 * length * width * (slots + 2 * width),
            bytes_accessed=(2 * slots + 24 * length) * width, transcendentals=0,
        ),
        name="token_backward",
    )(*operands, *after)


def fetch_layer(layer, local):
    width = local["w_query"].shape[2]
    shard = local["w_query"].shape[1]
    const_w = jnp.transpose(local["w_const"][layer], (1, 0, 2)).reshape(shard, 4)
    small = jnp.concatenate(
        [
            local["w_router"][layer], const_w, local["const_vec"][layer].T,
            local["norm_attn"][layer][:, None], local["norm_moe"][layer][:, None],
            jnp.zeros((shard, LANES - ROUTED - 8), bf16),
        ],
        axis=1,
    )
    packed = jnp.concatenate(
        [local["w_query"][layer], local["w_key"][layer], local["w_value"][layer],
         local["w_out"][layer], small],
        axis=1,
    )
    dense = lax.all_gather(packed, SHARDED, axis=0, tiled=True)
    gate_up = jnp.concatenate([local["w_gate"][layer], local["w_up"][layer]], axis=0)
    gate_up = lax.all_gather(gate_up, SHARDED, axis=1, tiled=True)
    down = lax.all_gather(local["w_down"][layer], SHARDED, axis=1, tiled=True)
    at = 4 * width + ROUTED + 4
    vectors = dense[:, at : at + 8].T.astype(f32)
    residual = local["w_res"][layer].astype(f32)
    blank = LANES - ROUTED
    return dict(
        dense=dense, vectors=vectors, gate_up=gate_up, down=down,
        residual=jnp.pad(residual, ((0, blank), (0, blank))),
    )


def per_device(
    hidden_in, segments, routes, prev_logits, out_grad, norm_attn, w_query, w_key, w_value,
    w_out, norm_moe, w_router, w_res, w_const, const_vec, w_gate, w_up, w_down,
):
    local = dict(
        norm_attn=norm_attn, w_query=w_query, w_key=w_key, w_value=w_value, w_out=w_out,
        norm_moe=norm_moe, w_router=w_router, w_res=w_res, w_const=w_const,
        const_vec=const_vec, w_gate=w_gate, w_up=w_up, w_down=w_down,
    )
    micro_count, _, length, width = hidden_in.shape
    micros = range(micro_count)
    layers = norm_attn.shape[0]
    groups = lax.axis_size("expert")
    hop_count = min((WINDOW + length - 2) // length, lax.axis_size("context") - 1)
    capacity = length // 4
    slots = EXPERTS * capacity
    block_start = lax.axis_index("context") * length
    hidden_earlier = earlier_rows(hidden_in[:, 0], hop_count)
    fetched = [fetch_layer(layer, local) for layer in range(layers)]
    routes = routes[:, 0]
    columns, slot_rows = routing_slots(routes, groups, capacity)
    blank_gates = jnp.zeros((8, length), f32)

    def to_experts(rows):
        return exchange(rows, groups, capacity).reshape(
            EXPERTS // groups, groups * capacity, rows.shape[1]
        )

    def to_tokens(rows):
        return exchange(rows.reshape(-1, width), groups, capacity).reshape(-1, width)

    def normed(hidden, gain):
        return (hidden * inverse_rms(hidden) * gain).astype(bf16)

    segs, early, state = [], [], []
    for micro in micros:
        whole = segments[micro, 0]
        padded = jnp.concatenate([jnp.full((WINDOW,), -1, jnp.int32), whole])
        query = lax.dynamic_slice_in_dim(whole, block_start, length, 0)
        key = lax.dynamic_slice_in_dim(padded, block_start, WINDOW + length, 0)
        segs.append((query, key))
        sent = dispatch(out_grad[micro, 0], slot_rows[micro], blank_gates, "plain", slots)
        early.append(to_experts(sent))
        hidden = hidden_in[micro, 0].astype(f32)
        gain = fetched[0]["vectors"][ATTN_GAIN_ROW : ATTN_GAIN_ROW + 1]
        prior = jnp.pad(prev_logits[micro, 0], ((0, 0), (0, LANES - ROUTED)))
        state.append(
            (
                hidden, normed(hidden, gain),
                normed(hidden_earlier[micro].astype(f32), gain), prior,
            )
        )

    saved = [[None] * layers for _ in micros]

    def attention_part(layer, micro, after):
        weights = fetched[layer]
        hidden, attn_in, attn_earlier, prior = state[micro]
        qkv = dot_on(attn_in, weights["dense"][:, : 3 * width], 1, 0).astype(bf16)
        kv_earlier = dot_on(attn_earlier, weights["dense"][:, width : 3 * width], 1, 0).astype(bf16)
        query, key = segs[micro]
        attended, lse = attention_forward(qkv, kv_earlier, query[:, None], key[None, :], after)
        mid, low, logits, scalars, gate_rows = attention_output(
            hidden, attended, weights, prior, routes[micro]
        )
        mode = "with gate" if layer == layers - 1 else "plain"
        sent = dispatch(low, slot_rows[micro], gate_rows, mode, slots)
        saved[micro][layer] = dict(
            hidden=hidden, attn_in=attn_in, attn_earlier=attn_earlier, prior=prior, qkv=qkv,
            kv_earlier=kv_earlier, attended=attended, lse=lse, mid=mid, low=low,
            scalars=scalars, gate_rows=gate_rows, logits=logits, arrived=to_experts(sent),
        )
        return sent

    def experts_part(layer, micro, after):
        kept = saved[micro][layer]
        produced, kept["gate_pre"], kept["up_pre"] = experts_forward(
            kept["arrived"], fetched[layer]["gate_up"], fetched[layer]["down"], after
        )
        kept["returned"] = to_tokens(produced)
        return produced

    def combine_part(layer, micro):
        kept = saved[micro][layer]
        last = layer == layers - 1
        outs = combine(
            kept["returned"], columns[micro], kept["mid"], kept["scalars"],
            fetched[layer]["vectors"], None if last else fetched[layer + 1]["vectors"],
        )
        kept["branch"] = outs[:TOP]
        if last:
            return outs[TOP]
        state[micro] = (
            outs[TOP], outs[TOP + 1], earlier_rows(outs[TOP + 1], hop_count), kept["logits"],
        )
        return None

    expert_sums = [None] * layers

    def experts_back_part(layer, micro, d_rows, after):
        kept = saved[micro][layer]
        dx, *expert_sums_new = experts_backward(
            kept["arrived"], d_rows, kept["gate_pre"], kept["up_pre"],
            fetched[layer]["gate_up"], fetched[layer]["down"], layer == layers - 1,
            expert_sums[layer], after,
        )
        expert_sums[layer] = tuple(expert_sums_new)
        kept["back"] = to_tokens(dx)
        return dx

    dense_parts = [[None] * micro_count for _ in range(layers)]
    residual_parts = [[None] * micro_count for _ in range(layers)]

    def attention_back_part(layer, micro, grad, d_prior, after):
        kept, weights = saved[micro][layer], fetched[layer]
        d_mid, d_att, d_prior, g_out, g_small, g_residual, g_moe_gain = token_backward(
            kept["back"], kept, grad, weights, columns[micro], routes[micro], d_prior, after
        )
        query, key = segs[micro]
        dq, dk, dv = attention_backward(
            kept["qkv"], kept["kv_earlier"], d_att, kept["attended"], kept["lse"],
            query[None, :], key[:, None], (),
        )
        dense = weights["dense"]
        query_w, key_w, value_w = (dense[:, i * width : (i + 1) * width] for i in range(3))
        d_earlier = (
            dot_on(dk[:WINDOW], key_w, 1, 1) + dot_on(dv[:WINDOW], value_w, 1, 1)
        ).astype(bf16)
        later = returned_rows(d_earlier, length, hop_count) if hop_count > 0 else 0.0
        d_attn = (
            dot_on(dq, query_w, 1, 1)
            + dot_on(dk[WINDOW:], key_w, 1, 1)
            + dot_on(dv[WINDOW:], value_w, 1, 1)
        )
        grads = [
            dot_on(kept["attn_in"], dq, 0, 0),
            dot_on(kept["attn_in"], dk[WINDOW:], 0, 0)
            + dot_on(kept["attn_earlier"], dk[:WINDOW], 0, 0),
            dot_on(kept["attn_in"], dv[WINDOW:], 0, 0)
            + dot_on(kept["attn_earlier"], dv[:WINDOW], 0, 0),
            g_out,
            g_small,
        ]
        residual_parts[layer][micro] = g_residual
        return d_mid, d_prior, d_attn, later, grads, g_moe_gain[0], dq

    def finish_back_part(layer, micro, parts):
        d_mid, d_prior, d_attn, later, grads, g_moe_gain, _ = parts
        hidden = saved[micro][layer]["hidden"]
        gain = fetched[layer]["vectors"][ATTN_GAIN_ROW : ATTN_GAIN_ROW + 1]
        d_attn = d_attn + later
        scale = inverse_rms(hidden)
        unit = hidden * scale
        g_attn_gain = jnp.sum(d_attn * unit, axis=0)
        d_unit = d_attn * gain
        d_hidden = d_mid + (
            d_unit - unit * jnp.mean(d_unit * unit, axis=-1, keepdims=True)
        ) * scale
        lane = jnp.arange(LANES)[None, :]
        grads[4] = (
            grads[4]
            + jnp.where(lane == ROUTED + 6, g_attn_gain[:, None], 0.0)
            + jnp.where(lane == ROUTED + 7, g_moe_gain[:, None], 0.0)
        )
        dense_parts[layer][micro] = grads
        return d_hidden, d_prior

    expert_shares, dense_shares = [None] * layers, [None] * layers

    def reduce_experts(layer):
        gate_up, down = expert_sums[layer]
        gate_up = gate_up.reshape((-1,) + gate_up.shape[2:])
        expert_shares[layer] = (
            lax.psum_scatter(gate_up, SHARDED, scatter_dimension=1, tiled=True),
            lax.psum_scatter(down, SHARDED, scatter_dimension=1, tiled=True),
        )
        return expert_shares[layer]

    def reduce_dense(layer):
        sums = [sum(parts[1:], parts[0]).astype(bf16) for parts in zip(*dense_parts[layer])]
        packed = jnp.concatenate(sums, axis=1)
        share = lax.psum_scatter(packed, SHARDED, scatter_dimension=0, tiled=True)
        dense_shares[layer] = lax.psum(share, "expert")
        return (dense_shares[layer],)

    last = layers - 1
    before = ()
    for layer in range(layers):
        for micro in micros:
            if layer > 0:
                combine_part(layer - 1, micro)
        for micro in micros:
            before = (attention_part(layer, micro, before),)
        for micro in micros:
            before = (experts_part(layer, micro, before),)
            if layer == last:
                before = (experts_back_part(layer, micro, early[micro], before),)
    hidden_out = [combine_part(last, micro) for micro in micros]
    expert_ready = reduce_experts(last)

    grads = [(out_grad[micro, 0], None) for micro in micros]
    waits = ()
    for layer in range(last, -1, -1):
        parts = []
        for micro in micros:
            parts.append(attention_back_part(layer, micro, *grads[micro], before + waits))
            before = (parts[-1][-1],)
        grads = [finish_back_part(layer, micro, parts[micro]) for micro in micros]
        if layer > 0:
            dense_ready = reduce_dense(layer)
            sent = [
                dispatch(
                    grads[micro][0], slot_rows[micro], saved[micro][layer - 1]["gate_rows"],
                    "scaled", slots, before,
                )
                for micro in micros
            ]
            before = (sent[-1],)
            d_rows = [to_experts(rows) for rows in sent]
            for micro in micros:
                before = (experts_back_part(layer - 1, micro, d_rows[micro], before),)
            waits = tuple(expert_ready)
            expert_ready = reduce_experts(layer - 1)
    reduce_dense(0)
    residual_total = lax.psum(
        jnp.stack([sum(parts[1:], parts[0]) for parts in residual_parts])[:, :ROUTED, :ROUTED],
        ("expert", "context", "dp"),
    )
    hidden_out = jnp.stack(hidden_out)[:, None]
    hidden_grad = jnp.stack([grad[0].astype(bf16) for grad in grads])[:, None]

    dense = jnp.stack(dense_shares).astype(f32)
    small = dense[:, :, 4 * width :]
    shard = small.shape[1]
    experts_total = [jnp.stack(parts).astype(f32) for parts in zip(*expert_shares)]
    per_dev = EXPERTS // groups
    return (
        hidden_out,
        hidden_grad,
        small[:, :, ROUTED + 6],
        dense[:, :, :width],
        dense[:, :, width : 2 * width],
        dense[:, :, 2 * width : 3 * width],
        dense[:, :, 3 * width : 4 * width],
        small[:, :, ROUTED + 7],
        small[:, :, :ROUTED],
        residual_total,
        jnp.transpose(
            small[:, :, ROUTED : ROUTED + 4].reshape(layers, shard, 2, 2), (0, 2, 1, 3)
        ),
        jnp.transpose(small[:, :, ROUTED + 4 : ROUTED + 6], (0, 2, 1)),
        experts_total[0][:, :per_dev],
        experts_total[0][:, per_dev:],
        experts_total[1],
    )


def solution(mesh):
    tokens = P(None, ("expert", "dp"), "context", None)
    rows = P(None, SHARDED, None)
    vector = P(None, SHARDED)
    experts = P(None, "expert", SHARDED, None)
    const = P(None, None, SHARDED, None)
    const_vector = P(None, None, SHARDED)
    return jax.shard_map(
        per_device,
        mesh=mesh,
        in_specs=(
            tokens, P(None, ("expert", "dp"), None), tokens, tokens, tokens, vector, rows, rows,
            rows, rows, vector, rows, P(), const, const_vector, experts, experts, experts,
        ),
        out_specs=(
            tokens, tokens, vector, rows, rows, rows, rows, vector, rows, P(), const,
            const_vector, experts, experts, experts,
        ),
        check_vma=False,
    )
```

time: 4370 us -> 2210 us (0.51)
  matrix products: 1860 us -> 163 us
  Pallas kernels: 0 us -> 853 us
  other arithmetic: 523 us -> 43.4 us
  waiting for transfers between devices: 1140 us -> 788 us
  local copies, waits for them, and re-layouts: 472 us -> 193 us
  blocking collectives: 236 us -> 40.6 us
    dot_general x162 -> x48, matrix products: 1690 us -> 163 us  [dot_on(): lax.dot_general(left_op, right_op, (((left_dim,), (right_dim,)), ((), ())...]
    pallas_call x0 -> x37, Pallas kernels: none -> 853 us  [the longest x4 211 us: experts_backward(): pl.pallas_call(functools.partial(experts_backward_kernel, chunks, has_gat...]
    convert_element_type x23 -> x6, other arithmetic: 347 us -> 10.2 us  [the longest x1 5.07 us: per_device(): hidden = hidden_in[micro, 0].astype(f32)]
    ppermute x8 -> x7, waiting for transfers between devices: 364 us -> 184 us  [passed_along(): return lax.ppermute(block, axis, route)]
    sub x4 -> x0, matrix products: 170 us -> none  [attention_forward(): exponent = jnp.exp(scores - row_max)]
    all_gather x6 -> x0, blocking collectives: 146 us -> none  [the longest x2 107 us: fetch_layer(): lax.all_gather(router_w[current_layer_index], ('context', 'dp'), axis=0,...]
    reduce_scatter x28 -> x6, waiting for transfers between devices: 307 us -> 219 us  [the longest x2 109 us: reduce_dense(): share = lax.psum_scatter(packed, SHARDED, scatter_dimension=0, tiled=True)]
    dot_general x8 -> x0, local copies, waits for them, and re-layouts: 82.1 us -> none  [mixture(): jnp.einsum('tkj,tjd->tkd', chosen_onehot[:, :, EXPERTS + 2:], constant, p...]
  transfers between devices with their start and end apart: 79 -> 36, of which waited for: 23 -> 21; matrix products, arithmetic and copies ran while one was open for 58% -> 14% of each run, Pallas kernels for 0% -> 32%
where the time goes in v1:
time: 2210 us; the launch traced here: 2200 us
  Pallas kernels  853 us (39%)
  waiting for transfers between devices  788 us (36%)
  local copies, waits for them, and re-layouts  193 us (9%)
  matrix products  163 us (7%)
  starting transfers between devices  99.3 us (4%)
  other arithmetic  43.4 us (2%)
  blocking collectives  40.6 us (2%)
    all_to_all x16, waiting for transfers between devices, exchange(): lax.all_to_all(rows.reshape((EXPERTS // groups, groups, capacity) + rows....  332 us
    pallas_call x4, Pallas kernels, experts_backward(): pl.pallas_call(functools.partial(experts_backward_kernel, chunks, has_gat...  211 us
    pallas_call x4, Pallas kernels, attention_backward(): pl.pallas_call(functools.partial(attention_backward_kernel, rows, keys, b...  193 us
    ppermute x7, waiting for transfers between devices, passed_along(): return lax.ppermute(block, axis, route)  184 us
    dot_general x48, matrix products, dot_on(): lax.dot_general(left_op, right_op, (((left_dim,), (right_dim,)), ((), ())...  163 us
    pallas_call x4, Pallas kernels, attention_forward(): pl.pallas_call(functools.partial(attention_forward_kernel, rows, keys, bl...  129 us
    reduce_scatter x2, waiting for transfers between devices, reduce_dense(): share = lax.psum_scatter(packed, SHARDED, scatter_dimension=0, tiled=True)  109 us
    pallas_call x4, Pallas kernels, experts_forward(): pl.pallas_call(functools.partial(experts_forward_kernel, chunks), grid=(c...  104 us
  transfers between devices with their start and end apart: 36, of which 21 were waited for; matrix products, arithmetic and copies ran while one was open for 14% of the time, Pallas kernels for 32%

profile of v1, /device:TPU:2, one launch (start us, length us, event | category | flops | bytes accessed | tf_op | source)
XLA Modules:
  0.0 2197.0 jit_solution(10223391063968877267)
XLA Ops:
  27.1 5.2 collective-permute-start
  63.8 72.5 %collective-permute-done = bf16[2,1024,768]{2,1,0:T(8,128)(2,1)} collective-permute-done((bf16[2,1024,768]{2,1,0:T(8,128)(2,1)}, bf16[2,1024,768]{2,1,0:T(8,128)(2,1)}, u32[]{:S(2)}, u32[]{:S(2)}) %collective-permute-start) | collective-permute-done | bytes 3145760 | tf_op jit(solution)/shard_map/ppermute | solution.py:417
  147.4 7.3 convolution_convert_fusion.3.q_ref.ko_ref.vo_ref
  154.7 32.2 %attention_forward.4 = (bf16[1024,768]{1,0:T(8,128)(2,1)S(1)}, f32[16,1024]{1,0:T(8,128)S(1)}) custom-call(bf16[1024,2304]{1,0:T(8,128)(2,1)S(1)} %convolution_convert_fusion.3.q_ref.ko_ref.vo_ref, bf16[1024,2304]{1,0:T(8,128)(2,1)S(1)} %convolution_convert_fusion.3.q_ref.ko_ref.vo_ref, bf16[1024,2304]{1,0:T(8,128)(2,1)S(1)} %convolution_convert_fusion.3.q_ref.ko_ref.vo_ref, ...), custom_call_target="tpu_custom_call" | custom-call | flops 16106127360 | bytes 9437184 | tf_op jit(solution)/shard_map/attention_forward/pallas_call | solution.py:116
  187.6 7.9 attention_output.4
  205.1 5.2 all-to-all-start
  219.8 7.2 convolution_convert_fusion.2.q_ref.ko_ref.vo_ref
  227.0 32.2 %attention_forward.5 = (bf16[1024,768]{1,0:T(8,128)(2,1)S(1)}, f32[16,1024]{1,0:T(8,128)S(1)}) custom-call(bf16[1024,2304]{1,0:T(8,128)(2,1)S(1)} %convolution_convert_fusion.2.q_ref.ko_ref.vo_ref, bf16[1024,2304]{1,0:T(8,128)(2,1)S(1)} %convolution_convert_fusion.2.q_ref.ko_ref.vo_ref, bf16[1024,2304]{1,0:T(8,128)(2,1)S(1)} %convolution_convert_fusion.2.q_ref.ko_ref.vo_ref, ...), custom_call_target="tpu_custom_call" | custom-call | flops 16106127360 | bytes 9437184 | tf_op jit(solution)/shard_map/attention_forward/pallas_call | solution.py:116
  259.9 7.9 attention_output.5
  267.9 5.3 dispatch.9.rest_0_
  288.6 26.3 %experts_forward.4 = (bf16[2,1024,768]{2,1,0:T(8,128)(2,1)S(1)}, bf16[2,1024,2048]{2,1,0:T(8,128)(2,1)}, bf16[2,1024,2048]{2,1,0:T(8,128)(2,1)}) custom-call(bf16[2,1024,768]{2,1,0:T(8,128)(2,1)} %bitcast.284, bf16[4,768,2048]{2,1,0:T(8,128)(2,1)} %all-gather.11.cloned.1.call-done.gate_w_ref.up_w_ref.refs_4_.refs_5_, ...), custom_call_target="tpu_custom_call" | custom-call | flops 19327352832 | bytes 41943040 | tf_op jit(solution)/shard_map/experts_forward/pallas_call | solution.py:291
  318.5 36.6 %all-to-all-done.2 = bf16[2,4,256,768]{3,2,0,1:T(8,128)(2,1)} async-done(((bf16[2,4,256,768]{3,2,0,1:T(8,128)(2,1)}), bf16[2,4,256,768]{3,2,0,1:T(8,128)(2,1)}, u32[]{:S(2)}, u32[]{:S(2)}) %all-to-all-start.2) | async-done | bytes 3145760 | tf_op jit(solution)/shard_map/all_to_all | solution.py:443
  369.5 60.5 %all-to-all-done.1 = bf16[2,4,256,768]{3,2,0,1:T(8,128)(2,1)} async-done(((bf16[2,4,256,768]{3,2,0,1:T(8,128)(2,1)}), bf16[2,4,256,768]{3,2,0,1:T(8,128)(2,1)}, u32[]{:S(2)}, u32[]{:S(2)}) %all-to-all-start.1) | async-done | bytes 3145760 | tf_op jit(solution)/shard_map/all_to_all | solution.py:443
  440.9 25.9 %experts_forward.5 = (bf16[2,1024,768]{2,1,0:T(8,128)(2,1)S(1)}, bf16[2,1024,2048]{2,1,0:T(8,128)(2,1)}, bf16[2,1024,2048]{2,1,0:T(8,128)(2,1)}) custom-call(bf16[2,1024,768]{2,1,0:T(8,128)(2,1)} %bitcast.286, bf16[4,768,2048]{2,1,0:T(8,128)(2,1)} %all-gather.11.cloned.1.call-done.gate_w_ref.up_w_ref.refs_4_.refs_5_, ...), custom_call_target="tpu_custom_call" | custom-call | flops 19327352832 | bytes 41943040 | tf_op jit(solution)/shard_map/experts_forward/pallas_call | solution.py:291
  473.3 31.9 %all-to-all-done.10 = bf16[2,4,256,768]{3,2,0,1:T(8,128)(2,1)} async-done(((bf16[2,4,256,768]{3,2,0,1:T(8,128)(2,1)}), bf16[2,4,256,768]{3,2,0,1:T(8,128)(2,1)}, u32[]{:S(2)}, u32[]{:S(2)}) %all-to-all-start.10) | async-done | bytes 3145760 | tf_op jit(solution)/shard_map/all_to_all | solution.py:443
  514.8 8.1 combine.4
  534.3 28.1 %collective-permute-done.1 = bf16[1024,768]{1,0:T(8,128)(2,1)S(1)} collective-permute-done((bf16[1024,768]{1,0:T(8,128)(2,1)S(1)}, bf16[1024,768]{1,0:T(8,128)(2,1)S(1)}, u32[]{:S(2)}, u32[]{:S(2)}) %collective-permute-start.1) | collective-permute-done | bytes 1572896 | tf_op jit(solution)/shard_map/ppermute | solution.py:417
  566.6 32.2 %attention_forward.6 = (bf16[1024,768]{1,0:T(8,128)(2,1)S(1)}, f32[16,1024]{1,0:T(8,128)S(1)}) custom-call(bf16[1024,2304]{1,0:T(8,128)(2,1)S(1)} %convolution_convert_fusion.1.q_ref.ko_ref.vo_ref, bf16[1024,2304]{1,0:T(8,128)(2,1)S(1)} %convolution_convert_fusion.1.q_ref.ko_ref.vo_ref, bf16[1024,2304]{1,0:T(8,128)(2,1)S(1)} %convolution_convert_fusion.1.q_ref.ko_ref.vo_ref, ...), custom_call_target="tpu_custom_call" | custom-call | flops 16106127360 | bytes 9437184 | tf_op jit(solution)/shard_map/attention_forward/pallas_call | solution.py:116
  598.9 8.1 attention_output.6
  607.0 5.6 dispatch.10.rest_0_
  625.9 8.0 combine.5
  644.9 27.7 %collective-permute-done.2 = bf16[1024,768]{1,0:T(8,128)(2,1)S(1)} collective-permute-done((bf16[1024,768]{1,0:T(8,128)(2,1)S(1)}, bf16[1024,768]{1,0:T(8,128)(2,1)S(1)}, u32[]{:S(2)}, u32[]{:S(2)}) %collective-permute-start.2) | collective-permute-done | bytes 1572896 | tf_op jit(solution)/shard_map/ppermute | solution.py:417
  676.6 32.3 %attention_forward.7 = (bf16[1024,768]{1,0:T(8,128)(2,1)S(1)}, f32[16,1024]{1,0:T(8,128)S(1)}) custom-call(bf16[1024,2304]{1,0:T(8,128)(2,1)S(1)} %convolution_convert_fusion.q_ref.ko_ref.vo_ref, bf16[1024,2304]{1,0:T(8,128)(2,1)S(1)} %convolution_convert_fusion.q_ref.ko_ref.vo_ref, bf16[1024,2304]{1,0:T(8,128)(2,1)S(1)} %convolution_convert_fusion.q_ref.ko_ref.vo_ref, ...), custom_call_target="tpu_custom_call" | custom-call | flops 16106127360 | bytes 9437184 | tf_op jit(solution)/shard_map/attention_forward/pallas_call | solution.py:116
  708.9 8.1 attention_output.7
  717.0 5.6 dispatch.11.rest_0_
  726.6 5.2 all-to-all-start.6
  735.9 25.9 %experts_forward.6 = (bf16[2,1024,768]{2,1,0:T(8,128)(2,1)S(1)}, bf16[2,1024,2048]{2,1,0:T(8,128)(2,1)}, bf16[2,1024,2048]{2,1,0:T(8,128)(2,1)}) custom-call(bf16[2,1024,896]{2,1,0:T(8,128)(2,1)} %bitcast.278, bf16[4,768,2048]{2,1,0:T(8,128)(2,1)} %all-gather.15.cloned.1.call-done.gate_w_ref.up_w_ref.refs_4_.refs_5_, ...), custom_call_target="tpu_custom_call" | custom-call | flops 19327352832 | bytes 41943040 | tf_op jit(solution)/shard_map/experts_forward/pallas_call | solution.py:291
  765.4 46.0 %all-to-all-done.6 = bf16[2,4,256,896]{3,2,0,1:T(8,128)(2,1)} async-done(((bf16[2,4,256,896]{3,2,0,1:T(8,128)(2,1)}), bf16[2,4,256,896]{3,2,0,1:T(8,128)(2,1)}, u32[]{:S(2)}, u32[]{:S(2)}) %all-to-all-start.6) | async-done | bytes 3670048 | tf_op jit(solution)/shard_map/all_to_all | solution.py:443
  819.8 53.0 %experts_backward.4 = (bf16[2,1024,768]{2,1,0:T(8,128)(2,1)}, bf16[2,2,768,2048]{3,2,1,0:T(8,128)(2,1)}, bf16[2,2048,768]{2,1,0:T(8,128)(2,1)}) custom-call(bf16[2,1024,896]{2,1,0:T(8,128)(2,1)} %bitcast.279, bf16[2,1024,768]{2,1,0:T(8,128)(2,1)} %bitcast.292, bf16[2,1024,2048]{2,1,0:T(8,128)(2,1)} %get-tuple-element.149.refs_2_, ...), custom_call_target="tpu_custom_call" | custom-call | flops 38654705664 | bytes 60817408 | tf_op jit(solution)/shard_map/experts_backward/pallas_call | solution.py:393
  876.6 9.7 all-to-all-done.5
  904.3 25.9 %experts_forward.7 = (bf16[2,1024,768]{2,1,0:T(8,128)(2,1)S(1)}, bf16[2,1024,2048]{2,1,0:T(8,128)(2,1)}, bf16[2,1024,2048]{2,1,0:T(8,128)(2,1)}) custom-call(bf16[2,1024,896]{2,1,0:T(8,128)(2,1)} %bitcast.281, bf16[4,768,2048]{2,1,0:T(8,128)(2,1)} %all-gather.15.cloned.1.call-done.gate_w_ref.up_w_ref.refs_4_.refs_5_, ...), custom_call_target="tpu_custom_call" | custom-call | flops 19327352832 | bytes 41943040 | tf_op jit(solution)/shard_map/experts_forward/pallas_call | solution.py:291
  933.0 28.4 %all-to-all-done.9 = bf16[2,4,256,768]{3,2,0,1:T(8,128)(2,1)} async-done(((bf16[2,4,256,768]{3,2,0,1:T(8,128)(2,1)}), bf16[2,4,256,768]{3,2,0,1:T(8,128)(2,1)}, u32[]{:S(2)}, u32[]{:S(2)}) %all-to-all-start.9) | async-done | bytes 3145760 | tf_op jit(solution)/shard_map/all_to_all | solution.py:443
  966.1 54.1 %experts_backward.5 = (bf16[2,1024,768]{2,1,0:T(8,128)(2,1)}, bf16[2,2,768,2048]{3,2,1,0:T(8,128)(2,1)}, bf16[2,2048,768]{2,1,0:T(8,128)(2,1)}) custom-call(bf16[2,1024,896]{2,1,0:T(8,128)(2,1)} %bitcast.282, bf16[2,1024,768]{2,1,0:T(8,128)(2,1)} %bitcast.289, bf16[2,1024,2048]{2,1,0:T(8,128)(2,1)} %get-tuple-element.158.refs_2_, ...), custom_call_target="tpu_custom_call" | custom-call | flops 38654705664 | bytes 60817408 | tf_op jit(solution)/shard_map/experts_backward/pallas_call | solution.py:393
  1030.0 8.0 combine.6
  1041.5 25.6 %token_backward.4 = (f32[1024,768]{1,0:T(8,128)}, bf16[1024,768]{1,0:T(8,128)(2,1)S(1)}, f32[1024,128]{1,0:T(8,128)S(1)}, f32[768,768]{1,0:T(8,128)}, f32[768,12...) custom-call(bf16[2048,768]{1,0:T(8,128)(2,1)} %bitcast.276, s32[1024,128]{1,0:T(8,128)S(1)} %copy-done.29, ...), custom_call_target="tpu_custom_call" | custom-call | flops 5637144576 | bytes 22020096 | tf_op jit(solution)/shard_map/token_backward/pallas_call | solution.py:827
  1070.5 5.5 all-to-all-start.11
  1077.8 48.1 %attention_backward.4 = (bf16[1024,768]{1,0:T(8,128)(2,1)S(1)}, bf16[2048,768]{1,0:T(8,128)(2,1)}, bf16[2048,768]{1,0:T(8,128)(2,1)}) custom-call(bf16[1024,2304]{1,0:T(8,128)(2,1)} %copy-done.139, bf16[1024,2304]{1,0:T(8,128)(2,1)} %copy-done.139, bf16[1024,2304]{1,0:T(8,128)(2,1)} %copy-done.139, bf16[1024,1536]{1,0:T(8,128)(2,1)} %copy-done.137, ...), custom_call_target="tpu_custom_call" | custom-call | flops 40265318400 | bytes 18874368 | tf_op jit(solution)/shard_map/attention_backward/pallas_call | solution.py:216
  1137.2 8.3 combine.7
  1152.9 25.6 %token_backward.5 = (f32[1024,768]{1,0:T(8,128)}, bf16[1024,768]{1,0:T(8,128)(2,1)S(1)}, f32[1024,128]{1,0:T(8,128)S(1)}, f32[768,768]{1,0:T(8,128)}, f32[768,12...) custom-call(bf16[2048,768]{1,0:T(8,128)(2,1)} %bitcast.277, s32[1024,128]{1,0:T(8,128)S(1)} %copy-done.36, ...), custom_call_target="tpu_custom_call" | custom-call | flops 5637144576 | bytes 22020096 | tf_op jit(solution)/shard_map/token_backward/pallas_call | solution.py:827
  1180.7 48.5 %attention_backward.5 = (bf16[1024,768]{1,0:T(8,128)(2,1)S(1)}, bf16[2048,768]{1,0:T(8,128)(2,1)}, bf16[2048,768]{1,0:T(8,128)(2,1)}) custom-call(bf16[1024,2304]{1,0:T(8,128)(2,1)} %copy-done.138, bf16[1024,2304]{1,0:T(8,128)(2,1)} %copy-done.138, bf16[1024,2304]{1,0:T(8,128)(2,1)} %copy-done.138, bf16[1024,1536]{1,0:T(8,128)(2,1)} %copy-done.136, ...), custom_call_target="tpu_custom_call" | custom-call | flops 40265318400 | bytes 18874368 | tf_op jit(solution)/shard_map/attention_backward/pallas_call | solution.py:216
  1250.4 22.2 %collective-permute-done.4 = bf16[1024,768]{1,0:T(8,128)(2,1)S(1)} collective-permute-done((bf16[1024,768]{1,0:T(8,128)(2,1)S(1)}, bf16[1024,768]{1,0:T(8,128)(2,1)S(1)}, u32[]{:S(2)}, u32[]{:S(2)}) %collective-permute-start.4) | collective-permute-done | bytes 1572896 | tf_op jit(solution)/shard_map/ppermute | solution.py:417
  1273.8 9.5 multiply_reduce_fusion
  1283.3 6.0 dispatch.14
  1300.5 6.2 dispatch.15.refs_7_
  1309.6 55.4 %all-to-all-done.12 = bf16[2,4,256,768]{3,2,0,1:T(8,128)(2,1)} async-done(((bf16[2,4,256,768]{3,2,0,1:T(8,128)(2,1)}), bf16[2,4,256,768]{3,2,0,1:T(8,128)(2,1)}, u32[]{:S(2)}, u32[]{:S(2)}) %all-to-all-start.12) | async-done | bytes 3145760 | tf_op jit(solution)/shard_map/all_to_all | solution.py:443
  1373.8 51.7 %experts_backward.6 = (bf16[2,1024,768]{2,1,0:T(8,128)(2,1)}, bf16[2,2,768,2048]{3,2,1,0:T(8,128)(2,1)}, bf16[2,2048,768]{2,1,0:T(8,128)(2,1)}) custom-call(bf16[2,1024,768]{2,1,0:T(8,128)(2,1)} %bitcast.285, bf16[2,1024,768]{2,1,0:T(8,128)(2,1)} %bitcast.293, bf16[2,1024,2048]{2,1,0:T(8,128)(2,1)} %get-tuple-element.174.refs_2_, ...), custom_call_target="tpu_custom_call" | custom-call | flops 38654705664 | bytes 60817408 | tf_op jit(solution)/shard_map/experts_backward/pallas_call | solution.py:393
  1429.2 10.9 all-to-all-done.14
  1451.8 52.2 %experts_backward.7 = (bf16[2,1024,768]{2,1,0:T(8,128)(2,1)}, bf16[2,2,768,2048]{3,2,1,0:T(8,128)(2,1)}, bf16[2,2048,768]{2,1,0:T(8,128)(2,1)}) custom-call(bf16[2,1024,768]{2,1,0:T(8,128)(2,1)} %bitcast.287, bf16[2,1024,768]{2,1,0:T(8,128)(2,1)} %bitcast.291, bf16[2,1024,2048]{2,1,0:T(8,128)(2,1)} %get-tuple-element.183.refs_2_, ...), custom_call_target="tpu_custom_call" | custom-call | flops 38654705664 | bytes 60817408 | tf_op jit(solution)/shard_map/experts_backward/pallas_call | solution.py:393
  1507.8 7.1 all-to-all-done.13
  1548.0 41.8 %all-to-all-done.15 = bf16[2,4,256,768]{3,2,0,1:T(8,128)(2,1)} async-done(((bf16[2,4,256,768]{3,2,0,1:T(8,128)(2,1)}), bf16[2,4,256,768]{3,2,0,1:T(8,128)(2,1)}, u32[]{:S(2)}, u32[]{:S(2)}) %all-to-all-start.15) | async-done | bytes 3145760 | tf_op jit(solution)/shard_map/all_to_all | solution.py:443
  1594.7 25.7 %token_backward.6 = (f32[1024,768]{1,0:T(8,128)}, bf16[1024,768]{1,0:T(8,128)(2,1)S(1)}, f32[1024,128]{1,0:T(8,128)}, f32[768,768]{1,0:T(8,128)}, f32[768,128]{1...) custom-call(bf16[2048,768]{1,0:T(8,128)(2,1)} %bitcast.272, s32[1024,128]{1,0:T(8,128)S(1)} %copy-done.30, ...), custom_call_target="tpu_custom_call" | custom-call | flops 5637144576 | bytes 22020096 | tf_op jit(solution)/shard_map/token_backward/pallas_call | solution.py:827
  1620.4 48.1 %attention_backward.6 = (bf16[1024,768]{1,0:T(8,128)(2,1)S(1)}, bf16[2048,768]{1,0:T(8,128)(2,1)}, bf16[2048,768]{1,0:T(8,128)(2,1)}) custom-call(bf16[1024,2304]{1,0:T(8,128)(2,1)} %copy-done.132, bf16[1024,2304]{1,0:T(8,128)(2,1)} %copy-done.132, bf16[1024,2304]{1,0:T(8,128)(2,1)} %copy-done.132, bf16[1024,1536]{1,0:T(8,128)(2,1)} %copy-done.134, ...), custom_call_target="tpu_custom_call" | custom-call | flops 40265318400 | bytes 18874368 | tf_op jit(solution)/shard_map/attention_backward/pallas_call | solution.py:216
  1673.7 26.3 %token_backward.7 = (f32[1024,768]{1,0:T(8,128)}, bf16[1024,768]{1,0:T(8,128)(2,1)S(1)}, f32[1024,128]{1,0:T(8,128)}, f32[768,768]{1,0:T(8,128)}, f32[768,128]{1...) custom-call(bf16[2048,768]{1,0:T(8,128)(2,1)} %bitcast.271, s32[1024,128]{1,0:T(8,128)S(1)} %copy-done.37, ...), custom_call_target="tpu_custom_call" | custom-call | flops 5637144576 | bytes 22020096 | tf_op jit(solution)/shard_map/token_backward/pallas_call | solution.py:827
  1700.0 48.3 %attention_backward.7 = (bf16[1024,768]{1,0:T(8,128)(2,1)S(1)}, bf16[2048,768]{1,0:T(8,128)(2,1)}, bf16[2048,768]{1,0:T(8,128)(2,1)}) custom-call(bf16[1024,2304]{1,0:T(8,128)(2,1)} %copy-done.133, bf16[1024,2304]{1,0:T(8,128)(2,1)} %copy-done.133, bf16[1024,2304]{1,0:T(8,128)(2,1)} %copy-done.133, bf16[1024,1536]{1,0:T(8,128)(2,1)} %copy-done.135, ...), custom_call_target="tpu_custom_call" | custom-call | flops 40265318400 | bytes 18874368 | tf_op jit(solution)/shard_map/attention_backward/pallas_call | solution.py:216
  1789.8 5.4 fusion.18
  1804.6 33.6 %collective-permute-done.5 = bf16[1024,768]{1,0:T(8,128)(2,1)S(1)} collective-permute-done((bf16[1024,768]{1,0:T(8,128)(2,1)S(1)}, bf16[1024,768]{1,0:T(8,128)(2,1)S(1)}, u32[]{:S(2)}, u32[]{:S(2)}) %collective-permute-start.5) | collective-permute-done | bytes 1572896 | tf_op jit(solution)/shard_map/ppermute | solution.py:417
  1840.2 7.7 multiply_reduce_fusion.2
  1853.4 50.8 %reduce-scatter.11.cloned.1.call-done = bf16[96,3200]{1,0:T(8,128)(2,1)} async-done(((bf16[768,3200]{1,0:T(8,128)(2,1)}), bf16[96,3200]{1,0:T(8,128)(2,1)}) %reduce-scatter.11.cloned.1.call-update) | async-done | bytes 614416 | tf_op jit(solution)/shard_map/reduce_scatter | solution.py:1065
  1904.2 58.3 %reduce-scatter.13.cloned.1.call-done = bf16[96,3200]{1,0:T(8,128)(2,1)} async-done(((bf16[768,3200]{1,0:T(8,128)(2,1)}), bf16[96,3200]{1,0:T(8,128)(2,1)}) %reduce-scatter.13.cloned.1.call-update) | async-done | bytes 614416 | tf_op jit(solution)/shard_map/reduce_scatter | solution.py:1065
  1967.4 40.6 %psum.23 = f32[2,12,12]{2,1,0:T(8,128)S(1)} all-reduce(f32[2,12,12]{2,1,0:T(8,128)S(1)} %pad_maximum_fusion.2), channel_id=1, replica_groups=mesh['expert'=4,'context'=2,'dp'=4] {'expert','context','dp'}, use_global_device_ids=true, to_apply=%region_20.21 | all-reduce | flops 288 | bytes 2304 | tf_op jit(solution)/shard_map/psum | solution.py:1108
  2008.6 20.1 reduce-scatter.17.cloned.1.call-done
  2031.9 5.6 fusion.14
  2039.4 49.8 %all-reduce.9.cloned.1.call-done = (bf16[1,96,3200]{2,1,0:T(8,128)(2,1)}, bf16[1,96,3200]{2,1,0:T(8,128)(2,1)}) async-done(((bf16[1,96,3200]{2,1,0:T(8,128)(2,1)}, bf16[1,96,3200]{2,1,0:T(8,128)(2,1)}), (bf16[1,96,3200]{2,1,0:T(8,128)(2,1)}, bf16[1,96,3200]{2,1,0:T(8,128)(2,1)})) %all-reduce.9.cloned.1.call-update) | async-done | bytes 1228816 | tf_op jit(solution)/shard_map/psum | solution.py:1066
  2095.5 89.6 %reduce-scatter.15.cloned.1.call-done = bf16[4,96,2048]{2,1,0:T(8,128)(2,1)} async-done(((bf16[4,768,2048]{2,1,0:T(8,128)(2,1)}), bf16[4,96,2048]{2,1,0:T(8,128)(2,1)}) %reduce-scatter.15.cloned.1.call-update) | async-done | bytes 1572880 | tf_op jit(solution)/shard_map/reduce_scatter | solution.py:1057
  (686 shorter events, 461.2 us)
Async XLA Ops:
  7.2 132.3 %all-gather.9.cloned.1.call-start = ((), (), s32[]{:S(2)}) async-start(), calls=%async_computation.22 | async-start | bytes 5529600 | tf_op jit(solution)/shard_map/all_gather | solution.py:870
  19.7 268.9 %all-gather.17.cloned.1.call-start = ((), (), s32[]{:S(2)}) async-start(), calls=%async_computation.32 | async-start | bytes 7077888 | tf_op jit(solution)/shard_map/all_gather | solution.py:873
  21.1 267.5 %all-gather.11.cloned.1.call-start = ((), (), s32[]{:S(2)}) async-start(), calls=%async_computation.23 | async-start | bytes 14155776 | tf_op jit(solution)/shard_map/all_gather | solution.py:872
  25.4 410.4 %all-gather.13.cloned.1.call-start = ((), (), s32[]{:S(2)}) async-start(), calls=%async_computation.24 | async-start | bytes 5529600 | tf_op jit(solution)/shard_map/all_gather | solution.py:870
  27.1 109.2 %collective-permute-start = (bf16[2,1024,768]{2,1,0:T(8,128)(2,1)}, bf16[2,1024,768]{2,1,0:T(8,128)(2,1)}, u32[]{:S(2)}, u32[]{:S(2)}) collective-permute-start(bf16[2,1024,768]{2,1,0:T(8,128)(2,1)} %bitcast.15), channel_id=1, source_target_pairs={{0,4},{1,5},{2,6},{3,7},{8,12},{9,13},{10,14},{11,15},{16,20},{17,... | collective-permute-start | bytes 9437192 | tf_op jit(solution)/shard_map/ppermute | solution.py:417
  39.3 323.3 %copy-start.24 = (bf16[1024,768]{1,0:T(8,128)(2,1)}, bf16[1024,768]{1,0:T(8,128)(2,1)S(1)}, u32[]{:S(2)}) copy-start(bf16[1024,768]{1,0:T(8,128)(2,1)S(1)} %get-tuple-element.305.rows_ref.grad_ref) | copy-start | bytes 4718596
  46.3 158.8 %all-to-all-start.7 = ((bf16[2,4,256,768]{3,2,0,1:T(8,128)(2,1)}), bf16[2,4,256,768]{3,2,0,1:T(8,128)(2,1)}, u32[]{:S(2)}, u32[]{:S(2)}) async-start(bf16[2,4,256,768]{3,2,0,1:T(8,128)(2,1)} %copy.281), calls=%async_computation.7 | async-start | bytes 6291456 | tf_op jit(solution)/shard_map/all_to_all | solution.py:443
  51.3 684.7 %all-gather.19.cloned.1.call-start = ((), (), s32[]{:S(2)}) async-start(), calls=%async_computation.33 | async-start | bytes 7077888 | tf_op jit(solution)/shard_map/all_gather | solution.py:873
  53.8 545.1 %copy-start.5 = (s32[1,1,1024,2]{3,2,1,0:T(8,128)}, s32[1,1,1024,2]{3,2,1,0:T(8,128)S(1)}, u32[]{:S(2)}) copy-start(s32[1,1,1024,2]{3,2,1,0:T(8,128)S(1)} %copy.354) | copy-start | bytes 24580
  55.4 132.3 %copy-start.31 = (f32[1024,128]{1,0:T(8,128)}, f32[1024,128]{1,0:T(8,128)S(1)}, u32[]{:S(2)}) copy-start(f32[1024,128]{1,0:T(8,128)S(1)} %pad.20.prior_ref) | copy-start | bytes 1572868
  58.7 161.0 %copy-start.186 = (f32[1024]{0:T(1024)}, f32[1024]{0:T(1024)S(1)}, u32[]{:S(2)}) copy-start(f32[1024]{0:T(1024)S(1)} %get-tuple-element.363) | copy-start | bytes 12292
  142.4 77.4 %copy-start.182 = (f32[768]{0:T(1024)}, f32[768]{0:T(1024)S(1)}, u32[]{:S(2)}) copy-start(f32[768]{0:T(1024)S(1)} %slice_reduce_fusion.1) | copy-start | bytes 9220
  154.7 32.9 %copy-start.15 = (f32[1024,768]{1,0:T(8,128)S(1)}, f32[1024,768]{1,0:T(8,128)}, u32[]{:S(2)}) copy-start(f32[1024,768]{1,0:T(8,128)} %get-tuple-element.307.hidden_ref) | copy-start | bytes 9437188
  205.1 75.1 %all-to-all-start = ((bf16[2,4,256,768]{3,2,0,1:T(8,128)(2,1)}), bf16[2,4,256,768]{3,2,0,1:T(8,128)(2,1)}, u32[]{:S(2)}, u32[]{:S(2)}) async-start(bf16[2,4,256,768]{3,2,0,1:T(8,128)(2,1)} %copy.255), calls=%async_computation | async-start | bytes 6291456 | tf_op jit(solution)/shard_map/all_to_all | solution.py:443
  211.6 48.3 %copy-start.8 = (s32[1,1,1024,2]{3,2,1,0:T(8,128)}, s32[1,1,1024,2]{3,2,1,0:T(8,128)S(1)}, u32[]{:S(2)}) copy-start(s32[1,1,1024,2]{3,2,1,0:T(8,128)S(1)} %copy.356) | copy-start | bytes 24580
  214.7 45.3 %copy-start.33 = (f32[1024,128]{1,0:T(8,128)}, f32[1024,128]{1,0:T(8,128)S(1)}, u32[]{:S(2)}) copy-start(f32[1024,128]{1,0:T(8,128)S(1)} %pad.23.prior_ref) | copy-start | bytes 1572868
  227.0 32.3 %copy-start.133 = (bf16[1024,2304]{1,0:T(8,128)(2,1)}, bf16[1024,2304]{1,0:T(8,128)(2,1)S(1)}, u32[]{:S(2)}) copy-start(bf16[1024,2304]{1,0:T(8,128)(2,1)S(1)} %convolution_convert_fusion.2.q_ref.ko_ref.vo_ref) | copy-start | bytes 14155780
  227.0 32.9 %copy-start.14 = (f32[1024,768]{1,0:T(8,128)S(1)}, f32[1024,768]{1,0:T(8,128)}, u32[]{:S(2)}) copy-start(f32[1024,768]{1,0:T(8,128)} %get-tuple-element.308.hidden_ref) | copy-start | bytes 9437188
  280.2 74.9 %all-to-all-start.2 = ((bf16[2,4,256,768]{3,2,0,1:T(8,128)(2,1)}), bf16[2,4,256,768]{3,2,0,1:T(8,128)(2,1)}, u32[]{:S(2)}, u32[]{:S(2)}) async-start(bf16[2,4,256,768]{3,2,0,1:T(8,128)(2,1)} %copy.268), calls=%async_computation.2 | async-start | bytes 6291456 | tf_op jit(solution)/shard_map/all_to_all | solution.py:443
  355.1 74.9 %all-to-all-start.1 = ((bf16[2,4,256,768]{3,2,0,1:T(8,128)(2,1)}), bf16[2,4,256,768]{3,2,0,1:T(8,128)(2,1)}, u32[]{:S(2)}, u32[]{:S(2)}) async-start(bf16[2,4,256,768]{3,2,0,1:T(8,128)(2,1)} %copy.260), calls=%async_computation.1 | async-start | bytes 6291456 | tf_op jit(solution)/shard_map/all_to_all | solution.py:443
  359.8 376.2 %all-gather.15.cloned.1.call-start = ((), (), s32[]{:S(2)}) async-start(), calls=%async_computation.25 | async-start | bytes 14155776 | tf_op jit(solution)/shard_map/all_gather | solution.py:872
  369.5 65.4 %copy-start.90 = (s32[2,1024,128]{2,1,0:T(8,128)S(1)}, s32[2,1024,128]{2,1,0:T(8,128)}, u32[]{:S(2)}) copy-start(s32[2,1024,128]{2,1,0:T(8,128)} %copy-done.89) | copy-start | bytes 3145732
  430.0 75.2 %all-to-all-start.10 = ((bf16[2,4,256,768]{3,2,0,1:T(8,128)(2,1)}), bf16[2,4,256,768]{3,2,0,1:T(8,128)(2,1)}, u32[]{:S(2)}, u32[]{:S(2)}) async-start(bf16[2,4,256,768]{3,2,0,1:T(8,128)(2,1)} %copy.287), calls=%async_computation.10 | async-start | bytes 6291456 | tf_op jit(solution)/shard_map/all_to_all | solution.py:443
  435.8 74.2 %copy-start.28 = (s32[1024,128]{1,0:T(8,128)}, s32[1024,128]{1,0:T(8,128)S(1)}, u32[]{:S(2)}) copy-start(s32[1024,128]{1,0:T(8,128)S(1)} %get-tuple-element.319.columns_ref) | copy-start | bytes 1572868
  505.2 111.4 %all-to-all-start.4 = ((bf16[2,4,256,768]{3,2,0,1:T(8,128)(2,1)}), bf16[2,4,256,768]{3,2,0,1:T(8,128)(2,1)}, u32[]{:S(2)}, u32[]{:S(2)}) async-start(bf16[2,4,256,768]{3,2,0,1:T(8,128)(2,1)} %copy.274), calls=%async_computation.4 | async-start | bytes 6291456 | tf_op jit(solution)/shard_map/all_to_all | solution.py:443
  525.3 73.6 %copy-start = (f32[1024,768]{1,0:T(8,128)}, f32[1024,768]{1,0:T(8,128)S(1)}, u32[]{:S(2)}) copy-start(f32[1024,768]{1,0:T(8,128)S(1)} %get-tuple-element.130.hidden_ref) | copy-start | bytes 9437188
  525.3 37.2 %collective-permute-start.1 = (bf16[1024,768]{1,0:T(8,128)(2,1)S(1)}, bf16[1024,768]{1,0:T(8,128)(2,1)S(1)}, u32[]{:S(2)}, u32[]{:S(2)}) collective-permute-start(bf16[1024,768]{1,0:T(8,128)(2,1)S(1)} %get-tuple-element.131), channel_id=1, source_target_pairs={{0,4},{1,5},{2,6},{3,7},{8,12},{9,13},{10,14},{11,15},{16,20},{17,... | collective-permute-start | bytes 4718600 | tf_op jit(solution)/shard_map/ppermute | solution.py:417
  566.5 32.3 %copy-start.60 = (f32[1024,128]{1,0:T(8,128)S(1)}, f32[1024,128]{1,0:T(8,128)}, u32[]{:S(2)}) copy-start(f32[1024,128]{1,0:T(8,128)} %copy-done.59) | copy-start | bytes 1572868
  616.6 110.0 %all-to-all-start.3 = ((bf16[2,4,256,896]{3,2,0,1:T(8,128)(2,1)}), bf16[2,4,256,896]{3,2,0,1:T(8,128)(2,1)}, u32[]{:S(2)}, u32[]{:S(2)}) async-start(bf16[2,4,256,896]{3,2,0,1:T(8,128)(2,1)} %copy.272), calls=%async_computation.3 | async-start | bytes 7340032 | tf_op jit(solution)/shard_map/all_to_all | solution.py:443
  636.3 262.9 %copy-start.3 = (f32[1024,768]{1,0:T(8,128)}, f32[1024,768]{1,0:T(8,128)S(1)}, u32[]{:S(2)}) copy-start(f32[1024,768]{1,0:T(8,128)S(1)} %get-tuple-element.139.hidden_ref) | copy-start | bytes 9437188
  636.3 36.3 %collective-permute-start.2 = (bf16[1024,768]{1,0:T(8,128)(2,1)S(1)}, bf16[1024,768]{1,0:T(8,128)(2,1)S(1)}, u32[]{:S(2)}, u32[]{:S(2)}) collective-permute-start(bf16[1024,768]{1,0:T(8,128)(2,1)S(1)} %get-tuple-element.140), channel_id=1, source_target_pairs={{0,4},{1,5},{2,6},{3,7},{8,12},{9,13},{10,14},{11,15},{16,20},{17,... | collective-permute-start | bytes 4718600 | tf_op jit(solution)/shard_map/ppermute | solution.py:417
  676.6 32.3 %copy-start.9 = (s32[1,1,1024,2]{3,2,1,0:T(8,128)S(1)}, s32[1,1,1024,2]{3,2,1,0:T(8,128)}, u32[]{:S(2)}) copy-start(s32[1,1,1024,2]{3,2,1,0:T(8,128)} %copy-done.8) | copy-start | bytes 24580
  676.6 32.3 %copy-start.63 = (f32[1024,128]{1,0:T(8,128)S(1)}, f32[1024,128]{1,0:T(8,128)}, u32[]{:S(2)}) copy-start(f32[1024,128]{1,0:T(8,128)} %copy-done.62) | copy-start | bytes 1572868
  726.6 84.8 %all-to-all-start.6 = ((bf16[2,4,256,896]{3,2,0,1:T(8,128)(2,1)}), bf16[2,4,256,896]{3,2,0,1:T(8,128)(2,1)}, u32[]{:S(2)}, u32[]{:S(2)}) async-start(bf16[2,4,256,896]{3,2,0,1:T(8,128)(2,1)} %copy.279), calls=%async_computation.6 | async-start | bytes 7340032 | tf_op jit(solution)/shard_map/all_to_all | solution.py:443
  811.4 74.9 %all-to-all-start.5 = ((bf16[2,4,256,768]{3,2,0,1:T(8,128)(2,1)}), bf16[2,4,256,768]{3,2,0,1:T(8,128)(2,1)}, u32[]{:S(2)}, u32[]{:S(2)}) async-start(bf16[2,4,256,768]{3,2,0,1:T(8,128)(2,1)} %copy.277), calls=%async_computation.5 | async-start | bytes 6291456 | tf_op jit(solution)/shard_map/all_to_all | solution.py:443
  886.3 75.1 %all-to-all-start.9 = ((bf16[2,4,256,768]{3,2,0,1:T(8,128)(2,1)}), bf16[2,4,256,768]{3,2,0,1:T(8,128)(2,1)}, u32[]{:S(2)}, u32[]{:S(2)}) async-start(bf16[2,4,256,768]{3,2,0,1:T(8,128)(2,1)} %copy.285), calls=%async_computation.9 | async-start | bytes 6291456 | tf_op jit(solution)/shard_map/all_to_all | solution.py:443
  961.3 108.6 %all-to-all-start.8 = ((bf16[2,4,256,768]{3,2,0,1:T(8,128)(2,1)}), bf16[2,4,256,768]{3,2,0,1:T(8,128)(2,1)}, u32[]{:S(2)}, u32[]{:S(2)}) async-start(bf16[2,4,256,768]{3,2,0,1:T(8,128)(2,1)} %copy.283), calls=%async_computation.8 | async-start | bytes 6291456 | tf_op jit(solution)/shard_map/all_to_all | solution.py:443
  966.0 627.5 %reduce-scatter.9.cloned.1.call-start = ((), (), s32[]{:S(2)}) async-start(), calls=%async_computation.27 | async-start | bytes 7077888 | tf_op jit(solution)/shard_map/reduce_scatter | solution.py:1058
  1070.5 78.5 %all-to-all-start.11 = ((bf16[2,4,256,768]{3,2,0,1:T(8,128)(2,1)}), bf16[2,4,256,768]{3,2,0,1:T(8,128)(2,1)}, u32[]{:S(2)}, u32[]{:S(2)}) async-start(bf16[2,4,256,768]{3,2,0,1:T(8,128)(2,1)} %copy.290), calls=%async_computation.11 | async-start | bytes 6291456 | tf_op jit(solution)/shard_map/all_to_all | solution.py:443
  1133.5 111.6 %collective-permute-start.3 = (bf16[1024,768]{1,0:T(8,128)(2,1)}, bf16[1024,768]{1,0:T(8,128)(2,1)}, u32[]{:S(2)}, u32[]{:S(2)}) collective-permute-start(bf16[1024,768]{1,0:T(8,128)(2,1)} %add_convert_fusion.5), channel_id=1, source_target_pairs={{4,0},{5,1},{6,2},{7,3},{12,8},{13,9},{14,10},{15,11},{20,16},{21,... | collective-permute-start | bytes 4718600 | tf_op jit(solution)/shard_map/ppermute | solution.py:417
  1152.9 76.3 %slice-start.4 = ((s8[4915200]{0:T(1024)(128)(4,1)}), s8[4194304]{0:T(1024)(128)(4,1)S(1)}, s32[]{:S(2)}) async-start(s8[4915200]{0:T(1024)(128)(4,1)} %bitcast.227), calls=%async_computation.39 | async-start | bytes 8388608
  1180.7 48.5 %slice-start.5 = ((s8[4915200]{0:T(1024)(128)(4,1)}), s8[720896]{0:T(1024)(128)(4,1)S(1)}, s32[]{:S(2)}) async-start(s8[4915200]{0:T(1024)(128)(4,1)} %bitcast.227), calls=%async_computation.40 | async-start | bytes 1441792
  1234.1 38.5 %collective-permute-start.4 = (bf16[1024,768]{1,0:T(8,128)(2,1)S(1)}, bf16[1024,768]{1,0:T(8,128)(2,1)S(1)}, u32[]{:S(2)}, u32[]{:S(2)}) collective-permute-start(bf16[1024,768]{1,0:T(8,128)(2,1)S(1)} %add_convert_fusion.4), channel_id=1, source_target_pairs={{4,0},{5,1},{6,2},{7,3},{12,8},{13,9},{14,10},{15,11},{20,16},{21,... | collective-permute-start | bytes 4718600 | tf_op jit(solution)/shard_map/ppermute | solution.py:417
  1291.1 73.9 %all-to-all-start.12 = ((bf16[2,4,256,768]{3,2,0,1:T(8,128)(2,1)}), bf16[2,4,256,768]{3,2,0,1:T(8,128)(2,1)}, u32[]{:S(2)}, u32[]{:S(2)}) async-start(bf16[2,4,256,768]{3,2,0,1:T(8,128)(2,1)} %copy.293), calls=%async_computation.12 | async-start | bytes 6291456 | tf_op jit(solution)/shard_map/all_to_all | solution.py:443
  1296.0 297.6 %reduce-scatter.7.cloned.1.call-start = ((), (), s32[]{:S(2)}) async-start(), calls=%async_computation.26 | async-start | bytes 14155776 | tf_op jit(solution)/shard_map/reduce_scatter | solution.py:1057
  1365.0 75.0 %all-to-all-start.14 = ((bf16[2,4,256,768]{3,2,0,1:T(8,128)(2,1)}), bf16[2,4,256,768]{3,2,0,1:T(8,128)(2,1)}, u32[]{:S(2)}, u32[]{:S(2)}) async-start(bf16[2,4,256,768]{3,2,0,1:T(8,128)(2,1)} %copy.297), calls=%async_computation.14 | async-start | bytes 6291456 | tf_op jit(solution)/shard_map/all_to_all | solution.py:443
  1440.1 74.9 %all-to-all-start.13 = ((bf16[2,4,256,768]{3,2,0,1:T(8,128)(2,1)}), bf16[2,4,256,768]{3,2,0,1:T(8,128)(2,1)}, u32[]{:S(2)}, u32[]{:S(2)}) async-start(bf16[2,4,256,768]{3,2,0,1:T(8,128)(2,1)} %copy.295), calls=%async_computation.13 | async-start | bytes 6291456 | tf_op jit(solution)/shard_map/all_to_all | solution.py:443
  1514.9 74.9 %all-to-all-start.15 = ((bf16[2,4,256,768]{3,2,0,1:T(8,128)(2,1)}), bf16[2,4,256,768]{3,2,0,1:T(8,128)(2,1)}, u32[]{:S(2)}, u32[]{:S(2)}) async-start(bf16[2,4,256,768]{3,2,0,1:T(8,128)(2,1)} %copy.300), calls=%async_computation.17 | async-start | bytes 6291456 | tf_op jit(solution)/shard_map/all_to_all | solution.py:443
  1519.6 384.6 %reduce-scatter.11.cloned.1.call-start = ((), (), s32[]{:S(2)}) async-start(), calls=%async_computation.28 | async-start | bytes 5529600 | tf_op jit(solution)/shard_map/reduce_scatter | solution.py:1065
  1548.0 45.6 %copy-start.7 = (s32[1,1,1024,2]{3,2,1,0:T(8,128)S(1)}, s32[1,1,1024,2]{3,2,1,0:T(8,128)}, u32[]{:S(2)}) copy-start(s32[1,1,1024,2]{3,2,1,0:T(8,128)} %copy-done.5) | copy-start | bytes 24580
  1548.0 45.6 %copy-start.30 = (s32[1024,128]{1,0:T(8,128)S(1)}, s32[1024,128]{1,0:T(8,128)}, u32[]{:S(2)}) copy-start(s32[1024,128]{1,0:T(8,128)} %copy-done.28) | copy-start | bytes 1572868
  1548.0 45.6 %copy-start.32 = (f32[1024,128]{1,0:T(8,128)S(1)}, f32[1024,128]{1,0:T(8,128)}, u32[]{:S(2)}) copy-start(f32[1024,128]{1,0:T(8,128)} %copy-done.31) | copy-start | bytes 1572868
  1548.0 45.6 %copy-start.93 = (f32[1024,128]{1,0:T(8,128)S(1)}, f32[1024,128]{1,0:T(8,128)}, u32[]{:S(2)}) copy-start(f32[1024,128]{1,0:T(8,128)} %copy-done.91) | copy-start | bytes 1572868
  1548.0 45.6 %copy-start.98 = (f32[1024,128]{1,0:T(8,128)S(1)}, f32[1024,128]{1,0:T(8,128)}, u32[]{:S(2)}) copy-start(f32[1024,128]{1,0:T(8,128)} %copy-done.97) | copy-start | bytes 1572868
  1620.4 48.1 %copy-start.183 = (f32[768]{0:T(1024)S(1)}, f32[768]{0:T(1024)}, u32[]{:S(2)}) copy-start(f32[768]{0:T(1024)} %copy-done.182) | copy-start | bytes 9220
  1620.4 48.1 %copy-start.189 = (f32[1024]{0:T(1024)S(1)}, f32[1024]{0:T(1024)}, u32[]{:S(2)}) copy-start(f32[1024]{0:T(1024)} %get-tuple-element.364) | copy-start | bytes 12292
  1700.0 48.3 %copy-start.187 = (f32[1024]{0:T(1024)S(1)}, f32[1024]{0:T(1024)}, u32[]{:S(2)}) copy-start(f32[1024]{0:T(1024)} %copy-done.186) | copy-start | bytes 12292
  1767.3 72.9 %collective-permute-start.6 = (bf16[1024,768]{1,0:T(8,128)(2,1)S(1)}, bf16[1024,768]{1,0:T(8,128)(2,1)S(1)}, u32[]{:S(2)}, u32[]{:S(2)}) collective-permute-start(bf16[1024,768]{1,0:T(8,128)(2,1)S(1)} %add_convert_fusion.1), channel_id=1, source_target_pairs={{4,0},{5,1},{6,2},{7,3},{12,8},{13,9},{14,10},{15,11},{20,16},{21,... | collective-permute-start | bytes 4718600 | tf_op jit(solution)/shard_map/ppermute | solution.py:417
  1771.5 66.8 %collective-permute-start.5 = (bf16[1024,768]{1,0:T(8,128)(2,1)S(1)}, bf16[1024,768]{1,0:T(8,128)(2,1)S(1)}, u32[]{:S(2)}, u32[]{:S(2)}) collective-permute-start(bf16[1024,768]{1,0:T(8,128)(2,1)S(1)} %add_convert_fusion.3), channel_id=1, source_target_pairs={{4,0},{5,1},{6,2},{7,3},{12,8},{13,9},{14,10},{15,11},{20,16},{21,... | collective-permute-start | bytes 4718600 | tf_op jit(solution)/shard_map/ppermute | solution.py:417
  1852.0 110.5 %reduce-scatter.13.cloned.1.call-start = ((), (), s32[]{:S(2)}) async-start(), calls=%async_computation.29 | async-start | bytes 5529600 | tf_op jit(solution)/shard_map/reduce_scatter | solution.py:1065
  1852.6 176.1 %reduce-scatter.17.cloned.1.call-start = ((), (), s32[]{:S(2)}) async-start(), calls=%async_computation.31 | async-start | bytes 7077888 | tf_op jit(solution)/shard_map/reduce_scatter | solution.py:1058
  1853.4 235.9 %all-reduce.9.cloned.1.call-start = ((), (), s32[]{:S(2)}) async-start(), calls=%async_computation.34 | async-start | bytes 2457600 | tf_op jit(solution)/shard_map/psum | solution.py:1066
  1962.5 222.6 %reduce-scatter.15.cloned.1.call-start = ((), (), s32[]{:S(2)}) async-start(), calls=%async_computation.30 | async-start | bytes 14155776 | tf_op jit(solution)/shard_map/reduce_scatter | solution.py:1057
  2094.0 91.1 %copy-start.150 = (bf16[4,96,2048]{2,1,0:T(8,128)(2,1)S(1)}, bf16[4,96,2048]{2,1,0:T(8,128)(2,1)}, u32[]{:S(2)}) copy-start(bf16[4,96,2048]{2,1,0:T(8,128)(2,1)} %reduce-scatter.7.cloned.1.call-done.rest_2_) | copy-start | bytes 4718596
  (193 other events, 1447.1 us)
Sparse Core Ops, SparseCore 0:
  19.8 55.9 all-gather.8
  77.8 64.4 all-gather.16
  144.2 75.7 all-gather.10
  221.8 39.7 all-gather.12
  263.3 45.5 all-gather.18
  362.6 74.4 all-gather.14
  1024.1 63.9 reduce-scatter.8
  1300.7 92.7 reduce-scatter.6
  1852.2 52.0 reduce-scatter.10
  1907.6 54.8 reduce-scatter.12
  1966.3 62.4 reduce-scatter.16
  2031.1 58.1 all-reduce.8
  2093.2 91.8 reduce-scatter.14

commit v2 on v1

--- a/solution.py
+++ b/solution.py
@@ -24,6 +24,15 @@
 SHARDED = ("context", "dp")
 
 
+COST_SHARE = 0.8
+
+
+def cost(microseconds):
+    return pl.CostEstimate(
+        flops=int(microseconds * COST_SHARE * 1.15e9), bytes_accessed=1, transcendentals=0
+    )
+
+
 ANY_SPEC = pl.BlockSpec(memory_space=pl.ANY)
 
 
@@ -33,6 +42,22 @@
         right_op,
         (((left_dim,), (right_dim,)), ((), ())),
         preferred_element_type=f32,
+    )
+
+
+def held(arrays, after):
+    count = len(arrays)
+    if not after:
+        return list(arrays)
+    return list(
+        pl.pallas_call(
+            lambda *refs: None,
+            in_specs=[ANY_SPEC] * (count + len(after)),
+            out_specs=[ANY_SPEC] * count,
+            out_shape=[jax.ShapeDtypeStruct(array.shape, array.dtype) for array in arrays],
+            input_output_aliases={index: index for index in range(count)},
+            name="held",
+        )(*arrays, *after)
     )
 
 
@@ -138,10 +163,7 @@
             pltpu.VMEM((span, LANES), bf16),
         ],
         compiler_params=pltpu.CompilerParams(vmem_limit_bytes=40 * MIB),
-        cost_estimate=pl.CostEstimate(
-            flops=4 * length * keys * width * 4, bytes_accessed=12 * length * width,
-            transcendentals=length * keys * HEADS,
-        ),
+        cost_estimate=cost(32),
         name="attention_forward",
     )(qkv, qkv, qkv, kv_earlier, kv_earlier, seg_query, seg_key, *after)
 
@@ -243,10 +265,7 @@
             pltpu.VMEM((span, LANES), f32),
         ],
         compiler_params=pltpu.CompilerParams(vmem_limit_bytes=48 * MIB),
-        cost_estimate=pl.CostEstimate(
-            flops=10 * length * keys * width * 4, bytes_accessed=24 * length * width,
-            transcendentals=length * keys * HEADS,
-        ),
+        cost_estimate=cost(48),
         name="attention_backward",
     )(
         qkv, qkv, qkv, kv_earlier, kv_earlier, grad_att, attended, lse, seg_query, seg_key, *after
@@ -257,88 +276,97 @@
     return 1.0 / (1.0 + jnp.exp(-values))
 
 
-def experts_forward_kernel(
-    chunks, x_ref, gate_w_ref, up_w_ref, down_w_ref, *rest
-):
-    out_ref, gate_ref, up_ref, total_ref = rest[-4:]
-    chunk = pl.program_id(1)
-    rows_in = x_ref[0]
+def gathered(rows_ref, block_refs):
+    count = block_refs[0].shape[0]
+    width = rows_ref.shape[1]
+    for index, block_ref in enumerate(block_refs):
+        rows_ref[index * count : (index + 1) * count, :] = block_ref[:, :width]
+
+
+def scattered(block_refs, rows, which=0):
+    count = block_refs[0].shape[1]
+    for index, block_ref in enumerate(block_refs):
+        block_ref[which] = rows[index * count : (index + 1) * count, :].astype(bf16)
+
+
+def experts_forward_kernel(groups, *refs):
+    block_refs, (gate_w_ref, up_w_ref, down_w_ref) = refs[:groups], refs[groups : groups + 3]
+    out_refs, (gate_ref, up_ref, rows_ref) = refs[-groups - 3 : -3], refs[-3:]
+    gathered(rows_ref, block_refs)
+    rows_in = rows_ref[...]
     gate_pre = dot_on(rows_in, gate_w_ref[0], 1, 0)
     up_pre = dot_on(rows_in, up_w_ref[0], 1, 0)
     activated = (gate_pre * sigmoid(gate_pre) * up_pre).astype(bf16)
     gate_ref[0] = gate_pre.astype(bf16)
     up_ref[0] = up_pre.astype(bf16)
-    part = dot_on(activated, down_w_ref[0], 1, 0)
+    scattered(out_refs, dot_on(activated, down_w_ref[0], 1, 0))
+
+
+def experts_forward(blocks, gate_up_w, down_w, after):
+    groups = len(blocks)
+    count = down_w.shape[0]
+    width, hidden = gate_up_w.shape[1:]
+    part = blocks[0].shape[0] // count
+    rows = groups * part
+    block_spec = pl.BlockSpec((part, width), lambda j: (j, 0))
+    hidden_spec = pl.BlockSpec((1, rows, hidden), lambda j: (j, 0, 0))
+    hidden_shape = jax.ShapeDtypeStruct((count, rows, hidden), bf16)
+    *produced, gate_pre, up_pre = pl.pallas_call(
+        functools.partial(experts_forward_kernel, groups),
+        grid=(count,),
+        in_specs=[block_spec] * groups
+        + [
+            pl.BlockSpec((1, width, hidden), lambda j: (j, 0, 0)),
+            pl.BlockSpec((1, width, hidden), lambda j: (count + j, 0, 0)),
+            pl.BlockSpec((1, hidden, width), lambda j: (j, 0, 0)),
+        ]
+        + [ANY_SPEC] * len(after),
+        out_specs=[pl.BlockSpec((1, part, width), lambda j: (0, j, 0))] * groups
+        + [hidden_spec, hidden_spec],
+        out_shape=[jax.ShapeDtypeStruct((1, count * part, width), bf16)] * groups
+        + [hidden_shape, hidden_shape],
+        scratch_shapes=[pltpu.VMEM((rows, width), bf16)],
+        compiler_params=pltpu.CompilerParams(vmem_limit_bytes=48 * MIB),
+        cost_estimate=cost(26),
+        name="experts_forward",
+    )(*blocks, gate_up_w, gate_up_w, down_w, *after)
+    return produced, gate_pre, up_pre
+
+
+def experts_backward_kernel(groups, chunks, whole, has_sums, *refs):
+    block_refs, d_refs, given = refs[:groups], refs[groups : 2 * groups], refs[2 * groups :]
+    gate_w_ref, up_w_ref, down_w_ref = given[:3]
+    if whole:
+        share_refs, given = given[3 : 3 + groups], given[3 + groups :]
+        *refs, produced_ref = refs
+    else:
+        (gate_ref, up_ref), given = given[3:5], given[5:]
+    out_refs = refs[-5 - groups : -5]
+    gate_up_grad_ref, down_grad_ref, total_ref, rows_ref, d_ref = refs[-5:]
+    chunk = pl.program_id(1)
 
     @pl.when(chunk == 0)
     def _():
-        total_ref[...] = part
-
-    @pl.when(chunk > 0)
-    def _():
-        total_ref[...] += part
-
-    @pl.when(chunk == chunks - 1)
-    def _():
-        out_ref[0] = total_ref[...].astype(bf16)
-
-
-def experts_forward(rows_in, gate_up_w, down_w, after):
-    count, rows, _ = rows_in.shape
-    width, hidden = gate_up_w.shape[1:]
-    chunk = hidden
-    chunks = hidden // chunk
-    return pl.pallas_call(
-        functools.partial(experts_forward_kernel, chunks),
-        grid=(count, chunks),
-        in_specs=[
-            pl.BlockSpec((1, rows, width), lambda j, f: (j, 0, 0)),
-            pl.BlockSpec((1, width, chunk), lambda j, f: (j, 0, f)),
-            pl.BlockSpec((1, width, chunk), lambda j, f: (count + j, 0, f)),
-            pl.BlockSpec((1, chunk, width), lambda j, f: (j, f, 0)),
-        ]
-        + [ANY_SPEC] * len(after),
-        out_specs=[
-            pl.BlockSpec((1, rows, width), lambda j, f: (j, 0, 0)),
-            pl.BlockSpec((1, rows, chunk), lambda j, f: (j, 0, f)),
-            pl.BlockSpec((1, rows, chunk), lambda j, f: (j, 0, f)),
-        ],
-        out_shape=[
-            jax.ShapeDtypeStruct((count, rows, width), bf16),
-            jax.ShapeDtypeStruct((count, rows, hidden), bf16),
-            jax.ShapeDtypeStruct((count, rows, hidden), bf16),
-        ],
-        scratch_shapes=[pltpu.VMEM((rows, width), f32)],
-        compiler_params=pltpu.CompilerParams(vmem_limit_bytes=48 * MIB),
-        cost_estimate=pl.CostEstimate(
-            flops=6 * count * rows * width * hidden,
-            bytes_accessed=6 * count * width * hidden + 4 * count * rows * (width + hidden),
-            transcendentals=count * rows * hidden,
-        ),
-        name="experts_forward",
-    )(rows_in, gate_up_w, gate_up_w, down_w, *after)
-
-
-def experts_backward_kernel(chunks, has_gate, has_sums, *refs):
-    x_ref, dy_ref, gate_ref, up_ref, gate_w_ref, up_w_ref, down_w_ref = refs[:7]
-    given = refs[7:]
-    dx_ref, gate_up_grad_ref, down_grad_ref, total_ref, scaled_ref = refs[-5:]
-    chunk = pl.program_id(1)
-    rows_in = x_ref[0]
-    if has_gate:
-        share_ref, given = given[0], given[1:]
-
-        @pl.when(chunk == 0)
-        def _():
-            share = share_ref[0].astype(f32)
-            share = share[:, 0:1] + share[:, 1:2]
-            scaled_ref[...] = (dy_ref[0].astype(f32) * share).astype(bf16)
-
-        d_out = scaled_ref[...]
+        gathered(rows_ref, block_refs)
+        if whole:
+            count = d_refs[0].shape[0]
+            for index in range(groups):
+                share = share_refs[index][...].astype(f32)
+                share = share[:, 0:1] + share[:, 1:2]
+                d_ref[index * count : (index + 1) * count, :] = (
+                    d_refs[index][...].astype(f32) * share
+                ).astype(bf16)
+        else:
+            gathered(d_ref, d_refs)
+
+    rows_in = rows_ref[...]
+    d_out = d_ref[...]
+    if whole:
+        gate_pre = dot_on(rows_in, gate_w_ref[0], 1, 0)
+        up_pre = dot_on(rows_in, up_w_ref[0], 1, 0)
     else:
-        d_out = dy_ref[0]
-    gate_pre = gate_ref[0].astype(f32)
-    up_pre = up_ref[0].astype(f32)
+        gate_pre = gate_ref[0].astype(f32)
+        up_pre = up_ref[0].astype(f32)
     share = sigmoid(gate_pre)
     swish = gate_pre * share
     activated = (swish * up_pre).astype(bf16)
@@ -357,58 +385,75 @@
     gate_up_grad_ref[0, 0] = gate_grad.astype(bf16)
     gate_up_grad_ref[1, 0] = up_grad.astype(bf16)
     down_grad_ref[0] = down_grad.astype(bf16)
+    sums = [(total_ref, part)]
+    if whole:
+        sums.append((produced_ref, dot_on(activated, down_w_ref[0], 1, 0)))
 
     @pl.when(chunk == 0)
     def _():
-        total_ref[...] = part
+        for sum_ref, value in sums:
+            sum_ref[...] = value
 
     @pl.when(chunk > 0)
     def _():
-        total_ref[...] += part
+        for sum_ref, value in sums:
+            sum_ref[...] += value
 
     @pl.when(chunk == chunks - 1)
     def _():
-        dx_ref[0] = total_ref[...].astype(bf16)
-
-
-def experts_backward(rows_in, d_out, gate_pre, up_pre, gate_up_w, down_w, has_gate, sums, after):
-    count, rows, _ = rows_in.shape
-    width, hidden = gate_up_w.shape[1:]
+        scattered(out_refs, total_ref[...], len(sums) - 1)
+        if whole:
+            scattered(out_refs, produced_ref[...])
+
+
+def experts_backward(blocks, d_blocks, pre, gate_up_w, down_w, sums, after):
+    groups = len(blocks)
+    count, hidden, width = down_w.shape
+    part = blocks[0].shape[0] // count
+    rows = groups * part
+    whole = pre is None
     chunk = min(512, hidden)
     chunks = hidden // chunk
-    row_spec = pl.BlockSpec((1, rows, width), lambda j, f: (j, 0, 0))
+    block_spec = pl.BlockSpec((part, width), lambda j, f: (j, 0))
     hidden_spec = pl.BlockSpec((1, rows, chunk), lambda j, f: (j, 0, f))
     wide_spec = pl.BlockSpec((1, width, chunk), lambda j, f: (j, 0, f))
     up_spec = pl.BlockSpec((1, width, chunk), lambda j, f: (count + j, 0, f))
     tall_spec = pl.BlockSpec((1, chunk, width), lambda j, f: (j, f, 0))
     both_spec = pl.BlockSpec((2, 1, width, chunk), lambda j, f: (0, j, 0, f))
-    operands = [rows_in, d_out, gate_pre, up_pre, gate_up_w, gate_up_w, down_w]
-    specs = [row_spec, row_spec, hidden_spec, hidden_spec, wide_spec, up_spec, tall_spec]
-    if has_gate:
-        operands.append(rows_in)
-        specs.append(pl.BlockSpec((1, rows, LANES), lambda j, f: (j, 0, width // LANES)))
+    operands = [*blocks, *d_blocks, gate_up_w, gate_up_w, down_w]
+    specs = [block_spec] * (2 * groups) + [wide_spec, up_spec, tall_spec]
+    if whole:
+        operands.extend(blocks)
+        specs += [pl.BlockSpec((part, LANES), lambda j, f: (j, width // LANES))] * groups
+    else:
+        operands.extend(pre)
+        specs += [hidden_spec, hidden_spec]
     if sums is not None:
         operands.extend(sums)
         specs.extend([both_spec, tall_spec])
-    return pl.pallas_call(
-        functools.partial(experts_backward_kernel, chunks, has_gate, sums is not None),
+    outs = 2 if whole else 1
+    *out, gate_up_grad, down_grad = pl.pallas_call(
+        functools.partial(experts_backward_kernel, groups, chunks, whole, sums is not None),
         grid=(count, chunks),
         in_specs=specs + [ANY_SPEC] * len(after),
-        out_specs=[row_spec, both_spec, tall_spec],
-        out_shape=[
-            jax.ShapeDtypeStruct((count, rows, width), bf16),
+        out_specs=[pl.BlockSpec((outs, part, width), lambda j, f: (0, j, 0))] * groups
+        + [both_spec, tall_spec],
+        out_shape=[jax.ShapeDtypeStruct((outs, count * part, width), bf16)] * groups
+        + [
             jax.ShapeDtypeStruct((2, count, width, hidden), bf16),
             jax.ShapeDtypeStruct((count, hidden, width), bf16),
         ],
-        scratch_shapes=[pltpu.VMEM((rows, width), f32), pltpu.VMEM((rows, width), bf16)],
-        compiler_params=pltpu.CompilerParams(vmem_limit_bytes=56 * MIB),
-        cost_estimate=pl.CostEstimate(
-            flops=12 * count * rows * width * hidden,
-            bytes_accessed=12 * count * width * hidden + 4 * count * rows * (width + hidden),
-            transcendentals=count * rows * hidden,
-        ),
-        name="experts_backward",
+        scratch_shapes=[
+            pltpu.VMEM((rows, width), f32),
+            pltpu.VMEM((rows, width), bf16),
+            pltpu.VMEM((rows, width), bf16),
+        ]
+        + ([pltpu.VMEM((rows, width), f32)] if whole else []),
+        compiler_params=pltpu.CompilerParams(vmem_limit_bytes=58 * MIB),
+        cost_estimate=cost(75 if whole else 52),
+        name="experts_whole" if whole else "experts_backward",
     )(*operands, *after)
+    return out, (gate_up_grad, down_grad)
 
 
 def passed_along(block, axis, distance):
@@ -439,17 +484,18 @@
     return total
 
 
-def exchange(rows, groups, capacity):
-    return lax.all_to_all(
-        rows.reshape((EXPERTS // groups, groups, capacity) + rows.shape[1:]),
-        "expert",
-        split_axis=1,
-        concat_axis=1,
-        tiled=True,
-    )
+def exchange(blocks, direction):
+    groups = lax.axis_size("expert")
+    out = []
+    for d, block in enumerate(blocks):
+        step = d * direction
+        route = [(i, (i + step) % groups) for i in range(groups)]
+        out.append(block if d == 0 else lax.ppermute(block, "expert", route))
+    return out
 
 
 GATE, OF_NORMED, NORMED_SHARE, VECTOR_SHARE, MIX, SCALE, CHOSEN = 0, 2, 4, 5, 7, 9, 10
+GAINS_LANE = 2 * ROUTED + 8
 VECTOR_ROW, ATTN_GAIN_ROW, MOE_GAIN_ROW = 0, 2, 3
 
 
@@ -469,20 +515,16 @@
     return total
 
 
-def routing_kernel(groups, capacity, routes_ref, columns_ref, rows_ref):
+def routing_kernel(routes_ref, base_ref, columns_ref, rows_ref):
     length = routes_ref.shape[1]
     lane = lane_iota(length)
-    per_dev = EXPERTS // groups
-    base = jnp.full((length, LANES), -1.0, f32)
-    for e in range(EXPERTS):
-        base = jnp.where(lane == e, float(e % per_dev * groups * capacity + e // per_dev * capacity), base)
     onehots = [(lane == routes_ref[0, :, k : k + 1]).astype(f32) for k in range(TOP)]
     counts = (onehots[0] + onehots[1]).astype(bf16)
     earlier = lax.broadcasted_iota(jnp.int32, (length, length), 0) > lax.broadcasted_iota(
         jnp.int32, (length, length), 1
     )
     rank = dot_on(jnp.where(earlier, 1.0, 0.0).astype(bf16), counts, 1, 0)
-    place = base + jnp.where(lane < EXPERTS, rank, 0.0)
+    place = base_ref[...] + jnp.where(lane < EXPERTS, rank, 0.0)
     slots = placed_on_lanes(
         length,
         {k: jnp.sum(onehots[k] * place, axis=1, keepdims=True) for k in range(TOP)},
@@ -493,10 +535,18 @@
 
 def routing_slots(routes, groups, capacity):
     count, length, _ = routes.shape
+    per_dev = EXPERTS // groups
+    expert = jnp.arange(LANES)
+    place = (expert // per_dev - lax.axis_index("expert")) % groups
+    base = (place * per_dev + expert % per_dev) * capacity
+    base = jnp.where(expert < EXPERTS, base, -1).astype(f32)[None, :]
     return pl.pallas_call(
-        functools.partial(routing_kernel, groups, capacity),
+        routing_kernel,
         grid=(count,),
-        in_specs=[pl.BlockSpec((1, length, TOP), lambda m: (m, 0, 0))],
+        in_specs=[
+            pl.BlockSpec((1, length, TOP), lambda m: (m, 0, 0)),
+            pl.BlockSpec((1, LANES), lambda m: (0, 0)),
+        ],
         out_specs=[
             pl.BlockSpec((1, length, LANES), lambda m: (m, 0, 0)),
             pl.BlockSpec((1, 8, length), lambda m: (m, 0, 0)),
@@ -506,58 +556,57 @@
             jax.ShapeDtypeStruct((count, 8, length), jnp.int32),
         ],
         compiler_params=pltpu.CompilerParams(vmem_limit_bytes=32 * MIB),
-        cost_estimate=pl.CostEstimate(
-            flops=2 * count * length * length * LANES, bytes_accessed=count * length * 1024,
-            transcendentals=0,
-        ),
+        cost_estimate=cost(4),
         name="routing",
-    )(routes)
-
-
-def dispatch_kernel(mode, rows_ref, slots_ref, gates_ref, *rest):
-    out_ref = rest[-1]
-    count, length = out_ref.shape[0], rows_ref.shape[0]
+    )(routes, base)
+
+
+def dispatch_kernel(mode, per_group, groups, rows_ref, slots_ref, gates_ref, *rest):
+    out_refs = rest[-groups:]
+    count, length = out_refs[0].shape[0], rows_ref.shape[0]
     width = rows_ref.shape[1]
-    slot = pl.program_id(0) * count + lax.broadcasted_iota(jnp.int32, (count, length), 0)
-    hits = [slot == slots_ref[k : k + 1, :] for k in range(TOP)]
-    table = jnp.where(hits[0] | hits[1], 1.0, 0.0).astype(bf16)
-    found = dot_on(table, rows_ref[...].astype(bf16), 1, 0)
-    if mode == "plain":
-        out_ref[...] = found.astype(bf16)
-        return
-    gate = jnp.sum(
-        jnp.where(hits[0], gates_ref[0:1, :], 0.0) + jnp.where(hits[1], gates_ref[1:2, :], 0.0),
-        axis=1,
-        keepdims=True,
-    )
-    if mode == "scaled":
-        out_ref[...] = (found * gate).astype(bf16)
-        return
-    out_ref[:, :width] = found.astype(bf16)
-    coarse = gate.astype(bf16).astype(f32)
-    out_ref[:, width:] = placed_on_lanes(count, {0: coarse, 1: gate - coarse}).astype(bf16)
-
-
-def dispatch(rows, slot_rows, gate_rows, mode, slots, after=()):
+    rows = rows_ref[...].astype(bf16)
+    for group, out_ref in enumerate(out_refs):
+        first = group * per_group + pl.program_id(0) * count
+        slot = first + lax.broadcasted_iota(jnp.int32, (count, length), 0)
+        hits = [slot == slots_ref[k : k + 1, :] for k in range(TOP)]
+        table = jnp.where(hits[0] | hits[1], 1.0, 0.0).astype(bf16)
+        found = dot_on(table, rows, 1, 0)
+        if mode == "plain":
+            out_ref[...] = found.astype(bf16)
+            continue
+        gate = jnp.sum(
+            jnp.where(hits[0], gates_ref[0:1, :], 0.0)
+            + jnp.where(hits[1], gates_ref[1:2, :], 0.0),
+            axis=1,
+            keepdims=True,
+        )
+        if mode == "scaled":
+            out_ref[...] = (found * gate).astype(bf16)
+            continue
+        out_ref[:, :width] = found.astype(bf16)
+        coarse = gate.astype(bf16).astype(f32)
+        out_ref[:, width:] = placed_on_lanes(count, {0: coarse, 1: gate - coarse}).astype(bf16)
+
+
+def dispatch(rows, slot_rows, gate_rows, mode, slots, groups, after=()):
     length, width = rows.shape
-    count = min(256, slots)
+    per_group = slots // groups
+    count = min(256, per_group)
     out_width = width + LANES if mode == "with gate" else width
     return pl.pallas_call(
-        functools.partial(dispatch_kernel, mode),
-        grid=(slots // count,),
+        functools.partial(dispatch_kernel, mode, per_group, groups),
+        grid=(per_group // count,),
         in_specs=[
             pl.BlockSpec((length, width), lambda s: (0, 0)),
             pl.BlockSpec((8, length), lambda s: (0, 0)),
             pl.BlockSpec((8, length), lambda s: (0, 0)),
         ]
         + [ANY_SPEC] * len(after),
-        out_specs=pl.BlockSpec((count, out_width), lambda s: (s, 0)),
-        out_shape=jax.ShapeDtypeStruct((slots, out_width), bf16),
-        compiler_params=pltpu.CompilerParams(vmem_limit_bytes=24 * MIB),
-        cost_estimate=pl.CostEstimate(
-            flops=2 * slots * length * out_width,
-            bytes_accessed=2 * (slots + length) * width, transcendentals=0,
-        ),
+        out_specs=[pl.BlockSpec((count, out_width), lambda s: (s, 0))] * groups,
+        out_shape=[jax.ShapeDtypeStruct((per_group, out_width), bf16)] * groups,
+        compiler_params=pltpu.CompilerParams(vmem_limit_bytes=32 * MIB),
+        cost_estimate=cost(6),
         name="dispatch",
     )(rows, slot_rows, gate_rows, *after)
 
@@ -643,10 +692,7 @@
             jax.ShapeDtypeStruct((8, length), f32),
         ],
         compiler_params=pltpu.CompilerParams(vmem_limit_bytes=24 * MIB),
-        cost_estimate=pl.CostEstimate(
-            flops=2 * length * width * (width + LANES), bytes_accessed=14 * length * width,
-            transcendentals=length,
-        ),
+        cost_estimate=cost(8),
         name="attention_output",
     )(
         hidden, attended, weights["dense"], weights["dense"], weights["vectors"], prior,
@@ -654,19 +700,27 @@
     )
 
 
-def selection(columns, slots, which):
-    slot = lax.broadcasted_iota(jnp.int32, (columns.shape[0], slots), 1)
-    hit = slot == columns[:, which[0] : which[0] + 1]
-    for k in which[1:]:
-        hit = hit | (slot == columns[:, k : k + 1])
-    return jnp.where(hit, 1.0, 0.0).astype(bf16)
-
-
-def combine_kernel(
-    last, back_ref, columns_ref, mid_ref, scalars_ref, vectors_ref, next_ref, *out_refs
-):
+def selected(columns, block_refs, which):
+    per_group = block_refs[0].shape[0]
+    total = None
+    for group, block_ref in enumerate(block_refs):
+        slot = group * per_group + lax.broadcasted_iota(
+            jnp.int32, (columns.shape[0], per_group), 1
+        )
+        hit = slot == columns[:, which[0] : which[0] + 1]
+        for k in which[1:]:
+            hit = hit | (slot == columns[:, k : k + 1])
+        part = dot_on(jnp.where(hit, 1.0, 0.0).astype(bf16), block_ref[...], 1, 0)
+        total = part if total is None else total + part
+    return total
+
+
+def combine_kernel(last, groups, waits, *refs):
+    back_refs, (columns_ref, mid_ref, scalars_ref, vectors_ref, next_ref) = (
+        refs[:groups], refs[groups : groups + 5],
+    )
+    out_refs = refs[groups + 5 + waits :]
     columns, scalars = columns_ref[...], scalars_ref[...]
-    slots = back_ref.shape[0]
     mid = mid_ref[...]
     normed = mid * scalars[:, SCALE : SCALE + 1] * vectors_ref[MOE_GAIN_ROW : MOE_GAIN_ROW + 1, :]
     total = mid + scalars[:, NORMED_SHARE : NORMED_SHARE + 1] * normed
@@ -674,7 +728,7 @@
         row = vectors_ref[VECTOR_ROW + j : VECTOR_ROW + j + 1, :]
         total += scalars[:, VECTOR_SHARE + j : VECTOR_SHARE + j + 1] * row
     for k in range(TOP):
-        branch = dot_on(selection(columns, slots, (k,)), back_ref[...], 1, 0)
+        branch = selected(columns, back_refs, (k,))
         out_refs[k][...] = branch.astype(bf16)
         total += scalars[:, GATE + k : GATE + k + 1] * branch
     if last:
@@ -686,40 +740,41 @@
         ).astype(bf16)
 
 
-def combine(back, columns, mid, scalars, vectors, next_vectors):
+def combine(back, columns, mid, scalars, vectors, next_vectors, after):
     last = next_vectors is None
     length, width = mid.shape
-    slots = back.shape[0]
+    back, which = back
+    groups, per_group = len(back), back[0].shape[1]
     rows = min(256, length)
     wide = pl.BlockSpec((rows, width), lambda t: (t, 0))
     lanes = pl.BlockSpec((rows, LANES), lambda t: (t, 0))
     vector_spec = pl.BlockSpec((8, width), lambda t: (0, 0))
     low = jax.ShapeDtypeStruct((length, width), bf16)
     return pl.pallas_call(
-        functools.partial(combine_kernel, last),
+        functools.partial(combine_kernel, last, groups, len(after)),
         grid=(length // rows,),
-        in_specs=[
-            pl.BlockSpec((slots, width), lambda t: (0, 0)), lanes, wide, lanes, vector_spec,
-            vector_spec,
-        ],
+        in_specs=[pl.BlockSpec((None, per_group, width), lambda t: (which, 0, 0))] * groups
+        + [lanes, wide, lanes, vector_spec, vector_spec]
+        + [ANY_SPEC] * len(after),
         out_specs=[wide] * (TOP + 1 if last else TOP + 2),
         out_shape=[low, low, low]
         if last
         else [low, low, jax.ShapeDtypeStruct((length, width), f32), low],
         compiler_params=pltpu.CompilerParams(vmem_limit_bytes=24 * MIB),
-        cost_estimate=pl.CostEstimate(
-            flops=4 * slots * length * width, bytes_accessed=(2 * slots + 14 * length) * width,
-            transcendentals=0,
-        ),
+        cost_estimate=cost(8),
         name="combine",
-    )(back, columns, mid, scalars, vectors, vectors if last else next_vectors)
+    )(*back, columns, mid, scalars, vectors, vectors if last else next_vectors, *after)
 
 
 def token_backward_kernel(
-    has_prior, back_ref, columns_ref, grad_ref, mid_ref, scalars_ref, branch0_ref, branch1_ref,
-    low_ref, prior_ref, attended_ref, routes_ref, out_w_ref, small_w_ref, vectors_ref,
-    residual_ref, *rest
+    has_prior, groups, *refs
 ):
+    back_refs, rest = refs[:groups], refs[groups:]
+    (
+        columns_ref, grad_ref, mid_ref, scalars_ref, branch0_ref, branch1_ref, low_ref, prior_ref,
+        attended_ref, routes_ref, out_w_ref, small_w_ref, vectors_ref, residual_ref,
+    ) = rest[:14]
+    rest = rest[14:]
     d_mid_ref, d_att_ref, d_prior_ref, g_out_ref, g_small_ref, g_residual_ref, g_gain_ref = (
         rest[-7:]
     )
@@ -774,7 +829,7 @@
         prior_ref[...], d_logits, (((0,), (0,)), ((), ())), precision=highest
     )
     d_normed = (
-        dot_on(selection(columns, back_ref.shape[0], (0, 1)), back_ref[...], 1, 0)
+        selected(columns, back_refs, (0, 1))
         + scalar(NORMED_SHARE) * grad
         + dot_on(d_small_low, small_w_ref[...], 1, 1)
     )
@@ -803,7 +858,8 @@
 
 def token_backward(back, kept, grad, weights, columns, routes, d_prior, after):
     length, width = grad.shape
-    slots = back.shape[0]
+    back, which = back
+    groups, per_group = len(back), back[0].shape[1]
     rows = min(256, length)
     wide = pl.BlockSpec((rows, width), lambda t: (t, 0))
     lanes = pl.BlockSpec((rows, LANES), lambda t: (t, 0))
@@ -812,12 +868,13 @@
         return pl.BlockSpec(shape, lambda t: (0, at))
 
     operands = [
-        back, columns, grad, kept["mid"], kept["scalars"], kept["branch"][0], kept["branch"][1],
+        *back, columns, grad, kept["mid"], kept["scalars"], kept["branch"][0], kept["branch"][1],
         kept["low"], kept["prior"], kept["attended"], routes, weights["dense"], weights["dense"],
         weights["vectors"], weights["residual"],
     ]
     specs = [
-        fixed(slots, width), lanes, wide, wide, lanes, wide, wide, wide, lanes, wide,
+        *[pl.BlockSpec((None, per_group, width), lambda t: (which, 0, 0))] * groups,
+        lanes, wide, wide, lanes, wide, wide, wide, lanes, wide,
         pl.BlockSpec((rows, TOP), lambda t: (t, 0)), fixed(width, width, at=3),
         fixed(width, LANES, at=4 * width // LANES), fixed(8, width), fixed(LANES, LANES),
     ]
@@ -825,7 +882,7 @@
         operands.append(d_prior)
         specs.append(lanes)
     return pl.pallas_call(
-        functools.partial(token_backward_kernel, d_prior is not None),
+        functools.partial(token_backward_kernel, d_prior is not None, groups),
         grid=(length // rows,),
         in_specs=specs + [ANY_SPEC] * len(after),
         out_specs=[
@@ -842,12 +899,55 @@
             jax.ShapeDtypeStruct((8, width), f32),
         ],
         compiler_params=pltpu.CompilerParams(vmem_limit_bytes=48 * MIB),
-        cost_estimate=pl.CostEstimate(
-            flops=2 * length * width * (slots + 2 * width),
-            bytes_accessed=(2 * slots + 24 * length) * width, transcendentals=0,
-        ),
+        cost_estimate=cost(25),
         name="token_backward",
     )(*operands, *after)
+
+
+def finish_backward_kernel(
+    has_later, hidden_ref, d_mid_ref, d_attn_ref, vectors_ref, *rest
+):
+    out_ref, g_gain_ref = rest[-2:]
+    hidden = hidden_ref[...]
+    d_attn = d_attn_ref[...]
+    if has_later:
+        d_attn += rest[0][...].astype(f32)
+    scale = inverse_rms(hidden)
+    unit = hidden * scale
+    g_gain = jnp.broadcast_to(jnp.sum(d_attn * unit, axis=0, keepdims=True), g_gain_ref.shape)
+    d_unit = d_attn * vectors_ref[ATTN_GAIN_ROW : ATTN_GAIN_ROW + 1, :]
+    out_ref[...] = (
+        d_mid_ref[...] + (d_unit - unit * jnp.mean(d_unit * unit, axis=-1, keepdims=True)) * scale
+    ).astype(out_ref.dtype)
+
+    @pl.when(pl.program_id(0) == 0)
+    def _():
+        g_gain_ref[...] = g_gain
+
+    @pl.when(pl.program_id(0) > 0)
+    def _():
+        g_gain_ref[...] += g_gain
+
+
+def finish_backward(hidden, d_mid, d_attn, vectors, later, out_type, after):
+    length, width = hidden.shape
+    rows = min(256, length)
+    wide = pl.BlockSpec((rows, width), lambda t: (t, 0))
+    vector_spec = pl.BlockSpec((8, width), lambda t: (0, 0))
+    extra = [] if later is None else [later]
+    return pl.pallas_call(
+        functools.partial(finish_backward_kernel, later is not None),
+        grid=(length // rows,),
+        in_specs=[wide, wide, wide, vector_spec] + [wide] * len(extra) + [ANY_SPEC] * len(after),
+        out_specs=[wide, vector_spec],
+        out_shape=[
+            jax.ShapeDtypeStruct((length, width), out_type),
+            jax.ShapeDtypeStruct((8, width), f32),
+        ],
+        compiler_params=pltpu.CompilerParams(vmem_limit_bytes=24 * MIB),
+        cost_estimate=cost(6),
+        name="finish_backward",
+    )(hidden, d_mid, d_attn, vectors, *extra, *after)
 
 
 def fetch_layer(layer, local):
@@ -898,19 +998,11 @@
     capacity = length // 4
     slots = EXPERTS * capacity
     block_start = lax.axis_index("context") * length
-    hidden_earlier = earlier_rows(hidden_in[:, 0], hop_count)
+    hidden_earlier = [earlier_rows(hidden_in[micro, 0], hop_count) for micro in micros]
     fetched = [fetch_layer(layer, local) for layer in range(layers)]
     routes = routes[:, 0]
     columns, slot_rows = routing_slots(routes, groups, capacity)
     blank_gates = jnp.zeros((8, length), f32)
-
-    def to_experts(rows):
-        return exchange(rows, groups, capacity).reshape(
-            EXPERTS // groups, groups * capacity, rows.shape[1]
-        )
-
-    def to_tokens(rows):
-        return exchange(rows.reshape(-1, width), groups, capacity).reshape(-1, width)
 
     def normed(hidden, gain):
         return (hidden * inverse_rms(hidden) * gain).astype(bf16)
@@ -922,8 +1014,8 @@
         query = lax.dynamic_slice_in_dim(whole, block_start, length, 0)
         key = lax.dynamic_slice_in_dim(padded, block_start, WINDOW + length, 0)
         segs.append((query, key))
-        sent = dispatch(out_grad[micro, 0], slot_rows[micro], blank_gates, "plain", slots)
-        early.append(to_experts(sent))
+        sent = dispatch(out_grad[micro, 0], slot_rows[micro], blank_gates, "plain", slots, groups)
+        early.append(exchange(sent, 1))
         hidden = hidden_in[micro, 0].astype(f32)
         gain = fetched[0]["vectors"][ATTN_GAIN_ROW : ATTN_GAIN_ROW + 1]
         prior = jnp.pad(prev_logits[micro, 0], ((0, 0), (0, LANES - ROUTED)))
@@ -935,8 +1027,10 @@
         )
 
     saved = [[None] * layers for _ in micros]
-
-    def attention_part(layer, micro, after):
+    expert_sums = [None] * layers
+    last_arrived = []
+
+    def attention_part(layer, micro, after, after_output):
         weights = fetched[layer]
         hidden, attn_in, attn_earlier, prior = state[micro]
         qkv = dot_on(attn_in, weights["dense"][:, : 3 * width], 1, 0).astype(bf16)
@@ -947,28 +1041,40 @@
             hidden, attended, weights, prior, routes[micro]
         )
         mode = "with gate" if layer == layers - 1 else "plain"
-        sent = dispatch(low, slot_rows[micro], gate_rows, mode, slots)
+        sent = dispatch(low, slot_rows[micro], gate_rows, mode, slots, groups, after_output)
         saved[micro][layer] = dict(
             hidden=hidden, attn_in=attn_in, attn_earlier=attn_earlier, prior=prior, qkv=qkv,
             kv_earlier=kv_earlier, attended=attended, lse=lse, mid=mid, low=low,
-            scalars=scalars, gate_rows=gate_rows, logits=logits, arrived=to_experts(sent),
-        )
-        return sent
+            scalars=scalars, gate_rows=gate_rows, logits=logits, arrived=exchange(sent, 1),
+        )
+        return sent[-1]
+
+    def send_out(blocks, micro):
+        own, others = blocks[:1], blocks[1:]
+        others = held(others, last_arrived[1:] if micro > 0 else ())
+        last_arrived[:] = exchange(list(own) + others, -1)
+        return list(last_arrived)
 
     def experts_part(layer, micro, after):
         kept = saved[micro][layer]
-        produced, kept["gate_pre"], kept["up_pre"] = experts_forward(
-            kept["arrived"], fetched[layer]["gate_up"], fetched[layer]["down"], after
-        )
-        kept["returned"] = to_tokens(produced)
-        return produced
-
-    def combine_part(layer, micro):
+        gate_up_w, down_w = fetched[layer]["gate_up"], fetched[layer]["down"]
+        if layer == layers - 1:
+            out, expert_sums[layer] = experts_backward(
+                kept["arrived"], early[micro], None, gate_up_w, down_w, expert_sums[layer], after
+            )
+            arrived = send_out(out, micro)
+            kept["returned"], kept["back"] = (arrived, 0), (arrived, 1)
+        else:
+            out, *kept["pre"] = experts_forward(kept["arrived"], gate_up_w, down_w, after)
+            kept["returned"] = (send_out(out, micro), 0)
+        return out[-1]
+
+    def combine_part(layer, micro, after):
         kept = saved[micro][layer]
         last = layer == layers - 1
         outs = combine(
             kept["returned"], columns[micro], kept["mid"], kept["scalars"],
-            fetched[layer]["vectors"], None if last else fetched[layer + 1]["vectors"],
+            fetched[layer]["vectors"], None if last else fetched[layer + 1]["vectors"], after,
         )
         kept["branch"] = outs[:TOP]
         if last:
@@ -976,82 +1082,71 @@
         state[micro] = (
             outs[TOP], outs[TOP + 1], earlier_rows(outs[TOP + 1], hop_count), kept["logits"],
         )
-        return None
-
-    expert_sums = [None] * layers
+        return outs[TOP]
 
     def experts_back_part(layer, micro, d_rows, after):
         kept = saved[micro][layer]
-        dx, *expert_sums_new = experts_backward(
-            kept["arrived"], d_rows, kept["gate_pre"], kept["up_pre"],
-            fetched[layer]["gate_up"], fetched[layer]["down"], layer == layers - 1,
-            expert_sums[layer], after,
-        )
-        expert_sums[layer] = tuple(expert_sums_new)
-        kept["back"] = to_tokens(dx)
-        return dx
-
-    dense_parts = [[None] * micro_count for _ in range(layers)]
-    residual_parts = [[None] * micro_count for _ in range(layers)]
-
-    def attention_back_part(layer, micro, grad, d_prior, after):
-        kept, weights = saved[micro][layer], fetched[layer]
-        d_mid, d_att, d_prior, g_out, g_small, g_residual, g_moe_gain = token_backward(
-            kept["back"], kept, grad, weights, columns[micro], routes[micro], d_prior, after
-        )
+        dx, expert_sums[layer] = experts_backward(
+            kept["arrived"], d_rows, kept["pre"], fetched[layer]["gate_up"],
+            fetched[layer]["down"], expert_sums[layer], after,
+        )
+        kept["back"] = (send_out(dx, micro), 0)
+        return dx[-1]
+
+    def token_back_part(layer, micro, grad, d_prior, after):
+        kept = saved[micro][layer]
+        (
+            kept["d_mid"], kept["d_att"], d_prior, kept["g_out"], kept["g_small"],
+            kept["g_residual"], g_moe_gain,
+        ) = token_backward(
+            kept["back"], kept, grad, fetched[layer], columns[micro], routes[micro], d_prior, after
+        )
+        kept["g_moe_gain"] = g_moe_gain[0]
+        return d_prior
+
+    def attention_back_part(layer, micro, after):
+        kept, dense = saved[micro][layer], fetched[layer]["dense"]
         query, key = segs[micro]
         dq, dk, dv = attention_backward(
-            kept["qkv"], kept["kv_earlier"], d_att, kept["attended"], kept["lse"],
-            query[None, :], key[:, None], (),
-        )
-        dense = weights["dense"]
+            kept["qkv"], kept["kv_earlier"], kept["d_att"], kept["attended"], kept["lse"],
+            query[None, :], key[:, None], after,
+        )
         query_w, key_w, value_w = (dense[:, i * width : (i + 1) * width] for i in range(3))
-        d_earlier = (
-            dot_on(dk[:WINDOW], key_w, 1, 1) + dot_on(dv[:WINDOW], value_w, 1, 1)
-        ).astype(bf16)
-        later = returned_rows(d_earlier, length, hop_count) if hop_count > 0 else 0.0
-        d_attn = (
+        kept["later"] = None
+        if hop_count > 0:
+            d_earlier = (
+                dot_on(dk[:WINDOW], key_w, 1, 1) + dot_on(dv[:WINDOW], value_w, 1, 1)
+            ).astype(bf16)
+            kept["later"] = returned_rows(d_earlier, length, hop_count)
+        kept["d_attn"] = (
             dot_on(dq, query_w, 1, 1)
             + dot_on(dk[WINDOW:], key_w, 1, 1)
             + dot_on(dv[WINDOW:], value_w, 1, 1)
         )
-        grads = [
+        kept["grads"] = [
             dot_on(kept["attn_in"], dq, 0, 0),
             dot_on(kept["attn_in"], dk[WINDOW:], 0, 0)
             + dot_on(kept["attn_earlier"], dk[:WINDOW], 0, 0),
             dot_on(kept["attn_in"], dv[WINDOW:], 0, 0)
             + dot_on(kept["attn_earlier"], dv[:WINDOW], 0, 0),
-            g_out,
-            g_small,
+            kept["g_out"],
+            kept["g_small"],
         ]
-        residual_parts[layer][micro] = g_residual
-        return d_mid, d_prior, d_attn, later, grads, g_moe_gain[0], dq
-
-    def finish_back_part(layer, micro, parts):
-        d_mid, d_prior, d_attn, later, grads, g_moe_gain, _ = parts
-        hidden = saved[micro][layer]["hidden"]
-        gain = fetched[layer]["vectors"][ATTN_GAIN_ROW : ATTN_GAIN_ROW + 1]
-        d_attn = d_attn + later
-        scale = inverse_rms(hidden)
-        unit = hidden * scale
-        g_attn_gain = jnp.sum(d_attn * unit, axis=0)
-        d_unit = d_attn * gain
-        d_hidden = d_mid + (
-            d_unit - unit * jnp.mean(d_unit * unit, axis=-1, keepdims=True)
-        ) * scale
-        lane = jnp.arange(LANES)[None, :]
-        grads[4] = (
-            grads[4]
-            + jnp.where(lane == ROUTED + 6, g_attn_gain[:, None], 0.0)
-            + jnp.where(lane == ROUTED + 7, g_moe_gain[:, None], 0.0)
-        )
-        dense_parts[layer][micro] = grads
-        return d_hidden, d_prior
+        return dq
+
+    def finish_back_part(layer, micro, after):
+        kept = saved[micro][layer]
+        d_hidden, g_attn_gain = finish_backward(
+            kept["hidden"], kept["d_mid"], kept["d_attn"], fetched[layer]["vectors"],
+            kept["later"], f32 if layer > 0 else bf16, after,
+        )
+        kept["g_attn_gain"] = g_attn_gain[0]
+        return d_hidden
 
     expert_shares, dense_shares = [None] * layers, [None] * layers
 
     def reduce_experts(layer):
-        gate_up, down = expert_sums[layer]
+        gate_up, down = held(expert_sums[layer], saved[0][layer]["back"][0][1:])
         gate_up = gate_up.reshape((-1,) + gate_up.shape[2:])
         expert_shares[layer] = (
             lax.psum_scatter(gate_up, SHARDED, scatter_dimension=1, tiled=True),
@@ -1059,60 +1154,98 @@
         )
         return expert_shares[layer]
 
+    def total_of(layer, name):
+        parts = [saved[micro][layer][name] for micro in micros]
+        return sum(parts[1:], parts[0])
+
+    def packed_dense(layer):
+        parts = [saved[micro][layer]["grads"] for micro in micros]
+        sums = [sum(values[1:], values[0]) for values in zip(*parts)]
+        shards = lax.axis_size("context") * lax.axis_size("dp")
+        at = ROUTED + 8
+        residual = jnp.pad(
+            total_of(layer, "g_residual")[:ROUTED, :ROUTED],
+            ((0, width // shards - ROUTED), (at, LANES - at - ROUTED)),
+        )
+        small = sums[-1] + jnp.tile(residual, (shards, 1))
+        if layer == 0:
+            gains = [total_of(l, "g_moe_gain") for l in range(layers)]
+            gains += [total_of(l, "g_attn_gain") for l in range(layers)]
+            blank = jnp.zeros((LANES - GAINS_LANE - len(gains), width), f32)
+            above = jnp.zeros((GAINS_LANE, width), f32)
+            small = small + jnp.concatenate([above, jnp.stack(gains), blank]).T
+        return jnp.concatenate([total.astype(bf16) for total in sums[:-1] + [small]], axis=1)
+
     def reduce_dense(layer):
-        sums = [sum(parts[1:], parts[0]).astype(bf16) for parts in zip(*dense_parts[layer])]
-        packed = jnp.concatenate(sums, axis=1)
-        share = lax.psum_scatter(packed, SHARDED, scatter_dimension=0, tiled=True)
-        dense_shares[layer] = lax.psum(share, "expert")
-        return (dense_shares[layer],)
+        packed = packed_dense(layer)
+        shards = lax.axis_size("context") * lax.axis_size("dp")
+        parts = packed.reshape(shards, width // shards, packed.shape[1])
+        parts = lax.all_to_all(parts, SHARDED, split_axis=0, concat_axis=0, tiled=True)
+        share = jnp.sum(parts.astype(f32), axis=0)
+        span = 1
+        while span < groups:
+            sent = share.astype(bf16)
+            route = [(i, i ^ span) for i in range(groups)]
+            share = sent.astype(f32) + lax.ppermute(sent, "expert", route).astype(f32)
+            span *= 2
+        dense_shares[layer] = share
+        return (share,)
 
     last = layers - 1
+    d_rows = [None] * micro_count
+
+    def send_back(layer, micro, after):
+        grads[micro] = finish_back_part(layer, micro, after)
+        sent = dispatch(
+            grads[micro], slot_rows[micro], saved[micro][layer - 1]["gate_rows"], "scaled", slots,
+            groups,
+        )
+        d_rows[micro] = exchange(sent, 1)
+        return sent[-1]
+
     before = ()
     for layer in range(layers):
         for micro in micros:
             if layer > 0:
-                combine_part(layer - 1, micro)
+                before = (combine_part(layer - 1, micro, before),)
         for micro in micros:
-            before = (attention_part(layer, micro, before),)
+            waits = tuple(early[micro][1:]) if layer == 0 else ()
+            before = (attention_part(layer, micro, before, waits),)
         for micro in micros:
             before = (experts_part(layer, micro, before),)
+    hidden_out = []
+
+    grads = [out_grad[micro, 0] for micro in micros]
+    d_priors = [None] * micro_count
+    dense_wait = ()
+    for layer in range(last, -1, -1):
+        experts_ready = reduce_experts(layer)
+        for micro in micros:
             if layer == last:
-                before = (experts_back_part(layer, micro, early[micro], before),)
-    hidden_out = [combine_part(last, micro) for micro in micros]
-    expert_ready = reduce_experts(last)
-
-    grads = [(out_grad[micro, 0], None) for micro in micros]
-    waits = ()
-    for layer in range(last, -1, -1):
-        parts = []
-        for micro in micros:
-            parts.append(attention_back_part(layer, micro, *grads[micro], before + waits))
-            before = (parts[-1][-1],)
-        grads = [finish_back_part(layer, micro, parts[micro]) for micro in micros]
+                hidden_out.append(combine_part(last, micro, before))
+                before = (hidden_out[-1],)
+            d_priors[micro] = token_back_part(layer, micro, grads[micro], d_priors[micro], before)
+            before = (saved[micro][layer]["d_att"],)
+            if micro > 0 and layer > 0:
+                before = (send_back(layer, micro - 1, before),)
+            if micro == micro_count - 1:
+                before += dense_wait
+            before = (attention_back_part(layer, micro, before),)
         if layer > 0:
-            dense_ready = reduce_dense(layer)
-            sent = [
-                dispatch(
-                    grads[micro][0], slot_rows[micro], saved[micro][layer - 1]["gate_rows"],
-                    "scaled", slots, before,
-                )
-                for micro in micros
-            ]
-            before = (sent[-1],)
-            d_rows = [to_experts(rows) for rows in sent]
+            before = (send_back(layer, micro_count - 1, before),)
+            dense_wait = reduce_dense(layer)
             for micro in micros:
+                if micro < len(experts_ready):
+                    before += (experts_ready[micro],)
                 before = (experts_back_part(layer - 1, micro, d_rows[micro], before),)
-            waits = tuple(expert_ready)
-            expert_ready = reduce_experts(layer - 1)
+        else:
+            for micro in micros:
+                grads[micro] = finish_back_part(layer, micro, tuple(experts_ready))
     reduce_dense(0)
-    residual_total = lax.psum(
-        jnp.stack([sum(parts[1:], parts[0]) for parts in residual_parts])[:, :ROUTED, :ROUTED],
-        ("expert", "context", "dp"),
-    )
     hidden_out = jnp.stack(hidden_out)[:, None]
-    hidden_grad = jnp.stack([grad[0].astype(bf16) for grad in grads])[:, None]
-
-    dense = jnp.stack(dense_shares).astype(f32)
+    hidden_grad = jnp.stack(grads)[:, None]
+
+    dense = jnp.stack(dense_shares)
     small = dense[:, :, 4 * width :]
     shard = small.shape[1]
     experts_total = [jnp.stack(parts).astype(f32) for parts in zip(*expert_shares)]
@@ -1120,14 +1253,14 @@
     return (
         hidden_out,
         hidden_grad,
-        small[:, :, ROUTED + 6],
+        jnp.stack([small[0, :, GAINS_LANE + layers + l] for l in range(layers)]),
         dense[:, :, :width],
         dense[:, :, width : 2 * width],
         dense[:, :, 2 * width : 3 * width],
         dense[:, :, 3 * width : 4 * width],
-        small[:, :, ROUTED + 7],
+        jnp.stack([small[0, :, GAINS_LANE + l] for l in range(layers)]),
         small[:, :, :ROUTED],
-        residual_total,
+        small[:, :ROUTED, ROUTED + 8 : 2 * ROUTED + 8],
         jnp.transpose(
             small[:, :, ROUTED : ROUTED + 4].reshape(layers, shard, 2, 2), (0, 2, 1, 3)
         ),
@@ -1136,7 +1269,6 @@
         experts_total[0][:, per_dev:],
         experts_total[1],
     )
-
 
 def solution(mesh):
     tokens = P(None, ("expert", "dp"), "context", None)

time: 2210 us -> 1930 us (0.87)
  waiting for transfers between devices: 788 us -> 513 us
  starting transfers between devices: 99.3 us -> 197 us
  local copies, waits for them, and re-layouts: 193 us -> 139 us
  blocking collectives: 40.6 us -> 0 us
    ppermute x0 -> x46, waiting for transfers between devices: none -> 395 us  [the longest x42 335 us: exchange(): out.append(block if d == 0 else lax.ppermute(block, 'expert', route))]
    all_to_all x16 -> x2, waiting for transfers between devices: 332 us -> 53.5 us  [reduce_dense(): lax.all_to_all(parts, SHARDED, split_axis=0, concat_axis=0, tiled=True)]
    ppermute x0 -> x46, starting transfers between devices: none -> 160 us  [the longest x42 131 us: exchange(): out.append(block if d == 0 else lax.ppermute(block, 'expert', route))]
    ppermute x7 -> x8, waiting for transfers between devices: 184 us -> 63.7 us  [passed_along(): return lax.ppermute(block, axis, route)]
    reduce_scatter x2 -> x0, waiting for transfers between devices: 109 us -> none  [reduce_dense(): share = lax.psum_scatter(packed, SHARDED, scatter_dimension=0, tiled=True)]
    reduce_scatter x2, waiting for transfers between devices: 89.6 us -> 0.02 us  [reduce_experts(): lax.psum_scatter(gate_up, SHARDED, scatter_dimension=1, tiled=True)]
    all_to_all x16 -> x2, starting transfers between devices: 78.1 us -> 12.9 us  [reduce_dense(): lax.all_to_all(parts, SHARDED, split_axis=0, concat_axis=0, tiled=True)]
    all_to_all x16 -> x0, local copies, waits for them, and re-layouts: 56.7 us -> none  [exchange(): lax.all_to_all(rows.reshape((EXPERTS // groups, groups, capacity) + rows....]
  transfers between devices with their start and end apart: 36 -> 66, of which waited for: 21 -> 17; matrix products, arithmetic and copies ran while one was open for 14% -> 12% of each run, Pallas kernels for 32% -> 44%
where the time goes in v2:
time: 1930 us; the launch traced here: 1920 us
  Pallas kernels  848 us (44%)
  waiting for transfers between devices  513 us (27%)
  starting transfers between devices  197 us (10%)
  matrix products  155 us (8%)
  local copies, waits for them, and re-layouts  139 us (7%)
  other arithmetic  46.7 us (2%)
    ppermute x42, waiting for transfers between devices, exchange(): out.append(block if d == 0 else lax.ppermute(block, 'expert', route))  335 us
    pallas_call x4, Pallas kernels, experts_backward(): pl.pallas_call(functools.partial(experts_backward_kernel, groups, chunks,...  254 us
    pallas_call x4, Pallas kernels, attention_backward(): pl.pallas_call(functools.partial(attention_backward_kernel, rows, keys, b...  193 us
    dot_general x48, matrix products, dot_on(): lax.dot_general(left_op, right_op, (((left_dim,), (right_dim,)), ((), ())...  155 us
    ppermute x42, starting transfers between devices, exchange(): out.append(block if d == 0 else lax.ppermute(block, 'expert', route))  131 us
    pallas_call x4, Pallas kernels, attention_forward(): pl.pallas_call(functools.partial(attention_forward_kernel, rows, keys, bl...  129 us
    pallas_call x4, Pallas kernels, token_backward(): pl.pallas_call(functools.partial(token_backward_kernel, d_prior is not No...  102 us
    unnamed x572, local copies, waits for them, and re-layouts  98.4 us
  transfers between devices with their start and end apart: 66, of which 17 were waited for; matrix products, arithmetic and copies ran while one was open for 12% of the time, Pallas kernels for 44%

profile of v2, /device:TPU:2, one launch (start us, length us, event | category | flops | bytes accessed | tf_op | source)
XLA Modules:
  0.0 1916.6 jit_solution(7756133176429690153)
XLA Ops:
  23.3 5.0 slice_bitcast_fusion.3
  28.3 4.6 collective-permute-start
  85.5 46.8 %collective-permute-done.7 = bf16[1024,768]{1,0:T(8,128)(2,1)} collective-permute-done((bf16[1024,768]{1,0:T(8,128)(2,1)}, bf16[1024,768]{1,0:T(8,128)(2,1)}, u32[]{:S(2)}, u32[]{:S(2)}) %collective-permute-start.7) | collective-permute-done | bytes 1572896 | tf_op jit(solution)/shard_map/ppermute | solution.py:462
  139.0 5.3 convolution_convert_fusion.7.kp_ref.vp_ref
  144.4 7.4 convolution_convert_fusion.3.q_ref.ko_ref.vo_ref
  151.9 32.2 %attention_forward.4 = (bf16[1024,768]{1,0:T(8,128)(2,1)S(1)}, f32[16,1024]{1,0:T(8,128)S(1)}) custom-call(bf16[1024,2304]{1,0:T(8,128)(2,1)S(1)} %convolution_convert_fusion.3.q_ref.ko_ref.vo_ref, bf16[1024,2304]{1,0:T(8,128)(2,1)S(1)} %convolution_convert_fusion.3.q_ref.ko_ref.vo_ref, bf16[1024,2304]{1,0:T(8,128)(2,1)S(1)} %convolution_convert_fusion.3.q_ref.ko_ref.vo_ref, ...), custom_call_target="tpu_custom_call" | custom-call | flops 29440000000 | bytes 1 | tf_op jit(solution)/shard_map/attention_forward/pallas_call | solution.py:141
  184.3 7.9 attention_output.4
  195.7 4.4 dispatch.9
  204.0 4.5 convolution_convert_fusion.6.kp_ref.vp_ref
  213.0 32.2 %attention_forward.5 = (bf16[1024,768]{1,0:T(8,128)(2,1)S(1)}, f32[16,1024]{1,0:T(8,128)S(1)}) custom-call(bf16[1024,2304]{1,0:T(8,128)(2,1)S(1)} %convolution_convert_fusion.2.q_ref.ko_ref.vo_ref, bf16[1024,2304]{1,0:T(8,128)(2,1)S(1)} %convolution_convert_fusion.2.q_ref.ko_ref.vo_ref, bf16[1024,2304]{1,0:T(8,128)(2,1)S(1)} %convolution_convert_fusion.2.q_ref.ko_ref.vo_ref, ...), custom_call_target="tpu_custom_call" | custom-call | flops 29440000000 | bytes 1 | tf_op jit(solution)/shard_map/attention_forward/pallas_call | solution.py:141
  245.4 7.9 attention_output.5
  253.4 27.1 %collective-permute-done.9.rest_1_.refs_6_ = bf16[512,768]{1,0:T(8,128)(2,1)S(1)} collective-permute-done((bf16[512,768]{1,0:T(8,128)(2,1)S(1)}, bf16[512,768]{1,0:T(8,128)(2,1)S(1)}, u32[]{:S(2)}, u32[]{:S(2)}) %collective-permute-start.9) | collective-permute-done | bytes 786464 | tf_op jit(solution)/shard_map/ppermute | solution.py:493
  280.5 4.4 dispatch.11
  291.1 40.2 %collective-permute-done.5.refs_2_ = bf16[512,768]{1,0:T(8,128)(2,1)} collective-permute-done((bf16[512,768]{1,0:T(8,128)(2,1)}, bf16[512,768]{1,0:T(8,128)(2,1)}, u32[]{:S(2)}, u32[]{:S(2)}) %collective-permute-start.5) | collective-permute-done | bytes 786464 | tf_op jit(solution)/shard_map/ppermute | solution.py:493
  331.3 27.6 %experts_forward.2 = (bf16[1,512,768]{2,1,0:T(8,128)(2,1)S(1)}, bf16[1,512,768]{2,1,0:T(8,128)(2,1)S(1)}, bf16[1,512,768]{2,1,0:T(8,128)(2,1)S(1)}, bf16[1,512,7...) custom-call(bf16[512,768]{1,0:T(8,128)(2,1)S(1)} %copy-done.179, ...), custom_call_target="tpu_custom_call" | custom-call | flops 23920001024 | bytes 1 | tf_op jit(solution)/shard_map/experts_forward/pallas_call | solution.py:314
  366.6 27.4 %experts_forward.3 = (bf16[1,512,768]{2,1,0:T(8,128)(2,1)S(1)}, bf16[1,512,768]{2,1,0:T(8,128)(2,1)S(1)}, bf16[1,512,768]{2,1,0:T(8,128)(2,1)S(1)}, bf16[1,512,7...) custom-call(bf16[512,768]{1,0:T(8,128)(2,1)S(1)} %copy-done.177, ...), custom_call_target="tpu_custom_call" | custom-call | flops 23920001024 | bytes 1 | tf_op jit(solution)/shard_map/experts_forward/pallas_call | solution.py:314
  394.0 37.1 %collective-permute-done.12.refs_2_.refs_4_ = bf16[1,512,768]{2,1,0:T(8,128)(2,1)S(1)} collective-permute-done((bf16[1,512,768]{2,1,0:T(8,128)(2,1)S(1)}, bf16[1,512,768]{2,1,0:T(8,128)(2,1)S(1)}, u32[]{:S(2)}, u32[]{:S(2)}) %collective-permute-start.12) | collective-permute-done | bytes 786464 | tf_op jit(solution)/shard_map/ppermute | solution.py:493
  431.1 8.0 combine.4
  447.8 4.8 collective-permute-start.17
  452.6 7.7 convolution_convert_fusion.1.q_ref.ko_ref.vo_ref
  464.2 48.7 %collective-permute-done.19.refs_2_ = bf16[1,512,768]{2,1,0:T(8,128)(2,1)S(1)} collective-permute-done((bf16[1,512,768]{2,1,0:T(8,128)(2,1)}, bf16[1,512,768]{2,1,0:T(8,128)(2,1)S(1)}, u32[]{:S(2)}, u32[]{:S(2)}) %collective-permute-start.19) | collective-permute-done | bytes 786464 | tf_op jit(solution)/shard_map/ppermute | solution.py:493
  513.0 8.0 combine.5
  521.1 5.9 collective-permute-start.24
  527.0 5.5 convolution_convert_fusion.q_ref.ko_ref.vo_ref
  535.6 32.2 %attention_forward.6 = (bf16[1024,768]{1,0:T(8,128)(2,1)S(1)}, f32[16,1024]{1,0:T(8,128)S(1)}) custom-call(bf16[1024,2304]{1,0:T(8,128)(2,1)S(1)} %bitcast.214, bf16[1024,2304]{1,0:T(8,128)(2,1)S(1)} %bitcast.214, bf16[1024,2304]{1,0:T(8,128)(2,1)S(1)} %bitcast.214, bf16[1024,1536]{1,0:T(8,128)(2,1)S(1)} %convolution_convert_fusion.5.kp_ref.vp_ref, ...), custom_call_target="tpu_custom_call" | custom-call | flops 29440000000 | bytes 1 | tf_op jit(solution)/shard_map/attention_forward/pallas_call | solution.py:141
  567.9 8.1 attention_output.6
  588.1 4.4 convolution_convert_fusion.4.kp_ref.vp_ref
  594.9 32.3 %attention_forward.7 = (bf16[1024,768]{1,0:T(8,128)(2,1)S(1)}, f32[16,1024]{1,0:T(8,128)S(1)}) custom-call(bf16[1024,2304]{1,0:T(8,128)(2,1)S(1)} %copy-done.138, bf16[1024,2304]{1,0:T(8,128)(2,1)S(1)} %copy-done.138, bf16[1024,2304]{1,0:T(8,128)(2,1)S(1)} %copy-done.138, bf16[1024,1536]{1,0:T(8,128)(2,1)S(1)} %convolution_convert_fusion.4.kp_ref.vp_ref, ...), custom_call_target="tpu_custom_call" | custom-call | flops 29440000000 | bytes 1 | tf_op jit(solution)/shard_map/attention_forward/pallas_call | solution.py:141
  627.2 8.1 attention_output.7
  635.4 5.2 dispatch.13
  646.3 74.0 %experts_whole.2 = (bf16[2,512,768]{2,1,0:T(8,128)(2,1)}, bf16[2,512,768]{2,1,0:T(8,128)(2,1)}, bf16[2,512,768]{2,1,0:T(8,128)(2,1)}, bf16[2,512,768]{2,1,0:T(8,...) custom-call(bf16[512,896]{1,0:T(8,128)(2,1)} %copy-done.185, bf16[512,896]{1,0:T(8,128)(2,1)} %copy-done.261, ...), custom_call_target="tpu_custom_call" | custom-call | flops 69000003584 | bytes 1 | tf_op jit(solution)/shard_map/experts_whole/pallas_call | solution.py:435
  720.3 61.5 %collective-permute-start.25 = (bf16[2,512,768]{2,1,0:T(8,128)(2,1)}, bf16[2,512,768]{2,1,0:T(8,128)(2,1)S(1)}, u32[]{:S(2)}, u32[]{:S(2)}) collective-permute-start(bf16[2,512,768]{2,1,0:T(8,128)(2,1)} %get-tuple-element.240), channel_id=1, source_target_pairs={{0,24},{8,0},{16,8},{24,16},{1,25},{9,1},{17,9},{25,17},{2,26},{10... | collective-permute-start | bytes 4718600 | tf_op jit(solution)/shard_map/ppermute | solution.py:493
  782.4 74.6 %experts_whole.3 = (bf16[2,512,768]{2,1,0:T(8,128)(2,1)}, bf16[2,512,768]{2,1,0:T(8,128)(2,1)}, bf16[2,512,768]{2,1,0:T(8,128)(2,1)}, bf16[2,512,768]{2,1,0:T(8,...) custom-call(bf16[512,896]{1,0:T(8,128)(2,1)} %copy-done.184, ...), custom_call_target="tpu_custom_call" | custom-call | flops 69000003584 | bytes 1 | tf_op jit(solution)/shard_map/experts_whole/pallas_call | solution.py:435
  857.0 57.6 %collective-permute-done.26.refs_2_.refs_4_.refs_3_ = bf16[2,512,768]{2,1,0:T(8,128)(2,1)S(1)} collective-permute-done((bf16[2,512,768]{2,1,0:T(8,128)(2,1)}, bf16[2,512,768]{2,1,0:T(8,128)(2,1)S(1)}, u32[]{:S(2)}, u32[]{:S(2)}) %collective-permute-start.26) | collective-permute-done | bytes 1572896 | tf_op jit(solution)/shard_map/ppermute | solution.py:493
  927.1 9.6 combine.6
  941.0 26.6 %token_backward.4 = (f32[1024,768]{1,0:T(8,128)}, bf16[1024,768]{1,0:T(8,128)(2,1)S(1)}, f32[1024,128]{1,0:T(8,128)S(1)}, f32[768,768]{1,0:T(8,128)}, f32[768,12...) custom-call(bf16[2,512,768]{2,1,0:T(8,128)(2,1)} %get-tuple-element.239.refs_0_, ...), custom_call_target="tpu_custom_call" | custom-call | flops 23000000512 | bytes 1 | tf_op jit(solution)/shard_map/token_backward/pallas_call | solution.py:884
  967.7 48.4 %attention_backward.4 = (bf16[1024,768]{1,0:T(8,128)(2,1)S(1)}, bf16[2048,768]{1,0:T(8,128)(2,1)}, bf16[2048,768]{1,0:T(8,128)(2,1)}) custom-call(bf16[1024,2304]{1,0:T(8,128)(2,1)} %convolution_convert_fusion.1.q_ref.ko_ref.vo_ref, bf16[1024,2304]{1,0:T(8,128)(2,1)} %convolution_convert_fusion.1.q_ref.ko_ref.vo_ref, ...), custom_call_target="tpu_custom_call" | custom-call | flops 44160000000 | bytes 1 | tf_op jit(solution)/shard_map/attention_backward/pallas_call | solution.py:238
  1049.4 8.3 collective-permute-done.34
  1060.0 95.2 %collective-permute-done.32.refs_2_ = bf16[2,512,768]{2,1,0:T(8,128)(2,1)} collective-permute-done((bf16[2,512,768]{2,1,0:T(8,128)(2,1)}, bf16[2,512,768]{2,1,0:T(8,128)(2,1)}, u32[]{:S(2)}, u32[]{:S(2)}) %collective-permute-start.32) | collective-permute-done | bytes 1572896 | tf_op jit(solution)/shard_map/ppermute | solution.py:493
  1155.2 9.5 combine.7
  1169.3 25.4 %token_backward.5 = (f32[1024,768]{1,0:T(8,128)}, bf16[1024,768]{1,0:T(8,128)(2,1)S(1)}, f32[1024,128]{1,0:T(8,128)S(1)}, f32[768,768]{1,0:T(8,128)}, f32[768,12...) custom-call(bf16[2,512,768]{2,1,0:T(8,128)(2,1)} %get-tuple-element.253.refs_0_, ...), custom_call_target="tpu_custom_call" | custom-call | flops 23000000512 | bytes 1 | tf_op jit(solution)/shard_map/token_backward/pallas_call | solution.py:884
  1202.4 5.1 dispatch.14
  1208.4 48.3 %attention_backward.5 = (bf16[1024,768]{1,0:T(8,128)(2,1)S(1)}, bf16[2048,768]{1,0:T(8,128)(2,1)}, bf16[2048,768]{1,0:T(8,128)(2,1)}) custom-call(bf16[1024,2304]{1,0:T(8,128)(2,1)} %convolution_convert_fusion.q_ref.ko_ref.vo_ref, bf16[1024,2304]{1,0:T(8,128)(2,1)} %convolution_convert_fusion.q_ref.ko_ref.vo_ref, ...), custom_call_target="tpu_custom_call" | custom-call | flops 44160000000 | bytes 1 | tf_op jit(solution)/shard_map/attention_backward/pallas_call | solution.py:238
  1290.9 7.2 all-to-all-start
  1311.4 4.4 dispatch.15
  1316.8 12.0 collective-permute-start.42
  1333.6 52.1 %experts_backward.2 = (bf16[1,512,768]{2,1,0:T(8,128)(2,1)}, bf16[1,512,768]{2,1,0:T(8,128)(2,1)}, bf16[1,512,768]{2,1,0:T(8,128)(2,1)}, bf16[1,512,768]{2,1,0:T...) custom-call(bf16[512,768]{1,0:T(8,128)(2,1)} %copy-done.178, ...), custom_call_target="tpu_custom_call" | custom-call | flops 47840002048 | bytes 1 | tf_op jit(solution)/shard_map/experts_backward/pallas_call | solution.py:435
  1388.6 52.8 %experts_backward.3 = (bf16[1,512,768]{2,1,0:T(8,128)(2,1)}, bf16[1,512,768]{2,1,0:T(8,128)(2,1)}, bf16[1,512,768]{2,1,0:T(8,128)(2,1)}, bf16[1,512,768]{2,1,0:T...) custom-call(bf16[512,768]{1,0:T(8,128)(2,1)} %copy-done.176, ...), custom_call_target="tpu_custom_call" | custom-call | flops 47840002048 | bytes 1 | tf_op jit(solution)/shard_map/experts_backward/pallas_call | solution.py:435
  1441.5 24.8 %collective-permute-done.40.refs_2_.refs_3_.refs_4_ = bf16[1,512,768]{2,1,0:T(8,128)(2,1)S(1)} collective-permute-done((bf16[1,512,768]{2,1,0:T(8,128)(2,1)}, bf16[1,512,768]{2,1,0:T(8,128)(2,1)S(1)}, u32[]{:S(2)}, u32[]{:S(2)}) %collective-permute-start.40) | collective-permute-done | bytes 786464 | tf_op jit(solution)/shard_map/ppermute | solution.py:493
  1470.5 20.7 %collective-permute-start.49 = (bf16[96,3200]{1,0:T(8,128)(2,1)S(1)}, bf16[96,3200]{1,0:T(8,128)(2,1)S(1)}, u32[]{:S(2)}, u32[]{:S(2)}) collective-permute-start(bf16[96,3200]{1,0:T(8,128)(2,1)S(1)} %reduce_sum.64), channel_id=1, source_target_pairs={{0,8},{8,0},{16,24},{24,16},{1,9},{9,1},{17,25},{25,17},{2,10},{10... | collective-permute-start | bytes 1843208 | tf_op jit(solution)/shard_map/ppermute | solution.py:1189
  1491.2 11.0 collective-permute-done.49
  1502.4 4.6 collective-permute-start.50
  1510.4 16.7 collective-permute-done.50
  1534.9 25.1 %token_backward.6 = (f32[1024,768]{1,0:T(8,128)}, bf16[1024,768]{1,0:T(8,128)(2,1)}, f32[1024,128]{1,0:T(8,128)}, f32[768,768]{1,0:T(8,128)}, f32[768,128]{1,0:T...) custom-call(bf16[1,512,768]{2,1,0:T(8,128)(2,1)S(1)} %copy-done.191, bf16[1,512,768]{2,1,0:T(8,128)(2,1)S(1)} %copy-done.14, ...), custom_call_target="tpu_custom_call" | custom-call | flops 23000000512 | bytes 1 | tf_op jit(solution)/shard_map/token_backward/pallas_call | solution.py:884
  1570.8 48.3 %attention_backward.6 = (bf16[1024,768]{1,0:T(8,128)(2,1)S(1)}, bf16[2048,768]{1,0:T(8,128)(2,1)}, bf16[2048,768]{1,0:T(8,128)(2,1)}) custom-call(bf16[1024,2304]{1,0:T(8,128)(2,1)} %copy-done.125, bf16[1024,2304]{1,0:T(8,128)(2,1)} %copy-done.125, bf16[1024,2304]{1,0:T(8,128)(2,1)} %copy-done.125, bf16[1024,1536]{1,0:T(8,128)(2,1)} %copy-done.127, ...), custom_call_target="tpu_custom_call" | custom-call | flops 44160000000 | bytes 1 | tf_op jit(solution)/shard_map/attention_backward/pallas_call | solution.py:238
  1628.3 4.5 fusion.36
  1632.8 4.6 fusion.33
  1648.4 25.3 %token_backward.7 = (f32[1024,768]{1,0:T(8,128)}, bf16[1024,768]{1,0:T(8,128)(2,1)}, f32[1024,128]{1,0:T(8,128)}, f32[768,768]{1,0:T(8,128)}, f32[768,128]{1,0:T...) custom-call(bf16[1,512,768]{2,1,0:T(8,128)(2,1)S(1)} %copy-done.190, ...), custom_call_target="tpu_custom_call" | custom-call | flops 23000000512 | bytes 1 | tf_op jit(solution)/shard_map/token_backward/pallas_call | solution.py:884
  1676.5 48.2 %attention_backward.7 = (bf16[1024,768]{1,0:T(8,128)(2,1)S(1)}, bf16[2048,768]{1,0:T(8,128)(2,1)}, bf16[2048,768]{1,0:T(8,128)(2,1)}) custom-call(bf16[1024,2304]{1,0:T(8,128)(2,1)} %copy-done.124, bf16[1024,2304]{1,0:T(8,128)(2,1)} %copy-done.124, bf16[1024,2304]{1,0:T(8,128)(2,1)} %copy-done.124, bf16[1024,1536]{1,0:T(8,128)(2,1)} %copy-done.126, ...), custom_call_target="tpu_custom_call" | custom-call | flops 44160000000 | bytes 1 | tf_op jit(solution)/shard_map/attention_backward/pallas_call | solution.py:238
  1761.9 8.5 collective-permute-done.51
  1793.0 5.7 all-to-all-start.1
  1800.6 53.5 %all-to-all-done.1 = bf16[8,96,3200]{2,1,0:T(8,128)(2,1)} async-done(((bf16[8,96,3200]{2,1,0:T(8,128)(2,1)}), bf16[8,96,3200]{2,1,0:T(8,128)(2,1)}, u32[]{:S(2)}, u32[]{:S(2)}) %all-to-all-start.1) | async-done | bytes 4915232 | tf_op jit(solution)/shard_map/all_to_all | solution.py:1183
  1866.5 7.6 collective-permute-done.52
  1879.0 24.7 %collective-permute-done.53 = bf16[96,3200]{1,0:T(8,128)(2,1)S(1)} collective-permute-done((bf16[96,3200]{1,0:T(8,128)(2,1)S(1)}, bf16[96,3200]{1,0:T(8,128)(2,1)S(1)}, u32[]{:S(2)}, u32[]{:S(2)}) %collective-permute-start.53) | collective-permute-done | bytes 614432 | tf_op jit(solution)/shard_map/ppermute | solution.py:1189
  (844 shorter events, 391.4 us)
Async XLA Ops:
  7.2 129.0 %all-gather.9.cloned.1.call-start = ((), (), s32[]{:S(2)}) async-start(), calls=%async_computation.6 | async-start | bytes 5529600 | tf_op jit(solution)/shard_map/all_gather | solution.py:970
  14.9 271.3 %all-gather.13.cloned.1.call-start = ((), (), s32[]{:S(2)}) async-start(), calls=%async_computation.8 | async-start | bytes 5529600 | tf_op jit(solution)/shard_map/all_gather | solution.py:970
  16.6 314.7 %all-gather.17.cloned.1.call-start = ((), (), s32[]{:S(2)}) async-start(), calls=%async_computation.14 | async-start | bytes 7077888 | tf_op jit(solution)/shard_map/all_gather | solution.py:973
  17.9 313.4 %all-gather.11.cloned.1.call-start = ((), (), s32[]{:S(2)}) async-start(), calls=%async_computation.7 | async-start | bytes 14155776 | tf_op jit(solution)/shard_map/all_gather | solution.py:972
  22.6 623.6 %all-gather.19.cloned.1.call-start = ((), (), s32[]{:S(2)}) async-start(), calls=%async_computation.15 | async-start | bytes 7077888 | tf_op jit(solution)/shard_map/all_gather | solution.py:973
  23.3 623.0 %all-gather.15.cloned.1.call-start = ((), (), s32[]{:S(2)}) async-start(), calls=%async_computation.9 | async-start | bytes 14155776 | tf_op jit(solution)/shard_map/all_gather | solution.py:972
  28.3 54.4 %collective-permute-start = (bf16[1024,768]{1,0:T(8,128)(2,1)}, bf16[1024,768]{1,0:T(8,128)(2,1)}, u32[]{:S(2)}, u32[]{:S(2)}) collective-permute-start(bf16[1024,768]{1,0:T(8,128)(2,1)} %get-tuple-element.423), channel_id=1, source_target_pairs={{0,4},{1,5},{2,6},{3,7},{8,12},{9,13},{10,14},{11,15},{16,20},{17,... | collective-permute-start | bytes 4718600 | tf_op jit(solution)/shard_map/ppermute | solution.py:462
  47.2 145.9 %collective-permute-start.1 = (bf16[512,768]{1,0:T(8,128)(2,1)}, bf16[512,768]{1,0:T(8,128)(2,1)}, u32[]{:S(2)}, u32[]{:S(2)}) collective-permute-start(bf16[512,768]{1,0:T(8,128)(2,1)} %get-tuple-element.188), channel_id=1, source_target_pairs={{0,8},{8,16},{16,24},{24,0},{1,9},{9,17},{17,25},{25,1},{2,10},{10... | collective-permute-start | bytes 2359304 | tf_op jit(solution)/shard_map/ppermute | solution.py:493
  48.7 147.0 %collective-permute-start.2 = (bf16[512,768]{1,0:T(8,128)(2,1)}, bf16[512,768]{1,0:T(8,128)(2,1)}, u32[]{:S(2)}, u32[]{:S(2)}) collective-permute-start(bf16[512,768]{1,0:T(8,128)(2,1)} %get-tuple-element.189), channel_id=1, source_target_pairs={{0,16},{8,24},{16,0},{24,8},{1,17},{9,25},{17,1},{25,9},{2,18},{10... | collective-permute-start | bytes 2359304 | tf_op jit(solution)/shard_map/ppermute | solution.py:493
  51.3 144.4 %collective-permute-start.3 = (bf16[512,768]{1,0:T(8,128)(2,1)}, bf16[512,768]{1,0:T(8,128)(2,1)}, u32[]{:S(2)}, u32[]{:S(2)}) collective-permute-start(bf16[512,768]{1,0:T(8,128)(2,1)} %get-tuple-element.190), channel_id=1, source_target_pairs={{0,24},{8,0},{16,8},{24,16},{1,25},{9,1},{17,9},{25,17},{2,26},{10... | collective-permute-start | bytes 2359304 | tf_op jit(solution)/shard_map/ppermute | solution.py:493
  52.7 79.6 %collective-permute-start.7 = (bf16[1024,768]{1,0:T(8,128)(2,1)}, bf16[1024,768]{1,0:T(8,128)(2,1)}, u32[]{:S(2)}, u32[]{:S(2)}) collective-permute-start(bf16[1024,768]{1,0:T(8,128)(2,1)} %get-tuple-element.426), channel_id=1, source_target_pairs={{0,4},{1,5},{2,6},{3,7},{8,12},{9,13},{10,14},{11,15},{16,20},{17,... | collective-permute-start | bytes 4718600 | tf_op jit(solution)/shard_map/ppermute | solution.py:462
  56.4 1277.2 %reduce-scatter.5.cloned.1.call-start = ((), (), s32[]{:S(2)}) async-start(), calls=%async_computation.10 | async-start | bytes 14155776 | tf_op jit(solution)/shard_map/reduce_scatter | solution.py:1152
  82.7 162.6 %collective-permute-start.10 = (bf16[512,768]{1,0:T(8,128)(2,1)}, bf16[512,768]{1,0:T(8,128)(2,1)}, u32[]{:S(2)}, u32[]{:S(2)}) collective-permute-start(bf16[512,768]{1,0:T(8,128)(2,1)} %get-tuple-element.200), channel_id=1, source_target_pairs={{0,24},{8,0},{16,8},{24,16},{1,25},{9,1},{17,9},{25,17},{2,26},{10... | collective-permute-start | bytes 2359304 | tf_op jit(solution)/shard_map/ppermute | solution.py:493
  132.3 121.1 %collective-permute-start.8 = (bf16[512,768]{1,0:T(8,128)(2,1)}, bf16[512,768]{1,0:T(8,128)(2,1)}, u32[]{:S(2)}, u32[]{:S(2)}) collective-permute-start(bf16[512,768]{1,0:T(8,128)(2,1)} %get-tuple-element.198), channel_id=1, source_target_pairs={{0,8},{8,16},{16,24},{24,0},{1,9},{9,17},{17,25},{25,1},{2,10},{10... | collective-permute-start | bytes 2359304 | tf_op jit(solution)/shard_map/ppermute | solution.py:493
  193.1 87.5 %collective-permute-start.9 = (bf16[512,768]{1,0:T(8,128)(2,1)S(1)}, bf16[512,768]{1,0:T(8,128)(2,1)S(1)}, u32[]{:S(2)}, u32[]{:S(2)}) collective-permute-start(bf16[512,768]{1,0:T(8,128)(2,1)S(1)} %copy-done.108), channel_id=1, source_target_pairs={{0,16},{8,24},{16,0},{24,8},{1,17},{9,25},{17,1},{25,9},{2,18},{10... | collective-permute-start | bytes 2359304 | tf_op jit(solution)/shard_map/ppermute | solution.py:493
  200.2 87.2 %collective-permute-start.4 = (bf16[512,768]{1,0:T(8,128)(2,1)}, bf16[512,768]{1,0:T(8,128)(2,1)}, u32[]{:S(2)}, u32[]{:S(2)}) collective-permute-start(bf16[512,768]{1,0:T(8,128)(2,1)} %get-tuple-element.192), channel_id=1, source_target_pairs={{0,8},{8,16},{16,24},{24,0},{1,9},{9,17},{17,25},{25,1},{2,10},{10... | collective-permute-start | bytes 2359304 | tf_op jit(solution)/shard_map/ppermute | solution.py:493
  200.3 131.0 %collective-permute-start.6 = (bf16[512,768]{1,0:T(8,128)(2,1)}, bf16[512,768]{1,0:T(8,128)(2,1)}, u32[]{:S(2)}, u32[]{:S(2)}) collective-permute-start(bf16[512,768]{1,0:T(8,128)(2,1)} %get-tuple-element.194.rest_0_), channel_id=1, source_target_pairs={{0,24},{8,0},{16,8},{24,16},{1,25},{9,1},{17,9},{25,17},{2,26},{10... | collective-permute-start | bytes 2359304 | tf_op jit(solution)/shard_map/ppermute | solution.py:493
  245.3 86.0 %collective-permute-start.5 = (bf16[512,768]{1,0:T(8,128)(2,1)}, bf16[512,768]{1,0:T(8,128)(2,1)}, u32[]{:S(2)}, u32[]{:S(2)}) collective-permute-start(bf16[512,768]{1,0:T(8,128)(2,1)} %get-tuple-element.193), channel_id=1, source_target_pairs={{0,16},{8,24},{16,0},{24,8},{1,17},{9,25},{17,1},{25,9},{2,18},{10... | collective-permute-start | bytes 2359304 | tf_op jit(solution)/shard_map/ppermute | solution.py:493
  285.9 75.5 %collective-permute-start.14 = (bf16[512,768]{1,0:T(8,128)(2,1)}, bf16[512,768]{1,0:T(8,128)(2,1)S(1)}, u32[]{:S(2)}, u32[]{:S(2)}) collective-permute-start(bf16[512,768]{1,0:T(8,128)(2,1)} %get-tuple-element.210), channel_id=1, source_target_pairs={{0,8},{8,16},{16,24},{24,0},{1,9},{9,17},{17,25},{25,1},{2,10},{10... | collective-permute-start | bytes 2359304 | tf_op jit(solution)/shard_map/ppermute | solution.py:493
  286.1 77.2 %collective-permute-start.15 = (bf16[512,768]{1,0:T(8,128)(2,1)}, bf16[512,768]{1,0:T(8,128)(2,1)S(1)}, u32[]{:S(2)}, u32[]{:S(2)}) collective-permute-start(bf16[512,768]{1,0:T(8,128)(2,1)} %get-tuple-element.211), channel_id=1, source_target_pairs={{0,16},{8,24},{16,0},{24,8},{1,17},{9,25},{17,1},{25,9},{2,18},{10... | collective-permute-start | bytes 2359304 | tf_op jit(solution)/shard_map/ppermute | solution.py:493
  287.4 76.8 %collective-permute-start.16 = (bf16[512,768]{1,0:T(8,128)(2,1)}, bf16[512,768]{1,0:T(8,128)(2,1)}, u32[]{:S(2)}, u32[]{:S(2)}) collective-permute-start(bf16[512,768]{1,0:T(8,128)(2,1)} %get-tuple-element.201.refs_7_), channel_id=1, source_target_pairs={{0,24},{8,0},{16,8},{24,16},{1,25},{9,1},{17,9},{25,17},{2,26},{10... | collective-permute-start | bytes 2359304 | tf_op jit(solution)/shard_map/ppermute | solution.py:493
  359.0 35.0 %collective-permute-start.11 = (bf16[1,512,768]{2,1,0:T(8,128)(2,1)S(1)}, bf16[1,512,768]{2,1,0:T(8,128)(2,1)S(1)}, u32[]{:S(2)}, u32[]{:S(2)}) collective-permute-start(bf16[1,512,768]{2,1,0:T(8,128)(2,1)S(1)} %get-tuple-element.203), channel_id=1, source_target_pairs={{0,24},{8,0},{16,8},{24,16},{1,25},{9,1},{17,9},{25,17},{2,26},{10... | collective-permute-start | bytes 2359304 | tf_op jit(solution)/shard_map/ppermute | solution.py:493
  361.3 69.8 %collective-permute-start.12 = (bf16[1,512,768]{2,1,0:T(8,128)(2,1)S(1)}, bf16[1,512,768]{2,1,0:T(8,128)(2,1)S(1)}, u32[]{:S(2)}, u32[]{:S(2)}) collective-permute-start(bf16[1,512,768]{2,1,0:T(8,128)(2,1)S(1)} %get-tuple-element.204), channel_id=1, source_target_pairs={{0,16},{8,24},{16,0},{24,8},{1,17},{9,25},{17,1},{25,9},{2,18},{10... | collective-permute-start | bytes 2359304 | tf_op jit(solution)/shard_map/ppermute | solution.py:493
  362.2 68.9 %collective-permute-start.13 = (bf16[1,512,768]{2,1,0:T(8,128)(2,1)S(1)}, bf16[1,512,768]{2,1,0:T(8,128)(2,1)S(1)}, u32[]{:S(2)}, u32[]{:S(2)}) collective-permute-start(bf16[1,512,768]{2,1,0:T(8,128)(2,1)S(1)} %get-tuple-element.205.refs_7_), channel_id=1, source_target_pairs={{0,8},{8,16},{16,24},{24,0},{1,9},{9,17},{17,25},{25,1},{2,10},{10... | collective-permute-start | bytes 2359304 | tf_op jit(solution)/shard_map/ppermute | solution.py:493
  444.9 68.0 %collective-permute-start.19 = (bf16[1,512,768]{2,1,0:T(8,128)(2,1)}, bf16[1,512,768]{2,1,0:T(8,128)(2,1)S(1)}, u32[]{:S(2)}, u32[]{:S(2)}) collective-permute-start(bf16[1,512,768]{2,1,0:T(8,128)(2,1)} %get-tuple-element.219), channel_id=1, source_target_pairs={{0,16},{8,24},{16,0},{24,8},{1,17},{9,25},{17,1},{25,9},{2,18},{10... | collective-permute-start | bytes 2359304 | tf_op jit(solution)/shard_map/ppermute | solution.py:493
  445.7 67.2 %collective-permute-start.20 = (bf16[1,512,768]{2,1,0:T(8,128)(2,1)}, bf16[1,512,768]{2,1,0:T(8,128)(2,1)S(1)}, u32[]{:S(2)}, u32[]{:S(2)}) collective-permute-start(bf16[1,512,768]{2,1,0:T(8,128)(2,1)} %get-tuple-element.220), channel_id=1, source_target_pairs={{0,8},{8,16},{16,24},{24,0},{1,9},{9,17},{17,25},{25,1},{2,10},{10... | collective-permute-start | bytes 2359304 | tf_op jit(solution)/shard_map/ppermute | solution.py:493
  447.8 84.8 %collective-permute-start.17 = (bf16[1024,768]{1,0:T(8,128)(2,1)S(1)}, bf16[1024,768]{1,0:T(8,128)(2,1)S(1)}, u32[]{:S(2)}, u32[]{:S(2)}) collective-permute-start(bf16[1024,768]{1,0:T(8,128)(2,1)S(1)} %copy-done.99), channel_id=1, source_target_pairs={{0,4},{1,5},{2,6},{3,7},{8,12},{9,13},{10,14},{11,15},{16,20},{17,... | collective-permute-start | bytes 4718600 | tf_op jit(solution)/shard_map/ppermute | solution.py:462
  521.1 67.0 %collective-permute-start.24 = (bf16[1024,768]{1,0:T(8,128)(2,1)S(1)}, bf16[1024,768]{1,0:T(8,128)(2,1)}, u32[]{:S(2)}, u32[]{:S(2)}) collective-permute-start(bf16[1024,768]{1,0:T(8,128)(2,1)S(1)} %get-tuple-element.233), channel_id=1, source_target_pairs={{0,4},{1,5},{2,6},{3,7},{8,12},{9,13},{10,14},{11,15},{16,20},{17,... | collective-permute-start | bytes 4718600 | tf_op jit(solution)/shard_map/ppermute | solution.py:462
  582.9 59.3 %collective-permute-start.21 = (bf16[512,896]{1,0:T(8,128)(2,1)S(1)}, bf16[512,896]{1,0:T(8,128)(2,1)S(1)}, u32[]{:S(2)}, u32[]{:S(2)}) collective-permute-start(bf16[512,896]{1,0:T(8,128)(2,1)S(1)} %get-tuple-element.229), channel_id=1, source_target_pairs={{0,8},{8,16},{16,24},{24,0},{1,9},{9,17},{17,25},{25,1},{2,10},{10... | collective-permute-start | bytes 2752520 | tf_op jit(solution)/shard_map/ppermute | solution.py:493
  583.3 63.0 %collective-permute-start.22 = (bf16[512,896]{1,0:T(8,128)(2,1)S(1)}, bf16[512,896]{1,0:T(8,128)(2,1)}, u32[]{:S(2)}, u32[]{:S(2)}) collective-permute-start(bf16[512,896]{1,0:T(8,128)(2,1)S(1)} %get-tuple-element.230), channel_id=1, source_target_pairs={{0,16},{8,24},{16,0},{24,8},{1,17},{9,25},{17,1},{25,9},{2,18},{10... | collective-permute-start | bytes 2752520 | tf_op jit(solution)/shard_map/ppermute | solution.py:493
  585.1 61.2 %collective-permute-start.23 = (bf16[512,896]{1,0:T(8,128)(2,1)S(1)}, bf16[512,896]{1,0:T(8,128)(2,1)}, u32[]{:S(2)}, u32[]{:S(2)}) collective-permute-start(bf16[512,896]{1,0:T(8,128)(2,1)S(1)} %get-tuple-element.231.rest_0_), channel_id=1, source_target_pairs={{0,24},{8,0},{16,8},{24,16},{1,25},{9,1},{17,9},{25,17},{2,26},{10... | collective-permute-start | bytes 2752520 | tf_op jit(solution)/shard_map/ppermute | solution.py:493
  641.5 140.3 %collective-permute-start.28 = (bf16[512,896]{1,0:T(8,128)(2,1)}, bf16[512,896]{1,0:T(8,128)(2,1)}, u32[]{:S(2)}, u32[]{:S(2)}) collective-permute-start(bf16[512,896]{1,0:T(8,128)(2,1)} %get-tuple-element.246), channel_id=1, source_target_pairs={{0,8},{8,16},{16,24},{24,0},{1,9},{9,17},{17,25},{25,1},{2,10},{10... | collective-permute-start | bytes 2752520 | tf_op jit(solution)/shard_map/ppermute | solution.py:493
  641.5 140.9 %collective-permute-start.29 = (bf16[512,896]{1,0:T(8,128)(2,1)}, bf16[512,896]{1,0:T(8,128)(2,1)}, u32[]{:S(2)}, u32[]{:S(2)}) collective-permute-start(bf16[512,896]{1,0:T(8,128)(2,1)} %get-tuple-element.247), channel_id=1, source_target_pairs={{0,16},{8,24},{16,0},{24,8},{1,17},{9,25},{17,1},{25,9},{2,18},{10... | collective-permute-start | bytes 2752520 | tf_op jit(solution)/shard_map/ppermute | solution.py:493
  643.1 139.3 %collective-permute-start.30 = (bf16[512,896]{1,0:T(8,128)(2,1)}, bf16[512,896]{1,0:T(8,128)(2,1)}, u32[]{:S(2)}, u32[]{:S(2)}) collective-permute-start(bf16[512,896]{1,0:T(8,128)(2,1)} %get-tuple-element.238.refs_15_), channel_id=1, source_target_pairs={{0,24},{8,0},{16,8},{24,16},{1,25},{9,1},{17,9},{25,17},{2,26},{10... | collective-permute-start | bytes 2752520 | tf_op jit(solution)/shard_map/ppermute | solution.py:493
  720.3 136.7 %collective-permute-start.25 = (bf16[2,512,768]{2,1,0:T(8,128)(2,1)}, bf16[2,512,768]{2,1,0:T(8,128)(2,1)S(1)}, u32[]{:S(2)}, u32[]{:S(2)}) collective-permute-start(bf16[2,512,768]{2,1,0:T(8,128)(2,1)} %get-tuple-element.240), channel_id=1, source_target_pairs={{0,24},{8,0},{16,8},{24,16},{1,25},{9,1},{17,9},{25,17},{2,26},{10... | collective-permute-start | bytes 4718600 | tf_op jit(solution)/shard_map/ppermute | solution.py:493
  781.8 132.8 %collective-permute-start.26 = (bf16[2,512,768]{2,1,0:T(8,128)(2,1)}, bf16[2,512,768]{2,1,0:T(8,128)(2,1)S(1)}, u32[]{:S(2)}, u32[]{:S(2)}) collective-permute-start(bf16[2,512,768]{2,1,0:T(8,128)(2,1)} %get-tuple-element.241), channel_id=1, source_target_pairs={{0,16},{8,24},{16,0},{24,8},{1,17},{9,25},{17,1},{25,9},{2,18},{10... | collective-permute-start | bytes 4718600 | tf_op jit(solution)/shard_map/ppermute | solution.py:493
  781.8 132.8 %collective-permute-start.27 = (bf16[2,512,768]{2,1,0:T(8,128)(2,1)}, bf16[2,512,768]{2,1,0:T(8,128)(2,1)}, u32[]{:S(2)}, u32[]{:S(2)}) collective-permute-start(bf16[2,512,768]{2,1,0:T(8,128)(2,1)} %get-tuple-element.242.refs_17_), channel_id=1, source_target_pairs={{0,8},{8,16},{16,24},{24,0},{1,9},{9,17},{17,25},{25,1},{2,10},{10... | collective-permute-start | bytes 4718600 | tf_op jit(solution)/shard_map/ppermute | solution.py:493
  915.8 472.8 %reduce-scatter.7.cloned.1.call-start = ((), (), s32[]{:S(2)}) async-start(), calls=%async_computation.11 | async-start | bytes 7077888 | tf_op jit(solution)/shard_map/reduce_scatter | solution.py:1153
  1023.3 34.4 %collective-permute-start.34 = (bf16[1024,768]{1,0:T(8,128)(2,1)}, bf16[1024,768]{1,0:T(8,128)(2,1)}, u32[]{:S(2)}, u32[]{:S(2)}) collective-permute-start(bf16[1024,768]{1,0:T(8,128)(2,1)} %add_convert_fusion.3), channel_id=1, source_target_pairs={{4,0},{5,1},{6,2},{7,3},{12,8},{13,9},{14,10},{15,11},{20,16},{21,... | collective-permute-start | bytes 4718600 | tf_op jit(solution)/shard_map/ppermute | solution.py:462
  1024.6 35.4 %collective-permute-start.31 = (bf16[2,512,768]{2,1,0:T(8,128)(2,1)}, bf16[2,512,768]{2,1,0:T(8,128)(2,1)}, u32[]{:S(2)}, u32[]{:S(2)}) collective-permute-start(bf16[2,512,768]{2,1,0:T(8,128)(2,1)} %get-tuple-element.256), channel_id=1, source_target_pairs={{0,24},{8,0},{16,8},{24,16},{1,25},{9,1},{17,9},{25,17},{2,26},{10... | collective-permute-start | bytes 4718600 | tf_op jit(solution)/shard_map/ppermute | solution.py:493
  1024.7 130.5 %collective-permute-start.32 = (bf16[2,512,768]{2,1,0:T(8,128)(2,1)}, bf16[2,512,768]{2,1,0:T(8,128)(2,1)}, u32[]{:S(2)}, u32[]{:S(2)}) collective-permute-start(bf16[2,512,768]{2,1,0:T(8,128)(2,1)} %get-tuple-element.257), channel_id=1, source_target_pairs={{0,16},{8,24},{16,0},{24,8},{1,17},{9,25},{17,1},{25,9},{2,18},{10... | collective-permute-start | bytes 4718600 | tf_op jit(solution)/shard_map/ppermute | solution.py:493
  1024.8 130.4 %collective-permute-start.33 = (bf16[2,512,768]{2,1,0:T(8,128)(2,1)}, bf16[2,512,768]{2,1,0:T(8,128)(2,1)}, u32[]{:S(2)}, u32[]{:S(2)}) collective-permute-start(bf16[2,512,768]{2,1,0:T(8,128)(2,1)} %get-tuple-element.258), channel_id=1, source_target_pairs={{0,8},{8,16},{16,24},{24,0},{1,9},{9,17},{17,25},{25,1},{2,10},{10... | collective-permute-start | bytes 4718600 | tf_op jit(solution)/shard_map/ppermute | solution.py:493
  1208.4 125.2 %collective-permute-start.37 = (bf16[512,768]{1,0:T(8,128)(2,1)}, bf16[512,768]{1,0:T(8,128)(2,1)}, u32[]{:S(2)}, u32[]{:S(2)}) collective-permute-start(bf16[512,768]{1,0:T(8,128)(2,1)} %get-tuple-element.277.rest_0_), channel_id=1, source_target_pairs={{0,24},{8,0},{16,8},{24,16},{1,25},{9,1},{17,9},{25,17},{2,26},{10... | collective-permute-start | bytes 2359304 | tf_op jit(solution)/shard_map/ppermute | solution.py:493
  1264.1 43.2 %collective-permute-start.38 = (bf16[1024,768]{1,0:T(8,128)(2,1)}, bf16[1024,768]{1,0:T(8,128)(2,1)}, u32[]{:S(2)}, u32[]{:S(2)}) collective-permute-start(bf16[1024,768]{1,0:T(8,128)(2,1)} %add_convert_fusion.2), channel_id=1, source_target_pairs={{4,0},{5,1},{6,2},{7,3},{12,8},{13,9},{14,10},{15,11},{20,16},{21,... | collective-permute-start | bytes 4718600 | tf_op jit(solution)/shard_map/ppermute | solution.py:462
  1265.4 67.3 %collective-permute-start.35 = (bf16[512,768]{1,0:T(8,128)(2,1)}, bf16[512,768]{1,0:T(8,128)(2,1)}, u32[]{:S(2)}, u32[]{:S(2)}) collective-permute-start(bf16[512,768]{1,0:T(8,128)(2,1)} %get-tuple-element.275), channel_id=1, source_target_pairs={{0,8},{8,16},{16,24},{24,0},{1,9},{9,17},{17,25},{25,1},{2,10},{10... | collective-permute-start | bytes 2359304 | tf_op jit(solution)/shard_map/ppermute | solution.py:493
  1268.3 65.3 %collective-permute-start.36 = (bf16[512,768]{1,0:T(8,128)(2,1)}, bf16[512,768]{1,0:T(8,128)(2,1)}, u32[]{:S(2)}, u32[]{:S(2)}) collective-permute-start(bf16[512,768]{1,0:T(8,128)(2,1)} %get-tuple-element.276), channel_id=1, source_target_pairs={{0,16},{8,24},{16,0},{24,8},{1,17},{9,25},{17,1},{25,9},{2,18},{10... | collective-permute-start | bytes 2359304 | tf_op jit(solution)/shard_map/ppermute | solution.py:493
  1290.9 176.4 %all-to-all-start = ((bf16[8,96,3200]{2,1,0:T(8,128)(2,1)}), bf16[8,96,3200]{2,1,0:T(8,128)(2,1)}, u32[]{:S(2)}, u32[]{:S(2)}) async-start(bf16[8,96,3200]{2,1,0:T(8,128)(2,1)} %bitcast.217), calls=%async_computation.4 | async-start | bytes 9830400 | tf_op jit(solution)/shard_map/all_to_all | solution.py:1183
  1298.1 473.9 %reduce-scatter.11.cloned.1.call-start = ((), (), s32[]{:S(2)}) async-start(), calls=%async_computation.13 | async-start | bytes 7077888 | tf_op jit(solution)/shard_map/reduce_scatter | solution.py:1153
  1316.8 71.6 %collective-permute-start.42 = (bf16[512,768]{1,0:T(8,128)(2,1)}, bf16[512,768]{1,0:T(8,128)(2,1)}, u32[]{:S(2)}, u32[]{:S(2)}) collective-permute-start(bf16[512,768]{1,0:T(8,128)(2,1)} %get-tuple-element.298), channel_id=1, source_target_pairs={{0,8},{8,16},{16,24},{24,0},{1,9},{9,17},{17,25},{25,1},{2,10},{10... | collective-permute-start | bytes 2359304 | tf_op jit(solution)/shard_map/ppermute | solution.py:493
  1328.7 59.9 %collective-permute-start.43 = (bf16[512,768]{1,0:T(8,128)(2,1)S(1)}, bf16[512,768]{1,0:T(8,128)(2,1)}, u32[]{:S(2)}, u32[]{:S(2)}) collective-permute-start(bf16[512,768]{1,0:T(8,128)(2,1)S(1)} %get-tuple-element.299), channel_id=1, source_target_pairs={{0,16},{8,24},{16,0},{24,8},{1,17},{9,25},{17,1},{25,9},{2,18},{10... | collective-permute-start | bytes 2359304 | tf_op jit(solution)/shard_map/ppermute | solution.py:493
  1332.7 55.9 %collective-permute-start.44 = (bf16[512,768]{1,0:T(8,128)(2,1)S(1)}, bf16[512,768]{1,0:T(8,128)(2,1)}, u32[]{:S(2)}, u32[]{:S(2)}) collective-permute-start(bf16[512,768]{1,0:T(8,128)(2,1)S(1)} %get-tuple-element.286.refs_13_), channel_id=1, source_target_pairs={{0,24},{8,0},{16,8},{24,16},{1,25},{9,1},{17,9},{25,17},{2,26},{10... | collective-permute-start | bytes 2359304 | tf_op jit(solution)/shard_map/ppermute | solution.py:493
  1385.7 55.8 %collective-permute-start.39 = (bf16[1,512,768]{2,1,0:T(8,128)(2,1)}, bf16[1,512,768]{2,1,0:T(8,128)(2,1)S(1)}, u32[]{:S(2)}, u32[]{:S(2)}) collective-permute-start(bf16[1,512,768]{2,1,0:T(8,128)(2,1)} %get-tuple-element.291), channel_id=1, source_target_pairs={{0,24},{8,0},{16,8},{24,16},{1,25},{9,1},{17,9},{25,17},{2,26},{10... | collective-permute-start | bytes 2359304 | tf_op jit(solution)/shard_map/ppermute | solution.py:493
  1386.4 79.9 %collective-permute-start.40 = (bf16[1,512,768]{2,1,0:T(8,128)(2,1)}, bf16[1,512,768]{2,1,0:T(8,128)(2,1)S(1)}, u32[]{:S(2)}, u32[]{:S(2)}) collective-permute-start(bf16[1,512,768]{2,1,0:T(8,128)(2,1)} %get-tuple-element.292), channel_id=1, source_target_pairs={{0,16},{8,24},{16,0},{24,8},{1,17},{9,25},{17,1},{25,9},{2,18},{10... | collective-permute-start | bytes 2359304 | tf_op jit(solution)/shard_map/ppermute | solution.py:493
  1388.4 77.9 %collective-permute-start.41 = (bf16[1,512,768]{2,1,0:T(8,128)(2,1)}, bf16[1,512,768]{2,1,0:T(8,128)(2,1)}, u32[]{:S(2)}, u32[]{:S(2)}) collective-permute-start(bf16[1,512,768]{2,1,0:T(8,128)(2,1)} %get-tuple-element.293.refs_15_), channel_id=1, source_target_pairs={{0,8},{8,16},{16,24},{24,0},{1,9},{9,17},{17,25},{25,1},{2,10},{10... | collective-permute-start | bytes 2359304 | tf_op jit(solution)/shard_map/ppermute | solution.py:493
  1467.2 304.9 %reduce-scatter.9.cloned.1.call-start = ((), (), s32[]{:S(2)}) async-start(), calls=%async_computation.12 | async-start | bytes 14155776 | tf_op jit(solution)/shard_map/reduce_scatter | solution.py:1152
  1470.5 31.6 %collective-permute-start.49 = (bf16[96,3200]{1,0:T(8,128)(2,1)S(1)}, bf16[96,3200]{1,0:T(8,128)(2,1)S(1)}, u32[]{:S(2)}, u32[]{:S(2)}) collective-permute-start(bf16[96,3200]{1,0:T(8,128)(2,1)S(1)} %reduce_sum.64), channel_id=1, source_target_pairs={{0,8},{8,0},{16,24},{24,16},{1,9},{9,1},{17,25},{25,17},{2,10},{10... | collective-permute-start | bytes 1843208 | tf_op jit(solution)/shard_map/ppermute | solution.py:1189
  1502.4 24.7 %collective-permute-start.50 = (bf16[96,3200]{1,0:T(8,128)(2,1)S(1)}, bf16[96,3200]{1,0:T(8,128)(2,1)}, u32[]{:S(2)}, u32[]{:S(2)}) collective-permute-start(bf16[96,3200]{1,0:T(8,128)(2,1)S(1)} %add_convert_fusion.13), channel_id=1, source_target_pairs={{0,16},{8,24},{16,0},{24,8},{1,17},{9,25},{17,1},{25,9},{2,18},{10... | collective-permute-start | bytes 1843208 | tf_op jit(solution)/shard_map/ppermute | solution.py:1189
  1561.4 86.9 %collective-permute-start.46 = (bf16[1,512,768]{2,1,0:T(8,128)(2,1)}, bf16[1,512,768]{2,1,0:T(8,128)(2,1)S(1)}, u32[]{:S(2)}, u32[]{:S(2)}) collective-permute-start(bf16[1,512,768]{2,1,0:T(8,128)(2,1)} %get-tuple-element.320), channel_id=1, source_target_pairs={{0,24},{8,0},{16,8},{24,16},{1,25},{9,1},{17,9},{25,17},{2,26},{10... | collective-permute-start | bytes 2359304 | tf_op jit(solution)/shard_map/ppermute | solution.py:493
  1565.0 83.3 %collective-permute-start.47 = (bf16[1,512,768]{2,1,0:T(8,128)(2,1)}, bf16[1,512,768]{2,1,0:T(8,128)(2,1)}, u32[]{:S(2)}, u32[]{:S(2)}) collective-permute-start(bf16[1,512,768]{2,1,0:T(8,128)(2,1)} %get-tuple-element.321), channel_id=1, source_target_pairs={{0,16},{8,24},{16,0},{24,8},{1,17},{9,25},{17,1},{25,9},{2,18},{10... | collective-permute-start | bytes 2359304 | tf_op jit(solution)/shard_map/ppermute | solution.py:493
  1565.0 83.3 %collective-permute-start.48 = (bf16[1,512,768]{2,1,0:T(8,128)(2,1)}, bf16[1,512,768]{2,1,0:T(8,128)(2,1)}, u32[]{:S(2)}, u32[]{:S(2)}) collective-permute-start(bf16[1,512,768]{2,1,0:T(8,128)(2,1)} %get-tuple-element.322), channel_id=1, source_target_pairs={{0,8},{8,16},{16,24},{24,0},{1,9},{9,17},{17,25},{25,1},{2,10},{10... | collective-permute-start | bytes 2359304 | tf_op jit(solution)/shard_map/ppermute | solution.py:493
  1625.2 133.4 %collective-permute-start.45 = (bf16[1024,768]{1,0:T(8,128)(2,1)}, bf16[1024,768]{1,0:T(8,128)(2,1)}, u32[]{:S(2)}, u32[]{:S(2)}) collective-permute-start(bf16[1024,768]{1,0:T(8,128)(2,1)} %add_convert_fusion.1), channel_id=1, source_target_pairs={{4,0},{5,1},{6,2},{7,3},{12,8},{13,9},{14,10},{15,11},{20,16},{21,... | collective-permute-start | bytes 4718600 | tf_op jit(solution)/shard_map/ppermute | solution.py:462
  1732.0 38.4 %collective-permute-start.51 = (bf16[1024,768]{1,0:T(8,128)(2,1)}, bf16[1024,768]{1,0:T(8,128)(2,1)}, u32[]{:S(2)}, u32[]{:S(2)}) collective-permute-start(bf16[1024,768]{1,0:T(8,128)(2,1)} %add_convert_fusion), channel_id=1, source_target_pairs={{4,0},{5,1},{6,2},{7,3},{12,8},{13,9},{14,10},{15,11},{20,16},{21,... | collective-permute-start | bytes 4718600 | tf_op jit(solution)/shard_map/ppermute | solution.py:462
  1793.0 61.2 %all-to-all-start.1 = ((bf16[8,96,3200]{2,1,0:T(8,128)(2,1)}), bf16[8,96,3200]{2,1,0:T(8,128)(2,1)}, u32[]{:S(2)}, u32[]{:S(2)}) async-start(bf16[8,96,3200]{2,1,0:T(8,128)(2,1)} %bitcast.218), calls=%async_computation.5 | async-start | bytes 9830400 | tf_op jit(solution)/shard_map/all_to_all | solution.py:1183
  1874.2 29.4 %collective-permute-start.53 = (bf16[96,3200]{1,0:T(8,128)(2,1)S(1)}, bf16[96,3200]{1,0:T(8,128)(2,1)S(1)}, u32[]{:S(2)}, u32[]{:S(2)}) collective-permute-start(bf16[96,3200]{1,0:T(8,128)(2,1)S(1)} %add_convert_fusion.12), channel_id=1, source_target_pairs={{0,16},{8,24},{16,0},{24,8},{1,17},{9,25},{17,1},{25,9},{2,18},{10... | collective-permute-start | bytes 1843208 | tf_op jit(solution)/shard_map/ppermute | solution.py:1189
  (280 other events, 7240.3 us)
Sparse Core Ops, SparseCore 0:
  15.0 50.6 all-gather.8
  67.6 59.7 all-gather.12
  129.2 49.0 all-gather.16
  180.7 72.1 all-gather.10
  254.7 45.5 all-gather.18
  302.0 72.1 all-gather.14
  915.9 89.4 reduce-scatter.4
  1034.6 64.3 reduce-scatter.6
  1467.3 81.8 reduce-scatter.10
  1566.1 113.6 reduce-scatter.8

commit v3 on v2

--- a/solution.py
+++ b/solution.py
@@ -162,7 +162,7 @@
             pltpu.VMEM((span, LANES), bf16),
             pltpu.VMEM((span, LANES), bf16),
         ],
-        compiler_params=pltpu.CompilerParams(vmem_limit_bytes=40 * MIB),
+        compiler_params=pltpu.CompilerParams(vmem_limit_bytes=60 * MIB),
         cost_estimate=cost(32),
         name="attention_forward",
     )(qkv, qkv, qkv, kv_earlier, kv_earlier, seg_query, seg_key, *after)
@@ -264,7 +264,7 @@
             pltpu.VMEM((span, LANES), f32),
             pltpu.VMEM((span, LANES), f32),
         ],
-        compiler_params=pltpu.CompilerParams(vmem_limit_bytes=48 * MIB),
+        compiler_params=pltpu.CompilerParams(vmem_limit_bytes=60 * MIB),
         cost_estimate=cost(48),
         name="attention_backward",
     )(
@@ -326,7 +326,7 @@
         out_shape=[jax.ShapeDtypeStruct((1, count * part, width), bf16)] * groups
         + [hidden_shape, hidden_shape],
         scratch_shapes=[pltpu.VMEM((rows, width), bf16)],
-        compiler_params=pltpu.CompilerParams(vmem_limit_bytes=48 * MIB),
+        compiler_params=pltpu.CompilerParams(vmem_limit_bytes=60 * MIB),
         cost_estimate=cost(26),
         name="experts_forward",
     )(*blocks, gate_up_w, gate_up_w, down_w, *after)
@@ -449,7 +449,7 @@
             pltpu.VMEM((rows, width), bf16),
         ]
         + ([pltpu.VMEM((rows, width), f32)] if whole else []),
-        compiler_params=pltpu.CompilerParams(vmem_limit_bytes=58 * MIB),
+        compiler_params=pltpu.CompilerParams(vmem_limit_bytes=60 * MIB),
         cost_estimate=cost(75 if whole else 52),
         name="experts_whole" if whole else "experts_backward",
     )(*operands, *after)
@@ -555,7 +555,7 @@
             jax.ShapeDtypeStruct((count, length, LANES), jnp.int32),
             jax.ShapeDtypeStruct((count, 8, length), jnp.int32),
         ],
-        compiler_params=pltpu.CompilerParams(vmem_limit_bytes=32 * MIB),
+        compiler_params=pltpu.CompilerParams(vmem_limit_bytes=60 * MIB),
         cost_estimate=cost(4),
         name="routing",
     )(routes, base)
@@ -605,7 +605,7 @@
         + [ANY_SPEC] * len(after),
         out_specs=[pl.BlockSpec((count, out_width), lambda s: (s, 0))] * groups,
         out_shape=[jax.ShapeDtypeStruct((per_group, out_width), bf16)] * groups,
-        compiler_params=pltpu.CompilerParams(vmem_limit_bytes=32 * MIB),
+        compiler_params=pltpu.CompilerParams(vmem_limit_bytes=60 * MIB),
         cost_estimate=cost(6),
         name="dispatch",
     )(rows, slot_rows, gate_rows, *after)
@@ -691,7 +691,7 @@
             jax.ShapeDtypeStruct((length, LANES), f32),
             jax.ShapeDtypeStruct((8, length), f32),
         ],
-        compiler_params=pltpu.CompilerParams(vmem_limit_bytes=24 * MIB),
+        compiler_params=pltpu.CompilerParams(vmem_limit_bytes=60 * MIB),
         cost_estimate=cost(8),
         name="attention_output",
     )(
@@ -760,7 +760,7 @@
         out_shape=[low, low, low]
         if last
         else [low, low, jax.ShapeDtypeStruct((length, width), f32), low],
-        compiler_params=pltpu.CompilerParams(vmem_limit_bytes=24 * MIB),
+        compiler_params=pltpu.CompilerParams(vmem_limit_bytes=60 * MIB),
         cost_estimate=cost(8),
         name="combine",
     )(*back, columns, mid, scalars, vectors, vectors if last else next_vectors, *after)
@@ -898,7 +898,7 @@
             jax.ShapeDtypeStruct((LANES, LANES), f32),
             jax.ShapeDtypeStruct((8, width), f32),
         ],
-        compiler_params=pltpu.CompilerParams(vmem_limit_bytes=48 * MIB),
+        compiler_params=pltpu.CompilerParams(vmem_limit_bytes=60 * MIB),
         cost_estimate=cost(25),
         name="token_backward",
     )(*operands, *after)
@@ -944,13 +944,13 @@
             jax.ShapeDtypeStruct((length, width), out_type),
             jax.ShapeDtypeStruct((8, width), f32),
         ],
-        compiler_params=pltpu.CompilerParams(vmem_limit_bytes=24 * MIB),
+        compiler_params=pltpu.CompilerParams(vmem_limit_bytes=60 * MIB),
         cost_estimate=cost(6),
         name="finish_backward",
     )(hidden, d_mid, d_attn, vectors, *extra, *after)
 
 
-def fetch_layer(layer, local):
+def fetch_layer(layer, local, first_arrived):
     width = local["w_query"].shape[2]
     shard = local["w_query"].shape[1]
     const_w = jnp.transpose(local["w_const"][layer], (1, 0, 2)).reshape(shard, 4)
@@ -969,6 +969,8 @@
     )
     dense = lax.all_gather(packed, SHARDED, axis=0, tiled=True)
     gate_up = jnp.concatenate([local["w_gate"][layer], local["w_up"][layer]], axis=0)
+    if layer == 0:
+        (gate_up,) = held([gate_up], first_arrived)
     gate_up = lax.all_gather(gate_up, SHARDED, axis=1, tiled=True)
     down = lax.all_gather(local["w_down"][layer], SHARDED, axis=1, tiled=True)
     at = 4 * width + ROUTED + 4
@@ -998,8 +1000,12 @@
     capacity = length // 4
     slots = EXPERTS * capacity
     block_start = lax.axis_index("context") * length
-    hidden_earlier = [earlier_rows(hidden_in[micro, 0], hop_count) for micro in micros]
-    fetched = [fetch_layer(layer, local) for layer in range(layers)]
+    hidden_earlier = []
+    for micro in micros:
+        block = hidden_in[micro, 0]
+        if micro > 0 and hop_count > 0:
+            (block,) = held([block], (hidden_earlier[-1],))
+        hidden_earlier.append(earlier_rows(block, hop_count))
     routes = routes[:, 0]
     columns, slot_rows = routing_slots(routes, groups, capacity)
     blank_gates = jnp.zeros((8, length), f32)
@@ -1007,32 +1013,48 @@
     def normed(hidden, gain):
         return (hidden * inverse_rms(hidden) * gain).astype(bf16)
 
-    segs, early, state = [], [], []
+    last_arrived = []
+
+    def in_turn(blocks, micro):
+        others = held(list(blocks[1:]), tuple(last_arrived[1:]) if micro > 0 else ())
+        last_arrived[:] = exchange(list(blocks[:1]) + others, -1)
+        return list(last_arrived)
+
+    early, sents = [], []
+    for micro in micros:
+        sent = dispatch(
+            out_grad[micro, 0], slot_rows[micro], blank_gates, "plain", slots, groups,
+        )
+        sents.append(sent[-1])
+        early.append(exchange(sent, 1))
+    first_ready = (hidden_earlier[0], *sents)
+    fetched = [fetch_layer(layer, local, first_ready) for layer in range(layers)]
+    segs, state = [], []
     for micro in micros:
         whole = segments[micro, 0]
         padded = jnp.concatenate([jnp.full((WINDOW,), -1, jnp.int32), whole])
         query = lax.dynamic_slice_in_dim(whole, block_start, length, 0)
         key = lax.dynamic_slice_in_dim(padded, block_start, WINDOW + length, 0)
         segs.append((query, key))
-        sent = dispatch(out_grad[micro, 0], slot_rows[micro], blank_gates, "plain", slots, groups)
-        early.append(exchange(sent, 1))
         hidden = hidden_in[micro, 0].astype(f32)
         gain = fetched[0]["vectors"][ATTN_GAIN_ROW : ATTN_GAIN_ROW + 1]
         prior = jnp.pad(prev_logits[micro, 0], ((0, 0), (0, LANES - ROUTED)))
         state.append(
             (
                 hidden, normed(hidden, gain),
-                normed(hidden_earlier[micro].astype(f32), gain), prior,
+                hidden_earlier[micro], prior,
             )
         )
 
     saved = [[None] * layers for _ in micros]
     expert_sums = [None] * layers
-    last_arrived = []
 
     def attention_part(layer, micro, after, after_output):
         weights = fetched[layer]
         hidden, attn_in, attn_earlier, prior = state[micro]
+        if layer == 0:
+            (attn_earlier,) = held([attn_earlier], after)
+            attn_earlier = normed(attn_earlier.astype(f32), weights["vectors"][ATTN_GAIN_ROW][None])
         qkv = dot_on(attn_in, weights["dense"][:, : 3 * width], 1, 0).astype(bf16)
         kv_earlier = dot_on(attn_earlier, weights["dense"][:, width : 3 * width], 1, 0).astype(bf16)
         query, key = segs[micro]
@@ -1048,12 +1070,6 @@
             scalars=scalars, gate_rows=gate_rows, logits=logits, arrived=exchange(sent, 1),
         )
         return sent[-1]
-
-    def send_out(blocks, micro):
-        own, others = blocks[:1], blocks[1:]
-        others = held(others, last_arrived[1:] if micro > 0 else ())
-        last_arrived[:] = exchange(list(own) + others, -1)
-        return list(last_arrived)
 
     def experts_part(layer, micro, after):
         kept = saved[micro][layer]
@@ -1062,11 +1078,11 @@
             out, expert_sums[layer] = experts_backward(
                 kept["arrived"], early[micro], None, gate_up_w, down_w, expert_sums[layer], after
             )
-            arrived = send_out(out, micro)
+            arrived = in_turn(out, 0)
             kept["returned"], kept["back"] = (arrived, 0), (arrived, 1)
         else:
             out, *kept["pre"] = experts_forward(kept["arrived"], gate_up_w, down_w, after)
-            kept["returned"] = (send_out(out, micro), 0)
+            kept["returned"] = (in_turn(out, 0), 0)
         return out[-1]
 
     def combine_part(layer, micro, after):
@@ -1090,7 +1106,7 @@
             kept["arrived"], d_rows, kept["pre"], fetched[layer]["gate_up"],
             fetched[layer]["down"], expert_sums[layer], after,
         )
-        kept["back"] = (send_out(dx, micro), 0)
+        kept["back"] = (in_turn(dx, 0), 0)
         return dx[-1]
 
     def token_back_part(layer, micro, grad, d_prior, after):
@@ -1176,18 +1192,20 @@
             small = small + jnp.concatenate([above, jnp.stack(gains), blank]).T
         return jnp.concatenate([total.astype(bf16) for total in sums[:-1] + [small]], axis=1)
 
-    def reduce_dense(layer):
-        packed = packed_dense(layer)
+    def reduce_dense(layer, packed):
         shards = lax.axis_size("context") * lax.axis_size("dp")
         parts = packed.reshape(shards, width // shards, packed.shape[1])
         parts = lax.all_to_all(parts, SHARDED, split_axis=0, concat_axis=0, tiled=True)
         share = jnp.sum(parts.astype(f32), axis=0)
-        span = 1
-        while span < groups:
-            sent = share.astype(bf16)
-            route = [(i, i ^ span) for i in range(groups)]
-            share = sent.astype(f32) + lax.ppermute(sent, "expert", route).astype(f32)
-            span *= 2
+        if layer > 0:
+            share = lax.psum(share.astype(bf16), "expert").astype(f32)
+        else:
+            span = 1
+            while span < groups:
+                sent = share.astype(bf16)
+                route = [(i, i ^ span) for i in range(groups)]
+                share = sent.astype(f32) + lax.ppermute(sent, "expert", route).astype(f32)
+                span *= 2
         dense_shares[layer] = share
         return (share,)
 
@@ -1226,22 +1244,19 @@
                 before = (hidden_out[-1],)
             d_priors[micro] = token_back_part(layer, micro, grads[micro], d_priors[micro], before)
             before = (saved[micro][layer]["d_att"],)
-            if micro > 0 and layer > 0:
-                before = (send_back(layer, micro - 1, before),)
-            if micro == micro_count - 1:
-                before += dense_wait
             before = (attention_back_part(layer, micro, before),)
+            if layer > 0:
+                before = (send_back(layer, micro, before),)
         if layer > 0:
-            before = (send_back(layer, micro_count - 1, before),)
-            dense_wait = reduce_dense(layer)
+            dense_wait = reduce_dense(layer, packed_dense(layer))
             for micro in micros:
                 if micro < len(experts_ready):
                     before += (experts_ready[micro],)
                 before = (experts_back_part(layer - 1, micro, d_rows[micro], before),)
         else:
             for micro in micros:
-                grads[micro] = finish_back_part(layer, micro, tuple(experts_ready))
-    reduce_dense(0)
+                grads[micro] = finish_back_part(layer, micro, tuple(experts_ready) + dense_wait)
+    reduce_dense(0, packed_dense(0))
     hidden_out = jnp.stack(hidden_out)[:, None]
     hidden_grad = jnp.stack(grads)[:, None]
 

time: 1930 us -> 1840 us (0.953)
  waiting for transfers between devices: 513 us -> 402 us
  Pallas kernels: 848 us -> 919 us
  local copies, waits for them, and re-layouts: 139 us -> 71.2 us
  starting transfers between devices: 197 us -> 219 us
    ppermute x42, waiting for transfers between devices: 335 us -> 216 us  [exchange(): out.append(block if d == 0 else lax.ppermute(block, 'expert', route))]
    unnamed x572 -> x234, local copies, waits for them, and re-layouts: 98.4 us -> 30.4 us
    ppermute x8, waiting for transfers between devices: 63.7 us -> 99.3 us  [passed_along(): return lax.ppermute(block, axis, route)]
    ppermute x42, starting transfers between devices: 131 us -> 161 us  [exchange(): out.append(block if d == 0 else lax.ppermute(block, 'expert', route))]
    ppermute x4 -> x2, waiting for transfers between devices: 60 us -> 33.4 us  [reduce_dense(): share = sent.astype(f32) + lax.ppermute(sent, 'expert', route).astype(f32)]
    ppermute x4 -> x2, starting transfers between devices: 29.5 us -> 4.22 us  [reduce_dense(): share = sent.astype(f32) + lax.ppermute(sent, 'expert', route).astype(f32)]
    pallas_call x4, Pallas kernels: 6.65 us -> 29 us  [finish_backward(): pl.pallas_call(functools.partial(finish_backward_kernel, later is not Non...]
  transfers between devices with their start and end apart: 66 -> 65, of which waited for: 17 -> 12; matrix products, arithmetic and copies ran while one was open for 12% -> 13% of each run, Pallas kernels for 44% -> 49%
where the time goes in v3:
time: 1840 us; the launch traced here: 1830 us
  Pallas kernels  919 us (50%)
  waiting for transfers between devices  402 us (22%)
  starting transfers between devices  219 us (12%)
  matrix products  154 us (8%)
  local copies, waits for them, and re-layouts  71.2 us (4%)
  other arithmetic  51.2 us (3%)
    pallas_call x4, Pallas kernels, experts_backward(): pl.pallas_call(functools.partial(experts_backward_kernel, groups, chunks,...  253 us
    ppermute x42, waiting for transfers between devices, exchange(): out.append(block if d == 0 else lax.ppermute(block, 'expert', route))  216 us
    pallas_call x4, Pallas kernels, attention_backward(): pl.pallas_call(functools.partial(attention_backward_kernel, rows, keys, b...  195 us
    ppermute x42, starting transfers between devices, exchange(): out.append(block if d == 0 else lax.ppermute(block, 'expert', route))  161 us
    dot_general x48, matrix products, dot_on(): lax.dot_general(left_op, right_op, (((left_dim,), (right_dim,)), ((), ())...  154 us
    pallas_call x4, Pallas kernels, attention_forward(): pl.pallas_call(functools.partial(attention_forward_kernel, rows, keys, bl...  133 us
    pallas_call x4, Pallas kernels, token_backward(): pl.pallas_call(functools.partial(token_backward_kernel, d_prior is not No...  107 us
    ppermute x8, waiting for transfers between devices, passed_along(): return lax.ppermute(block, axis, route)  99.3 us
  transfers between devices with their start and end apart: 65, of which 12 were waited for; matrix products, arithmetic and copies ran while one was open for 13% of the time, Pallas kernels for 49%

profile of v3, /device:TPU:2, one launch (start us, length us, event | category | flops | bytes accessed | tf_op | source)
XLA Modules:
  0.0 1832.6 jit_solution(15444143604048830034)
XLA Ops:
  33.5 5.7 routing.1
  45.1 5.8 dispatch.8
  50.9 5.9 dispatch.10
  56.7 21.7 %collective-permute-done.refs_1_ = bf16[1024,768]{1,0:T(8,128)(2,1)S(1)} collective-permute-done((bf16[1024,768]{1,0:T(8,128)(2,1)}, bf16[1024,768]{1,0:T(8,128)(2,1)S(1)}, u32[]{:S(2)}, u32[]{:S(2)}) %collective-permute-start) | collective-permute-done | bytes 1572896 | tf_op jit(solution)/shard_map/ppermute | solution.py:462
  107.0 6.1 convolution_convert_fusion.7.kp_ref.vp_ref
  113.1 7.8 convolution_convert_fusion.3.q_ref.ko_ref.vo_ref
  120.9 33.2 %attention_forward.4 = (bf16[1024,768]{1,0:T(8,128)(2,1)}, f32[16,1024]{1,0:T(8,128)}) custom-call(bf16[1024,2304]{1,0:T(8,128)(2,1)} %convolution_convert_fusion.3.q_ref.ko_ref.vo_ref, bf16[1024,2304]{1,0:T(8,128)(2,1)} %convolution_convert_fusion.3.q_ref.ko_ref.vo_ref, bf16[1024,2304]{1,0:T(8,128)(2,1)} %convolution_convert_fusion.3.q_ref.ko_ref.vo_ref, ...), custom_call_target="tpu_custom_call" | custom-call | flops 29440000000 | bytes 1 | tf_op jit(solution)/shard_map/attention_forward/pallas_call | solution.py:141
  154.1 10.3 attention_output.4
  167.4 33.4 %collective-permute-done.2.rest_1_.refs_6_ = bf16[512,768]{1,0:T(8,128)(2,1)} collective-permute-done((bf16[512,768]{1,0:T(8,128)(2,1)}, bf16[512,768]{1,0:T(8,128)(2,1)}, u32[]{:S(2)}, u32[]{:S(2)}) %collective-permute-start.2) | collective-permute-done | bytes 786464 | tf_op jit(solution)/shard_map/ppermute | solution.py:493
  200.8 5.8 dispatch.9
  211.8 6.7 convolution_convert_fusion.6.kp_ref.vp_ref
  218.6 5.7 convolution_convert_fusion.2.q_ref.ko_ref.vo_ref
  224.3 33.2 %attention_forward.5 = (bf16[1024,768]{1,0:T(8,128)(2,1)}, f32[16,1024]{1,0:T(8,128)}) custom-call(bf16[1024,2304]{1,0:T(8,128)(2,1)} %convolution_convert_fusion.2.q_ref.ko_ref.vo_ref, bf16[1024,2304]{1,0:T(8,128)(2,1)} %convolution_convert_fusion.2.q_ref.ko_ref.vo_ref, bf16[1024,2304]{1,0:T(8,128)(2,1)} %convolution_convert_fusion.2.q_ref.ko_ref.vo_ref, ...), custom_call_target="tpu_custom_call" | custom-call | flops 29440000000 | bytes 1 | tf_op jit(solution)/shard_map/attention_forward/pallas_call | solution.py:141
  257.6 10.4 attention_output.5
  268.9 5.8 dispatch.11
  281.7 38.8 %collective-permute-done.5.refs_2_ = bf16[512,768]{1,0:T(8,128)(2,1)} collective-permute-done((bf16[512,768]{1,0:T(8,128)(2,1)}, bf16[512,768]{1,0:T(8,128)(2,1)}, u32[]{:S(2)}, u32[]{:S(2)}) %collective-permute-start.5) | collective-permute-done | bytes 786464 | tf_op jit(solution)/shard_map/ppermute | solution.py:493
  321.4 28.3 %experts_forward.2 = (bf16[1,512,768]{2,1,0:T(8,128)(2,1)}, bf16[1,512,768]{2,1,0:T(8,128)(2,1)}, bf16[1,512,768]{2,1,0:T(8,128)(2,1)}, bf16[1,512,768]{2,1,0:T(...) custom-call(bf16[512,768]{1,0:T(8,128)(2,1)} %get-tuple-element.182.refs_0_, ...), custom_call_target="tpu_custom_call" | custom-call | flops 23920001024 | bytes 1 | tf_op jit(solution)/shard_map/experts_forward/pallas_call | solution.py:314
  355.1 28.4 %experts_forward.3 = (bf16[1,512,768]{2,1,0:T(8,128)(2,1)}, bf16[1,512,768]{2,1,0:T(8,128)(2,1)}, bf16[1,512,768]{2,1,0:T(8,128)(2,1)}, bf16[1,512,768]{2,1,0:T(...) custom-call(bf16[512,768]{1,0:T(8,128)(2,1)} %get-tuple-element.200.refs_0_, ...), custom_call_target="tpu_custom_call" | custom-call | flops 23920001024 | bytes 1 | tf_op jit(solution)/shard_map/experts_forward/pallas_call | solution.py:314
  388.9 32.9 %collective-permute-done.12.refs_2_ = bf16[1,512,768]{2,1,0:T(8,128)(2,1)} collective-permute-done((bf16[1,512,768]{2,1,0:T(8,128)(2,1)}, bf16[1,512,768]{2,1,0:T(8,128)(2,1)}, u32[]{:S(2)}, u32[]{:S(2)}) %collective-permute-start.12) | collective-permute-done | bytes 786464 | tf_op jit(solution)/shard_map/ppermute | solution.py:493
  421.8 11.8 combine.4
  433.6 12.9 collective-permute-start.17
  446.5 42.0 %collective-permute-done.19.refs_2_ = bf16[1,512,768]{2,1,0:T(8,128)(2,1)S(1)} collective-permute-done((bf16[1,512,768]{2,1,0:T(8,128)(2,1)}, bf16[1,512,768]{2,1,0:T(8,128)(2,1)S(1)}, u32[]{:S(2)}, u32[]{:S(2)}) %collective-permute-start.19) | collective-permute-done | bytes 786464 | tf_op jit(solution)/shard_map/ppermute | solution.py:493
  489.7 11.9 combine.5
  501.7 12.6 collective-permute-start.24
  514.3 7.7 convolution_convert_fusion.1.q_ref.ko_ref.vo_ref
  532.9 33.2 %attention_forward.6 = (bf16[1024,768]{1,0:T(8,128)(2,1)}, f32[16,1024]{1,0:T(8,128)}) custom-call(bf16[1024,2304]{1,0:T(8,128)(2,1)} %convolution_convert_fusion.1.q_ref.ko_ref.vo_ref, bf16[1024,2304]{1,0:T(8,128)(2,1)} %convolution_convert_fusion.1.q_ref.ko_ref.vo_ref, bf16[1024,2304]{1,0:T(8,128)(2,1)} %convolution_convert_fusion.1.q_ref.ko_ref.vo_ref, ...), custom_call_target="tpu_custom_call" | custom-call | flops 29440000000 | bytes 1 | tf_op jit(solution)/shard_map/attention_forward/pallas_call | solution.py:141
  566.1 10.3 attention_output.6
  576.5 7.1 dispatch.12
  587.3 6.2 convolution_convert_fusion.4.kp_ref.vp_ref
  593.5 33.2 %attention_forward.7 = (bf16[1024,768]{1,0:T(8,128)(2,1)}, f32[16,1024]{1,0:T(8,128)}) custom-call(bf16[1024,2304]{1,0:T(8,128)(2,1)} %convolution_convert_fusion.q_ref.ko_ref.vo_ref, bf16[1024,2304]{1,0:T(8,128)(2,1)} %convolution_convert_fusion.q_ref.ko_ref.vo_ref, bf16[1024,2304]{1,0:T(8,128)(2,1)} %convolution_convert_fusion.q_ref.ko_ref.vo_ref, ...), custom_call_target="tpu_custom_call" | custom-call | flops 29440000000 | bytes 1 | tf_op jit(solution)/shard_map/attention_forward/pallas_call | solution.py:141
  626.7 10.4 attention_output.7
  637.1 6.8 dispatch.13
  649.8 74.0 %experts_whole.2 = (bf16[2,512,768]{2,1,0:T(8,128)(2,1)}, bf16[2,512,768]{2,1,0:T(8,128)(2,1)}, bf16[2,512,768]{2,1,0:T(8,128)(2,1)}, bf16[2,512,768]{2,1,0:T(8,...) custom-call(bf16[512,896]{1,0:T(8,128)(2,1)} %get-tuple-element.216.refs_0_.refs_11_, ...), custom_call_target="tpu_custom_call" | custom-call | flops 69000003584 | bytes 1 | tf_op jit(solution)/shard_map/experts_whole/pallas_call | solution.py:435
  723.8 20.5 %collective-permute-start.25 = (bf16[2,512,768]{2,1,0:T(8,128)(2,1)}, bf16[2,512,768]{2,1,0:T(8,128)(2,1)S(1)}, u32[]{:S(2)}, u32[]{:S(2)}) collective-permute-start(bf16[2,512,768]{2,1,0:T(8,128)(2,1)} %get-tuple-element.228), channel_id=1, source_target_pairs={{0,24},{8,0},{16,8},{24,16},{1,25},{9,1},{17,9},{25,17},{2,26},{10... | collective-permute-start | bytes 4718600 | tf_op jit(solution)/shard_map/ppermute | solution.py:493
  744.3 37.9 %collective-permute-start.26 = (bf16[2,512,768]{2,1,0:T(8,128)(2,1)}, bf16[2,512,768]{2,1,0:T(8,128)(2,1)S(1)}, u32[]{:S(2)}, u32[]{:S(2)}) collective-permute-start(bf16[2,512,768]{2,1,0:T(8,128)(2,1)} %get-tuple-element.229), channel_id=1, source_target_pairs={{0,16},{8,24},{16,0},{24,8},{1,17},{9,25},{17,1},{25,9},{2,18},{10... | collective-permute-start | bytes 4718600 | tf_op jit(solution)/shard_map/ppermute | solution.py:493
  782.2 74.5 %experts_whole.3 = (bf16[2,512,768]{2,1,0:T(8,128)(2,1)}, bf16[2,512,768]{2,1,0:T(8,128)(2,1)}, bf16[2,512,768]{2,1,0:T(8,128)(2,1)}, bf16[2,512,768]{2,1,0:T(8,...) custom-call(bf16[512,896]{1,0:T(8,128)(2,1)} %get-tuple-element.233.refs_0_.refs_11_, ...), custom_call_target="tpu_custom_call" | custom-call | flops 69000003584 | bytes 1 | tf_op jit(solution)/shard_map/experts_whole/pallas_call | solution.py:435
  856.8 59.1 %collective-permute-done.26.refs_2_.refs_3_ = bf16[2,512,768]{2,1,0:T(8,128)(2,1)S(1)} collective-permute-done((bf16[2,512,768]{2,1,0:T(8,128)(2,1)}, bf16[2,512,768]{2,1,0:T(8,128)(2,1)S(1)}, u32[]{:S(2)}, u32[]{:S(2)}) %collective-permute-start.26) | collective-permute-done | bytes 1572896 | tf_op jit(solution)/shard_map/ppermute | solution.py:493
  922.5 12.6 combine.6
  935.1 26.1 %token_backward.4 = (f32[1024,768]{1,0:T(8,128)}, bf16[1024,768]{1,0:T(8,128)(2,1)}, f32[1024,128]{1,0:T(8,128)}, f32[768,768]{1,0:T(8,128)}, f32[768,128]{1,0:T...) custom-call(bf16[2,512,768]{2,1,0:T(8,128)(2,1)} %get-tuple-element.227.refs_0_, bf16[2,512,768]{2,1,0:T(8,128)(2,1)} %copy-done.28, ...), custom_call_target="tpu_custom_call" | custom-call | flops 23000000512 | bytes 1 | tf_op jit(solution)/shard_map/token_backward/pallas_call | solution.py:884
  961.3 48.6 %attention_backward.4 = (bf16[1024,768]{1,0:T(8,128)(2,1)}, bf16[2048,768]{1,0:T(8,128)(2,1)}, bf16[2048,768]{1,0:T(8,128)(2,1)}) custom-call(bf16[1024,2304]{1,0:T(8,128)(2,1)} %convolution_convert_fusion.1.q_ref.ko_ref.vo_ref, bf16[1024,2304]{1,0:T(8,128)(2,1)} %convolution_convert_fusion.1.q_ref.ko_ref.vo_ref, ...), custom_call_target="tpu_custom_call" | custom-call | flops 44160000000 | bytes 1 | tf_op jit(solution)/shard_map/attention_backward/pallas_call | solution.py:238
  1043.3 11.3 collective-permute-done.34
  1057.9 7.7 finish_backward.4
  1065.6 7.1 dispatch.14
  1072.7 11.1 combine.7
  1083.9 26.1 %token_backward.5 = (f32[1024,768]{1,0:T(8,128)}, bf16[1024,768]{1,0:T(8,128)(2,1)}, f32[1024,128]{1,0:T(8,128)}, f32[768,768]{1,0:T(8,128)}, f32[768,128]{1,0:T...) custom-call(bf16[2,512,768]{2,1,0:T(8,128)(2,1)} %get-tuple-element.241.refs_0_, ...), custom_call_target="tpu_custom_call" | custom-call | flops 23000000512 | bytes 1 | tf_op jit(solution)/shard_map/token_backward/pallas_call | solution.py:884
  1110.0 49.0 %attention_backward.5 = (bf16[1024,768]{1,0:T(8,128)(2,1)}, bf16[2048,768]{1,0:T(8,128)(2,1)}, bf16[2048,768]{1,0:T(8,128)(2,1)}) custom-call(bf16[1024,2304]{1,0:T(8,128)(2,1)} %convolution_convert_fusion.q_ref.ko_ref.vo_ref, bf16[1024,2304]{1,0:T(8,128)(2,1)} %convolution_convert_fusion.q_ref.ko_ref.vo_ref, ...), custom_call_target="tpu_custom_call" | custom-call | flops 44160000000 | bytes 1 | tf_op jit(solution)/shard_map/attention_backward/pallas_call | solution.py:238
  1204.5 66.2 %collective-permute-done.38 = bf16[1024,768]{1,0:T(8,128)(2,1)S(1)} collective-permute-done((bf16[1024,768]{1,0:T(8,128)(2,1)S(1)}, bf16[1024,768]{1,0:T(8,128)(2,1)S(1)}, u32[]{:S(2)}, u32[]{:S(2)}) %collective-permute-start.38) | collective-permute-done | bytes 1572896 | tf_op jit(solution)/shard_map/ppermute | solution.py:462
  1272.5 7.3 finish_backward.5
  1279.8 7.0 dispatch.15
  1298.0 52.1 %experts_backward.2 = (bf16[1,512,768]{2,1,0:T(8,128)(2,1)}, bf16[1,512,768]{2,1,0:T(8,128)(2,1)}, bf16[1,512,768]{2,1,0:T(8,128)(2,1)}, bf16[1,512,768]{2,1,0:T...) custom-call(bf16[512,768]{1,0:T(8,128)(2,1)} %get-tuple-element.182.refs_0_, ...), custom_call_target="tpu_custom_call" | custom-call | flops 47840002048 | bytes 1 | tf_op jit(solution)/shard_map/experts_backward/pallas_call | solution.py:435
  1350.6 33.6 %collective-permute-start.41 = (bf16[1,512,768]{2,1,0:T(8,128)(2,1)}, bf16[1,512,768]{2,1,0:T(8,128)(2,1)S(1)}, u32[]{:S(2)}, u32[]{:S(2)}) collective-permute-start(bf16[1,512,768]{2,1,0:T(8,128)(2,1)} %get-tuple-element.278.refs_15_), channel_id=1, source_target_pairs={{0,8},{8,16},{16,24},{24,0},{1,9},{9,17},{17,25},{25,1},{2,10},{10... | collective-permute-start | bytes 2359304 | tf_op jit(solution)/shard_map/ppermute | solution.py:493
  1384.3 52.8 %experts_backward.3 = (bf16[1,512,768]{2,1,0:T(8,128)(2,1)}, bf16[1,512,768]{2,1,0:T(8,128)(2,1)}, bf16[1,512,768]{2,1,0:T(8,128)(2,1)}, bf16[1,512,768]{2,1,0:T...) custom-call(bf16[512,768]{1,0:T(8,128)(2,1)} %get-tuple-element.200.refs_0_, ...), custom_call_target="tpu_custom_call" | custom-call | flops 47840002048 | bytes 1 | tf_op jit(solution)/shard_map/experts_backward/pallas_call | solution.py:435
  1437.1 9.2 collective-permute-done.40.refs_2_.refs_3_
  1453.8 19.8 %collective-permute-start.46 = (bf16[1,512,768]{2,1,0:T(8,128)(2,1)S(1)}, bf16[1,512,768]{2,1,0:T(8,128)(2,1)S(1)}, u32[]{:S(2)}, u32[]{:S(2)}) collective-permute-start(bf16[1,512,768]{2,1,0:T(8,128)(2,1)S(1)} %copy-done.86), channel_id=1, source_target_pairs={{0,24},{8,0},{16,8},{24,16},{1,25},{9,1},{17,9},{25,17},{2,26},{10... | collective-permute-start | bytes 2359304 | tf_op jit(solution)/shard_map/ppermute | solution.py:493
  1474.5 27.6 %token_backward.6 = (f32[1024,768]{1,0:T(8,128)}, bf16[1024,768]{1,0:T(8,128)(2,1)}, f32[1024,128]{1,0:T(8,128)}, f32[768,768]{1,0:T(8,128)}, f32[768,128]{1,0:T...) custom-call(bf16[1,512,768]{2,1,0:T(8,128)(2,1)} %get-tuple-element.275.refs_0_, bf16[1,512,768]{2,1,0:T(8,128)(2,1)} %copy-done.49, ...), custom_call_target="tpu_custom_call" | custom-call | flops 23000000512 | bytes 1 | tf_op jit(solution)/shard_map/token_backward/pallas_call | solution.py:884
  1502.1 48.3 %attention_backward.6 = (bf16[1024,768]{1,0:T(8,128)(2,1)}, bf16[2048,768]{1,0:T(8,128)(2,1)}, bf16[2048,768]{1,0:T(8,128)(2,1)}) custom-call(bf16[1024,2304]{1,0:T(8,128)(2,1)} %convolution_convert_fusion.3.q_ref.ko_ref.vo_ref, bf16[1024,2304]{1,0:T(8,128)(2,1)} %convolution_convert_fusion.3.q_ref.ko_ref.vo_ref, ...), custom_call_target="tpu_custom_call" | custom-call | flops 44160000000 | bytes 1 | tf_op jit(solution)/shard_map/attention_backward/pallas_call | solution.py:238
  1551.3 26.7 %token_backward.7 = (f32[1024,768]{1,0:T(8,128)}, bf16[1024,768]{1,0:T(8,128)(2,1)}, f32[1024,128]{1,0:T(8,128)}, f32[768,768]{1,0:T(8,128)}, f32[768,128]{1,0:T...) custom-call(bf16[1,512,768]{2,1,0:T(8,128)(2,1)} %get-tuple-element.308.refs_0_, bf16[1,512,768]{2,1,0:T(8,128)(2,1)} %copy-done.89, ...), custom_call_target="tpu_custom_call" | custom-call | flops 23000000512 | bytes 1 | tf_op jit(solution)/shard_map/token_backward/pallas_call | solution.py:884
  1588.0 48.6 %attention_backward.7 = (bf16[1024,768]{1,0:T(8,128)(2,1)}, bf16[2048,768]{1,0:T(8,128)(2,1)}, bf16[2048,768]{1,0:T(8,128)(2,1)}) custom-call(bf16[1024,2304]{1,0:T(8,128)(2,1)} %convolution_convert_fusion.2.q_ref.ko_ref.vo_ref, bf16[1024,2304]{1,0:T(8,128)(2,1)} %convolution_convert_fusion.2.q_ref.ko_ref.vo_ref, ...), custom_call_target="tpu_custom_call" | custom-call | flops 44160000000 | bytes 1 | tf_op jit(solution)/shard_map/attention_backward/pallas_call | solution.py:238
  1689.3 6.9 finish_backward.6
  1696.3 7.0 finish_backward.7
  1706.9 8.2 all-to-all-start.1
  1717.1 53.4 %all-to-all-done.1 = bf16[8,96,3200]{2,1,0:T(8,128)(2,1)} async-done(((bf16[8,96,3200]{2,1,0:T(8,128)(2,1)}), bf16[8,96,3200]{2,1,0:T(8,128)(2,1)}, u32[]{:S(2)}, u32[]{:S(2)}) %all-to-all-start.1) | async-done | bytes 4915232 | tf_op jit(solution)/shard_map/all_to_all | solution.py:1198
  1781.8 8.7 collective-permute-done.50
  1795.3 24.7 %collective-permute-done.51 = bf16[96,3200]{1,0:T(8,128)(2,1)S(1)} collective-permute-done((bf16[96,3200]{1,0:T(8,128)(2,1)S(1)}, bf16[96,3200]{1,0:T(8,128)(2,1)S(1)}, u32[]{:S(2)}, u32[]{:S(2)}) %collective-permute-start.51) | collective-permute-done | bytes 614432 | tf_op jit(solution)/shard_map/ppermute | solution.py:1207
  (501 shorter events, 310.5 us)
Async XLA Ops:
  7.2 98.6 %all-gather.9.cloned.1.call-start = ((), (), s32[]{:S(2)}) async-start(), calls=%async_computation.6 | async-start | bytes 5529600 | tf_op jit(solution)/shard_map/all_gather | solution.py:970
  14.9 262.7 %all-gather.13.cloned.1.call-start = ((), (), s32[]{:S(2)}) async-start(), calls=%async_computation.8 | async-start | bytes 5529600 | tf_op jit(solution)/shard_map/all_gather | solution.py:970
  16.6 303.9 %all-gather.17.cloned.1.call-start = ((), (), s32[]{:S(2)}) async-start(), calls=%async_computation.15 | async-start | bytes 7077888 | tf_op jit(solution)/shard_map/all_gather | solution.py:975
  19.5 301.1 %all-gather.11.cloned.1.call-start = ((), (), s32[]{:S(2)}) async-start(), calls=%async_computation.7 | async-start | bytes 14155776 | tf_op jit(solution)/shard_map/all_gather | solution.py:974
  23.5 55.0 %collective-permute-start = (bf16[1024,768]{1,0:T(8,128)(2,1)}, bf16[1024,768]{1,0:T(8,128)(2,1)S(1)}, u32[]{:S(2)}, u32[]{:S(2)}) collective-permute-start(bf16[1024,768]{1,0:T(8,128)(2,1)} %get-tuple-element.408), channel_id=1, source_target_pairs={{0,4},{1,5},{2,6},{3,7},{8,12},{9,13},{10,14},{11,15},{16,20},{17,... | collective-permute-start | bytes 4718600 | tf_op jit(solution)/shard_map/ppermute | solution.py:462
  79.7 569.1 %all-gather.19.cloned.1.call-start = ((), (), s32[]{:S(2)}) async-start(), calls=%async_computation.16 | async-start | bytes 7077888 | tf_op jit(solution)/shard_map/all_gather | solution.py:975
  80.3 568.5 %all-gather.15.cloned.1.call-start = ((), (), s32[]{:S(2)}) async-start(), calls=%async_computation.9 | async-start | bytes 14155776 | tf_op jit(solution)/shard_map/all_gather | solution.py:974
  80.4 84.1 %collective-permute-start.3 = (bf16[512,768]{1,0:T(8,128)(2,1)}, bf16[512,768]{1,0:T(8,128)(2,1)}, u32[]{:S(2)}, u32[]{:S(2)}) collective-permute-start(bf16[512,768]{1,0:T(8,128)(2,1)} %get-tuple-element.181.refs_2_), channel_id=1, source_target_pairs={{0,24},{8,0},{16,8},{24,16},{1,25},{9,1},{17,9},{25,17},{2,26},{10... | collective-permute-start | bytes 2359304 | tf_op jit(solution)/shard_map/ppermute | solution.py:493
  83.8 173.8 %collective-permute-start.10 = (bf16[512,768]{1,0:T(8,128)(2,1)}, bf16[512,768]{1,0:T(8,128)(2,1)}, u32[]{:S(2)}, u32[]{:S(2)}) collective-permute-start(bf16[512,768]{1,0:T(8,128)(2,1)} %get-tuple-element.186.refs_3_), channel_id=1, source_target_pairs={{0,24},{8,0},{16,8},{24,16},{1,25},{9,1},{17,9},{25,17},{2,26},{10... | collective-permute-start | bytes 2359304 | tf_op jit(solution)/shard_map/ppermute | solution.py:493
  84.3 83.0 %collective-permute-start.1 = (bf16[512,768]{1,0:T(8,128)(2,1)}, bf16[512,768]{1,0:T(8,128)(2,1)}, u32[]{:S(2)}, u32[]{:S(2)}) collective-permute-start(bf16[512,768]{1,0:T(8,128)(2,1)} %get-tuple-element.179), channel_id=1, source_target_pairs={{0,8},{8,16},{16,24},{24,0},{1,9},{9,17},{17,25},{25,1},{2,10},{10... | collective-permute-start | bytes 2359304 | tf_op jit(solution)/shard_map/ppermute | solution.py:493
  85.8 115.0 %collective-permute-start.2 = (bf16[512,768]{1,0:T(8,128)(2,1)}, bf16[512,768]{1,0:T(8,128)(2,1)}, u32[]{:S(2)}, u32[]{:S(2)}) collective-permute-start(bf16[512,768]{1,0:T(8,128)(2,1)} %get-tuple-element.180), channel_id=1, source_target_pairs={{0,16},{8,24},{16,0},{24,8},{1,17},{9,25},{17,1},{25,9},{2,18},{10... | collective-permute-start | bytes 2359304 | tf_op jit(solution)/shard_map/ppermute | solution.py:493
  88.5 1208.6 %reduce-scatter.5.cloned.1.call-start = ((), (), s32[]{:S(2)}) async-start(), calls=%async_computation.10 | async-start | bytes 14155776 | tf_op jit(solution)/shard_map/reduce_scatter | solution.py:1168
  100.8 106.0 %collective-permute-start.7 = (bf16[1024,768]{1,0:T(8,128)(2,1)}, bf16[1024,768]{1,0:T(8,128)(2,1)S(1)}, u32[]{:S(2)}, u32[]{:S(2)}) collective-permute-start(bf16[1024,768]{1,0:T(8,128)(2,1)} %held.6), channel_id=1, source_target_pairs={{0,4},{1,5},{2,6},{3,7},{8,12},{9,13},{10,14},{11,15},{16,20},{17,... | collective-permute-start | bytes 4718600 | tf_op jit(solution)/shard_map/ppermute | solution.py:462
  164.5 103.5 %collective-permute-start.8 = (bf16[512,768]{1,0:T(8,128)(2,1)}, bf16[512,768]{1,0:T(8,128)(2,1)S(1)}, u32[]{:S(2)}, u32[]{:S(2)}) collective-permute-start(bf16[512,768]{1,0:T(8,128)(2,1)} %get-tuple-element.190), channel_id=1, source_target_pairs={{0,8},{8,16},{16,24},{24,0},{1,9},{9,17},{17,25},{25,1},{2,10},{10... | collective-permute-start | bytes 2359304 | tf_op jit(solution)/shard_map/ppermute | solution.py:493
  167.3 100.7 %collective-permute-start.9 = (bf16[512,768]{1,0:T(8,128)(2,1)}, bf16[512,768]{1,0:T(8,128)(2,1)}, u32[]{:S(2)}, u32[]{:S(2)}) collective-permute-start(bf16[512,768]{1,0:T(8,128)(2,1)} %get-tuple-element.191), channel_id=1, source_target_pairs={{0,16},{8,24},{16,0},{24,8},{1,17},{9,25},{17,1},{25,9},{2,18},{10... | collective-permute-start | bytes 2359304 | tf_op jit(solution)/shard_map/ppermute | solution.py:493
  206.6 113.9 %collective-permute-start.6 = (bf16[512,768]{1,0:T(8,128)(2,1)}, bf16[512,768]{1,0:T(8,128)(2,1)S(1)}, u32[]{:S(2)}, u32[]{:S(2)}) collective-permute-start(bf16[512,768]{1,0:T(8,128)(2,1)} %get-tuple-element.185.refs_1_.rest_0_), channel_id=1, source_target_pairs={{0,24},{8,0},{16,8},{24,16},{1,25},{9,1},{17,9},{25,17},{2,26},{10... | collective-permute-start | bytes 2359304 | tf_op jit(solution)/shard_map/ppermute | solution.py:493
  209.8 69.0 %collective-permute-start.4 = (bf16[512,768]{1,0:T(8,128)(2,1)}, bf16[512,768]{1,0:T(8,128)(2,1)}, u32[]{:S(2)}, u32[]{:S(2)}) collective-permute-start(bf16[512,768]{1,0:T(8,128)(2,1)} %get-tuple-element.183), channel_id=1, source_target_pairs={{0,8},{8,16},{16,24},{24,0},{1,9},{9,17},{17,25},{25,1},{2,10},{10... | collective-permute-start | bytes 2359304 | tf_op jit(solution)/shard_map/ppermute | solution.py:493
  257.6 63.0 %collective-permute-start.5 = (bf16[512,768]{1,0:T(8,128)(2,1)}, bf16[512,768]{1,0:T(8,128)(2,1)}, u32[]{:S(2)}, u32[]{:S(2)}) collective-permute-start(bf16[512,768]{1,0:T(8,128)(2,1)} %get-tuple-element.184), channel_id=1, source_target_pairs={{0,16},{8,24},{16,0},{24,8},{1,17},{9,25},{17,1},{25,9},{2,18},{10... | collective-permute-start | bytes 2359304 | tf_op jit(solution)/shard_map/ppermute | solution.py:493
  274.7 78.9 %collective-permute-start.14 = (bf16[512,768]{1,0:T(8,128)(2,1)}, bf16[512,768]{1,0:T(8,128)(2,1)S(1)}, u32[]{:S(2)}, u32[]{:S(2)}) collective-permute-start(bf16[512,768]{1,0:T(8,128)(2,1)} %get-tuple-element.201), channel_id=1, source_target_pairs={{0,8},{8,16},{16,24},{24,0},{1,9},{9,17},{17,25},{25,1},{2,10},{10... | collective-permute-start | bytes 2359304 | tf_op jit(solution)/shard_map/ppermute | solution.py:493
  277.0 77.3 %collective-permute-start.15 = (bf16[512,768]{1,0:T(8,128)(2,1)}, bf16[512,768]{1,0:T(8,128)(2,1)S(1)}, u32[]{:S(2)}, u32[]{:S(2)}) collective-permute-start(bf16[512,768]{1,0:T(8,128)(2,1)} %get-tuple-element.202), channel_id=1, source_target_pairs={{0,16},{8,24},{16,0},{24,8},{1,17},{9,25},{17,1},{25,9},{2,18},{10... | collective-permute-start | bytes 2359304 | tf_op jit(solution)/shard_map/ppermute | solution.py:493
  278.8 75.5 %collective-permute-start.16 = (bf16[512,768]{1,0:T(8,128)(2,1)}, bf16[512,768]{1,0:T(8,128)(2,1)}, u32[]{:S(2)}, u32[]{:S(2)}) collective-permute-start(bf16[512,768]{1,0:T(8,128)(2,1)} %get-tuple-element.192.refs_7_), channel_id=1, source_target_pairs={{0,24},{8,0},{16,8},{24,16},{1,25},{9,1},{17,9},{25,17},{2,26},{10... | collective-permute-start | bytes 2359304 | tf_op jit(solution)/shard_map/ppermute | solution.py:493
  349.8 38.2 %collective-permute-start.11 = (bf16[1,512,768]{2,1,0:T(8,128)(2,1)}, bf16[1,512,768]{2,1,0:T(8,128)(2,1)S(1)}, u32[]{:S(2)}, u32[]{:S(2)}) collective-permute-start(bf16[1,512,768]{2,1,0:T(8,128)(2,1)} %get-tuple-element.194), channel_id=1, source_target_pairs={{0,24},{8,0},{16,8},{24,16},{1,25},{9,1},{17,9},{25,17},{2,26},{10... | collective-permute-start | bytes 2359304 | tf_op jit(solution)/shard_map/ppermute | solution.py:493
  353.6 68.2 %collective-permute-start.12 = (bf16[1,512,768]{2,1,0:T(8,128)(2,1)}, bf16[1,512,768]{2,1,0:T(8,128)(2,1)}, u32[]{:S(2)}, u32[]{:S(2)}) collective-permute-start(bf16[1,512,768]{2,1,0:T(8,128)(2,1)} %get-tuple-element.195), channel_id=1, source_target_pairs={{0,16},{8,24},{16,0},{24,8},{1,17},{9,25},{17,1},{25,9},{2,18},{10... | collective-permute-start | bytes 2359304 | tf_op jit(solution)/shard_map/ppermute | solution.py:493
  353.6 68.2 %collective-permute-start.13 = (bf16[1,512,768]{2,1,0:T(8,128)(2,1)}, bf16[1,512,768]{2,1,0:T(8,128)(2,1)}, u32[]{:S(2)}, u32[]{:S(2)}) collective-permute-start(bf16[1,512,768]{2,1,0:T(8,128)(2,1)} %get-tuple-element.196.refs_7_), channel_id=1, source_target_pairs={{0,8},{8,16},{16,24},{24,0},{1,9},{9,17},{17,25},{25,1},{2,10},{10... | collective-permute-start | bytes 2359304 | tf_op jit(solution)/shard_map/ppermute | solution.py:493
  383.5 63.0 %collective-permute-start.18 = (bf16[1,512,768]{2,1,0:T(8,128)(2,1)}, bf16[1,512,768]{2,1,0:T(8,128)(2,1)S(1)}, u32[]{:S(2)}, u32[]{:S(2)}) collective-permute-start(bf16[1,512,768]{2,1,0:T(8,128)(2,1)} %get-tuple-element.207), channel_id=1, source_target_pairs={{0,24},{8,0},{16,8},{24,16},{1,25},{9,1},{17,9},{25,17},{2,26},{10... | collective-permute-start | bytes 2359304 | tf_op jit(solution)/shard_map/ppermute | solution.py:493
  387.2 101.3 %collective-permute-start.19 = (bf16[1,512,768]{2,1,0:T(8,128)(2,1)}, bf16[1,512,768]{2,1,0:T(8,128)(2,1)S(1)}, u32[]{:S(2)}, u32[]{:S(2)}) collective-permute-start(bf16[1,512,768]{2,1,0:T(8,128)(2,1)} %get-tuple-element.208), channel_id=1, source_target_pairs={{0,16},{8,24},{16,0},{24,8},{1,17},{9,25},{17,1},{25,9},{2,18},{10... | collective-permute-start | bytes 2359304 | tf_op jit(solution)/shard_map/ppermute | solution.py:493
  388.0 100.6 %collective-permute-start.20 = (bf16[1,512,768]{2,1,0:T(8,128)(2,1)}, bf16[1,512,768]{2,1,0:T(8,128)(2,1)S(1)}, u32[]{:S(2)}, u32[]{:S(2)}) collective-permute-start(bf16[1,512,768]{2,1,0:T(8,128)(2,1)} %get-tuple-element.203.refs_9_), channel_id=1, source_target_pairs={{0,8},{8,16},{16,24},{24,0},{1,9},{9,17},{17,25},{25,1},{2,10},{10... | collective-permute-start | bytes 2359304 | tf_op jit(solution)/shard_map/ppermute | solution.py:493
  433.6 93.9 %collective-permute-start.17 = (bf16[1024,768]{1,0:T(8,128)(2,1)}, bf16[1024,768]{1,0:T(8,128)(2,1)}, u32[]{:S(2)}, u32[]{:S(2)}) collective-permute-start(bf16[1024,768]{1,0:T(8,128)(2,1)} %get-tuple-element.205), channel_id=1, source_target_pairs={{0,4},{1,5},{2,6},{3,7},{8,12},{9,13},{10,14},{11,15},{16,20},{17,... | collective-permute-start | bytes 4718600 | tf_op jit(solution)/shard_map/ppermute | solution.py:462
  501.7 85.6 %collective-permute-start.24 = (bf16[1024,768]{1,0:T(8,128)(2,1)}, bf16[1024,768]{1,0:T(8,128)(2,1)S(1)}, u32[]{:S(2)}, u32[]{:S(2)}) collective-permute-start(bf16[1024,768]{1,0:T(8,128)(2,1)} %get-tuple-element.221), channel_id=1, source_target_pairs={{0,4},{1,5},{2,6},{3,7},{8,12},{9,13},{10,14},{11,15},{16,20},{17,... | collective-permute-start | bytes 4718600 | tf_op jit(solution)/shard_map/ppermute | solution.py:462
  583.5 62.4 %collective-permute-start.21 = (bf16[512,896]{1,0:T(8,128)(2,1)}, bf16[512,896]{1,0:T(8,128)(2,1)S(1)}, u32[]{:S(2)}, u32[]{:S(2)}) collective-permute-start(bf16[512,896]{1,0:T(8,128)(2,1)} %get-tuple-element.217), channel_id=1, source_target_pairs={{0,8},{8,16},{16,24},{24,0},{1,9},{9,17},{17,25},{25,1},{2,10},{10... | collective-permute-start | bytes 2752520 | tf_op jit(solution)/shard_map/ppermute | solution.py:493
  583.5 65.3 %collective-permute-start.22 = (bf16[512,896]{1,0:T(8,128)(2,1)}, bf16[512,896]{1,0:T(8,128)(2,1)S(1)}, u32[]{:S(2)}, u32[]{:S(2)}) collective-permute-start(bf16[512,896]{1,0:T(8,128)(2,1)} %get-tuple-element.218), channel_id=1, source_target_pairs={{0,16},{8,24},{16,0},{24,8},{1,17},{9,25},{17,1},{25,9},{2,18},{10... | collective-permute-start | bytes 2752520 | tf_op jit(solution)/shard_map/ppermute | solution.py:493
  584.3 64.6 %collective-permute-start.23 = (bf16[512,896]{1,0:T(8,128)(2,1)}, bf16[512,896]{1,0:T(8,128)(2,1)}, u32[]{:S(2)}, u32[]{:S(2)}) collective-permute-start(bf16[512,896]{1,0:T(8,128)(2,1)} %get-tuple-element.219.rest_0_), channel_id=1, source_target_pairs={{0,24},{8,0},{16,8},{24,16},{1,25},{9,1},{17,9},{25,17},{2,26},{10... | collective-permute-start | bytes 2752520 | tf_op jit(solution)/shard_map/ppermute | solution.py:493
  643.9 138.3 %collective-permute-start.28 = (bf16[512,896]{1,0:T(8,128)(2,1)}, bf16[512,896]{1,0:T(8,128)(2,1)}, u32[]{:S(2)}, u32[]{:S(2)}) collective-permute-start(bf16[512,896]{1,0:T(8,128)(2,1)} %get-tuple-element.234), channel_id=1, source_target_pairs={{0,8},{8,16},{16,24},{24,0},{1,9},{9,17},{17,25},{25,1},{2,10},{10... | collective-permute-start | bytes 2752520 | tf_op jit(solution)/shard_map/ppermute | solution.py:493
  644.5 137.7 %collective-permute-start.29 = (bf16[512,896]{1,0:T(8,128)(2,1)}, bf16[512,896]{1,0:T(8,128)(2,1)}, u32[]{:S(2)}, u32[]{:S(2)}) collective-permute-start(bf16[512,896]{1,0:T(8,128)(2,1)} %get-tuple-element.235), channel_id=1, source_target_pairs={{0,16},{8,24},{16,0},{24,8},{1,17},{9,25},{17,1},{25,9},{2,18},{10... | collective-permute-start | bytes 2752520 | tf_op jit(solution)/shard_map/ppermute | solution.py:493
  645.9 136.3 %collective-permute-start.30 = (bf16[512,896]{1,0:T(8,128)(2,1)}, bf16[512,896]{1,0:T(8,128)(2,1)}, u32[]{:S(2)}, u32[]{:S(2)}) collective-permute-start(bf16[512,896]{1,0:T(8,128)(2,1)} %get-tuple-element.226.refs_15_), channel_id=1, source_target_pairs={{0,24},{8,0},{16,8},{24,16},{1,25},{9,1},{17,9},{25,17},{2,26},{10... | collective-permute-start | bytes 2752520 | tf_op jit(solution)/shard_map/ppermute | solution.py:493
  723.8 132.9 %collective-permute-start.25 = (bf16[2,512,768]{2,1,0:T(8,128)(2,1)}, bf16[2,512,768]{2,1,0:T(8,128)(2,1)S(1)}, u32[]{:S(2)}, u32[]{:S(2)}) collective-permute-start(bf16[2,512,768]{2,1,0:T(8,128)(2,1)} %get-tuple-element.228), channel_id=1, source_target_pairs={{0,24},{8,0},{16,8},{24,16},{1,25},{9,1},{17,9},{25,17},{2,26},{10... | collective-permute-start | bytes 4718600 | tf_op jit(solution)/shard_map/ppermute | solution.py:493
  744.3 171.6 %collective-permute-start.26 = (bf16[2,512,768]{2,1,0:T(8,128)(2,1)}, bf16[2,512,768]{2,1,0:T(8,128)(2,1)S(1)}, u32[]{:S(2)}, u32[]{:S(2)}) collective-permute-start(bf16[2,512,768]{2,1,0:T(8,128)(2,1)} %get-tuple-element.229), channel_id=1, source_target_pairs={{0,16},{8,24},{16,0},{24,8},{1,17},{9,25},{17,1},{25,9},{2,18},{10... | collective-permute-start | bytes 4718600 | tf_op jit(solution)/shard_map/ppermute | solution.py:493
  782.2 133.7 %collective-permute-start.27 = (bf16[2,512,768]{2,1,0:T(8,128)(2,1)}, bf16[2,512,768]{2,1,0:T(8,128)(2,1)}, u32[]{:S(2)}, u32[]{:S(2)}) collective-permute-start(bf16[2,512,768]{2,1,0:T(8,128)(2,1)} %get-tuple-element.230.refs_17_), channel_id=1, source_target_pairs={{0,8},{8,16},{16,24},{24,0},{1,9},{9,17},{17,25},{25,1},{2,10},{10... | collective-permute-start | bytes 4718600 | tf_op jit(solution)/shard_map/ppermute | solution.py:493
  917.1 467.2 %reduce-scatter.7.cloned.1.call-start = ((), (), s32[]{:S(2)}) async-start(), calls=%async_computation.11 | async-start | bytes 7077888 | tf_op jit(solution)/shard_map/reduce_scatter | solution.py:1169
  920.5 152.2 %collective-permute-start.31 = (bf16[2,512,768]{2,1,0:T(8,128)(2,1)}, bf16[2,512,768]{2,1,0:T(8,128)(2,1)}, u32[]{:S(2)}, u32[]{:S(2)}) collective-permute-start(bf16[2,512,768]{2,1,0:T(8,128)(2,1)} %get-tuple-element.242), channel_id=1, source_target_pairs={{0,24},{8,0},{16,8},{24,16},{1,25},{9,1},{17,9},{25,17},{2,26},{10... | collective-permute-start | bytes 4718600 | tf_op jit(solution)/shard_map/ppermute | solution.py:493
  920.5 152.2 %collective-permute-start.32 = (bf16[2,512,768]{2,1,0:T(8,128)(2,1)}, bf16[2,512,768]{2,1,0:T(8,128)(2,1)}, u32[]{:S(2)}, u32[]{:S(2)}) collective-permute-start(bf16[2,512,768]{2,1,0:T(8,128)(2,1)} %get-tuple-element.243), channel_id=1, source_target_pairs={{0,16},{8,24},{16,0},{24,8},{1,17},{9,25},{17,1},{25,9},{2,18},{10... | collective-permute-start | bytes 4718600 | tf_op jit(solution)/shard_map/ppermute | solution.py:493
  920.5 152.2 %collective-permute-start.33 = (bf16[2,512,768]{2,1,0:T(8,128)(2,1)}, bf16[2,512,768]{2,1,0:T(8,128)(2,1)}, u32[]{:S(2)}, u32[]{:S(2)}) collective-permute-start(bf16[2,512,768]{2,1,0:T(8,128)(2,1)} %get-tuple-element.239.refs_9_), channel_id=1, source_target_pairs={{0,8},{8,16},{16,24},{24,0},{1,9},{9,17},{17,25},{25,1},{2,10},{10... | collective-permute-start | bytes 4718600 | tf_op jit(solution)/shard_map/ppermute | solution.py:493
  1017.3 37.3 %collective-permute-start.34 = (bf16[1024,768]{1,0:T(8,128)(2,1)}, bf16[1024,768]{1,0:T(8,128)(2,1)}, u32[]{:S(2)}, u32[]{:S(2)}) collective-permute-start(bf16[1024,768]{1,0:T(8,128)(2,1)} %add_convert_fusion.3), channel_id=1, source_target_pairs={{4,0},{5,1},{6,2},{7,3},{12,8},{13,9},{14,10},{15,11},{20,16},{21,... | collective-permute-start | bytes 4718600 | tf_op jit(solution)/shard_map/ppermute | solution.py:462
  1176.6 113.2 %all-to-all-start = ((bf16[8,96,3200]{2,1,0:T(8,128)(2,1)}), bf16[8,96,3200]{2,1,0:T(8,128)(2,1)}, u32[]{:S(2)}, u32[]{:S(2)}) async-start(bf16[8,96,3200]{2,1,0:T(8,128)(2,1)} %bitcast.186), calls=%async_computation.4 | async-start | bytes 9830400 | tf_op jit(solution)/shard_map/all_to_all | solution.py:1198
  1181.6 269.6 %all-reduce.10.cloned.1.call-start = ((), (), s32[]{:S(2)}) async-start(), calls=%async_computation.14 | async-start | bytes 1228800 | tf_op jit(solution)/shard_map/psum | solution.py:1201
  1187.8 82.8 %collective-permute-start.38 = (bf16[1024,768]{1,0:T(8,128)(2,1)S(1)}, bf16[1024,768]{1,0:T(8,128)(2,1)S(1)}, u32[]{:S(2)}, u32[]{:S(2)}) collective-permute-start(bf16[1024,768]{1,0:T(8,128)(2,1)S(1)} %add_convert_fusion.2), channel_id=1, source_target_pairs={{4,0},{5,1},{6,2},{7,3},{12,8},{13,9},{14,10},{15,11},{20,16},{21,... | collective-permute-start | bytes 4718600 | tf_op jit(solution)/shard_map/ppermute | solution.py:462
  1189.1 108.0 %collective-permute-start.37 = (bf16[512,768]{1,0:T(8,128)(2,1)}, bf16[512,768]{1,0:T(8,128)(2,1)S(1)}, u32[]{:S(2)}, u32[]{:S(2)}) collective-permute-start(bf16[512,768]{1,0:T(8,128)(2,1)} %get-tuple-element.255.refs_9_), channel_id=1, source_target_pairs={{0,24},{8,0},{16,8},{24,16},{1,25},{9,1},{17,9},{25,17},{2,26},{10... | collective-permute-start | bytes 2359304 | tf_op jit(solution)/shard_map/ppermute | solution.py:493
  1190.0 103.9 %collective-permute-start.35 = (bf16[512,768]{1,0:T(8,128)(2,1)}, bf16[512,768]{1,0:T(8,128)(2,1)}, u32[]{:S(2)}, u32[]{:S(2)}) collective-permute-start(bf16[512,768]{1,0:T(8,128)(2,1)} %get-tuple-element.258), channel_id=1, source_target_pairs={{0,8},{8,16},{16,24},{24,0},{1,9},{9,17},{17,25},{25,1},{2,10},{10... | collective-permute-start | bytes 2359304 | tf_op jit(solution)/shard_map/ppermute | solution.py:493
  1191.6 105.5 %collective-permute-start.36 = (bf16[512,768]{1,0:T(8,128)(2,1)}, bf16[512,768]{1,0:T(8,128)(2,1)}, u32[]{:S(2)}, u32[]{:S(2)}) collective-permute-start(bf16[512,768]{1,0:T(8,128)(2,1)} %get-tuple-element.259), channel_id=1, source_target_pairs={{0,16},{8,24},{16,0},{24,8},{1,17},{9,25},{17,1},{25,9},{2,18},{10... | collective-permute-start | bytes 2359304 | tf_op jit(solution)/shard_map/ppermute | solution.py:493
  1286.9 63.8 %collective-permute-start.42 = (bf16[512,768]{1,0:T(8,128)(2,1)}, bf16[512,768]{1,0:T(8,128)(2,1)S(1)}, u32[]{:S(2)}, u32[]{:S(2)}) collective-permute-start(bf16[512,768]{1,0:T(8,128)(2,1)} %get-tuple-element.283), channel_id=1, source_target_pairs={{0,8},{8,16},{16,24},{24,0},{1,9},{9,17},{17,25},{25,1},{2,10},{10... | collective-permute-start | bytes 2359304 | tf_op jit(solution)/shard_map/ppermute | solution.py:493
  1288.5 95.7 %collective-permute-start.43 = (bf16[512,768]{1,0:T(8,128)(2,1)}, bf16[512,768]{1,0:T(8,128)(2,1)}, u32[]{:S(2)}, u32[]{:S(2)}) collective-permute-start(bf16[512,768]{1,0:T(8,128)(2,1)} %get-tuple-element.284), channel_id=1, source_target_pairs={{0,16},{8,24},{16,0},{24,8},{1,17},{9,25},{17,1},{25,9},{2,18},{10... | collective-permute-start | bytes 2359304 | tf_op jit(solution)/shard_map/ppermute | solution.py:493
  1293.9 395.4 %reduce-scatter.11.cloned.1.call-start = ((), (), s32[]{:S(2)}) async-start(), calls=%async_computation.13 | async-start | bytes 7077888 | tf_op jit(solution)/shard_map/reduce_scatter | solution.py:1169
  1293.9 90.3 %collective-permute-start.44 = (bf16[512,768]{1,0:T(8,128)(2,1)}, bf16[512,768]{1,0:T(8,128)(2,1)}, u32[]{:S(2)}, u32[]{:S(2)}) collective-permute-start(bf16[512,768]{1,0:T(8,128)(2,1)} %get-tuple-element.271.refs_13_), channel_id=1, source_target_pairs={{0,24},{8,0},{16,8},{24,16},{1,25},{9,1},{17,9},{25,17},{2,26},{10... | collective-permute-start | bytes 2359304 | tf_op jit(solution)/shard_map/ppermute | solution.py:493
  1350.1 87.0 %collective-permute-start.39 = (bf16[1,512,768]{2,1,0:T(8,128)(2,1)}, bf16[1,512,768]{2,1,0:T(8,128)(2,1)S(1)}, u32[]{:S(2)}, u32[]{:S(2)}) collective-permute-start(bf16[1,512,768]{2,1,0:T(8,128)(2,1)} %get-tuple-element.276), channel_id=1, source_target_pairs={{0,24},{8,0},{16,8},{24,16},{1,25},{9,1},{17,9},{25,17},{2,26},{10... | collective-permute-start | bytes 2359304 | tf_op jit(solution)/shard_map/ppermute | solution.py:493
  1350.3 96.0 %collective-permute-start.40 = (bf16[1,512,768]{2,1,0:T(8,128)(2,1)}, bf16[1,512,768]{2,1,0:T(8,128)(2,1)S(1)}, u32[]{:S(2)}, u32[]{:S(2)}) collective-permute-start(bf16[1,512,768]{2,1,0:T(8,128)(2,1)} %get-tuple-element.277), channel_id=1, source_target_pairs={{0,16},{8,24},{16,0},{24,8},{1,17},{9,25},{17,1},{25,9},{2,18},{10... | collective-permute-start | bytes 2359304 | tf_op jit(solution)/shard_map/ppermute | solution.py:493
  1350.6 95.7 %collective-permute-start.41 = (bf16[1,512,768]{2,1,0:T(8,128)(2,1)}, bf16[1,512,768]{2,1,0:T(8,128)(2,1)S(1)}, u32[]{:S(2)}, u32[]{:S(2)}) collective-permute-start(bf16[1,512,768]{2,1,0:T(8,128)(2,1)} %get-tuple-element.278.refs_15_), channel_id=1, source_target_pairs={{0,8},{8,16},{16,24},{24,0},{1,9},{9,17},{17,25},{25,1},{2,10},{10... | collective-permute-start | bytes 2359304 | tf_op jit(solution)/shard_map/ppermute | solution.py:493
  1447.5 241.8 %reduce-scatter.9.cloned.1.call-start = ((), (), s32[]{:S(2)}) async-start(), calls=%async_computation.12 | async-start | bytes 14155776 | tf_op jit(solution)/shard_map/reduce_scatter | solution.py:1168
  1453.8 96.6 %collective-permute-start.46 = (bf16[1,512,768]{2,1,0:T(8,128)(2,1)S(1)}, bf16[1,512,768]{2,1,0:T(8,128)(2,1)S(1)}, u32[]{:S(2)}, u32[]{:S(2)}) collective-permute-start(bf16[1,512,768]{2,1,0:T(8,128)(2,1)S(1)} %copy-done.86), channel_id=1, source_target_pairs={{0,24},{8,0},{16,8},{24,16},{1,25},{9,1},{17,9},{25,17},{2,26},{10... | collective-permute-start | bytes 2359304 | tf_op jit(solution)/shard_map/ppermute | solution.py:493
  1473.7 76.8 %collective-permute-start.47 = (bf16[1,512,768]{2,1,0:T(8,128)(2,1)S(1)}, bf16[1,512,768]{2,1,0:T(8,128)(2,1)}, u32[]{:S(2)}, u32[]{:S(2)}) collective-permute-start(bf16[1,512,768]{2,1,0:T(8,128)(2,1)S(1)} %copy-done.85), channel_id=1, source_target_pairs={{0,16},{8,24},{16,0},{24,8},{1,17},{9,25},{17,1},{25,9},{2,18},{10... | collective-permute-start | bytes 2359304 | tf_op jit(solution)/shard_map/ppermute | solution.py:493
  1473.7 76.8 %collective-permute-start.48 = (bf16[1,512,768]{2,1,0:T(8,128)(2,1)S(1)}, bf16[1,512,768]{2,1,0:T(8,128)(2,1)}, u32[]{:S(2)}, u32[]{:S(2)}) collective-permute-start(bf16[1,512,768]{2,1,0:T(8,128)(2,1)S(1)} %copy-done.84), channel_id=1, source_target_pairs={{0,8},{8,16},{16,24},{24,0},{1,9},{9,17},{17,25},{25,1},{2,10},{10... | collective-permute-start | bytes 2359304 | tf_op jit(solution)/shard_map/ppermute | solution.py:493
  1586.7 95.9 %collective-permute-start.45 = (bf16[1024,768]{1,0:T(8,128)(2,1)}, bf16[1024,768]{1,0:T(8,128)(2,1)}, u32[]{:S(2)}, u32[]{:S(2)}) collective-permute-start(bf16[1024,768]{1,0:T(8,128)(2,1)} %add_convert_fusion.1), channel_id=1, source_target_pairs={{4,0},{5,1},{6,2},{7,3},{12,8},{13,9},{14,10},{15,11},{20,16},{21,... | collective-permute-start | bytes 4718600 | tf_op jit(solution)/shard_map/ppermute | solution.py:462
  1644.0 42.0 %collective-permute-start.49 = (bf16[1024,768]{1,0:T(8,128)(2,1)}, bf16[1024,768]{1,0:T(8,128)(2,1)}, u32[]{:S(2)}, u32[]{:S(2)}) collective-permute-start(bf16[1024,768]{1,0:T(8,128)(2,1)} %add_convert_fusion), channel_id=1, source_target_pairs={{4,0},{5,1},{6,2},{7,3},{12,8},{13,9},{14,10},{15,11},{20,16},{21,... | collective-permute-start | bytes 4718600 | tf_op jit(solution)/shard_map/ppermute | solution.py:462
  1706.9 63.6 %all-to-all-start.1 = ((bf16[8,96,3200]{2,1,0:T(8,128)(2,1)}), bf16[8,96,3200]{2,1,0:T(8,128)(2,1)}, u32[]{:S(2)}, u32[]{:S(2)}) async-start(bf16[8,96,3200]{2,1,0:T(8,128)(2,1)} %bitcast.187), calls=%async_computation.5 | async-start | bytes 9830400 | tf_op jit(solution)/shard_map/all_to_all | solution.py:1198
  1790.6 29.4 %collective-permute-start.51 = (bf16[96,3200]{1,0:T(8,128)(2,1)S(1)}, bf16[96,3200]{1,0:T(8,128)(2,1)S(1)}, u32[]{:S(2)}, u32[]{:S(2)}) collective-permute-start(bf16[96,3200]{1,0:T(8,128)(2,1)S(1)} %add_convert_fusion.12), channel_id=1, source_target_pairs={{0,16},{8,24},{16,0},{24,8},{1,17},{9,25},{17,1},{25,9},{2,18},{10... | collective-permute-start | bytes 1843208 | tf_op jit(solution)/shard_map/ppermute | solution.py:1207
  (110 other events, 1096.5 us)
Sparse Core Ops, SparseCore 0:
  15.0 54.6 all-gather.8
  71.6 46.1 all-gather.12
  119.7 58.5 all-gather.16
  180.1 72.1 all-gather.10
  254.1 45.5 all-gather.18
  301.4 72.1 all-gather.14
  917.2 89.4 reduce-scatter.4
  1023.5 64.5 reduce-scatter.6
  1294.0 122.8 all-reduce.9
  1447.6 78.1 reduce-scatter.10
  1529.3 113.3 reduce-scatter.8

commit v4 on v3

--- a/solution.py
+++ b/solution.py
@@ -24,7 +24,7 @@
 SHARDED = ("context", "dp")
 
 
-COST_SHARE = 0.8
+COST_SHARE = 0.3
 
 
 def cost(microseconds):
@@ -162,7 +162,7 @@
             pltpu.VMEM((span, LANES), bf16),
             pltpu.VMEM((span, LANES), bf16),
         ],
-        compiler_params=pltpu.CompilerParams(vmem_limit_bytes=60 * MIB),
+        compiler_params=pltpu.CompilerParams(vmem_limit_bytes=40 * MIB),
         cost_estimate=cost(32),
         name="attention_forward",
     )(qkv, qkv, qkv, kv_earlier, kv_earlier, seg_query, seg_key, *after)
@@ -264,7 +264,7 @@
             pltpu.VMEM((span, LANES), f32),
             pltpu.VMEM((span, LANES), f32),
         ],
-        compiler_params=pltpu.CompilerParams(vmem_limit_bytes=60 * MIB),
+        compiler_params=pltpu.CompilerParams(vmem_limit_bytes=48 * MIB),
         cost_estimate=cost(48),
         name="attention_backward",
     )(
@@ -326,7 +326,7 @@
         out_shape=[jax.ShapeDtypeStruct((1, count * part, width), bf16)] * groups
         + [hidden_shape, hidden_shape],
         scratch_shapes=[pltpu.VMEM((rows, width), bf16)],
-        compiler_params=pltpu.CompilerParams(vmem_limit_bytes=60 * MIB),
+        compiler_params=pltpu.CompilerParams(vmem_limit_bytes=48 * MIB),
         cost_estimate=cost(26),
         name="experts_forward",
     )(*blocks, gate_up_w, gate_up_w, down_w, *after)
@@ -449,7 +449,7 @@
             pltpu.VMEM((rows, width), bf16),
         ]
         + ([pltpu.VMEM((rows, width), f32)] if whole else []),
-        compiler_params=pltpu.CompilerParams(vmem_limit_bytes=60 * MIB),
+        compiler_params=pltpu.CompilerParams(vmem_limit_bytes=58 * MIB),
         cost_estimate=cost(75 if whole else 52),
         name="experts_whole" if whole else "experts_backward",
     )(*operands, *after)
@@ -555,7 +555,7 @@
             jax.ShapeDtypeStruct((count, length, LANES), jnp.int32),
             jax.ShapeDtypeStruct((count, 8, length), jnp.int32),
         ],
-        compiler_params=pltpu.CompilerParams(vmem_limit_bytes=60 * MIB),
+        compiler_params=pltpu.CompilerParams(vmem_limit_bytes=32 * MIB),
         cost_estimate=cost(4),
         name="routing",
     )(routes, base)
@@ -605,7 +605,7 @@
         + [ANY_SPEC] * len(after),
         out_specs=[pl.BlockSpec((count, out_width), lambda s: (s, 0))] * groups,
         out_shape=[jax.ShapeDtypeStruct((per_group, out_width), bf16)] * groups,
-        compiler_params=pltpu.CompilerParams(vmem_limit_bytes=60 * MIB),
+        compiler_params=pltpu.CompilerParams(vmem_limit_bytes=32 * MIB),
         cost_estimate=cost(6),
         name="dispatch",
     )(rows, slot_rows, gate_rows, *after)
@@ -691,7 +691,7 @@
             jax.ShapeDtypeStruct((length, LANES), f32),
             jax.ShapeDtypeStruct((8, length), f32),
         ],
-        compiler_params=pltpu.CompilerParams(vmem_limit_bytes=60 * MIB),
+        compiler_params=pltpu.CompilerParams(vmem_limit_bytes=24 * MIB),
         cost_estimate=cost(8),
         name="attention_output",
     )(
@@ -760,7 +760,7 @@
         out_shape=[low, low, low]
         if last
         else [low, low, jax.ShapeDtypeStruct((length, width), f32), low],
-        compiler_params=pltpu.CompilerParams(vmem_limit_bytes=60 * MIB),
+        compiler_params=pltpu.CompilerParams(vmem_limit_bytes=24 * MIB),
         cost_estimate=cost(8),
         name="combine",
     )(*back, columns, mid, scalars, vectors, vectors if last else next_vectors, *after)
@@ -898,7 +898,7 @@
             jax.ShapeDtypeStruct((LANES, LANES), f32),
             jax.ShapeDtypeStruct((8, width), f32),
         ],
-        compiler_params=pltpu.CompilerParams(vmem_limit_bytes=60 * MIB),
+        compiler_params=pltpu.CompilerParams(vmem_limit_bytes=48 * MIB),
         cost_estimate=cost(25),
         name="token_backward",
     )(*operands, *after)
@@ -944,13 +944,13 @@
             jax.ShapeDtypeStruct((length, width), out_type),
             jax.ShapeDtypeStruct((8, width), f32),
         ],
-        compiler_params=pltpu.CompilerParams(vmem_limit_bytes=60 * MIB),
+        compiler_params=pltpu.CompilerParams(vmem_limit_bytes=24 * MIB),
         cost_estimate=cost(6),
         name="finish_backward",
     )(hidden, d_mid, d_attn, vectors, *extra, *after)
 
 
-def fetch_layer(layer, local, first_arrived):
+def fetch_layer(layer, local):
     width = local["w_query"].shape[2]
     shard = local["w_query"].shape[1]
     const_w = jnp.transpose(local["w_const"][layer], (1, 0, 2)).reshape(shard, 4)
@@ -969,8 +969,6 @@
     )
     dense = lax.all_gather(packed, SHARDED, axis=0, tiled=True)
     gate_up = jnp.concatenate([local["w_gate"][layer], local["w_up"][layer]], axis=0)
-    if layer == 0:
-        (gate_up,) = held([gate_up], first_arrived)
     gate_up = lax.all_gather(gate_up, SHARDED, axis=1, tiled=True)
     down = lax.all_gather(local["w_down"][layer], SHARDED, axis=1, tiled=True)
     at = 4 * width + ROUTED + 4
@@ -1000,12 +998,6 @@
     capacity = length // 4
     slots = EXPERTS * capacity
     block_start = lax.axis_index("context") * length
-    hidden_earlier = []
-    for micro in micros:
-        block = hidden_in[micro, 0]
-        if micro > 0 and hop_count > 0:
-            (block,) = held([block], (hidden_earlier[-1],))
-        hidden_earlier.append(earlier_rows(block, hop_count))
     routes = routes[:, 0]
     columns, slot_rows = routing_slots(routes, groups, capacity)
     blank_gates = jnp.zeros((8, length), f32)
@@ -1020,15 +1012,16 @@
         last_arrived[:] = exchange(list(blocks[:1]) + others, -1)
         return list(last_arrived)
 
-    early, sents = [], []
-    for micro in micros:
+    early = []
+
+    def send_early(micro, after):
         sent = dispatch(
-            out_grad[micro, 0], slot_rows[micro], blank_gates, "plain", slots, groups,
-        )
-        sents.append(sent[-1])
+            out_grad[micro, 0], slot_rows[micro], blank_gates, "plain", slots, groups, after
+        )
         early.append(exchange(sent, 1))
-    first_ready = (hidden_earlier[0], *sents)
-    fetched = [fetch_layer(layer, local, first_ready) for layer in range(layers)]
+
+    send_early(0, ())
+    fetched = [fetch_layer(layer, local) for layer in range(layers)]
     segs, state = [], []
     for micro in micros:
         whole = segments[micro, 0]
@@ -1042,7 +1035,7 @@
         state.append(
             (
                 hidden, normed(hidden, gain),
-                hidden_earlier[micro], prior,
+                None if micro > 0 else earlier_rows(hidden_in[micro, 0], hop_count), prior,
             )
         )
 
@@ -1053,7 +1046,9 @@
         weights = fetched[layer]
         hidden, attn_in, attn_earlier, prior = state[micro]
         if layer == 0:
-            (attn_earlier,) = held([attn_earlier], after)
+            if micro > 0:
+                (block,) = held([hidden_in[micro, 0]], (saved[micro - 1][0]["attended"],))
+                attn_earlier = earlier_rows(block, hop_count)
             attn_earlier = normed(attn_earlier.astype(f32), weights["vectors"][ATTN_GAIN_ROW][None])
         qkv = dot_on(attn_in, weights["dense"][:, : 3 * width], 1, 0).astype(bf16)
         kv_earlier = dot_on(attn_earlier, weights["dense"][:, width : 3 * width], 1, 0).astype(bf16)
@@ -1226,8 +1221,11 @@
         for micro in micros:
             if layer > 0:
                 before = (combine_part(layer - 1, micro, before),)
+        if layer == last:
+            for micro in micros[1:]:
+                send_early(micro, before)
         for micro in micros:
-            waits = tuple(early[micro][1:]) if layer == 0 else ()
+            waits = tuple(early[-1][1:]) if micro == 0 else ()
             before = (attention_part(layer, micro, before, waits),)
         for micro in micros:
             before = (experts_part(layer, micro, before),)
@@ -1248,7 +1246,8 @@
             if layer > 0:
                 before = (send_back(layer, micro, before),)
         if layer > 0:
-            dense_wait = reduce_dense(layer, packed_dense(layer))
+            (packed,) = held([packed_dense(layer)], before)
+            dense_wait = reduce_dense(layer, packed)
             for micro in micros:
                 if micro < len(experts_ready):
                     before += (experts_ready[micro],)

time: 1840 us -> 1790 us (0.973)
  Pallas kernels: 919 us -> 856 us
  waiting for transfers between devices: 402 us -> 347 us
  local copies, waits for them, and re-layouts: 71.2 us -> 125 us
  starting transfers between devices: 219 us -> 267 us
  matrix products: 154 us -> 125 us
    ppermute x42, waiting for transfers between devices: 216 us -> 130 us  [exchange(): out.append(block if d == 0 else lax.ppermute(block, 'expert', route))]
    ppermute x42, starting transfers between devices: 161 us -> 223 us  [exchange(): out.append(block if d == 0 else lax.ppermute(block, 'expert', route))]
    unnamed x234 -> x574, local copies, waits for them, and re-layouts: 30.4 us -> 91.3 us
    all_to_all x2, waiting for transfers between devices: 53.4 us -> 100 us  [reduce_dense(): lax.all_to_all(parts, SHARDED, split_axis=0, concat_axis=0, tiled=True)]
    dot_general x48, matrix products: 154 us -> 125 us  [dot_on(): lax.dot_general(left_op, right_op, (((left_dim,), (right_dim,)), ((), ())...]
    pallas_call x4, Pallas kernels: 29 us -> 6.77 us  [finish_backward(): pl.pallas_call(functools.partial(finish_backward_kernel, later is not Non...]
  transfers between devices with their start and end apart: 65 -> 65, of which waited for: 12 -> 13; matrix products, arithmetic and copies ran while one was open for 13% -> 11% of each run, Pallas kernels for 49% -> 48%
where the time goes in v4:
time: 1790 us; the launch traced here: 1780 us
  Pallas kernels  856 us (48%)
  waiting for transfers between devices  347 us (19%)
  starting transfers between devices  267 us (15%)
  local copies, waits for them, and re-layouts  125 us (7%)
  matrix products  125 us (7%)
  other arithmetic  45.6 us (3%)
    pallas_call x4, Pallas kernels, experts_backward(): pl.pallas_call(functools.partial(experts_backward_kernel, groups, chunks,...  254 us
    ppermute x42, starting transfers between devices, exchange(): out.append(block if d == 0 else lax.ppermute(block, 'expert', route))  223 us
    pallas_call x4, Pallas kernels, attention_backward(): pl.pallas_call(functools.partial(attention_backward_kernel, rows, keys, b...  194 us
    ppermute x42, waiting for transfers between devices, exchange(): out.append(block if d == 0 else lax.ppermute(block, 'expert', route))  130 us
    pallas_call x4, Pallas kernels, attention_forward(): pl.pallas_call(functools.partial(attention_forward_kernel, rows, keys, bl...  129 us
    dot_general x48, matrix products, dot_on(): lax.dot_general(left_op, right_op, (((left_dim,), (right_dim,)), ((), ())...  125 us
    pallas_call x4, Pallas kernels, token_backward(): pl.pallas_call(functools.partial(token_backward_kernel, d_prior is not No...  104 us
    all_to_all x2, waiting for transfers between devices, reduce_dense(): lax.all_to_all(parts, SHARDED, split_axis=0, concat_axis=0, tiled=True)  100 us
  transfers between devices with their start and end apart: 65, of which 13 were waited for; matrix products, arithmetic and copies ran while one was open for 11% of the time, Pallas kernels for 48%

profile of v4, /device:TPU:2, one launch (start us, length us, event | category | flops | bytes accessed | tf_op | source)
XLA Modules:
  0.0 1783.3 jit_solution(6376412014242824534)
XLA Ops:
  31.1 4.5 collective-permute-start
  42.6 4.4 dispatch.8
  61.3 21.8 %collective-permute-done = bf16[1024,768]{1,0:T(8,128)(2,1)} collective-permute-done((bf16[1024,768]{1,0:T(8,128)(2,1)}, bf16[1024,768]{1,0:T(8,128)(2,1)}, u32[]{:S(2)}, u32[]{:S(2)}) %collective-permute-start) | collective-permute-done | bytes 1572896 | tf_op jit(solution)/shard_map/ppermute | solution.py:462
  86.1 4.9 convolution_convert_fusion.7.kp_ref.vp_ref
  91.2 4.3 convolution_convert_fusion.3.q_ref.ko_ref.vo_ref
  95.5 32.2 %attention_forward.4 = (bf16[1024,768]{1,0:T(8,128)(2,1)S(1)}, f32[16,1024]{1,0:T(8,128)S(1)}) custom-call(bf16[1024,2304]{1,0:T(8,128)(2,1)S(1)} %convolution_convert_fusion.3.q_ref.ko_ref.vo_ref, bf16[1024,2304]{1,0:T(8,128)(2,1)S(1)} %convolution_convert_fusion.3.q_ref.ko_ref.vo_ref, bf16[1024,2304]{1,0:T(8,128)(2,1)S(1)} %convolution_convert_fusion.3.q_ref.ko_ref.vo_ref, ...), custom_call_target="tpu_custom_call" | custom-call | flops 11040000000 | bytes 1 | tf_op jit(solution)/shard_map/attention_forward/pallas_call | solution.py:141
  129.5 5.1 collective-permute-start.7
  140.1 7.8 attention_output.4
  151.3 4.5 dispatch.9
  161.7 4.3 convolution_convert_fusion.2.q_ref.ko_ref.vo_ref
  166.0 28.3 %collective-permute-done.7 = bf16[1024,768]{1,0:T(8,128)(2,1)S(1)} collective-permute-done((bf16[1024,768]{1,0:T(8,128)(2,1)}, bf16[1024,768]{1,0:T(8,128)(2,1)S(1)}, u32[]{:S(2)}, u32[]{:S(2)}) %collective-permute-start.7) | collective-permute-done | bytes 1572896 | tf_op jit(solution)/shard_map/ppermute | solution.py:462
  197.7 32.2 %attention_forward.5 = (bf16[1024,768]{1,0:T(8,128)(2,1)S(1)}, f32[16,1024]{1,0:T(8,128)S(1)}) custom-call(bf16[1024,2304]{1,0:T(8,128)(2,1)S(1)} %convolution_convert_fusion.2.q_ref.ko_ref.vo_ref, bf16[1024,2304]{1,0:T(8,128)(2,1)S(1)} %convolution_convert_fusion.2.q_ref.ko_ref.vo_ref, bf16[1024,2304]{1,0:T(8,128)(2,1)S(1)} %convolution_convert_fusion.2.q_ref.ko_ref.vo_ref, ...), custom_call_target="tpu_custom_call" | custom-call | flops 11040000000 | bytes 1 | tf_op jit(solution)/shard_map/attention_forward/pallas_call | solution.py:141
  230.0 8.0 attention_output.5
  238.9 4.6 dispatch.10
  250.1 28.1 %experts_forward.2 = (bf16[1,512,768]{2,1,0:T(8,128)(2,1)S(1)}, bf16[1,512,768]{2,1,0:T(8,128)(2,1)}, bf16[1,512,768]{2,1,0:T(8,128)(2,1)}, bf16[1,512,768]{2,1,...) custom-call(bf16[512,768]{1,0:T(8,128)(2,1)S(1)} %copy-done.91, ...), custom_call_target="tpu_custom_call" | custom-call | flops 8970000384 | bytes 1 | tf_op jit(solution)/shard_map/experts_forward/pallas_call | solution.py:314
  282.1 18.4 %collective-permute-start.9 = (bf16[1,512,768]{2,1,0:T(8,128)(2,1)}, bf16[1,512,768]{2,1,0:T(8,128)(2,1)}, u32[]{:S(2)}, u32[]{:S(2)}) collective-permute-start(bf16[1,512,768]{2,1,0:T(8,128)(2,1)} %get-tuple-element.192), channel_id=1, source_target_pairs={{0,16},{8,24},{16,0},{24,8},{1,17},{9,25},{17,1},{25,9},{2,18},{10... | collective-permute-start | bytes 2359304 | tf_op jit(solution)/shard_map/ppermute | solution.py:493
  300.5 28.3 %experts_forward.3 = (bf16[1,512,768]{2,1,0:T(8,128)(2,1)S(1)}, bf16[1,512,768]{2,1,0:T(8,128)(2,1)}, bf16[1,512,768]{2,1,0:T(8,128)(2,1)}, bf16[1,512,768]{2,1,...) custom-call(bf16[512,768]{1,0:T(8,128)(2,1)S(1)} %get-tuple-element.197.refs_0_, ...), custom_call_target="tpu_custom_call" | custom-call | flops 8970000384 | bytes 1 | tf_op jit(solution)/shard_map/experts_forward/pallas_call | solution.py:314
  329.7 59.8 %collective-permute-start.15 = (bf16[1,512,768]{2,1,0:T(8,128)(2,1)}, bf16[1,512,768]{2,1,0:T(8,128)(2,1)S(1)}, u32[]{:S(2)}, u32[]{:S(2)}) collective-permute-start(bf16[1,512,768]{2,1,0:T(8,128)(2,1)} %get-tuple-element.204), channel_id=1, source_target_pairs={{0,24},{8,0},{16,8},{24,16},{1,25},{9,1},{17,9},{25,17},{2,26},{10... | collective-permute-start | bytes 2359304 | tf_op jit(solution)/shard_map/ppermute | solution.py:493
  400.9 9.6 combine.4
  412.9 4.5 collective-permute-start.14
  418.3 28.8 %collective-permute-done.16.refs_2_ = bf16[1,512,768]{2,1,0:T(8,128)(2,1)S(1)} collective-permute-done((bf16[1,512,768]{2,1,0:T(8,128)(2,1)}, bf16[1,512,768]{2,1,0:T(8,128)(2,1)S(1)}, u32[]{:S(2)}, u32[]{:S(2)}) %collective-permute-start.16) | collective-permute-done | bytes 786464 | tf_op jit(solution)/shard_map/ppermute | solution.py:493
  450.3 9.4 combine.5
  460.9 4.5 dispatch.11
  469.2 5.5 collective-permute-start.24
  474.8 4.3 convolution_convert_fusion.1.q_ref.ko_ref.vo_ref
  479.1 5.5 convolution_convert_fusion.q_ref.ko_ref.vo_ref
  488.7 32.2 %attention_forward.6 = (bf16[1024,768]{1,0:T(8,128)(2,1)S(1)}, f32[16,1024]{1,0:T(8,128)S(1)}) custom-call(bf16[1024,2304]{1,0:T(8,128)(2,1)S(1)} %convolution_convert_fusion.1.q_ref.ko_ref.vo_ref, bf16[1024,2304]{1,0:T(8,128)(2,1)S(1)} %convolution_convert_fusion.1.q_ref.ko_ref.vo_ref, bf16[1024,2304]{1,0:T(8,128)(2,1)S(1)} %convolution_convert_fusion.1.q_ref.ko_ref.vo_ref, ...), custom_call_target="tpu_custom_call" | custom-call | flops 11040000000 | bytes 1 | tf_op jit(solution)/shard_map/attention_forward/pallas_call | solution.py:141
  521.0 8.1 attention_output.6
  529.9 5.3 dispatch.12
  536.2 7.4 collective-permute-start.21
  550.3 32.2 %attention_forward.7 = (bf16[1024,768]{1,0:T(8,128)(2,1)S(1)}, f32[16,1024]{1,0:T(8,128)S(1)}) custom-call(bf16[1024,2304]{1,0:T(8,128)(2,1)S(1)} %bitcast.220, bf16[1024,2304]{1,0:T(8,128)(2,1)S(1)} %bitcast.220, bf16[1024,2304]{1,0:T(8,128)(2,1)S(1)} %bitcast.220, bf16[1024,1536]{1,0:T(8,128)(2,1)S(1)} %convolution_convert_fusion.4.kp_ref.vp_ref, ...), custom_call_target="tpu_custom_call" | custom-call | flops 11040000000 | bytes 1 | tf_op jit(solution)/shard_map/attention_forward/pallas_call | solution.py:141
  582.6 8.1 attention_output.7
  590.8 5.2 dispatch.13
  600.8 39.1 %collective-permute-done.22.refs_2_.refs_13_ = bf16[512,896]{1,0:T(8,128)(2,1)} collective-permute-done((bf16[512,896]{1,0:T(8,128)(2,1)}, bf16[512,896]{1,0:T(8,128)(2,1)}, u32[]{:S(2)}, u32[]{:S(2)}) %collective-permute-start.22) | collective-permute-done | bytes 917536 | tf_op jit(solution)/shard_map/ppermute | solution.py:493
  639.9 74.0 %experts_whole.2 = (bf16[2,512,768]{2,1,0:T(8,128)(2,1)}, bf16[2,512,768]{2,1,0:T(8,128)(2,1)}, bf16[2,512,768]{2,1,0:T(8,128)(2,1)}, bf16[2,512,768]{2,1,0:T(8,...) custom-call(bf16[512,896]{1,0:T(8,128)(2,1)} %copy-done.185, ...), custom_call_target="tpu_custom_call" | custom-call | flops 25874999296 | bytes 1 | tf_op jit(solution)/shard_map/experts_whole/pallas_call | solution.py:435
  713.9 25.8 %collective-permute-start.25 = (bf16[2,512,768]{2,1,0:T(8,128)(2,1)}, bf16[2,512,768]{2,1,0:T(8,128)(2,1)S(1)}, u32[]{:S(2)}, u32[]{:S(2)}) collective-permute-start(bf16[2,512,768]{2,1,0:T(8,128)(2,1)} %get-tuple-element.228), channel_id=1, source_target_pairs={{0,24},{8,0},{16,8},{24,16},{1,25},{9,1},{17,9},{25,17},{2,26},{10... | collective-permute-start | bytes 4718600 | tf_op jit(solution)/shard_map/ppermute | solution.py:493
  740.3 74.6 %experts_whole.3 = (bf16[2,512,768]{2,1,0:T(8,128)(2,1)}, bf16[2,512,768]{2,1,0:T(8,128)(2,1)}, bf16[2,512,768]{2,1,0:T(8,128)(2,1)}, bf16[2,512,768]{2,1,0:T(8,...) custom-call(bf16[512,896]{1,0:T(8,128)(2,1)} %copy-done.193, ...), custom_call_target="tpu_custom_call" | custom-call | flops 25874999296 | bytes 1 | tf_op jit(solution)/shard_map/experts_whole/pallas_call | solution.py:435
  814.9 57.5 %collective-permute-done.26.refs_2_.refs_3_ = bf16[2,512,768]{2,1,0:T(8,128)(2,1)S(1)} collective-permute-done((bf16[2,512,768]{2,1,0:T(8,128)(2,1)}, bf16[2,512,768]{2,1,0:T(8,128)(2,1)S(1)}, u32[]{:S(2)}, u32[]{:S(2)}) %collective-permute-start.26) | collective-permute-done | bytes 1572896 | tf_op jit(solution)/shard_map/ppermute | solution.py:493
  886.4 9.5 combine.6
  899.5 26.6 %token_backward.4 = (f32[1024,768]{1,0:T(8,128)}, bf16[1024,768]{1,0:T(8,128)(2,1)S(1)}, f32[1024,128]{1,0:T(8,128)S(1)}, f32[768,768]{1,0:T(8,128)}, f32[768,12...) custom-call(bf16[2,512,768]{2,1,0:T(8,128)(2,1)} %get-tuple-element.227.refs_0_, ...), custom_call_target="tpu_custom_call" | custom-call | flops 8625000448 | bytes 1 | tf_op jit(solution)/shard_map/token_backward/pallas_call | solution.py:884
  926.2 48.5 %attention_backward.4 = (bf16[1024,768]{1,0:T(8,128)(2,1)S(1)}, bf16[2048,768]{1,0:T(8,128)(2,1)}, bf16[2048,768]{1,0:T(8,128)(2,1)}) custom-call(bf16[1024,2304]{1,0:T(8,128)(2,1)} %copy-done.194, bf16[1024,2304]{1,0:T(8,128)(2,1)} %copy-done.194, bf16[1024,2304]{1,0:T(8,128)(2,1)} %copy-done.194, bf16[1024,1536]{1,0:T(8,128)(2,1)} %copy-done.192, ...), custom_call_target="tpu_custom_call" | custom-call | flops 16560000000 | bytes 1 | tf_op jit(solution)/shard_map/attention_backward/pallas_call | solution.py:238
  989.6 4.9 fusion.64
  1002.2 20.1 %collective-permute-done.34 = bf16[1024,768]{1,0:T(8,128)(2,1)} collective-permute-done((bf16[1024,768]{1,0:T(8,128)(2,1)}, bf16[1024,768]{1,0:T(8,128)(2,1)}, u32[]{:S(2)}, u32[]{:S(2)}) %collective-permute-start.34) | collective-permute-done | bytes 1572896 | tf_op jit(solution)/shard_map/ppermute | solution.py:462
  1026.5 4.4 dispatch.14
  1032.8 9.6 combine.7
  1045.9 25.7 %token_backward.5 = (f32[1024,768]{1,0:T(8,128)}, bf16[1024,768]{1,0:T(8,128)(2,1)S(1)}, f32[1024,128]{1,0:T(8,128)S(1)}, f32[768,768]{1,0:T(8,128)}, f32[768,12...) custom-call(bf16[2,512,768]{2,1,0:T(8,128)(2,1)} %get-tuple-element.241.refs_0_, ...), custom_call_target="tpu_custom_call" | custom-call | flops 8625000448 | bytes 1 | tf_op jit(solution)/shard_map/token_backward/pallas_call | solution.py:884
  1073.0 48.3 %attention_backward.5 = (bf16[1024,768]{1,0:T(8,128)(2,1)S(1)}, bf16[2048,768]{1,0:T(8,128)(2,1)}, bf16[2048,768]{1,0:T(8,128)(2,1)}) custom-call(bf16[1024,2304]{1,0:T(8,128)(2,1)} %convolution_convert_fusion.q_ref.ko_ref.vo_ref, bf16[1024,2304]{1,0:T(8,128)(2,1)} %convolution_convert_fusion.q_ref.ko_ref.vo_ref, ...), custom_call_target="tpu_custom_call" | custom-call | flops 16560000000 | bytes 1 | tf_op jit(solution)/shard_map/attention_backward/pallas_call | solution.py:238
  1150.6 11.1 collective-permute-done.38
  1163.8 5.4 dispatch.15
  1171.8 4.8 all-to-all-start
  1184.0 46.7 %all-to-all-done = bf16[8,96,3200]{2,1,0:T(8,128)(2,1)} async-done(((bf16[8,96,3200]{2,1,0:T(8,128)(2,1)}), bf16[8,96,3200]{2,1,0:T(8,128)(2,1)}, u32[]{:S(2)}, u32[]{:S(2)}) %all-to-all-start) | async-done | bytes 4915232 | tf_op jit(solution)/shard_map/all_to_all | solution.py:1193
  1234.9 19.6 %collective-permute-start.43 = (bf16[512,768]{1,0:T(8,128)(2,1)}, bf16[512,768]{1,0:T(8,128)(2,1)}, u32[]{:S(2)}, u32[]{:S(2)}) collective-permute-start(bf16[512,768]{1,0:T(8,128)(2,1)} %copy-done.162), channel_id=1, source_target_pairs={{0,16},{8,24},{16,0},{24,8},{1,17},{9,25},{17,1},{25,9},{2,18},{10... | collective-permute-start | bytes 2359304 | tf_op jit(solution)/shard_map/ppermute | solution.py:493
  1254.5 52.1 %experts_backward.2 = (bf16[1,512,768]{2,1,0:T(8,128)(2,1)}, bf16[1,512,768]{2,1,0:T(8,128)(2,1)}, bf16[1,512,768]{2,1,0:T(8,128)(2,1)}, bf16[1,512,768]{2,1,0:T...) custom-call(bf16[512,768]{1,0:T(8,128)(2,1)} %copy-done.90, ...), custom_call_target="tpu_custom_call" | custom-call | flops 17940000768 | bytes 1 | tf_op jit(solution)/shard_map/experts_backward/pallas_call | solution.py:435
  1306.6 40.5 %collective-permute-start.39 = (bf16[1,512,768]{2,1,0:T(8,128)(2,1)}, bf16[1,512,768]{2,1,0:T(8,128)(2,1)S(1)}, u32[]{:S(2)}, u32[]{:S(2)}) collective-permute-start(bf16[1,512,768]{2,1,0:T(8,128)(2,1)} %get-tuple-element.276), channel_id=1, source_target_pairs={{0,24},{8,0},{16,8},{24,16},{1,25},{9,1},{17,9},{25,17},{2,26},{10... | collective-permute-start | bytes 2359304 | tf_op jit(solution)/shard_map/ppermute | solution.py:493
  1347.9 52.9 %experts_backward.3 = (bf16[1,512,768]{2,1,0:T(8,128)(2,1)}, bf16[1,512,768]{2,1,0:T(8,128)(2,1)}, bf16[1,512,768]{2,1,0:T(8,128)(2,1)}, bf16[1,512,768]{2,1,0:T...) custom-call(bf16[512,768]{1,0:T(8,128)(2,1)} %copy-done.35, bf16[512,768]{1,0:T(8,128)(2,1)} %copy-done.36, ...), custom_call_target="tpu_custom_call" | custom-call | flops 17940000768 | bytes 1 | tf_op jit(solution)/shard_map/experts_backward/pallas_call | solution.py:435
  1410.4 8.8 collective-permute-start.46
  1422.2 25.6 %token_backward.6 = (f32[1024,768]{1,0:T(8,128)}, bf16[1024,768]{1,0:T(8,128)(2,1)}, f32[1024,128]{1,0:T(8,128)}, f32[768,768]{1,0:T(8,128)}, f32[768,128]{1,0:T...) custom-call(bf16[1,512,768]{2,1,0:T(8,128)(2,1)S(1)} %copy-done.183, bf16[1,512,768]{2,1,0:T(8,128)(2,1)S(1)} %copy-done.95, ...), custom_call_target="tpu_custom_call" | custom-call | flops 8625000448 | bytes 1 | tf_op jit(solution)/shard_map/token_backward/pallas_call | solution.py:884
  1450.6 48.8 %attention_backward.6 = (bf16[1024,768]{1,0:T(8,128)(2,1)S(1)}, bf16[2048,768]{1,0:T(8,128)(2,1)}, bf16[2048,768]{1,0:T(8,128)(2,1)}) custom-call(bf16[1024,2304]{1,0:T(8,128)(2,1)} %copy-done.188, bf16[1024,2304]{1,0:T(8,128)(2,1)} %copy-done.188, bf16[1024,2304]{1,0:T(8,128)(2,1)} %copy-done.188, bf16[1024,1536]{1,0:T(8,128)(2,1)} %copy-done.190, ...), custom_call_target="tpu_custom_call" | custom-call | flops 16560000000 | bytes 1 | tf_op jit(solution)/shard_map/attention_backward/pallas_call | solution.py:238
  1500.6 26.3 %token_backward.7 = (f32[1024,768]{1,0:T(8,128)}, bf16[1024,768]{1,0:T(8,128)(2,1)}, f32[1024,128]{1,0:T(8,128)}, f32[768,768]{1,0:T(8,128)}, f32[768,128]{1,0:T...) custom-call(bf16[1,512,768]{2,1,0:T(8,128)(2,1)S(1)} %copy-done.161, ...), custom_call_target="tpu_custom_call" | custom-call | flops 8625000448 | bytes 1 | tf_op jit(solution)/shard_map/token_backward/pallas_call | solution.py:884
  1534.7 48.3 %attention_backward.7 = (bf16[1024,768]{1,0:T(8,128)(2,1)S(1)}, bf16[2048,768]{1,0:T(8,128)(2,1)}, bf16[2048,768]{1,0:T(8,128)(2,1)}) custom-call(bf16[1024,2304]{1,0:T(8,128)(2,1)} %copy-done.187, bf16[1024,2304]{1,0:T(8,128)(2,1)} %copy-done.187, bf16[1024,2304]{1,0:T(8,128)(2,1)} %copy-done.187, bf16[1024,1536]{1,0:T(8,128)(2,1)} %copy-done.189, ...), custom_call_target="tpu_custom_call" | custom-call | flops 16560000000 | bytes 1 | tf_op jit(solution)/shard_map/attention_backward/pallas_call | solution.py:238
  1657.1 8.2 all-to-all-start.1
  1667.2 53.4 %all-to-all-done.1 = bf16[8,96,3200]{2,1,0:T(8,128)(2,1)} async-done(((bf16[8,96,3200]{2,1,0:T(8,128)(2,1)}), bf16[8,96,3200]{2,1,0:T(8,128)(2,1)}, u32[]{:S(2)}, u32[]{:S(2)}) %all-to-all-start.1) | async-done | bytes 4915232 | tf_op jit(solution)/shard_map/all_to_all | solution.py:1193
  1732.5 8.7 collective-permute-done.50
  1745.4 25.3 %collective-permute-done.51 = bf16[96,3200]{1,0:T(8,128)(2,1)S(1)} collective-permute-done((bf16[96,3200]{1,0:T(8,128)(2,1)S(1)}, bf16[96,3200]{1,0:T(8,128)(2,1)S(1)}, u32[]{:S(2)}, u32[]{:S(2)}) %collective-permute-start.51) | collective-permute-done | bytes 614432 | tf_op jit(solution)/shard_map/ppermute | solution.py:1202
  (846 shorter events, 338.8 us)
Async XLA Ops:
  7.2 77.7 %all-gather.9.cloned.1.call-start = ((), (), s32[]{:S(2)}) async-start(), calls=%async_computation.6 | async-start | bytes 5529600 | tf_op jit(solution)/shard_map/all_gather | solution.py:970
  15.6 233.3 %all-gather.17.cloned.1.call-start = ((), (), s32[]{:S(2)}) async-start(), calls=%async_computation.15 | async-start | bytes 7077888 | tf_op jit(solution)/shard_map/all_gather | solution.py:973
  17.0 232.0 %all-gather.11.cloned.1.call-start = ((), (), s32[]{:S(2)}) async-start(), calls=%async_computation.7 | async-start | bytes 14155776 | tf_op jit(solution)/shard_map/all_gather | solution.py:972
  21.7 370.2 %all-gather.13.cloned.1.call-start = ((), (), s32[]{:S(2)}) async-start(), calls=%async_computation.8 | async-start | bytes 5529600 | tf_op jit(solution)/shard_map/all_gather | solution.py:970
  23.4 577.4 %all-gather.19.cloned.1.call-start = ((), (), s32[]{:S(2)}) async-start(), calls=%async_computation.16 | async-start | bytes 7077888 | tf_op jit(solution)/shard_map/all_gather | solution.py:973
  24.0 576.8 %all-gather.15.cloned.1.call-start = ((), (), s32[]{:S(2)}) async-start(), calls=%async_computation.9 | async-start | bytes 14155776 | tf_op jit(solution)/shard_map/all_gather | solution.py:972
  27.1 1227.4 %reduce-scatter.5.cloned.1.call-start = ((), (), s32[]{:S(2)}) async-start(), calls=%async_computation.10 | async-start | bytes 14155776 | tf_op jit(solution)/shard_map/reduce_scatter | solution.py:1163
  31.1 52.0 %collective-permute-start = (bf16[1024,768]{1,0:T(8,128)(2,1)}, bf16[1024,768]{1,0:T(8,128)(2,1)}, u32[]{:S(2)}, u32[]{:S(2)}) collective-permute-start(bf16[1024,768]{1,0:T(8,128)(2,1)} %get-tuple-element.408), channel_id=1, source_target_pairs={{0,4},{1,5},{2,6},{3,7},{8,12},{9,13},{10,14},{11,15},{16,20},{17,... | collective-permute-start | bytes 4718600 | tf_op jit(solution)/shard_map/ppermute | solution.py:462
  47.9 103.4 %collective-permute-start.1 = (bf16[512,768]{1,0:T(8,128)(2,1)}, bf16[512,768]{1,0:T(8,128)(2,1)}, u32[]{:S(2)}, u32[]{:S(2)}) collective-permute-start(bf16[512,768]{1,0:T(8,128)(2,1)} %get-tuple-element.179), channel_id=1, source_target_pairs={{0,8},{8,16},{16,24},{24,0},{1,9},{9,17},{17,25},{25,1},{2,10},{10... | collective-permute-start | bytes 2359304 | tf_op jit(solution)/shard_map/ppermute | solution.py:493
  49.4 101.8 %collective-permute-start.2 = (bf16[512,768]{1,0:T(8,128)(2,1)}, bf16[512,768]{1,0:T(8,128)(2,1)}, u32[]{:S(2)}, u32[]{:S(2)}) collective-permute-start(bf16[512,768]{1,0:T(8,128)(2,1)} %get-tuple-element.180), channel_id=1, source_target_pairs={{0,16},{8,24},{16,0},{24,8},{1,17},{9,25},{17,1},{25,9},{2,18},{10... | collective-permute-start | bytes 2359304 | tf_op jit(solution)/shard_map/ppermute | solution.py:493
  52.0 99.3 %collective-permute-start.3 = (bf16[512,768]{1,0:T(8,128)(2,1)}, bf16[512,768]{1,0:T(8,128)(2,1)}, u32[]{:S(2)}, u32[]{:S(2)}) collective-permute-start(bf16[512,768]{1,0:T(8,128)(2,1)} %get-tuple-element.181), channel_id=1, source_target_pairs={{0,24},{8,0},{16,8},{24,16},{1,25},{9,1},{17,9},{25,17},{2,26},{10... | collective-permute-start | bytes 2359304 | tf_op jit(solution)/shard_map/ppermute | solution.py:493
  129.5 64.7 %collective-permute-start.7 = (bf16[1024,768]{1,0:T(8,128)(2,1)}, bf16[1024,768]{1,0:T(8,128)(2,1)S(1)}, u32[]{:S(2)}, u32[]{:S(2)}) collective-permute-start(bf16[1024,768]{1,0:T(8,128)(2,1)} %held.4), channel_id=1, source_target_pairs={{0,4},{1,5},{2,6},{3,7},{8,12},{9,13},{10,14},{11,15},{16,20},{17,... | collective-permute-start | bytes 4718600 | tf_op jit(solution)/shard_map/ppermute | solution.py:462
  155.7 91.8 %collective-permute-start.4 = (bf16[512,768]{1,0:T(8,128)(2,1)}, bf16[512,768]{1,0:T(8,128)(2,1)}, u32[]{:S(2)}, u32[]{:S(2)}) collective-permute-start(bf16[512,768]{1,0:T(8,128)(2,1)} %get-tuple-element.183), channel_id=1, source_target_pairs={{0,8},{8,16},{16,24},{24,0},{1,9},{9,17},{17,25},{25,1},{2,10},{10... | collective-permute-start | bytes 2359304 | tf_op jit(solution)/shard_map/ppermute | solution.py:493
  157.5 91.4 %collective-permute-start.5 = (bf16[512,768]{1,0:T(8,128)(2,1)}, bf16[512,768]{1,0:T(8,128)(2,1)}, u32[]{:S(2)}, u32[]{:S(2)}) collective-permute-start(bf16[512,768]{1,0:T(8,128)(2,1)} %get-tuple-element.184), channel_id=1, source_target_pairs={{0,16},{8,24},{16,0},{24,8},{1,17},{9,25},{17,1},{25,9},{2,18},{10... | collective-permute-start | bytes 2359304 | tf_op jit(solution)/shard_map/ppermute | solution.py:493
  160.4 88.5 %collective-permute-start.6 = (bf16[512,768]{1,0:T(8,128)(2,1)}, bf16[512,768]{1,0:T(8,128)(2,1)}, u32[]{:S(2)}, u32[]{:S(2)}) collective-permute-start(bf16[512,768]{1,0:T(8,128)(2,1)} %get-tuple-element.185.rest_0_), channel_id=1, source_target_pairs={{0,24},{8,0},{16,8},{24,16},{1,25},{9,1},{17,9},{25,17},{2,26},{10... | collective-permute-start | bytes 2359304 | tf_op jit(solution)/shard_map/ppermute | solution.py:493
  243.5 38.6 %collective-permute-start.11 = (bf16[512,768]{1,0:T(8,128)(2,1)}, bf16[512,768]{1,0:T(8,128)(2,1)S(1)}, u32[]{:S(2)}, u32[]{:S(2)}) collective-permute-start(bf16[512,768]{1,0:T(8,128)(2,1)} %get-tuple-element.198), channel_id=1, source_target_pairs={{0,8},{8,16},{16,24},{24,0},{1,9},{9,17},{17,25},{25,1},{2,10},{10... | collective-permute-start | bytes 2359304 | tf_op jit(solution)/shard_map/ppermute | solution.py:493
  245.1 55.4 %collective-permute-start.12 = (bf16[512,768]{1,0:T(8,128)(2,1)}, bf16[512,768]{1,0:T(8,128)(2,1)S(1)}, u32[]{:S(2)}, u32[]{:S(2)}) collective-permute-start(bf16[512,768]{1,0:T(8,128)(2,1)} %get-tuple-element.199), channel_id=1, source_target_pairs={{0,16},{8,24},{16,0},{24,8},{1,17},{9,25},{17,1},{25,9},{2,18},{10... | collective-permute-start | bytes 2359304 | tf_op jit(solution)/shard_map/ppermute | solution.py:493
  247.5 52.9 %collective-permute-start.13 = (bf16[512,768]{1,0:T(8,128)(2,1)}, bf16[512,768]{1,0:T(8,128)(2,1)}, u32[]{:S(2)}, u32[]{:S(2)}) collective-permute-start(bf16[512,768]{1,0:T(8,128)(2,1)} %get-tuple-element.189.refs_7_), channel_id=1, source_target_pairs={{0,24},{8,0},{16,8},{24,16},{1,25},{9,1},{17,9},{25,17},{2,26},{10... | collective-permute-start | bytes 2359304 | tf_op jit(solution)/shard_map/ppermute | solution.py:493
  278.2 111.4 %collective-permute-start.10 = (bf16[1,512,768]{2,1,0:T(8,128)(2,1)S(1)}, bf16[1,512,768]{2,1,0:T(8,128)(2,1)S(1)}, u32[]{:S(2)}, u32[]{:S(2)}) collective-permute-start(bf16[1,512,768]{2,1,0:T(8,128)(2,1)S(1)} %get-tuple-element.193.refs_7_), channel_id=1, source_target_pairs={{0,8},{8,16},{16,24},{24,0},{1,9},{9,17},{17,25},{25,1},{2,10},{10... | collective-permute-start | bytes 2359304 | tf_op jit(solution)/shard_map/ppermute | solution.py:493
  278.9 114.4 %collective-permute-start.8 = (bf16[1,512,768]{2,1,0:T(8,128)(2,1)}, bf16[1,512,768]{2,1,0:T(8,128)(2,1)}, u32[]{:S(2)}, u32[]{:S(2)}) collective-permute-start(bf16[1,512,768]{2,1,0:T(8,128)(2,1)} %get-tuple-element.191), channel_id=1, source_target_pairs={{0,24},{8,0},{16,8},{24,16},{1,25},{9,1},{17,9},{25,17},{2,26},{10... | collective-permute-start | bytes 2359304 | tf_op jit(solution)/shard_map/ppermute | solution.py:493
  282.1 114.7 %collective-permute-start.9 = (bf16[1,512,768]{2,1,0:T(8,128)(2,1)}, bf16[1,512,768]{2,1,0:T(8,128)(2,1)}, u32[]{:S(2)}, u32[]{:S(2)}) collective-permute-start(bf16[1,512,768]{2,1,0:T(8,128)(2,1)} %get-tuple-element.192), channel_id=1, source_target_pairs={{0,16},{8,24},{16,0},{24,8},{1,17},{9,25},{17,1},{25,9},{2,18},{10... | collective-permute-start | bytes 2359304 | tf_op jit(solution)/shard_map/ppermute | solution.py:493
  329.7 87.6 %collective-permute-start.15 = (bf16[1,512,768]{2,1,0:T(8,128)(2,1)}, bf16[1,512,768]{2,1,0:T(8,128)(2,1)S(1)}, u32[]{:S(2)}, u32[]{:S(2)}) collective-permute-start(bf16[1,512,768]{2,1,0:T(8,128)(2,1)} %get-tuple-element.204), channel_id=1, source_target_pairs={{0,24},{8,0},{16,8},{24,16},{1,25},{9,1},{17,9},{25,17},{2,26},{10... | collective-permute-start | bytes 2359304 | tf_op jit(solution)/shard_map/ppermute | solution.py:493
  389.6 57.5 %collective-permute-start.16 = (bf16[1,512,768]{2,1,0:T(8,128)(2,1)}, bf16[1,512,768]{2,1,0:T(8,128)(2,1)S(1)}, u32[]{:S(2)}, u32[]{:S(2)}) collective-permute-start(bf16[1,512,768]{2,1,0:T(8,128)(2,1)} %get-tuple-element.205), channel_id=1, source_target_pairs={{0,16},{8,24},{16,0},{24,8},{1,17},{9,25},{17,1},{25,9},{2,18},{10... | collective-permute-start | bytes 2359304 | tf_op jit(solution)/shard_map/ppermute | solution.py:493
  390.5 57.5 %collective-permute-start.17 = (bf16[1,512,768]{2,1,0:T(8,128)(2,1)}, bf16[1,512,768]{2,1,0:T(8,128)(2,1)}, u32[]{:S(2)}, u32[]{:S(2)}) collective-permute-start(bf16[1,512,768]{2,1,0:T(8,128)(2,1)} %get-tuple-element.200.refs_9_), channel_id=1, source_target_pairs={{0,8},{8,16},{16,24},{24,0},{1,9},{9,17},{17,25},{25,1},{2,10},{10... | collective-permute-start | bytes 2359304 | tf_op jit(solution)/shard_map/ppermute | solution.py:493
  412.9 71.8 %collective-permute-start.14 = (bf16[1024,768]{1,0:T(8,128)(2,1)S(1)}, bf16[1024,768]{1,0:T(8,128)(2,1)S(1)}, u32[]{:S(2)}, u32[]{:S(2)}) collective-permute-start(bf16[1024,768]{1,0:T(8,128)(2,1)S(1)} %get-tuple-element.202), channel_id=1, source_target_pairs={{0,4},{1,5},{2,6},{3,7},{8,12},{9,13},{10,14},{11,15},{16,20},{17,... | collective-permute-start | bytes 4718600 | tf_op jit(solution)/shard_map/ppermute | solution.py:462
  465.4 64.5 %collective-permute-start.18 = (bf16[512,768]{1,0:T(8,128)(2,1)}, bf16[512,768]{1,0:T(8,128)(2,1)}, u32[]{:S(2)}, u32[]{:S(2)}) collective-permute-start(bf16[512,768]{1,0:T(8,128)(2,1)} %get-tuple-element.213), channel_id=1, source_target_pairs={{0,8},{8,16},{16,24},{24,0},{1,9},{9,17},{17,25},{25,1},{2,10},{10... | collective-permute-start | bytes 2359304 | tf_op jit(solution)/shard_map/ppermute | solution.py:493
  465.4 64.5 %collective-permute-start.19 = (bf16[512,768]{1,0:T(8,128)(2,1)}, bf16[512,768]{1,0:T(8,128)(2,1)}, u32[]{:S(2)}, u32[]{:S(2)}) collective-permute-start(bf16[512,768]{1,0:T(8,128)(2,1)} %get-tuple-element.214), channel_id=1, source_target_pairs={{0,16},{8,24},{16,0},{24,8},{1,17},{9,25},{17,1},{25,9},{2,18},{10... | collective-permute-start | bytes 2359304 | tf_op jit(solution)/shard_map/ppermute | solution.py:493
  465.5 64.4 %collective-permute-start.20 = (bf16[512,768]{1,0:T(8,128)(2,1)}, bf16[512,768]{1,0:T(8,128)(2,1)}, u32[]{:S(2)}, u32[]{:S(2)}) collective-permute-start(bf16[512,768]{1,0:T(8,128)(2,1)} %get-tuple-element.215), channel_id=1, source_target_pairs={{0,24},{8,0},{16,8},{24,16},{1,25},{9,1},{17,9},{25,17},{2,26},{10... | collective-permute-start | bytes 2359304 | tf_op jit(solution)/shard_map/ppermute | solution.py:493
  469.2 76.8 %collective-permute-start.24 = (bf16[1024,768]{1,0:T(8,128)(2,1)S(1)}, bf16[1024,768]{1,0:T(8,128)(2,1)}, u32[]{:S(2)}, u32[]{:S(2)}) collective-permute-start(bf16[1024,768]{1,0:T(8,128)(2,1)S(1)} %get-tuple-element.221), channel_id=1, source_target_pairs={{0,4},{1,5},{2,6},{3,7},{8,12},{9,13},{10,14},{11,15},{16,20},{17,... | collective-permute-start | bytes 4718600 | tf_op jit(solution)/shard_map/ppermute | solution.py:462
  536.2 63.4 %collective-permute-start.21 = (bf16[512,896]{1,0:T(8,128)(2,1)S(1)}, bf16[512,896]{1,0:T(8,128)(2,1)}, u32[]{:S(2)}, u32[]{:S(2)}) collective-permute-start(bf16[512,896]{1,0:T(8,128)(2,1)S(1)} %get-tuple-element.217), channel_id=1, source_target_pairs={{0,8},{8,16},{16,24},{24,0},{1,9},{9,17},{17,25},{25,1},{2,10},{10... | collective-permute-start | bytes 2752520 | tf_op jit(solution)/shard_map/ppermute | solution.py:493
  543.6 96.3 %collective-permute-start.22 = (bf16[512,896]{1,0:T(8,128)(2,1)}, bf16[512,896]{1,0:T(8,128)(2,1)}, u32[]{:S(2)}, u32[]{:S(2)}) collective-permute-start(bf16[512,896]{1,0:T(8,128)(2,1)} %get-tuple-element.218), channel_id=1, source_target_pairs={{0,16},{8,24},{16,0},{24,8},{1,17},{9,25},{17,1},{25,9},{2,18},{10... | collective-permute-start | bytes 2752520 | tf_op jit(solution)/shard_map/ppermute | solution.py:493
  543.6 96.3 %collective-permute-start.23 = (bf16[512,896]{1,0:T(8,128)(2,1)}, bf16[512,896]{1,0:T(8,128)(2,1)}, u32[]{:S(2)}, u32[]{:S(2)}) collective-permute-start(bf16[512,896]{1,0:T(8,128)(2,1)} %get-tuple-element.219.rest_0_), channel_id=1, source_target_pairs={{0,24},{8,0},{16,8},{24,16},{1,25},{9,1},{17,9},{25,17},{2,26},{10... | collective-permute-start | bytes 2752520 | tf_op jit(solution)/shard_map/ppermute | solution.py:493
  597.0 142.7 %collective-permute-start.28 = (bf16[512,896]{1,0:T(8,128)(2,1)}, bf16[512,896]{1,0:T(8,128)(2,1)}, u32[]{:S(2)}, u32[]{:S(2)}) collective-permute-start(bf16[512,896]{1,0:T(8,128)(2,1)} %get-tuple-element.234), channel_id=1, source_target_pairs={{0,8},{8,16},{16,24},{24,0},{1,9},{9,17},{17,25},{25,1},{2,10},{10... | collective-permute-start | bytes 2752520 | tf_op jit(solution)/shard_map/ppermute | solution.py:493
  597.0 143.4 %collective-permute-start.29 = (bf16[512,896]{1,0:T(8,128)(2,1)}, bf16[512,896]{1,0:T(8,128)(2,1)}, u32[]{:S(2)}, u32[]{:S(2)}) collective-permute-start(bf16[512,896]{1,0:T(8,128)(2,1)} %get-tuple-element.235), channel_id=1, source_target_pairs={{0,16},{8,24},{16,0},{24,8},{1,17},{9,25},{17,1},{25,9},{2,18},{10... | collective-permute-start | bytes 2752520 | tf_op jit(solution)/shard_map/ppermute | solution.py:493
  599.6 140.8 %collective-permute-start.30 = (bf16[512,896]{1,0:T(8,128)(2,1)}, bf16[512,896]{1,0:T(8,128)(2,1)}, u32[]{:S(2)}, u32[]{:S(2)}) collective-permute-start(bf16[512,896]{1,0:T(8,128)(2,1)} %get-tuple-element.226.refs_15_), channel_id=1, source_target_pairs={{0,24},{8,0},{16,8},{24,16},{1,25},{9,1},{17,9},{25,17},{2,26},{10... | collective-permute-start | bytes 2752520 | tf_op jit(solution)/shard_map/ppermute | solution.py:493
  713.9 101.0 %collective-permute-start.25 = (bf16[2,512,768]{2,1,0:T(8,128)(2,1)}, bf16[2,512,768]{2,1,0:T(8,128)(2,1)S(1)}, u32[]{:S(2)}, u32[]{:S(2)}) collective-permute-start(bf16[2,512,768]{2,1,0:T(8,128)(2,1)} %get-tuple-element.228), channel_id=1, source_target_pairs={{0,24},{8,0},{16,8},{24,16},{1,25},{9,1},{17,9},{25,17},{2,26},{10... | collective-permute-start | bytes 4718600 | tf_op jit(solution)/shard_map/ppermute | solution.py:493
  739.7 132.7 %collective-permute-start.26 = (bf16[2,512,768]{2,1,0:T(8,128)(2,1)}, bf16[2,512,768]{2,1,0:T(8,128)(2,1)S(1)}, u32[]{:S(2)}, u32[]{:S(2)}) collective-permute-start(bf16[2,512,768]{2,1,0:T(8,128)(2,1)} %get-tuple-element.229), channel_id=1, source_target_pairs={{0,16},{8,24},{16,0},{24,8},{1,17},{9,25},{17,1},{25,9},{2,18},{10... | collective-permute-start | bytes 4718600 | tf_op jit(solution)/shard_map/ppermute | solution.py:493
  739.7 132.7 %collective-permute-start.27 = (bf16[2,512,768]{2,1,0:T(8,128)(2,1)}, bf16[2,512,768]{2,1,0:T(8,128)(2,1)}, u32[]{:S(2)}, u32[]{:S(2)}) collective-permute-start(bf16[2,512,768]{2,1,0:T(8,128)(2,1)} %get-tuple-element.230.refs_17_), channel_id=1, source_target_pairs={{0,8},{8,16},{16,24},{24,0},{1,9},{9,17},{17,25},{25,1},{2,10},{10... | collective-permute-start | bytes 4718600 | tf_op jit(solution)/shard_map/ppermute | solution.py:493
  873.6 474.3 %reduce-scatter.7.cloned.1.call-start = ((), (), s32[]{:S(2)}) async-start(), calls=%async_computation.11 | async-start | bytes 7077888 | tf_op jit(solution)/shard_map/reduce_scatter | solution.py:1164
  876.4 155.5 %collective-permute-start.31 = (bf16[2,512,768]{2,1,0:T(8,128)(2,1)}, bf16[2,512,768]{2,1,0:T(8,128)(2,1)}, u32[]{:S(2)}, u32[]{:S(2)}) collective-permute-start(bf16[2,512,768]{2,1,0:T(8,128)(2,1)} %get-tuple-element.242), channel_id=1, source_target_pairs={{0,24},{8,0},{16,8},{24,16},{1,25},{9,1},{17,9},{25,17},{2,26},{10... | collective-permute-start | bytes 4718600 | tf_op jit(solution)/shard_map/ppermute | solution.py:493
  876.4 155.5 %collective-permute-start.32 = (bf16[2,512,768]{2,1,0:T(8,128)(2,1)}, bf16[2,512,768]{2,1,0:T(8,128)(2,1)}, u32[]{:S(2)}, u32[]{:S(2)}) collective-permute-start(bf16[2,512,768]{2,1,0:T(8,128)(2,1)} %get-tuple-element.243), channel_id=1, source_target_pairs={{0,16},{8,24},{16,0},{24,8},{1,17},{9,25},{17,1},{25,9},{2,18},{10... | collective-permute-start | bytes 4718600 | tf_op jit(solution)/shard_map/ppermute | solution.py:493
  876.4 155.5 %collective-permute-start.33 = (bf16[2,512,768]{2,1,0:T(8,128)(2,1)}, bf16[2,512,768]{2,1,0:T(8,128)(2,1)}, u32[]{:S(2)}, u32[]{:S(2)}) collective-permute-start(bf16[2,512,768]{2,1,0:T(8,128)(2,1)} %get-tuple-element.239.refs_9_), channel_id=1, source_target_pairs={{0,8},{8,16},{16,24},{24,0},{1,9},{9,17},{17,25},{25,1},{2,10},{10... | collective-permute-start | bytes 4718600 | tf_op jit(solution)/shard_map/ppermute | solution.py:493
  982.1 40.3 %collective-permute-start.34 = (bf16[1024,768]{1,0:T(8,128)(2,1)}, bf16[1024,768]{1,0:T(8,128)(2,1)}, u32[]{:S(2)}, u32[]{:S(2)}) collective-permute-start(bf16[1024,768]{1,0:T(8,128)(2,1)} %add_convert_fusion.3), channel_id=1, source_target_pairs={{4,0},{5,1},{6,2},{7,3},{12,8},{13,9},{14,10},{15,11},{20,16},{21,... | collective-permute-start | bytes 4718600 | tf_op jit(solution)/shard_map/ppermute | solution.py:462
  1127.0 34.7 %collective-permute-start.38 = (bf16[1024,768]{1,0:T(8,128)(2,1)}, bf16[1024,768]{1,0:T(8,128)(2,1)S(1)}, u32[]{:S(2)}, u32[]{:S(2)}) collective-permute-start(bf16[1024,768]{1,0:T(8,128)(2,1)} %add_convert_fusion.2), channel_id=1, source_target_pairs={{4,0},{5,1},{6,2},{7,3},{12,8},{13,9},{14,10},{15,11},{20,16},{21,... | collective-permute-start | bytes 4718600 | tf_op jit(solution)/shard_map/ppermute | solution.py:462
  1171.8 58.9 %all-to-all-start = ((bf16[8,96,3200]{2,1,0:T(8,128)(2,1)}), bf16[8,96,3200]{2,1,0:T(8,128)(2,1)}, u32[]{:S(2)}, u32[]{:S(2)}) async-start(bf16[8,96,3200]{2,1,0:T(8,128)(2,1)} %bitcast.227), calls=%async_computation.4 | async-start | bytes 9830400 | tf_op jit(solution)/shard_map/all_to_all | solution.py:1193
  1176.6 231.0 %all-reduce.10.cloned.1.call-start = ((), (), s32[]{:S(2)}) async-start(), calls=%async_computation.14 | async-start | bytes 1228800 | tf_op jit(solution)/shard_map/psum | solution.py:1196
  1176.6 58.2 %collective-permute-start.35 = (bf16[512,768]{1,0:T(8,128)(2,1)}, bf16[512,768]{1,0:T(8,128)(2,1)}, u32[]{:S(2)}, u32[]{:S(2)}) collective-permute-start(bf16[512,768]{1,0:T(8,128)(2,1)} %copy-done.160), channel_id=1, source_target_pairs={{0,8},{8,16},{16,24},{24,0},{1,9},{9,17},{17,25},{25,1},{2,10},{10... | collective-permute-start | bytes 2359304 | tf_op jit(solution)/shard_map/ppermute | solution.py:493
  1178.2 76.3 %collective-permute-start.36 = (bf16[512,768]{1,0:T(8,128)(2,1)S(1)}, bf16[512,768]{1,0:T(8,128)(2,1)}, u32[]{:S(2)}, u32[]{:S(2)}) collective-permute-start(bf16[512,768]{1,0:T(8,128)(2,1)S(1)} %copy-done.159), channel_id=1, source_target_pairs={{0,16},{8,24},{16,0},{24,8},{1,17},{9,25},{17,1},{25,9},{2,18},{10... | collective-permute-start | bytes 2359304 | tf_op jit(solution)/shard_map/ppermute | solution.py:493
  1179.1 75.3 %collective-permute-start.37 = (bf16[512,768]{1,0:T(8,128)(2,1)S(1)}, bf16[512,768]{1,0:T(8,128)(2,1)}, u32[]{:S(2)}, u32[]{:S(2)}) collective-permute-start(bf16[512,768]{1,0:T(8,128)(2,1)S(1)} %copy-done.93), channel_id=1, source_target_pairs={{0,24},{8,0},{16,8},{24,16},{1,25},{9,1},{17,9},{25,17},{2,26},{10... | collective-permute-start | bytes 2359304 | tf_op jit(solution)/shard_map/ppermute | solution.py:493
  1182.0 166.0 %collective-permute-start.44 = (bf16[512,768]{1,0:T(8,128)(2,1)}, bf16[512,768]{1,0:T(8,128)(2,1)}, u32[]{:S(2)}, u32[]{:S(2)}) collective-permute-start(bf16[512,768]{1,0:T(8,128)(2,1)} %get-tuple-element.271.refs_13_.refs_1_), channel_id=1, source_target_pairs={{0,24},{8,0},{16,8},{24,16},{1,25},{9,1},{17,9},{25,17},{2,26},{10... | collective-permute-start | bytes 2359304 | tf_op jit(solution)/shard_map/ppermute | solution.py:493
  1182.6 164.5 %collective-permute-start.42 = (bf16[512,768]{1,0:T(8,128)(2,1)}, bf16[512,768]{1,0:T(8,128)(2,1)}, u32[]{:S(2)}, u32[]{:S(2)}) collective-permute-start(bf16[512,768]{1,0:T(8,128)(2,1)} %copy-done.163), channel_id=1, source_target_pairs={{0,8},{8,16},{16,24},{24,0},{1,9},{9,17},{17,25},{25,1},{2,10},{10... | collective-permute-start | bytes 2359304 | tf_op jit(solution)/shard_map/ppermute | solution.py:493
  1234.8 402.0 %reduce-scatter.11.cloned.1.call-start = ((), (), s32[]{:S(2)}) async-start(), calls=%async_computation.13 | async-start | bytes 7077888 | tf_op jit(solution)/shard_map/reduce_scatter | solution.py:1164
  1234.9 113.1 %collective-permute-start.43 = (bf16[512,768]{1,0:T(8,128)(2,1)}, bf16[512,768]{1,0:T(8,128)(2,1)}, u32[]{:S(2)}, u32[]{:S(2)}) collective-permute-start(bf16[512,768]{1,0:T(8,128)(2,1)} %copy-done.162), channel_id=1, source_target_pairs={{0,16},{8,24},{16,0},{24,8},{1,17},{9,25},{17,1},{25,9},{2,18},{10... | collective-permute-start | bytes 2359304 | tf_op jit(solution)/shard_map/ppermute | solution.py:493
  1306.6 94.2 %collective-permute-start.39 = (bf16[1,512,768]{2,1,0:T(8,128)(2,1)}, bf16[1,512,768]{2,1,0:T(8,128)(2,1)S(1)}, u32[]{:S(2)}, u32[]{:S(2)}) collective-permute-start(bf16[1,512,768]{2,1,0:T(8,128)(2,1)} %get-tuple-element.276), channel_id=1, source_target_pairs={{0,24},{8,0},{16,8},{24,16},{1,25},{9,1},{17,9},{25,17},{2,26},{10... | collective-permute-start | bytes 2359304 | tf_op jit(solution)/shard_map/ppermute | solution.py:493
  1347.1 55.2 %collective-permute-start.40 = (bf16[1,512,768]{2,1,0:T(8,128)(2,1)}, bf16[1,512,768]{2,1,0:T(8,128)(2,1)S(1)}, u32[]{:S(2)}, u32[]{:S(2)}) collective-permute-start(bf16[1,512,768]{2,1,0:T(8,128)(2,1)} %get-tuple-element.277), channel_id=1, source_target_pairs={{0,16},{8,24},{16,0},{24,8},{1,17},{9,25},{17,1},{25,9},{2,18},{10... | collective-permute-start | bytes 2359304 | tf_op jit(solution)/shard_map/ppermute | solution.py:493
  1347.1 55.2 %collective-permute-start.41 = (bf16[1,512,768]{2,1,0:T(8,128)(2,1)}, bf16[1,512,768]{2,1,0:T(8,128)(2,1)}, u32[]{:S(2)}, u32[]{:S(2)}) collective-permute-start(bf16[1,512,768]{2,1,0:T(8,128)(2,1)} %get-tuple-element.278.refs_15_), channel_id=1, source_target_pairs={{0,8},{8,16},{16,24},{24,0},{1,9},{9,17},{17,25},{25,1},{2,10},{10... | collective-permute-start | bytes 2359304 | tf_op jit(solution)/shard_map/ppermute | solution.py:493
  1403.3 233.6 %reduce-scatter.9.cloned.1.call-start = ((), (), s32[]{:S(2)}) async-start(), calls=%async_computation.12 | async-start | bytes 14155776 | tf_op jit(solution)/shard_map/reduce_scatter | solution.py:1163
  1410.4 90.2 %collective-permute-start.46 = (bf16[1,512,768]{2,1,0:T(8,128)(2,1)}, bf16[1,512,768]{2,1,0:T(8,128)(2,1)}, u32[]{:S(2)}, u32[]{:S(2)}) collective-permute-start(bf16[1,512,768]{2,1,0:T(8,128)(2,1)} %get-tuple-element.309), channel_id=1, source_target_pairs={{0,24},{8,0},{16,8},{24,16},{1,25},{9,1},{17,9},{25,17},{2,26},{10... | collective-permute-start | bytes 2359304 | tf_op jit(solution)/shard_map/ppermute | solution.py:493
  1419.1 81.4 %collective-permute-start.47 = (bf16[1,512,768]{2,1,0:T(8,128)(2,1)}, bf16[1,512,768]{2,1,0:T(8,128)(2,1)}, u32[]{:S(2)}, u32[]{:S(2)}) collective-permute-start(bf16[1,512,768]{2,1,0:T(8,128)(2,1)} %get-tuple-element.310), channel_id=1, source_target_pairs={{0,16},{8,24},{16,0},{24,8},{1,17},{9,25},{17,1},{25,9},{2,18},{10... | collective-permute-start | bytes 2359304 | tf_op jit(solution)/shard_map/ppermute | solution.py:493
  1419.1 81.4 %collective-permute-start.48 = (bf16[1,512,768]{2,1,0:T(8,128)(2,1)}, bf16[1,512,768]{2,1,0:T(8,128)(2,1)}, u32[]{:S(2)}, u32[]{:S(2)}) collective-permute-start(bf16[1,512,768]{2,1,0:T(8,128)(2,1)} %get-tuple-element.290.refs_19_), channel_id=1, source_target_pairs={{0,8},{8,16},{16,24},{24,0},{1,9},{9,17},{17,25},{25,1},{2,10},{10... | collective-permute-start | bytes 2359304 | tf_op jit(solution)/shard_map/ppermute | solution.py:493
  1533.3 96.7 %collective-permute-start.45 = (bf16[1024,768]{1,0:T(8,128)(2,1)}, bf16[1024,768]{1,0:T(8,128)(2,1)}, u32[]{:S(2)}, u32[]{:S(2)}) collective-permute-start(bf16[1024,768]{1,0:T(8,128)(2,1)} %add_convert_fusion.1), channel_id=1, source_target_pairs={{4,0},{5,1},{6,2},{7,3},{12,8},{13,9},{14,10},{15,11},{20,16},{21,... | collective-permute-start | bytes 4718600 | tf_op jit(solution)/shard_map/ppermute | solution.py:462
  1588.6 44.8 %collective-permute-start.49 = (bf16[1024,768]{1,0:T(8,128)(2,1)}, bf16[1024,768]{1,0:T(8,128)(2,1)}, u32[]{:S(2)}, u32[]{:S(2)}) collective-permute-start(bf16[1024,768]{1,0:T(8,128)(2,1)} %add_convert_fusion), channel_id=1, source_target_pairs={{4,0},{5,1},{6,2},{7,3},{12,8},{13,9},{14,10},{15,11},{20,16},{21,... | collective-permute-start | bytes 4718600 | tf_op jit(solution)/shard_map/ppermute | solution.py:462
  1657.1 63.6 %all-to-all-start.1 = ((bf16[8,96,3200]{2,1,0:T(8,128)(2,1)}), bf16[8,96,3200]{2,1,0:T(8,128)(2,1)}, u32[]{:S(2)}, u32[]{:S(2)}) async-start(bf16[8,96,3200]{2,1,0:T(8,128)(2,1)} %bitcast.228), calls=%async_computation.5 | async-start | bytes 9830400 | tf_op jit(solution)/shard_map/all_to_all | solution.py:1193
  1741.4 29.4 %collective-permute-start.51 = (bf16[96,3200]{1,0:T(8,128)(2,1)S(1)}, bf16[96,3200]{1,0:T(8,128)(2,1)S(1)}, u32[]{:S(2)}, u32[]{:S(2)}) collective-permute-start(bf16[96,3200]{1,0:T(8,128)(2,1)S(1)} %add_convert_fusion.12), channel_id=1, source_target_pairs={{0,16},{8,24},{16,0},{24,8},{1,17},{9,25},{17,1},{25,9},{2,18},{10... | collective-permute-start | bytes 1843208 | tf_op jit(solution)/shard_map/ppermute | solution.py:1202
  (280 other events, 4820.4 us)
Sparse Core Ops, SparseCore 0:
  15.8 50.6 all-gather.8
  68.4 50.1 all-gather.16
  121.0 94.0 all-gather.10
  216.9 43.8 all-gather.12
  262.5 45.5 all-gather.18
  309.8 72.1 all-gather.14
  873.7 91.4 reduce-scatter.4
  989.8 64.8 reduce-scatter.6
  1234.9 81.4 all-reduce.9
  1403.4 67.1 reduce-scatter.10
  1474.0 113.8 reduce-scatter.8

commit v5 on v4

--- a/solution.py
+++ b/solution.py
@@ -1181,19 +1181,20 @@
         small = sums[-1] + jnp.tile(residual, (shards, 1))
         if layer == 0:
             gains = [total_of(l, "g_moe_gain") for l in range(layers)]
-            gains += [total_of(l, "g_attn_gain") for l in range(layers)]
+            gains += [total_of(l, "g_attn_gain") for l in range(1, layers)]
             blank = jnp.zeros((LANES - GAINS_LANE - len(gains), width), f32)
             above = jnp.zeros((GAINS_LANE, width), f32)
             small = small + jnp.concatenate([above, jnp.stack(gains), blank]).T
         return jnp.concatenate([total.astype(bf16) for total in sums[:-1] + [small]], axis=1)
 
-    def reduce_dense(layer, packed):
+    def reduce_dense(layer, packed, after):
         shards = lax.axis_size("context") * lax.axis_size("dp")
         parts = packed.reshape(shards, width // shards, packed.shape[1])
         parts = lax.all_to_all(parts, SHARDED, split_axis=0, concat_axis=0, tiled=True)
         share = jnp.sum(parts.astype(f32), axis=0)
         if layer > 0:
-            share = lax.psum(share.astype(bf16), "expert").astype(f32)
+            (share,) = held([share.astype(bf16)], after)
+            share = lax.psum(share, "expert").astype(f32)
         else:
             span = 1
             while span < groups:
@@ -1246,16 +1247,25 @@
             if layer > 0:
                 before = (send_back(layer, micro, before),)
         if layer > 0:
-            (packed,) = held([packed_dense(layer)], before)
-            dense_wait = reduce_dense(layer, packed)
             for micro in micros:
                 if micro < len(experts_ready):
                     before += (experts_ready[micro],)
                 before = (experts_back_part(layer - 1, micro, d_rows[micro], before),)
+                if micro == 0:
+                    first = before
+            (packed,) = held([packed_dense(layer)], first)
+            dense_wait = reduce_dense(layer, packed, before)
         else:
+            packed = packed_dense(layer)
             for micro in micros:
                 grads[micro] = finish_back_part(layer, micro, tuple(experts_ready) + dense_wait)
-    reduce_dense(0, packed_dense(0))
+    reduce_dense(0, packed, ())
+    first_gain = lax.psum(
+        total_of(0, "g_attn_gain").astype(bf16), ("expert", "context", "dp")
+    ).astype(f32)
+    first_gain = lax.dynamic_slice_in_dim(
+        first_gain, lax.axis_index(SHARDED) * w_query.shape[1], w_query.shape[1], 0
+    )
     hidden_out = jnp.stack(hidden_out)[:, None]
     hidden_grad = jnp.stack(grads)[:, None]
 
@@ -1267,7 +1277,10 @@
     return (
         hidden_out,
         hidden_grad,
-        jnp.stack([small[0, :, GAINS_LANE + layers + l] for l in range(layers)]),
+        jnp.stack(
+            [first_gain]
+            + [small[0, :, GAINS_LANE + layers + l - 1] for l in range(1, layers)]
+        ),
         dense[:, :, :width],
         dense[:, :, width : 2 * width],
         dense[:, :, 2 * width : 3 * width],

time: 1790 us -> 1860 us (1.039)
  waiting for transfers between devices: 347 us -> 387 us
  blocking collectives: 0 us -> 39.5 us
  starting transfers between devices: 267 us -> 237 us
    ppermute x42, waiting for transfers between devices: 130 us -> 177 us  [exchange(): out.append(block if d == 0 else lax.ppermute(block, 'expert', route))]
    ppermute x8, waiting for transfers between devices: 81.3 us -> 128 us  [passed_along(): return lax.ppermute(block, axis, route)]
    all_to_all x2, waiting for transfers between devices: 100 us -> 55.9 us  [reduce_dense(): lax.all_to_all(parts, SHARDED, split_axis=0, concat_axis=0, tiled=True)]
    psum x0 -> x1, blocking collectives: none -> 39.5 us  [per_device(): lax.psum(total_of(0, 'g_attn_gain').astype(bf16), ('expert', 'context', '...]
    ppermute x42, starting transfers between devices: 223 us -> 197 us  [exchange(): out.append(block if d == 0 else lax.ppermute(block, 'expert', route))]
    unnamed x574 -> x544, local copies, waits for them, and re-layouts: 91.3 us -> 94.2 us
  transfers between devices with their start and end apart: 65 -> 65, of which waited for: 13 -> 17; matrix products, arithmetic and copies ran while one was open for 11% -> 11% of each run, Pallas kernels for 48% -> 46%
where the time goes in v5:
time: 1860 us; the launch traced here: 1850 us
  Pallas kernels  856 us (46%)
  waiting for transfers between devices  387 us (21%)
  starting transfers between devices  237 us (13%)
  matrix products  130 us (7%)
  local copies, waits for them, and re-layouts  128 us (7%)
  other arithmetic  56.1 us (3%)
  blocking collectives  39.5 us (2%)
    pallas_call x4, Pallas kernels, experts_backward(): pl.pallas_call(functools.partial(experts_backward_kernel, groups, chunks,...  254 us
    ppermute x42, starting transfers between devices, exchange(): out.append(block if d == 0 else lax.ppermute(block, 'expert', route))  197 us
    pallas_call x4, Pallas kernels, attention_backward(): pl.pallas_call(functools.partial(attention_backward_kernel, rows, keys, b...  195 us
    ppermute x42, waiting for transfers between devices, exchange(): out.append(block if d == 0 else lax.ppermute(block, 'expert', route))  177 us
    dot_general x48, matrix products, dot_on(): lax.dot_general(left_op, right_op, (((left_dim,), (right_dim,)), ((), ())...  130 us
    pallas_call x4, Pallas kernels, attention_forward(): pl.pallas_call(functools.partial(attention_forward_kernel, rows, keys, bl...  129 us
    ppermute x8, waiting for transfers between devices, passed_along(): return lax.ppermute(block, axis, route)  128 us
    pallas_call x4, Pallas kernels, token_backward(): pl.pallas_call(functools.partial(token_backward_kernel, d_prior is not No...  104 us
  transfers between devices with their start and end apart: 65, of which 17 were waited for; matrix products, arithmetic and copies ran while one was open for 11% of the time, Pallas kernels for 46%

profile of v5, /device:TPU:2, one launch (start us, length us, event | category | flops | bytes accessed | tf_op | source)
XLA Modules:
  0.0 1849.8 jit_solution(10644571989856633461)
XLA Ops:
  31.0 4.6 collective-permute-start
  42.5 4.4 dispatch.8
  60.0 22.8 %collective-permute-done = bf16[1024,768]{1,0:T(8,128)(2,1)} collective-permute-done((bf16[1024,768]{1,0:T(8,128)(2,1)}, bf16[1024,768]{1,0:T(8,128)(2,1)}, u32[]{:S(2)}, u32[]{:S(2)}) %collective-permute-start) | collective-permute-done | bytes 1572896 | tf_op jit(solution)/shard_map/ppermute | solution.py:462
  86.0 4.9 convolution_convert_fusion.7.kp_ref.vp_ref
  95.3 32.2 %attention_forward.4 = (bf16[1024,768]{1,0:T(8,128)(2,1)S(1)}, f32[16,1024]{1,0:T(8,128)S(1)}) custom-call(bf16[1024,2304]{1,0:T(8,128)(2,1)S(1)} %convolution_convert_fusion.3.q_ref.ko_ref.vo_ref, bf16[1024,2304]{1,0:T(8,128)(2,1)S(1)} %convolution_convert_fusion.3.q_ref.ko_ref.vo_ref, bf16[1024,2304]{1,0:T(8,128)(2,1)S(1)} %convolution_convert_fusion.3.q_ref.ko_ref.vo_ref, ...), custom_call_target="tpu_custom_call" | custom-call | flops 11040000000 | bytes 1 | tf_op jit(solution)/shard_map/attention_forward/pallas_call | solution.py:141
  129.4 5.1 collective-permute-start.7
  139.9 7.8 attention_output.4
  151.0 4.4 dispatch.9
  165.7 28.5 %collective-permute-done.7 = bf16[1024,768]{1,0:T(8,128)(2,1)S(1)} collective-permute-done((bf16[1024,768]{1,0:T(8,128)(2,1)}, bf16[1024,768]{1,0:T(8,128)(2,1)S(1)}, u32[]{:S(2)}, u32[]{:S(2)}) %collective-permute-start.7) | collective-permute-done | bytes 1572896 | tf_op jit(solution)/shard_map/ppermute | solution.py:462
  197.6 32.2 %attention_forward.5 = (bf16[1024,768]{1,0:T(8,128)(2,1)S(1)}, f32[16,1024]{1,0:T(8,128)S(1)}) custom-call(bf16[1024,2304]{1,0:T(8,128)(2,1)S(1)} %convolution_convert_fusion.2.q_ref.ko_ref.vo_ref, bf16[1024,2304]{1,0:T(8,128)(2,1)S(1)} %convolution_convert_fusion.2.q_ref.ko_ref.vo_ref, bf16[1024,2304]{1,0:T(8,128)(2,1)S(1)} %convolution_convert_fusion.2.q_ref.ko_ref.vo_ref, ...), custom_call_target="tpu_custom_call" | custom-call | flops 11040000000 | bytes 1 | tf_op jit(solution)/shard_map/attention_forward/pallas_call | solution.py:141
  229.9 7.9 attention_output.5
  237.9 4.6 dispatch.10
  253.2 27.7 %experts_forward.2 = (bf16[1,512,768]{2,1,0:T(8,128)(2,1)S(1)}, bf16[1,512,768]{2,1,0:T(8,128)(2,1)}, bf16[1,512,768]{2,1,0:T(8,128)(2,1)}, bf16[1,512,768]{2,1,...) custom-call(bf16[512,768]{1,0:T(8,128)(2,1)S(1)} %copy-done.78, ...), custom_call_target="tpu_custom_call" | custom-call | flops 8970000384 | bytes 1 | tf_op jit(solution)/shard_map/experts_forward/pallas_call | solution.py:314
  285.7 13.9 collective-permute-start.9
  299.6 28.2 %experts_forward.3 = (bf16[1,512,768]{2,1,0:T(8,128)(2,1)S(1)}, bf16[1,512,768]{2,1,0:T(8,128)(2,1)}, bf16[1,512,768]{2,1,0:T(8,128)(2,1)}, bf16[1,512,768]{2,1,...) custom-call(bf16[512,768]{1,0:T(8,128)(2,1)S(1)} %get-tuple-element.197.refs_0_, ...), custom_call_target="tpu_custom_call" | custom-call | flops 8970000384 | bytes 1 | tf_op jit(solution)/shard_map/experts_forward/pallas_call | solution.py:314
  328.7 59.9 %collective-permute-start.15 = (bf16[1,512,768]{2,1,0:T(8,128)(2,1)}, bf16[1,512,768]{2,1,0:T(8,128)(2,1)}, u32[]{:S(2)}, u32[]{:S(2)}) collective-permute-start(bf16[1,512,768]{2,1,0:T(8,128)(2,1)} %get-tuple-element.204), channel_id=1, source_target_pairs={{0,24},{8,0},{16,8},{24,16},{1,25},{9,1},{17,9},{25,17},{2,26},{10... | collective-permute-start | bytes 2359304 | tf_op jit(solution)/shard_map/ppermute | solution.py:493
  400.1 9.6 combine.4
  410.9 4.5 collective-permute-start.14
  415.4 31.0 %collective-permute-done.16.refs_2_ = bf16[1,512,768]{2,1,0:T(8,128)(2,1)} collective-permute-done((bf16[1,512,768]{2,1,0:T(8,128)(2,1)}, bf16[1,512,768]{2,1,0:T(8,128)(2,1)}, u32[]{:S(2)}, u32[]{:S(2)}) %collective-permute-start.16) | collective-permute-done | bytes 786464 | tf_op jit(solution)/shard_map/ppermute | solution.py:493
  446.5 9.8 combine.5
  458.8 4.4 dispatch.11
  467.0 5.5 collective-permute-start.24
  472.5 5.7 convolution_convert_fusion.1.q_ref.ko_ref.vo_ref
  478.2 5.5 convolution_convert_fusion.q_ref.ko_ref.vo_ref
  487.8 32.2 %attention_forward.6 = (bf16[1024,768]{1,0:T(8,128)(2,1)S(1)}, f32[16,1024]{1,0:T(8,128)S(1)}) custom-call(bf16[1024,2304]{1,0:T(8,128)(2,1)S(1)} %copy-done.178, bf16[1024,2304]{1,0:T(8,128)(2,1)S(1)} %copy-done.178, bf16[1024,2304]{1,0:T(8,128)(2,1)S(1)} %copy-done.178, bf16[1024,1536]{1,0:T(8,128)(2,1)S(1)} %convolution_convert_fusion.5.kp_ref.vp_ref, ...), custom_call_target="tpu_custom_call" | custom-call | flops 11040000000 | bytes 1 | tf_op jit(solution)/shard_map/attention_forward/pallas_call | solution.py:141
  520.1 8.0 attention_output.6
  530.7 5.3 dispatch.12
  547.1 32.2 %attention_forward.7 = (bf16[1024,768]{1,0:T(8,128)(2,1)S(1)}, f32[16,1024]{1,0:T(8,128)S(1)}) custom-call(bf16[1024,2304]{1,0:T(8,128)(2,1)S(1)} %bitcast.219, bf16[1024,2304]{1,0:T(8,128)(2,1)S(1)} %bitcast.219, bf16[1024,2304]{1,0:T(8,128)(2,1)S(1)} %bitcast.219, bf16[1024,1536]{1,0:T(8,128)(2,1)S(1)} %convolution_convert_fusion.4.kp_ref.vp_ref, ...), custom_call_target="tpu_custom_call" | custom-call | flops 11040000000 | bytes 1 | tf_op jit(solution)/shard_map/attention_forward/pallas_call | solution.py:141
  579.4 8.0 attention_output.7
  589.9 5.2 dispatch.13
  600.7 74.1 %experts_whole.2 = (bf16[2,512,768]{2,1,0:T(8,128)(2,1)}, bf16[2,512,768]{2,1,0:T(8,128)(2,1)}, bf16[2,512,768]{2,1,0:T(8,128)(2,1)}, bf16[2,512,768]{2,1,0:T(8,...) custom-call(bf16[512,896]{1,0:T(8,128)(2,1)} %copy-done.169, ...), custom_call_target="tpu_custom_call" | custom-call | flops 25874999296 | bytes 1 | tf_op jit(solution)/shard_map/experts_whole/pallas_call | solution.py:435
  674.7 61.8 %collective-permute-start.25 = (bf16[2,512,768]{2,1,0:T(8,128)(2,1)}, bf16[2,512,768]{2,1,0:T(8,128)(2,1)S(1)}, u32[]{:S(2)}, u32[]{:S(2)}) collective-permute-start(bf16[2,512,768]{2,1,0:T(8,128)(2,1)} %get-tuple-element.228), channel_id=1, source_target_pairs={{0,24},{8,0},{16,8},{24,16},{1,25},{9,1},{17,9},{25,17},{2,26},{10... | collective-permute-start | bytes 4718600 | tf_op jit(solution)/shard_map/ppermute | solution.py:493
  737.2 74.6 %experts_whole.3 = (bf16[2,512,768]{2,1,0:T(8,128)(2,1)}, bf16[2,512,768]{2,1,0:T(8,128)(2,1)}, bf16[2,512,768]{2,1,0:T(8,128)(2,1)}, bf16[2,512,768]{2,1,0:T(8,...) custom-call(bf16[512,896]{1,0:T(8,128)(2,1)} %copy-done.177, ...), custom_call_target="tpu_custom_call" | custom-call | flops 25874999296 | bytes 1 | tf_op jit(solution)/shard_map/experts_whole/pallas_call | solution.py:435
  811.8 57.6 %collective-permute-done.26.refs_2_.refs_3_ = bf16[2,512,768]{2,1,0:T(8,128)(2,1)S(1)} collective-permute-done((bf16[2,512,768]{2,1,0:T(8,128)(2,1)}, bf16[2,512,768]{2,1,0:T(8,128)(2,1)S(1)}, u32[]{:S(2)}, u32[]{:S(2)}) %collective-permute-start.26) | collective-permute-done | bytes 1572896 | tf_op jit(solution)/shard_map/ppermute | solution.py:493
  883.5 9.6 combine.6
  896.5 26.6 %token_backward.4 = (f32[1024,768]{1,0:T(8,128)}, bf16[1024,768]{1,0:T(8,128)(2,1)S(1)}, f32[1024,128]{1,0:T(8,128)S(1)}, f32[768,768]{1,0:T(8,128)}, f32[768,12...) custom-call(bf16[2,512,768]{2,1,0:T(8,128)(2,1)} %get-tuple-element.227.refs_0_, ...), custom_call_target="tpu_custom_call" | custom-call | flops 8625000448 | bytes 1 | tf_op jit(solution)/shard_map/token_backward/pallas_call | solution.py:884
  923.2 48.6 %attention_backward.4 = (bf16[1024,768]{1,0:T(8,128)(2,1)S(1)}, bf16[2048,768]{1,0:T(8,128)(2,1)}, bf16[2048,768]{1,0:T(8,128)(2,1)}) custom-call(bf16[1024,2304]{1,0:T(8,128)(2,1)} %convolution_convert_fusion.1.q_ref.ko_ref.vo_ref, bf16[1024,2304]{1,0:T(8,128)(2,1)} %convolution_convert_fusion.1.q_ref.ko_ref.vo_ref, ...), custom_call_target="tpu_custom_call" | custom-call | flops 16560000000 | bytes 1 | tf_op jit(solution)/shard_map/attention_backward/pallas_call | solution.py:238
  986.5 4.9 fusion.64
  999.1 20.1 %collective-permute-done.34 = bf16[1024,768]{1,0:T(8,128)(2,1)} collective-permute-done((bf16[1024,768]{1,0:T(8,128)(2,1)}, bf16[1024,768]{1,0:T(8,128)(2,1)}, u32[]{:S(2)}, u32[]{:S(2)}) %collective-permute-start.34) | collective-permute-done | bytes 1572896 | tf_op jit(solution)/shard_map/ppermute | solution.py:462
  1023.4 4.4 dispatch.14
  1029.8 9.4 combine.7
  1042.8 25.6 %token_backward.5 = (f32[1024,768]{1,0:T(8,128)}, bf16[1024,768]{1,0:T(8,128)(2,1)S(1)}, f32[1024,128]{1,0:T(8,128)S(1)}, f32[768,768]{1,0:T(8,128)}, f32[768,12...) custom-call(bf16[2,512,768]{2,1,0:T(8,128)(2,1)} %get-tuple-element.241.refs_0_, ...), custom_call_target="tpu_custom_call" | custom-call | flops 8625000448 | bytes 1 | tf_op jit(solution)/shard_map/token_backward/pallas_call | solution.py:884
  1070.0 48.7 %attention_backward.5 = (bf16[1024,768]{1,0:T(8,128)(2,1)S(1)}, bf16[2048,768]{1,0:T(8,128)(2,1)}, bf16[2048,768]{1,0:T(8,128)(2,1)}) custom-call(bf16[1024,2304]{1,0:T(8,128)(2,1)} %convolution_convert_fusion.q_ref.ko_ref.vo_ref, bf16[1024,2304]{1,0:T(8,128)(2,1)} %convolution_convert_fusion.q_ref.ko_ref.vo_ref, ...), custom_call_target="tpu_custom_call" | custom-call | flops 16560000000 | bytes 1 | tf_op jit(solution)/shard_map/attention_backward/pallas_call | solution.py:238
  1154.2 4.5 collective-permute-done.38
  1161.0 5.2 dispatch.15
  1167.0 9.7 collective-permute-done.36.refs_6_
  1177.6 52.1 %experts_backward.2 = (bf16[1,512,768]{2,1,0:T(8,128)(2,1)}, bf16[1,512,768]{2,1,0:T(8,128)(2,1)}, bf16[1,512,768]{2,1,0:T(8,128)(2,1)}, bf16[1,512,768]{2,1,0:T...) custom-call(bf16[512,768]{1,0:T(8,128)(2,1)} %copy-done.77, bf16[512,768]{1,0:T(8,128)(2,1)} %copy-done.79, ...), custom_call_target="tpu_custom_call" | custom-call | flops 17940000768 | bytes 1 | tf_op jit(solution)/shard_map/experts_backward/pallas_call | solution.py:435
  1229.7 5.2 all-to-all-start
  1243.0 14.3 collective-permute-done.42.refs_5_
  1258.2 32.9 %collective-permute-done.43.refs_6_ = bf16[512,768]{1,0:T(8,128)(2,1)} collective-permute-done((bf16[512,768]{1,0:T(8,128)(2,1)}, bf16[512,768]{1,0:T(8,128)(2,1)}, u32[]{:S(2)}, u32[]{:S(2)}) %collective-permute-start.43) | collective-permute-done | bytes 786464 | tf_op jit(solution)/shard_map/ppermute | solution.py:493
  1291.1 52.9 %experts_backward.3 = (bf16[1,512,768]{2,1,0:T(8,128)(2,1)}, bf16[1,512,768]{2,1,0:T(8,128)(2,1)}, bf16[1,512,768]{2,1,0:T(8,128)(2,1)}, bf16[1,512,768]{2,1,0:T...) custom-call(bf16[512,768]{1,0:T(8,128)(2,1)} %copy-done.31, bf16[512,768]{1,0:T(8,128)(2,1)} %copy-done.32, ...), custom_call_target="tpu_custom_call" | custom-call | flops 17940000768 | bytes 1 | tf_op jit(solution)/shard_map/experts_backward/pallas_call | solution.py:435
  1348.1 25.6 %collective-permute-done.40.refs_2_.refs_3_ = bf16[1,512,768]{2,1,0:T(8,128)(2,1)S(1)} collective-permute-done((bf16[1,512,768]{2,1,0:T(8,128)(2,1)}, bf16[1,512,768]{2,1,0:T(8,128)(2,1)S(1)}, u32[]{:S(2)}, u32[]{:S(2)}) %collective-permute-start.40) | collective-permute-done | bytes 786464 | tf_op jit(solution)/shard_map/ppermute | solution.py:493
  1378.1 8.9 collective-permute-start.48
  1394.4 25.2 %token_backward.6 = (f32[1024,768]{1,0:T(8,128)}, bf16[1024,768]{1,0:T(8,128)(2,1)}, f32[1024,128]{1,0:T(8,128)}, f32[768,768]{1,0:T(8,128)}, f32[768,128]{1,0:T...) custom-call(bf16[1,512,768]{2,1,0:T(8,128)(2,1)S(1)} %copy-done.167, bf16[1,512,768]{2,1,0:T(8,128)(2,1)S(1)} %copy-done.84, ...), custom_call_target="tpu_custom_call" | custom-call | flops 8625000448 | bytes 1 | tf_op jit(solution)/shard_map/token_backward/pallas_call | solution.py:884
  1421.8 48.5 %attention_backward.6 = (bf16[1024,768]{1,0:T(8,128)(2,1)S(1)}, bf16[2048,768]{1,0:T(8,128)(2,1)}, bf16[2048,768]{1,0:T(8,128)(2,1)}) custom-call(bf16[1024,2304]{1,0:T(8,128)(2,1)} %copy-done.172, bf16[1024,2304]{1,0:T(8,128)(2,1)} %copy-done.172, bf16[1024,2304]{1,0:T(8,128)(2,1)} %copy-done.172, bf16[1024,1536]{1,0:T(8,128)(2,1)} %copy-done.174, ...), custom_call_target="tpu_custom_call" | custom-call | flops 16560000000 | bytes 1 | tf_op jit(solution)/shard_map/attention_backward/pallas_call | solution.py:238
  1471.5 26.4 %token_backward.7 = (f32[1024,768]{1,0:T(8,128)}, bf16[1024,768]{1,0:T(8,128)(2,1)}, f32[1024,128]{1,0:T(8,128)}, f32[768,768]{1,0:T(8,128)}, f32[768,128]{1,0:T...) custom-call(bf16[1,512,768]{2,1,0:T(8,128)(2,1)S(1)} %copy-done.143, ...), custom_call_target="tpu_custom_call" | custom-call | flops 8625000448 | bytes 1 | tf_op jit(solution)/shard_map/token_backward/pallas_call | solution.py:884
  1504.0 48.8 %attention_backward.7 = (bf16[1024,768]{1,0:T(8,128)(2,1)S(1)}, bf16[2048,768]{1,0:T(8,128)(2,1)}, bf16[2048,768]{1,0:T(8,128)(2,1)}) custom-call(bf16[1024,2304]{1,0:T(8,128)(2,1)} %copy-done.171, bf16[1024,2304]{1,0:T(8,128)(2,1)} %copy-done.171, bf16[1024,2304]{1,0:T(8,128)(2,1)} %copy-done.171, bf16[1024,1536]{1,0:T(8,128)(2,1)} %copy-done.173, ...), custom_call_target="tpu_custom_call" | custom-call | flops 16560000000 | bytes 1 | tf_op jit(solution)/shard_map/attention_backward/pallas_call | solution.py:238
  1578.1 4.6 all-to-all-start.1
  1609.1 55.9 %all-to-all-done.1 = bf16[8,96,3200]{2,1,0:T(8,128)(2,1)} async-done(((bf16[8,96,3200]{2,1,0:T(8,128)(2,1)}), bf16[8,96,3200]{2,1,0:T(8,128)(2,1)}, u32[]{:S(2)}, u32[]{:S(2)}) %all-to-all-start.1) | async-done | bytes 4915232 | tf_op jit(solution)/shard_map/all_to_all | solution.py:1193
  1674.1 4.5 add_add_fusion.d_attn_ref
  1678.6 21.5 %collective-permute-done.45 = bf16[1024,768]{1,0:T(8,128)(2,1)} collective-permute-done((bf16[1024,768]{1,0:T(8,128)(2,1)}, bf16[1024,768]{1,0:T(8,128)(2,1)}, u32[]{:S(2)}, u32[]{:S(2)}) %collective-permute-start.45) | collective-permute-done | bytes 1572896 | tf_op jit(solution)/shard_map/ppermute | solution.py:462
  1703.4 30.2 %collective-permute-done.49 = bf16[1024,768]{1,0:T(8,128)(2,1)} collective-permute-done((bf16[1024,768]{1,0:T(8,128)(2,1)}, bf16[1024,768]{1,0:T(8,128)(2,1)}, u32[]{:S(2)}, u32[]{:S(2)}) %collective-permute-start.49) | collective-permute-done | bytes 1572896 | tf_op jit(solution)/shard_map/ppermute | solution.py:462
  1742.0 25.4 %collective-permute-done.51 = bf16[96,3200]{1,0:T(8,128)(2,1)} collective-permute-done((bf16[96,3200]{1,0:T(8,128)(2,1)}, bf16[96,3200]{1,0:T(8,128)(2,1)}, u32[]{:S(2)}, u32[]{:S(2)}) %collective-permute-start.51) | collective-permute-done | bytes 614432 | tf_op jit(solution)/shard_map/ppermute | solution.py:1203
  1799.0 39.5 %psum.15 = bf16[768]{0:T(1024)(128)(2,1)S(1)} all-reduce(bf16[768]{0:T(1024)(128)(2,1)S(1)} %convert_reduce_fusion), channel_id=1, replica_groups=mesh['expert'=4,'context'=2,'dp'=4] {'expert','context','dp'}, use_global_device_ids=true, to_apply=%region_10.11 | all-reduce | flops 768 | bytes 3072 | tf_op jit(solution)/shard_map/psum | solution.py:1263
  (818 shorter events, 368.7 us)
Async XLA Ops:
  7.2 77.5 %all-gather.9.cloned.1.call-start = ((), (), s32[]{:S(2)}) async-start(), calls=%async_computation.6 | async-start | bytes 5529600 | tf_op jit(solution)/shard_map/all_gather | solution.py:970
  15.7 234.2 %all-gather.17.cloned.1.call-start = ((), (), s32[]{:S(2)}) async-start(), calls=%async_computation.15 | async-start | bytes 7077888 | tf_op jit(solution)/shard_map/all_gather | solution.py:973
  17.0 232.8 %all-gather.11.cloned.1.call-start = ((), (), s32[]{:S(2)}) async-start(), calls=%async_computation.7 | async-start | bytes 14155776 | tf_op jit(solution)/shard_map/all_gather | solution.py:972
  21.7 368.5 %all-gather.13.cloned.1.call-start = ((), (), s32[]{:S(2)}) async-start(), calls=%async_computation.8 | async-start | bytes 5529600 | tf_op jit(solution)/shard_map/all_gather | solution.py:970
  23.4 575.4 %all-gather.19.cloned.1.call-start = ((), (), s32[]{:S(2)}) async-start(), calls=%async_computation.16 | async-start | bytes 7077888 | tf_op jit(solution)/shard_map/all_gather | solution.py:973
  24.0 574.8 %all-gather.15.cloned.1.call-start = ((), (), s32[]{:S(2)}) async-start(), calls=%async_computation.9 | async-start | bytes 14155776 | tf_op jit(solution)/shard_map/all_gather | solution.py:972
  27.0 1150.6 %reduce-scatter.5.cloned.1.call-start = ((), (), s32[]{:S(2)}) async-start(), calls=%async_computation.10 | async-start | bytes 14155776 | tf_op jit(solution)/shard_map/reduce_scatter | solution.py:1163
  31.0 51.8 %collective-permute-start = (bf16[1024,768]{1,0:T(8,128)(2,1)}, bf16[1024,768]{1,0:T(8,128)(2,1)}, u32[]{:S(2)}, u32[]{:S(2)}) collective-permute-start(bf16[1024,768]{1,0:T(8,128)(2,1)} %get-tuple-element.407), channel_id=1, source_target_pairs={{0,4},{1,5},{2,6},{3,7},{8,12},{9,13},{10,14},{11,15},{16,20},{17,... | collective-permute-start | bytes 4718600 | tf_op jit(solution)/shard_map/ppermute | solution.py:462
  47.8 103.2 %collective-permute-start.1 = (bf16[512,768]{1,0:T(8,128)(2,1)}, bf16[512,768]{1,0:T(8,128)(2,1)}, u32[]{:S(2)}, u32[]{:S(2)}) collective-permute-start(bf16[512,768]{1,0:T(8,128)(2,1)} %get-tuple-element.179), channel_id=1, source_target_pairs={{0,8},{8,16},{16,24},{24,0},{1,9},{9,17},{17,25},{25,1},{2,10},{10... | collective-permute-start | bytes 2359304 | tf_op jit(solution)/shard_map/ppermute | solution.py:493
  49.4 101.6 %collective-permute-start.2 = (bf16[512,768]{1,0:T(8,128)(2,1)}, bf16[512,768]{1,0:T(8,128)(2,1)}, u32[]{:S(2)}, u32[]{:S(2)}) collective-permute-start(bf16[512,768]{1,0:T(8,128)(2,1)} %get-tuple-element.180), channel_id=1, source_target_pairs={{0,16},{8,24},{16,0},{24,8},{1,17},{9,25},{17,1},{25,9},{2,18},{10... | collective-permute-start | bytes 2359304 | tf_op jit(solution)/shard_map/ppermute | solution.py:493
  51.9 99.1 %collective-permute-start.3 = (bf16[512,768]{1,0:T(8,128)(2,1)}, bf16[512,768]{1,0:T(8,128)(2,1)}, u32[]{:S(2)}, u32[]{:S(2)}) collective-permute-start(bf16[512,768]{1,0:T(8,128)(2,1)} %get-tuple-element.181), channel_id=1, source_target_pairs={{0,24},{8,0},{16,8},{24,16},{1,25},{9,1},{17,9},{25,17},{2,26},{10... | collective-permute-start | bytes 2359304 | tf_op jit(solution)/shard_map/ppermute | solution.py:493
  129.4 64.8 %collective-permute-start.7 = (bf16[1024,768]{1,0:T(8,128)(2,1)}, bf16[1024,768]{1,0:T(8,128)(2,1)S(1)}, u32[]{:S(2)}, u32[]{:S(2)}) collective-permute-start(bf16[1024,768]{1,0:T(8,128)(2,1)} %held.5), channel_id=1, source_target_pairs={{0,4},{1,5},{2,6},{3,7},{8,12},{9,13},{10,14},{11,15},{16,20},{17,... | collective-permute-start | bytes 4718600 | tf_op jit(solution)/shard_map/ppermute | solution.py:462
  155.5 91.2 %collective-permute-start.4 = (bf16[512,768]{1,0:T(8,128)(2,1)}, bf16[512,768]{1,0:T(8,128)(2,1)S(1)}, u32[]{:S(2)}, u32[]{:S(2)}) collective-permute-start(bf16[512,768]{1,0:T(8,128)(2,1)} %get-tuple-element.183), channel_id=1, source_target_pairs={{0,8},{8,16},{16,24},{24,0},{1,9},{9,17},{17,25},{25,1},{2,10},{10... | collective-permute-start | bytes 2359304 | tf_op jit(solution)/shard_map/ppermute | solution.py:493
  157.3 91.7 %collective-permute-start.5 = (bf16[512,768]{1,0:T(8,128)(2,1)}, bf16[512,768]{1,0:T(8,128)(2,1)S(1)}, u32[]{:S(2)}, u32[]{:S(2)}) collective-permute-start(bf16[512,768]{1,0:T(8,128)(2,1)} %get-tuple-element.184), channel_id=1, source_target_pairs={{0,16},{8,24},{16,0},{24,8},{1,17},{9,25},{17,1},{25,9},{2,18},{10... | collective-permute-start | bytes 2359304 | tf_op jit(solution)/shard_map/ppermute | solution.py:493
  160.2 89.7 %collective-permute-start.6 = (bf16[512,768]{1,0:T(8,128)(2,1)}, bf16[512,768]{1,0:T(8,128)(2,1)}, u32[]{:S(2)}, u32[]{:S(2)}) collective-permute-start(bf16[512,768]{1,0:T(8,128)(2,1)} %get-tuple-element.185.rest_0_), channel_id=1, source_target_pairs={{0,24},{8,0},{16,8},{24,16},{1,25},{9,1},{17,9},{25,17},{2,26},{10... | collective-permute-start | bytes 2359304 | tf_op jit(solution)/shard_map/ppermute | solution.py:493
  242.5 43.1 %collective-permute-start.11 = (bf16[512,768]{1,0:T(8,128)(2,1)}, bf16[512,768]{1,0:T(8,128)(2,1)S(1)}, u32[]{:S(2)}, u32[]{:S(2)}) collective-permute-start(bf16[512,768]{1,0:T(8,128)(2,1)} %get-tuple-element.198), channel_id=1, source_target_pairs={{0,8},{8,16},{16,24},{24,0},{1,9},{9,17},{17,25},{25,1},{2,10},{10... | collective-permute-start | bytes 2359304 | tf_op jit(solution)/shard_map/ppermute | solution.py:493
  244.1 55.4 %collective-permute-start.12 = (bf16[512,768]{1,0:T(8,128)(2,1)}, bf16[512,768]{1,0:T(8,128)(2,1)}, u32[]{:S(2)}, u32[]{:S(2)}) collective-permute-start(bf16[512,768]{1,0:T(8,128)(2,1)} %get-tuple-element.199), channel_id=1, source_target_pairs={{0,16},{8,24},{16,0},{24,8},{1,17},{9,25},{17,1},{25,9},{2,18},{10... | collective-permute-start | bytes 2359304 | tf_op jit(solution)/shard_map/ppermute | solution.py:493
  247.5 52.0 %collective-permute-start.13 = (bf16[512,768]{1,0:T(8,128)(2,1)}, bf16[512,768]{1,0:T(8,128)(2,1)}, u32[]{:S(2)}, u32[]{:S(2)}) collective-permute-start(bf16[512,768]{1,0:T(8,128)(2,1)} %get-tuple-element.189.refs_7_), channel_id=1, source_target_pairs={{0,24},{8,0},{16,8},{24,16},{1,25},{9,1},{17,9},{25,17},{2,26},{10... | collective-permute-start | bytes 2359304 | tf_op jit(solution)/shard_map/ppermute | solution.py:493
  281.8 106.8 %collective-permute-start.10 = (bf16[1,512,768]{2,1,0:T(8,128)(2,1)S(1)}, bf16[1,512,768]{2,1,0:T(8,128)(2,1)S(1)}, u32[]{:S(2)}, u32[]{:S(2)}) collective-permute-start(bf16[1,512,768]{2,1,0:T(8,128)(2,1)S(1)} %get-tuple-element.193.refs_7_), channel_id=1, source_target_pairs={{0,8},{8,16},{16,24},{24,0},{1,9},{9,17},{17,25},{25,1},{2,10},{10... | collective-permute-start | bytes 2359304 | tf_op jit(solution)/shard_map/ppermute | solution.py:493
  282.6 109.1 %collective-permute-start.8 = (bf16[1,512,768]{2,1,0:T(8,128)(2,1)}, bf16[1,512,768]{2,1,0:T(8,128)(2,1)}, u32[]{:S(2)}, u32[]{:S(2)}) collective-permute-start(bf16[1,512,768]{2,1,0:T(8,128)(2,1)} %get-tuple-element.191), channel_id=1, source_target_pairs={{0,24},{8,0},{16,8},{24,16},{1,25},{9,1},{17,9},{25,17},{2,26},{10... | collective-permute-start | bytes 2359304 | tf_op jit(solution)/shard_map/ppermute | solution.py:493
  285.7 110.3 %collective-permute-start.9 = (bf16[1,512,768]{2,1,0:T(8,128)(2,1)}, bf16[1,512,768]{2,1,0:T(8,128)(2,1)}, u32[]{:S(2)}, u32[]{:S(2)}) collective-permute-start(bf16[1,512,768]{2,1,0:T(8,128)(2,1)} %get-tuple-element.192), channel_id=1, source_target_pairs={{0,16},{8,24},{16,0},{24,8},{1,17},{9,25},{17,1},{25,9},{2,18},{10... | collective-permute-start | bytes 2359304 | tf_op jit(solution)/shard_map/ppermute | solution.py:493
  328.7 86.7 %collective-permute-start.15 = (bf16[1,512,768]{2,1,0:T(8,128)(2,1)}, bf16[1,512,768]{2,1,0:T(8,128)(2,1)}, u32[]{:S(2)}, u32[]{:S(2)}) collective-permute-start(bf16[1,512,768]{2,1,0:T(8,128)(2,1)} %get-tuple-element.204), channel_id=1, source_target_pairs={{0,24},{8,0},{16,8},{24,16},{1,25},{9,1},{17,9},{25,17},{2,26},{10... | collective-permute-start | bytes 2359304 | tf_op jit(solution)/shard_map/ppermute | solution.py:493
  388.6 57.8 %collective-permute-start.16 = (bf16[1,512,768]{2,1,0:T(8,128)(2,1)}, bf16[1,512,768]{2,1,0:T(8,128)(2,1)}, u32[]{:S(2)}, u32[]{:S(2)}) collective-permute-start(bf16[1,512,768]{2,1,0:T(8,128)(2,1)} %get-tuple-element.205), channel_id=1, source_target_pairs={{0,16},{8,24},{16,0},{24,8},{1,17},{9,25},{17,1},{25,9},{2,18},{10... | collective-permute-start | bytes 2359304 | tf_op jit(solution)/shard_map/ppermute | solution.py:493
  389.5 56.9 %collective-permute-start.17 = (bf16[1,512,768]{2,1,0:T(8,128)(2,1)}, bf16[1,512,768]{2,1,0:T(8,128)(2,1)}, u32[]{:S(2)}, u32[]{:S(2)}) collective-permute-start(bf16[1,512,768]{2,1,0:T(8,128)(2,1)} %get-tuple-element.200.refs_9_), channel_id=1, source_target_pairs={{0,8},{8,16},{16,24},{24,0},{1,9},{9,17},{17,25},{25,1},{2,10},{10... | collective-permute-start | bytes 2359304 | tf_op jit(solution)/shard_map/ppermute | solution.py:493
  410.9 72.8 %collective-permute-start.14 = (bf16[1024,768]{1,0:T(8,128)(2,1)S(1)}, bf16[1024,768]{1,0:T(8,128)(2,1)S(1)}, u32[]{:S(2)}, u32[]{:S(2)}) collective-permute-start(bf16[1024,768]{1,0:T(8,128)(2,1)S(1)} %get-tuple-element.202), channel_id=1, source_target_pairs={{0,4},{1,5},{2,6},{3,7},{8,12},{9,13},{10,14},{11,15},{16,20},{17,... | collective-permute-start | bytes 4718600 | tf_op jit(solution)/shard_map/ppermute | solution.py:462
  463.2 67.5 %collective-permute-start.18 = (bf16[512,768]{1,0:T(8,128)(2,1)}, bf16[512,768]{1,0:T(8,128)(2,1)}, u32[]{:S(2)}, u32[]{:S(2)}) collective-permute-start(bf16[512,768]{1,0:T(8,128)(2,1)} %get-tuple-element.213), channel_id=1, source_target_pairs={{0,8},{8,16},{16,24},{24,0},{1,9},{9,17},{17,25},{25,1},{2,10},{10... | collective-permute-start | bytes 2359304 | tf_op jit(solution)/shard_map/ppermute | solution.py:493
  463.2 67.5 %collective-permute-start.19 = (bf16[512,768]{1,0:T(8,128)(2,1)}, bf16[512,768]{1,0:T(8,128)(2,1)}, u32[]{:S(2)}, u32[]{:S(2)}) collective-permute-start(bf16[512,768]{1,0:T(8,128)(2,1)} %get-tuple-element.214), channel_id=1, source_target_pairs={{0,16},{8,24},{16,0},{24,8},{1,17},{9,25},{17,1},{25,9},{2,18},{10... | collective-permute-start | bytes 2359304 | tf_op jit(solution)/shard_map/ppermute | solution.py:493
  463.5 67.1 %collective-permute-start.20 = (bf16[512,768]{1,0:T(8,128)(2,1)}, bf16[512,768]{1,0:T(8,128)(2,1)}, u32[]{:S(2)}, u32[]{:S(2)}) collective-permute-start(bf16[512,768]{1,0:T(8,128)(2,1)} %get-tuple-element.215), channel_id=1, source_target_pairs={{0,24},{8,0},{16,8},{24,16},{1,25},{9,1},{17,9},{25,17},{2,26},{10... | collective-permute-start | bytes 2359304 | tf_op jit(solution)/shard_map/ppermute | solution.py:493
  467.0 75.8 %collective-permute-start.24 = (bf16[1024,768]{1,0:T(8,128)(2,1)S(1)}, bf16[1024,768]{1,0:T(8,128)(2,1)}, u32[]{:S(2)}, u32[]{:S(2)}) collective-permute-start(bf16[1024,768]{1,0:T(8,128)(2,1)S(1)} %get-tuple-element.221), channel_id=1, source_target_pairs={{0,4},{1,5},{2,6},{3,7},{8,12},{9,13},{10,14},{11,15},{16,20},{17,... | collective-permute-start | bytes 4718600 | tf_op jit(solution)/shard_map/ppermute | solution.py:462
  536.0 61.6 %collective-permute-start.21 = (bf16[512,896]{1,0:T(8,128)(2,1)S(1)}, bf16[512,896]{1,0:T(8,128)(2,1)}, u32[]{:S(2)}, u32[]{:S(2)}) collective-permute-start(bf16[512,896]{1,0:T(8,128)(2,1)S(1)} %get-tuple-element.217), channel_id=1, source_target_pairs={{0,8},{8,16},{16,24},{24,0},{1,9},{9,17},{17,25},{25,1},{2,10},{10... | collective-permute-start | bytes 2752520 | tf_op jit(solution)/shard_map/ppermute | solution.py:493
  540.3 58.8 %collective-permute-start.22 = (bf16[512,896]{1,0:T(8,128)(2,1)}, bf16[512,896]{1,0:T(8,128)(2,1)}, u32[]{:S(2)}, u32[]{:S(2)}) collective-permute-start(bf16[512,896]{1,0:T(8,128)(2,1)} %get-tuple-element.218), channel_id=1, source_target_pairs={{0,16},{8,24},{16,0},{24,8},{1,17},{9,25},{17,1},{25,9},{2,18},{10... | collective-permute-start | bytes 2752520 | tf_op jit(solution)/shard_map/ppermute | solution.py:493
  540.3 60.3 %collective-permute-start.23 = (bf16[512,896]{1,0:T(8,128)(2,1)}, bf16[512,896]{1,0:T(8,128)(2,1)}, u32[]{:S(2)}, u32[]{:S(2)}) collective-permute-start(bf16[512,896]{1,0:T(8,128)(2,1)} %get-tuple-element.219.rest_0_), channel_id=1, source_target_pairs={{0,24},{8,0},{16,8},{24,16},{1,25},{9,1},{17,9},{25,17},{2,26},{10... | collective-permute-start | bytes 2752520 | tf_op jit(solution)/shard_map/ppermute | solution.py:493
  595.0 141.5 %collective-permute-start.28 = (bf16[512,896]{1,0:T(8,128)(2,1)}, bf16[512,896]{1,0:T(8,128)(2,1)}, u32[]{:S(2)}, u32[]{:S(2)}) collective-permute-start(bf16[512,896]{1,0:T(8,128)(2,1)} %get-tuple-element.234), channel_id=1, source_target_pairs={{0,8},{8,16},{16,24},{24,0},{1,9},{9,17},{17,25},{25,1},{2,10},{10... | collective-permute-start | bytes 2752520 | tf_op jit(solution)/shard_map/ppermute | solution.py:493
  595.0 142.2 %collective-permute-start.29 = (bf16[512,896]{1,0:T(8,128)(2,1)}, bf16[512,896]{1,0:T(8,128)(2,1)}, u32[]{:S(2)}, u32[]{:S(2)}) collective-permute-start(bf16[512,896]{1,0:T(8,128)(2,1)} %get-tuple-element.235), channel_id=1, source_target_pairs={{0,16},{8,24},{16,0},{24,8},{1,17},{9,25},{17,1},{25,9},{2,18},{10... | collective-permute-start | bytes 2752520 | tf_op jit(solution)/shard_map/ppermute | solution.py:493
  597.5 139.7 %collective-permute-start.30 = (bf16[512,896]{1,0:T(8,128)(2,1)}, bf16[512,896]{1,0:T(8,128)(2,1)}, u32[]{:S(2)}, u32[]{:S(2)}) collective-permute-start(bf16[512,896]{1,0:T(8,128)(2,1)} %get-tuple-element.226.refs_15_), channel_id=1, source_target_pairs={{0,24},{8,0},{16,8},{24,16},{1,25},{9,1},{17,9},{25,17},{2,26},{10... | collective-permute-start | bytes 2752520 | tf_op jit(solution)/shard_map/ppermute | solution.py:493
  674.7 137.1 %collective-permute-start.25 = (bf16[2,512,768]{2,1,0:T(8,128)(2,1)}, bf16[2,512,768]{2,1,0:T(8,128)(2,1)S(1)}, u32[]{:S(2)}, u32[]{:S(2)}) collective-permute-start(bf16[2,512,768]{2,1,0:T(8,128)(2,1)} %get-tuple-element.228), channel_id=1, source_target_pairs={{0,24},{8,0},{16,8},{24,16},{1,25},{9,1},{17,9},{25,17},{2,26},{10... | collective-permute-start | bytes 4718600 | tf_op jit(solution)/shard_map/ppermute | solution.py:493
  736.5 132.9 %collective-permute-start.26 = (bf16[2,512,768]{2,1,0:T(8,128)(2,1)}, bf16[2,512,768]{2,1,0:T(8,128)(2,1)S(1)}, u32[]{:S(2)}, u32[]{:S(2)}) collective-permute-start(bf16[2,512,768]{2,1,0:T(8,128)(2,1)} %get-tuple-element.229), channel_id=1, source_target_pairs={{0,16},{8,24},{16,0},{24,8},{1,17},{9,25},{17,1},{25,9},{2,18},{10... | collective-permute-start | bytes 4718600 | tf_op jit(solution)/shard_map/ppermute | solution.py:493
  736.5 132.9 %collective-permute-start.27 = (bf16[2,512,768]{2,1,0:T(8,128)(2,1)}, bf16[2,512,768]{2,1,0:T(8,128)(2,1)}, u32[]{:S(2)}, u32[]{:S(2)}) collective-permute-start(bf16[2,512,768]{2,1,0:T(8,128)(2,1)} %get-tuple-element.230.refs_17_), channel_id=1, source_target_pairs={{0,8},{8,16},{16,24},{24,0},{1,9},{9,17},{17,25},{25,1},{2,10},{10... | collective-permute-start | bytes 4718600 | tf_op jit(solution)/shard_map/ppermute | solution.py:493
  870.6 420.5 %reduce-scatter.7.cloned.1.call-start = ((), (), s32[]{:S(2)}) async-start(), calls=%async_computation.11 | async-start | bytes 7077888 | tf_op jit(solution)/shard_map/reduce_scatter | solution.py:1164
  873.4 156.3 %collective-permute-start.31 = (bf16[2,512,768]{2,1,0:T(8,128)(2,1)}, bf16[2,512,768]{2,1,0:T(8,128)(2,1)}, u32[]{:S(2)}, u32[]{:S(2)}) collective-permute-start(bf16[2,512,768]{2,1,0:T(8,128)(2,1)} %get-tuple-element.242), channel_id=1, source_target_pairs={{0,24},{8,0},{16,8},{24,16},{1,25},{9,1},{17,9},{25,17},{2,26},{10... | collective-permute-start | bytes 4718600 | tf_op jit(solution)/shard_map/ppermute | solution.py:493
  873.4 156.3 %collective-permute-start.32 = (bf16[2,512,768]{2,1,0:T(8,128)(2,1)}, bf16[2,512,768]{2,1,0:T(8,128)(2,1)}, u32[]{:S(2)}, u32[]{:S(2)}) collective-permute-start(bf16[2,512,768]{2,1,0:T(8,128)(2,1)} %get-tuple-element.243), channel_id=1, source_target_pairs={{0,16},{8,24},{16,0},{24,8},{1,17},{9,25},{17,1},{25,9},{2,18},{10... | collective-permute-start | bytes 4718600 | tf_op jit(solution)/shard_map/ppermute | solution.py:493
  873.4 156.3 %collective-permute-start.33 = (bf16[2,512,768]{2,1,0:T(8,128)(2,1)}, bf16[2,512,768]{2,1,0:T(8,128)(2,1)}, u32[]{:S(2)}, u32[]{:S(2)}) collective-permute-start(bf16[2,512,768]{2,1,0:T(8,128)(2,1)} %get-tuple-element.239.refs_9_), channel_id=1, source_target_pairs={{0,8},{8,16},{16,24},{24,0},{1,9},{9,17},{17,25},{25,1},{2,10},{10... | collective-permute-start | bytes 4718600 | tf_op jit(solution)/shard_map/ppermute | solution.py:493
  979.2 40.0 %collective-permute-start.34 = (bf16[1024,768]{1,0:T(8,128)(2,1)}, bf16[1024,768]{1,0:T(8,128)(2,1)}, u32[]{:S(2)}, u32[]{:S(2)}) collective-permute-start(bf16[1024,768]{1,0:T(8,128)(2,1)} %add_convert_fusion.3), channel_id=1, source_target_pairs={{4,0},{5,1},{6,2},{7,3},{12,8},{13,9},{14,10},{15,11},{20,16},{21,... | collective-permute-start | bytes 4718600 | tf_op jit(solution)/shard_map/ppermute | solution.py:462
  1029.5 148.1 %collective-permute-start.37 = (bf16[512,768]{1,0:T(8,128)(2,1)S(1)}, bf16[512,768]{1,0:T(8,128)(2,1)}, u32[]{:S(2)}, u32[]{:S(2)}) collective-permute-start(bf16[512,768]{1,0:T(8,128)(2,1)S(1)} %get-tuple-element.255.refs_9_), channel_id=1, source_target_pairs={{0,24},{8,0},{16,8},{24,16},{1,25},{9,1},{17,9},{25,17},{2,26},{10... | collective-permute-start | bytes 2359304 | tf_op jit(solution)/shard_map/ppermute | solution.py:493
  1124.4 34.3 %collective-permute-start.38 = (bf16[1024,768]{1,0:T(8,128)(2,1)}, bf16[1024,768]{1,0:T(8,128)(2,1)S(1)}, u32[]{:S(2)}, u32[]{:S(2)}) collective-permute-start(bf16[1024,768]{1,0:T(8,128)(2,1)} %add_convert_fusion.2), channel_id=1, source_target_pairs={{4,0},{5,1},{6,2},{7,3},{12,8},{13,9},{14,10},{15,11},{20,16},{21,... | collective-permute-start | bytes 4718600 | tf_op jit(solution)/shard_map/ppermute | solution.py:462
  1125.7 41.3 %collective-permute-start.35 = (bf16[512,768]{1,0:T(8,128)(2,1)S(1)}, bf16[512,768]{1,0:T(8,128)(2,1)S(1)}, u32[]{:S(2)}, u32[]{:S(2)}) collective-permute-start(bf16[512,768]{1,0:T(8,128)(2,1)S(1)} %copy-done.147), channel_id=1, source_target_pairs={{0,8},{8,16},{16,24},{24,0},{1,9},{9,17},{17,25},{25,1},{2,10},{10... | collective-permute-start | bytes 2359304 | tf_op jit(solution)/shard_map/ppermute | solution.py:493
  1127.8 48.9 %collective-permute-start.36 = (bf16[512,768]{1,0:T(8,128)(2,1)S(1)}, bf16[512,768]{1,0:T(8,128)(2,1)S(1)}, u32[]{:S(2)}, u32[]{:S(2)}) collective-permute-start(bf16[512,768]{1,0:T(8,128)(2,1)S(1)} %copy-done.145), channel_id=1, source_target_pairs={{0,16},{8,24},{16,0},{24,8},{1,17},{9,25},{17,1},{25,9},{2,18},{10... | collective-permute-start | bytes 2359304 | tf_op jit(solution)/shard_map/ppermute | solution.py:493
  1229.7 114.3 %all-to-all-start = ((bf16[8,96,3200]{2,1,0:T(8,128)(2,1)}), bf16[8,96,3200]{2,1,0:T(8,128)(2,1)}, u32[]{:S(2)}, u32[]{:S(2)}) async-start(bf16[8,96,3200]{2,1,0:T(8,128)(2,1)} %bitcast.226), calls=%async_computation.4 | async-start | bytes 9830400 | tf_op jit(solution)/shard_map/all_to_all | solution.py:1193
  1234.9 504.8 %all-reduce.10.cloned.1.call-start = ((), (), s32[]{:S(2)}) async-start(), calls=%async_computation.14 | async-start | bytes 1228800 | tf_op jit(solution)/shard_map/psum | solution.py:1197
  1234.9 56.2 %collective-permute-start.43 = (bf16[512,768]{1,0:T(8,128)(2,1)}, bf16[512,768]{1,0:T(8,128)(2,1)}, u32[]{:S(2)}, u32[]{:S(2)}) collective-permute-start(bf16[512,768]{1,0:T(8,128)(2,1)} %get-tuple-element.284), channel_id=1, source_target_pairs={{0,16},{8,24},{16,0},{24,8},{1,17},{9,25},{17,1},{25,9},{2,18},{10... | collective-permute-start | bytes 2359304 | tf_op jit(solution)/shard_map/ppermute | solution.py:493
  1237.4 53.7 %collective-permute-start.44 = (bf16[512,768]{1,0:T(8,128)(2,1)}, bf16[512,768]{1,0:T(8,128)(2,1)}, u32[]{:S(2)}, u32[]{:S(2)}) collective-permute-start(bf16[512,768]{1,0:T(8,128)(2,1)} %get-tuple-element.271.refs_13_), channel_id=1, source_target_pairs={{0,24},{8,0},{16,8},{24,16},{1,25},{9,1},{17,9},{25,17},{2,26},{10... | collective-permute-start | bytes 2359304 | tf_op jit(solution)/shard_map/ppermute | solution.py:493
  1238.8 135.0 %collective-permute-start.41 = (bf16[1,512,768]{2,1,0:T(8,128)(2,1)}, bf16[1,512,768]{2,1,0:T(8,128)(2,1)}, u32[]{:S(2)}, u32[]{:S(2)}) collective-permute-start(bf16[1,512,768]{2,1,0:T(8,128)(2,1)} %get-tuple-element.278.refs_15_.refs_1_), channel_id=1, source_target_pairs={{0,8},{8,16},{16,24},{24,0},{1,9},{9,17},{17,25},{25,1},{2,10},{10... | collective-permute-start | bytes 2359304 | tf_op jit(solution)/shard_map/ppermute | solution.py:493
  1239.5 108.7 %collective-permute-start.39 = (bf16[1,512,768]{2,1,0:T(8,128)(2,1)}, bf16[1,512,768]{2,1,0:T(8,128)(2,1)S(1)}, u32[]{:S(2)}, u32[]{:S(2)}) collective-permute-start(bf16[1,512,768]{2,1,0:T(8,128)(2,1)} %get-tuple-element.276), channel_id=1, source_target_pairs={{0,24},{8,0},{16,8},{24,16},{1,25},{9,1},{17,9},{25,17},{2,26},{10... | collective-permute-start | bytes 2359304 | tf_op jit(solution)/shard_map/ppermute | solution.py:493
  1258.2 115.6 %collective-permute-start.40 = (bf16[1,512,768]{2,1,0:T(8,128)(2,1)}, bf16[1,512,768]{2,1,0:T(8,128)(2,1)S(1)}, u32[]{:S(2)}, u32[]{:S(2)}) collective-permute-start(bf16[1,512,768]{2,1,0:T(8,128)(2,1)} %get-tuple-element.277), channel_id=1, source_target_pairs={{0,16},{8,24},{16,0},{24,8},{1,17},{9,25},{17,1},{25,9},{2,18},{10... | collective-permute-start | bytes 2359304 | tf_op jit(solution)/shard_map/ppermute | solution.py:493
  1348.1 431.2 %reduce-scatter.11.cloned.1.call-start = ((), (), s32[]{:S(2)}) async-start(), calls=%async_computation.13 | async-start | bytes 7077888 | tf_op jit(solution)/shard_map/reduce_scatter | solution.py:1164
  1374.7 407.9 %reduce-scatter.9.cloned.1.call-start = ((), (), s32[]{:S(2)}) async-start(), calls=%async_computation.12 | async-start | bytes 14155776 | tf_op jit(solution)/shard_map/reduce_scatter | solution.py:1163
  1378.1 93.3 %collective-permute-start.48 = (bf16[1,512,768]{2,1,0:T(8,128)(2,1)}, bf16[1,512,768]{2,1,0:T(8,128)(2,1)}, u32[]{:S(2)}, u32[]{:S(2)}) collective-permute-start(bf16[1,512,768]{2,1,0:T(8,128)(2,1)} %get-tuple-element.290.refs_19_.refs_1_), channel_id=1, source_target_pairs={{0,8},{8,16},{16,24},{24,0},{1,9},{9,17},{17,25},{25,1},{2,10},{10... | collective-permute-start | bytes 2359304 | tf_op jit(solution)/shard_map/ppermute | solution.py:493
  1387.0 84.4 %collective-permute-start.46 = (bf16[1,512,768]{2,1,0:T(8,128)(2,1)}, bf16[1,512,768]{2,1,0:T(8,128)(2,1)}, u32[]{:S(2)}, u32[]{:S(2)}) collective-permute-start(bf16[1,512,768]{2,1,0:T(8,128)(2,1)} %get-tuple-element.309), channel_id=1, source_target_pairs={{0,24},{8,0},{16,8},{24,16},{1,25},{9,1},{17,9},{25,17},{2,26},{10... | collective-permute-start | bytes 2359304 | tf_op jit(solution)/shard_map/ppermute | solution.py:493
  1387.0 84.4 %collective-permute-start.47 = (bf16[1,512,768]{2,1,0:T(8,128)(2,1)}, bf16[1,512,768]{2,1,0:T(8,128)(2,1)}, u32[]{:S(2)}, u32[]{:S(2)}) collective-permute-start(bf16[1,512,768]{2,1,0:T(8,128)(2,1)} %get-tuple-element.310), channel_id=1, source_target_pairs={{0,16},{8,24},{16,0},{24,8},{1,17},{9,25},{17,1},{25,9},{2,18},{10... | collective-permute-start | bytes 2359304 | tf_op jit(solution)/shard_map/ppermute | solution.py:493
  1578.1 87.0 %all-to-all-start.1 = ((bf16[8,96,3200]{2,1,0:T(8,128)(2,1)}), bf16[8,96,3200]{2,1,0:T(8,128)(2,1)}, u32[]{:S(2)}, u32[]{:S(2)}) async-start(bf16[8,96,3200]{2,1,0:T(8,128)(2,1)} %bitcast.227), calls=%async_computation.5 | async-start | bytes 9830400 | tf_op jit(solution)/shard_map/all_to_all | solution.py:1193
  1592.9 107.2 %collective-permute-start.45 = (bf16[1024,768]{1,0:T(8,128)(2,1)}, bf16[1024,768]{1,0:T(8,128)(2,1)}, u32[]{:S(2)}, u32[]{:S(2)}) collective-permute-start(bf16[1024,768]{1,0:T(8,128)(2,1)} %add_convert_fusion.1), channel_id=1, source_target_pairs={{4,0},{5,1},{6,2},{7,3},{12,8},{13,9},{14,10},{15,11},{20,16},{21,... | collective-permute-start | bytes 4718600 | tf_op jit(solution)/shard_map/ppermute | solution.py:462
  1598.5 135.1 %collective-permute-start.49 = (bf16[1024,768]{1,0:T(8,128)(2,1)}, bf16[1024,768]{1,0:T(8,128)(2,1)}, u32[]{:S(2)}, u32[]{:S(2)}) collective-permute-start(bf16[1024,768]{1,0:T(8,128)(2,1)} %add_convert_fusion), channel_id=1, source_target_pairs={{4,0},{5,1},{6,2},{7,3},{12,8},{13,9},{14,10},{15,11},{20,16},{21,... | collective-permute-start | bytes 4718600 | tf_op jit(solution)/shard_map/ppermute | solution.py:462
  1669.1 66.1 %collective-permute-start.50 = (bf16[96,3200]{1,0:T(8,128)(2,1)}, bf16[96,3200]{1,0:T(8,128)(2,1)S(1)}, u32[]{:S(2)}, u32[]{:S(2)}) collective-permute-start(bf16[96,3200]{1,0:T(8,128)(2,1)} %reduce_sum.65), channel_id=1, source_target_pairs={{0,8},{8,0},{16,24},{24,16},{1,9},{9,1},{17,25},{25,17},{2,10},{10... | collective-permute-start | bytes 1843208 | tf_op jit(solution)/shard_map/ppermute | solution.py:1203
  1737.3 30.0 %collective-permute-start.51 = (bf16[96,3200]{1,0:T(8,128)(2,1)}, bf16[96,3200]{1,0:T(8,128)(2,1)}, u32[]{:S(2)}, u32[]{:S(2)}) collective-permute-start(bf16[96,3200]{1,0:T(8,128)(2,1)} %add_convert_fusion.12), channel_id=1, source_target_pairs={{0,16},{8,24},{16,0},{24,8},{1,17},{9,25},{17,1},{25,9},{2,18},{10... | collective-permute-start | bytes 1843208 | tf_op jit(solution)/shard_map/ppermute | solution.py:1203
  (265 other events, 4794.8 us)
Sparse Core Ops, SparseCore 0:
  15.8 50.7 all-gather.8
  68.5 49.9 all-gather.16
  121.0 94.0 all-gather.10
  216.8 43.8 all-gather.12
  262.4 45.5 all-gather.18
  309.8 72.1 all-gather.14
  870.7 90.2 reduce-scatter.4
  986.6 64.7 reduce-scatter.6
  1348.2 107.3 all-reduce.9
  1459.2 69.3 reduce-scatter.10
  1532.0 139.6 reduce-scatter.8

commit v6 on v4

--- a/solution.py
+++ b/solution.py
@@ -1187,13 +1187,14 @@
             small = small + jnp.concatenate([above, jnp.stack(gains), blank]).T
         return jnp.concatenate([total.astype(bf16) for total in sums[:-1] + [small]], axis=1)
 
-    def reduce_dense(layer, packed):
+    def reduce_dense(layer, packed, after):
         shards = lax.axis_size("context") * lax.axis_size("dp")
         parts = packed.reshape(shards, width // shards, packed.shape[1])
         parts = lax.all_to_all(parts, SHARDED, split_axis=0, concat_axis=0, tiled=True)
         share = jnp.sum(parts.astype(f32), axis=0)
         if layer > 0:
-            share = lax.psum(share.astype(bf16), "expert").astype(f32)
+            (share,) = held([share.astype(bf16)], after)
+            share = lax.psum(share, "expert").astype(f32)
         else:
             span = 1
             while span < groups:
@@ -1246,16 +1247,18 @@
             if layer > 0:
                 before = (send_back(layer, micro, before),)
         if layer > 0:
-            (packed,) = held([packed_dense(layer)], before)
-            dense_wait = reduce_dense(layer, packed)
             for micro in micros:
                 if micro < len(experts_ready):
                     before += (experts_ready[micro],)
                 before = (experts_back_part(layer - 1, micro, d_rows[micro], before),)
+                if micro == 0:
+                    first = before
+            (packed,) = held([packed_dense(layer)], first)
+            dense_wait = reduce_dense(layer, packed, before)
         else:
             for micro in micros:
                 grads[micro] = finish_back_part(layer, micro, tuple(experts_ready) + dense_wait)
-    reduce_dense(0, packed_dense(0))
+    reduce_dense(0, packed_dense(0), ())
     hidden_out = jnp.stack(hidden_out)[:, None]
     hidden_grad = jnp.stack(grads)[:, None]
 

time: 1790 us -> 1810 us (1.011)
  waiting for transfers between devices: 347 us -> 423 us
  starting transfers between devices: 267 us -> 210 us
    ppermute x42, waiting for transfers between devices: 130 us -> 212 us  [exchange(): out.append(block if d == 0 else lax.ppermute(block, 'expert', route))]
    ppermute x42, starting transfers between devices: 223 us -> 169 us  [exchange(): out.append(block if d == 0 else lax.ppermute(block, 'expert', route))]
    all_to_all x2, waiting for transfers between devices: 100 us -> 53.4 us  [reduce_dense(): lax.all_to_all(parts, SHARDED, split_axis=0, concat_axis=0, tiled=True)]
    reduce_scatter x2, waiting for transfers between devices: 0.01 us -> 31.6 us  [reduce_experts(): lax.psum_scatter(gate_up, SHARDED, scatter_dimension=1, tiled=True)]
    unnamed x574 -> x578, local copies, waits for them, and re-layouts: 91.3 us -> 94.3 us
  transfers between devices with their start and end apart: 65 -> 65, of which waited for: 13 -> 17; matrix products, arithmetic and copies ran while one was open for 11% -> 11% of each run, Pallas kernels for 48% -> 47%
where the time goes in v6:
time: 1810 us
  Pallas kernels  856 us (47%)
  waiting for transfers between devices  423 us (23%)
  starting transfers between devices  210 us (12%)
  local copies, waits for them, and re-layouts  128 us (7%)
  matrix products  127 us (7%)
  other arithmetic  45.7 us (3%)
    pallas_call x4, Pallas kernels, experts_backward(): pl.pallas_call(functools.partial(experts_backward_kernel, groups, chunks,...  254 us
    ppermute x42, waiting for transfers between devices, exchange(): out.append(block if d == 0 else lax.ppermute(block, 'expert', route))  212 us
    pallas_call x4, Pallas kernels, attention_backward(): pl.pallas_call(functools.partial(attention_backward_kernel, rows, keys, b...  194 us
    ppermute x42, starting transfers between devices, exchange(): out.append(block if d == 0 else lax.ppermute(block, 'expert', route))  169 us
    pallas_call x4, Pallas kernels, attention_forward(): pl.pallas_call(functools.partial(attention_forward_kernel, rows, keys, bl...  129 us
    dot_general x48, matrix products, dot_on(): lax.dot_general(left_op, right_op, (((left_dim,), (right_dim,)), ((), ())...  127 us
    pallas_call x4, Pallas kernels, token_backward(): pl.pallas_call(functools.partial(token_backward_kernel, d_prior is not No...  104 us
    unnamed x578, local copies, waits for them, and re-layouts  94.3 us
  transfers between devices with their start and end apart: 65, of which 17 were waited for; matrix products, arithmetic and copies ran while one was open for 11% of the time, Pallas kernels for 47%

profile of v6, /device:TPU:2, one launch (start us, length us, event | category | flops | bytes accessed | tf_op | source)
XLA Modules:
  0.0 1806.4 jit_solution(6969298880296169188)
XLA Ops:
  31.1 4.6 collective-permute-start
  42.6 4.4 dispatch.8
  61.2 21.8 %collective-permute-done = bf16[1024,768]{1,0:T(8,128)(2,1)} collective-permute-done((bf16[1024,768]{1,0:T(8,128)(2,1)}, bf16[1024,768]{1,0:T(8,128)(2,1)}, u32[]{:S(2)}, u32[]{:S(2)}) %collective-permute-start) | collective-permute-done | bytes 1572896 | tf_op jit(solution)/shard_map/ppermute | solution.py:462
  86.1 4.9 convolution_convert_fusion.7.kp_ref.vp_ref
  95.5 32.2 %attention_forward.4 = (bf16[1024,768]{1,0:T(8,128)(2,1)S(1)}, f32[16,1024]{1,0:T(8,128)S(1)}) custom-call(bf16[1024,2304]{1,0:T(8,128)(2,1)S(1)} %convolution_convert_fusion.3.q_ref.ko_ref.vo_ref, bf16[1024,2304]{1,0:T(8,128)(2,1)S(1)} %convolution_convert_fusion.3.q_ref.ko_ref.vo_ref, bf16[1024,2304]{1,0:T(8,128)(2,1)S(1)} %convolution_convert_fusion.3.q_ref.ko_ref.vo_ref, ...), custom_call_target="tpu_custom_call" | custom-call | flops 11040000000 | bytes 1 | tf_op jit(solution)/shard_map/attention_forward/pallas_call | solution.py:141
  129.6 5.1 collective-permute-start.7
  140.1 7.8 attention_output.4
  151.3 4.5 dispatch.9
  161.7 4.3 convolution_convert_fusion.2.q_ref.ko_ref.vo_ref
  166.0 28.3 %collective-permute-done.7 = bf16[1024,768]{1,0:T(8,128)(2,1)S(1)} collective-permute-done((bf16[1024,768]{1,0:T(8,128)(2,1)}, bf16[1024,768]{1,0:T(8,128)(2,1)S(1)}, u32[]{:S(2)}, u32[]{:S(2)}) %collective-permute-start.7) | collective-permute-done | bytes 1572896 | tf_op jit(solution)/shard_map/ppermute | solution.py:462
  197.7 32.2 %attention_forward.5 = (bf16[1024,768]{1,0:T(8,128)(2,1)S(1)}, f32[16,1024]{1,0:T(8,128)S(1)}) custom-call(bf16[1024,2304]{1,0:T(8,128)(2,1)S(1)} %convolution_convert_fusion.2.q_ref.ko_ref.vo_ref, bf16[1024,2304]{1,0:T(8,128)(2,1)S(1)} %convolution_convert_fusion.2.q_ref.ko_ref.vo_ref, bf16[1024,2304]{1,0:T(8,128)(2,1)S(1)} %convolution_convert_fusion.2.q_ref.ko_ref.vo_ref, ...), custom_call_target="tpu_custom_call" | custom-call | flops 11040000000 | bytes 1 | tf_op jit(solution)/shard_map/attention_forward/pallas_call | solution.py:141
  230.0 8.0 attention_output.5
  238.9 4.6 dispatch.10
  250.2 28.1 %experts_forward.2 = (bf16[1,512,768]{2,1,0:T(8,128)(2,1)S(1)}, bf16[1,512,768]{2,1,0:T(8,128)(2,1)}, bf16[1,512,768]{2,1,0:T(8,128)(2,1)}, bf16[1,512,768]{2,1,...) custom-call(bf16[512,768]{1,0:T(8,128)(2,1)S(1)} %copy-done.91, ...), custom_call_target="tpu_custom_call" | custom-call | flops 8970000384 | bytes 1 | tf_op jit(solution)/shard_map/experts_forward/pallas_call | solution.py:314
  282.1 18.4 %collective-permute-start.9 = (bf16[1,512,768]{2,1,0:T(8,128)(2,1)}, bf16[1,512,768]{2,1,0:T(8,128)(2,1)}, u32[]{:S(2)}, u32[]{:S(2)}) collective-permute-start(bf16[1,512,768]{2,1,0:T(8,128)(2,1)} %get-tuple-element.192), channel_id=1, source_target_pairs={{0,16},{8,24},{16,0},{24,8},{1,17},{9,25},{17,1},{25,9},{2,18},{10... | collective-permute-start | bytes 2359304 | tf_op jit(solution)/shard_map/ppermute | solution.py:493
  300.5 28.3 %experts_forward.3 = (bf16[1,512,768]{2,1,0:T(8,128)(2,1)S(1)}, bf16[1,512,768]{2,1,0:T(8,128)(2,1)}, bf16[1,512,768]{2,1,0:T(8,128)(2,1)}, bf16[1,512,768]{2,1,...) custom-call(bf16[512,768]{1,0:T(8,128)(2,1)S(1)} %get-tuple-element.197.refs_0_, ...), custom_call_target="tpu_custom_call" | custom-call | flops 8970000384 | bytes 1 | tf_op jit(solution)/shard_map/experts_forward/pallas_call | solution.py:314
  329.8 59.9 %collective-permute-start.15 = (bf16[1,512,768]{2,1,0:T(8,128)(2,1)}, bf16[1,512,768]{2,1,0:T(8,128)(2,1)S(1)}, u32[]{:S(2)}, u32[]{:S(2)}) collective-permute-start(bf16[1,512,768]{2,1,0:T(8,128)(2,1)} %get-tuple-element.204), channel_id=1, source_target_pairs={{0,24},{8,0},{16,8},{24,16},{1,25},{9,1},{17,9},{25,17},{2,26},{10... | collective-permute-start | bytes 2359304 | tf_op jit(solution)/shard_map/ppermute | solution.py:493
  401.0 9.6 combine.4
  412.9 4.5 collective-permute-start.14
  418.3 28.8 %collective-permute-done.16.refs_2_ = bf16[1,512,768]{2,1,0:T(8,128)(2,1)S(1)} collective-permute-done((bf16[1,512,768]{2,1,0:T(8,128)(2,1)}, bf16[1,512,768]{2,1,0:T(8,128)(2,1)S(1)}, u32[]{:S(2)}, u32[]{:S(2)}) %collective-permute-start.16) | collective-permute-done | bytes 786464 | tf_op jit(solution)/shard_map/ppermute | solution.py:493
  450.4 9.4 combine.5
  460.9 4.5 dispatch.11
  469.3 5.5 collective-permute-start.24
  479.1 5.5 convolution_convert_fusion.q_ref.ko_ref.vo_ref
  488.7 32.2 %attention_forward.6 = (bf16[1024,768]{1,0:T(8,128)(2,1)S(1)}, f32[16,1024]{1,0:T(8,128)S(1)}) custom-call(bf16[1024,2304]{1,0:T(8,128)(2,1)S(1)} %convolution_convert_fusion.1.q_ref.ko_ref.vo_ref, bf16[1024,2304]{1,0:T(8,128)(2,1)S(1)} %convolution_convert_fusion.1.q_ref.ko_ref.vo_ref, bf16[1024,2304]{1,0:T(8,128)(2,1)S(1)} %convolution_convert_fusion.1.q_ref.ko_ref.vo_ref, ...), custom_call_target="tpu_custom_call" | custom-call | flops 11040000000 | bytes 1 | tf_op jit(solution)/shard_map/attention_forward/pallas_call | solution.py:141
  521.1 8.1 attention_output.6
  530.0 5.3 dispatch.12
  536.3 7.3 collective-permute-start.21
  550.3 32.2 %attention_forward.7 = (bf16[1024,768]{1,0:T(8,128)(2,1)S(1)}, f32[16,1024]{1,0:T(8,128)S(1)}) custom-call(bf16[1024,2304]{1,0:T(8,128)(2,1)S(1)} %bitcast.220, bf16[1024,2304]{1,0:T(8,128)(2,1)S(1)} %bitcast.220, bf16[1024,2304]{1,0:T(8,128)(2,1)S(1)} %bitcast.220, bf16[1024,1536]{1,0:T(8,128)(2,1)S(1)} %convolution_convert_fusion.4.kp_ref.vp_ref, ...), custom_call_target="tpu_custom_call" | custom-call | flops 11040000000 | bytes 1 | tf_op jit(solution)/shard_map/attention_forward/pallas_call | solution.py:141
  582.7 8.1 attention_output.7
  590.8 5.2 dispatch.13
  600.8 39.1 %collective-permute-done.22.refs_2_.refs_13_ = bf16[512,896]{1,0:T(8,128)(2,1)} collective-permute-done((bf16[512,896]{1,0:T(8,128)(2,1)}, bf16[512,896]{1,0:T(8,128)(2,1)}, u32[]{:S(2)}, u32[]{:S(2)}) %collective-permute-start.22) | collective-permute-done | bytes 917536 | tf_op jit(solution)/shard_map/ppermute | solution.py:493
  639.9 74.0 %experts_whole.2 = (bf16[2,512,768]{2,1,0:T(8,128)(2,1)}, bf16[2,512,768]{2,1,0:T(8,128)(2,1)}, bf16[2,512,768]{2,1,0:T(8,128)(2,1)}, bf16[2,512,768]{2,1,0:T(8,...) custom-call(bf16[512,896]{1,0:T(8,128)(2,1)} %copy-done.184, ...), custom_call_target="tpu_custom_call" | custom-call | flops 25874999296 | bytes 1 | tf_op jit(solution)/shard_map/experts_whole/pallas_call | solution.py:435
  713.9 25.8 %collective-permute-start.25 = (bf16[2,512,768]{2,1,0:T(8,128)(2,1)}, bf16[2,512,768]{2,1,0:T(8,128)(2,1)S(1)}, u32[]{:S(2)}, u32[]{:S(2)}) collective-permute-start(bf16[2,512,768]{2,1,0:T(8,128)(2,1)} %get-tuple-element.228), channel_id=1, source_target_pairs={{0,24},{8,0},{16,8},{24,16},{1,25},{9,1},{17,9},{25,17},{2,26},{10... | collective-permute-start | bytes 4718600 | tf_op jit(solution)/shard_map/ppermute | solution.py:493
  740.4 74.6 %experts_whole.3 = (bf16[2,512,768]{2,1,0:T(8,128)(2,1)}, bf16[2,512,768]{2,1,0:T(8,128)(2,1)}, bf16[2,512,768]{2,1,0:T(8,128)(2,1)}, bf16[2,512,768]{2,1,0:T(8,...) custom-call(bf16[512,896]{1,0:T(8,128)(2,1)} %copy-done.192, ...), custom_call_target="tpu_custom_call" | custom-call | flops 25874999296 | bytes 1 | tf_op jit(solution)/shard_map/experts_whole/pallas_call | solution.py:435
  815.0 57.5 %collective-permute-done.26.refs_2_.refs_3_ = bf16[2,512,768]{2,1,0:T(8,128)(2,1)S(1)} collective-permute-done((bf16[2,512,768]{2,1,0:T(8,128)(2,1)}, bf16[2,512,768]{2,1,0:T(8,128)(2,1)S(1)}, u32[]{:S(2)}, u32[]{:S(2)}) %collective-permute-start.26) | collective-permute-done | bytes 1572896 | tf_op jit(solution)/shard_map/ppermute | solution.py:493
  886.5 9.5 combine.6
  899.6 26.6 %token_backward.4 = (f32[1024,768]{1,0:T(8,128)}, bf16[1024,768]{1,0:T(8,128)(2,1)S(1)}, f32[1024,128]{1,0:T(8,128)S(1)}, f32[768,768]{1,0:T(8,128)}, f32[768,12...) custom-call(bf16[2,512,768]{2,1,0:T(8,128)(2,1)} %get-tuple-element.227.refs_0_, ...), custom_call_target="tpu_custom_call" | custom-call | flops 8625000448 | bytes 1 | tf_op jit(solution)/shard_map/token_backward/pallas_call | solution.py:884
  926.3 48.6 %attention_backward.4 = (bf16[1024,768]{1,0:T(8,128)(2,1)S(1)}, bf16[2048,768]{1,0:T(8,128)(2,1)}, bf16[2048,768]{1,0:T(8,128)(2,1)}) custom-call(bf16[1024,2304]{1,0:T(8,128)(2,1)} %copy-done.193, bf16[1024,2304]{1,0:T(8,128)(2,1)} %copy-done.193, bf16[1024,2304]{1,0:T(8,128)(2,1)} %copy-done.193, bf16[1024,1536]{1,0:T(8,128)(2,1)} %copy-done.191, ...), custom_call_target="tpu_custom_call" | custom-call | flops 16560000000 | bytes 1 | tf_op jit(solution)/shard_map/attention_backward/pallas_call | solution.py:238
  989.6 4.9 fusion.64
  1002.2 21.1 %collective-permute-done.34 = bf16[1024,768]{1,0:T(8,128)(2,1)} collective-permute-done((bf16[1024,768]{1,0:T(8,128)(2,1)}, bf16[1024,768]{1,0:T(8,128)(2,1)}, u32[]{:S(2)}, u32[]{:S(2)}) %collective-permute-start.34) | collective-permute-done | bytes 1572896 | tf_op jit(solution)/shard_map/ppermute | solution.py:462
  1027.3 4.4 dispatch.14
  1032.2 9.9 combine.7
  1045.6 25.6 %token_backward.5 = (f32[1024,768]{1,0:T(8,128)}, bf16[1024,768]{1,0:T(8,128)(2,1)S(1)}, f32[1024,128]{1,0:T(8,128)S(1)}, f32[768,768]{1,0:T(8,128)}, f32[768,12...) custom-call(bf16[2,512,768]{2,1,0:T(8,128)(2,1)} %get-tuple-element.241.refs_0_, ...), custom_call_target="tpu_custom_call" | custom-call | flops 8625000448 | bytes 1 | tf_op jit(solution)/shard_map/token_backward/pallas_call | solution.py:884
  1074.1 48.5 %attention_backward.5 = (bf16[1024,768]{1,0:T(8,128)(2,1)S(1)}, bf16[2048,768]{1,0:T(8,128)(2,1)}, bf16[2048,768]{1,0:T(8,128)(2,1)}) custom-call(bf16[1024,2304]{1,0:T(8,128)(2,1)} %convolution_convert_fusion.q_ref.ko_ref.vo_ref, bf16[1024,2304]{1,0:T(8,128)(2,1)} %convolution_convert_fusion.q_ref.ko_ref.vo_ref, ...), custom_call_target="tpu_custom_call" | custom-call | flops 16560000000 | bytes 1 | tf_op jit(solution)/shard_map/attention_backward/pallas_call | solution.py:238
  1164.5 5.1 dispatch.15
  1170.5 10.0 collective-permute-done.36.refs_6_
  1180.5 52.1 %experts_backward.2 = (bf16[1,512,768]{2,1,0:T(8,128)(2,1)}, bf16[1,512,768]{2,1,0:T(8,128)(2,1)}, bf16[1,512,768]{2,1,0:T(8,128)(2,1)}, bf16[1,512,768]{2,1,0:T...) custom-call(bf16[512,768]{1,0:T(8,128)(2,1)} %copy-done.90, ...), custom_call_target="tpu_custom_call" | custom-call | flops 17940000768 | bytes 1 | tf_op jit(solution)/shard_map/experts_backward/pallas_call | solution.py:435
  1232.6 5.2 all-to-all-start
  1245.8 14.3 collective-permute-done.42.refs_5_
  1261.0 32.9 %collective-permute-done.43.refs_6_ = bf16[512,768]{1,0:T(8,128)(2,1)} collective-permute-done((bf16[512,768]{1,0:T(8,128)(2,1)}, bf16[512,768]{1,0:T(8,128)(2,1)}, u32[]{:S(2)}, u32[]{:S(2)}) %collective-permute-start.43) | collective-permute-done | bytes 786464 | tf_op jit(solution)/shard_map/ppermute | solution.py:493
  1294.0 52.9 %experts_backward.3 = (bf16[1,512,768]{2,1,0:T(8,128)(2,1)}, bf16[1,512,768]{2,1,0:T(8,128)(2,1)}, bf16[1,512,768]{2,1,0:T(8,128)(2,1)}, bf16[1,512,768]{2,1,0:T...) custom-call(bf16[512,768]{1,0:T(8,128)(2,1)} %copy-done.35, bf16[512,768]{1,0:T(8,128)(2,1)} %copy-done.36, ...), custom_call_target="tpu_custom_call" | custom-call | flops 17940000768 | bytes 1 | tf_op jit(solution)/shard_map/experts_backward/pallas_call | solution.py:435
  1351.1 25.6 %collective-permute-done.40.refs_2_.refs_3_ = bf16[1,512,768]{2,1,0:T(8,128)(2,1)S(1)} collective-permute-done((bf16[1,512,768]{2,1,0:T(8,128)(2,1)}, bf16[1,512,768]{2,1,0:T(8,128)(2,1)S(1)}, u32[]{:S(2)}, u32[]{:S(2)}) %collective-permute-start.40) | collective-permute-done | bytes 786464 | tf_op jit(solution)/shard_map/ppermute | solution.py:493
  1381.7 8.9 collective-permute-start.48
  1396.5 25.2 %token_backward.6 = (f32[1024,768]{1,0:T(8,128)}, bf16[1024,768]{1,0:T(8,128)(2,1)}, f32[1024,128]{1,0:T(8,128)}, f32[768,768]{1,0:T(8,128)}, f32[768,128]{1,0:T...) custom-call(bf16[1,512,768]{2,1,0:T(8,128)(2,1)S(1)} %copy-done.182, bf16[1,512,768]{2,1,0:T(8,128)(2,1)S(1)} %copy-done.93, ...), custom_call_target="tpu_custom_call" | custom-call | flops 8625000448 | bytes 1 | tf_op jit(solution)/shard_map/token_backward/pallas_call | solution.py:884
  1424.6 48.5 %attention_backward.6 = (bf16[1024,768]{1,0:T(8,128)(2,1)S(1)}, bf16[2048,768]{1,0:T(8,128)(2,1)}, bf16[2048,768]{1,0:T(8,128)(2,1)}) custom-call(bf16[1024,2304]{1,0:T(8,128)(2,1)} %copy-done.187, bf16[1024,2304]{1,0:T(8,128)(2,1)} %copy-done.187, bf16[1024,2304]{1,0:T(8,128)(2,1)} %copy-done.187, bf16[1024,1536]{1,0:T(8,128)(2,1)} %copy-done.189, ...), custom_call_target="tpu_custom_call" | custom-call | flops 16560000000 | bytes 1 | tf_op jit(solution)/shard_map/attention_backward/pallas_call | solution.py:238
  1474.3 26.1 %token_backward.7 = (f32[1024,768]{1,0:T(8,128)}, bf16[1024,768]{1,0:T(8,128)(2,1)}, f32[1024,128]{1,0:T(8,128)}, f32[768,768]{1,0:T(8,128)}, f32[768,128]{1,0:T...) custom-call(bf16[1,512,768]{2,1,0:T(8,128)(2,1)S(1)} %copy-done.158, ...), custom_call_target="tpu_custom_call" | custom-call | flops 8625000448 | bytes 1 | tf_op jit(solution)/shard_map/token_backward/pallas_call | solution.py:884
  1508.2 48.5 %attention_backward.7 = (bf16[1024,768]{1,0:T(8,128)(2,1)S(1)}, bf16[2048,768]{1,0:T(8,128)(2,1)}, bf16[2048,768]{1,0:T(8,128)(2,1)}) custom-call(bf16[1024,2304]{1,0:T(8,128)(2,1)} %copy-done.186, bf16[1024,2304]{1,0:T(8,128)(2,1)} %copy-done.186, bf16[1024,2304]{1,0:T(8,128)(2,1)} %copy-done.186, bf16[1024,1536]{1,0:T(8,128)(2,1)} %copy-done.188, ...), custom_call_target="tpu_custom_call" | custom-call | flops 16560000000 | bytes 1 | tf_op jit(solution)/shard_map/attention_backward/pallas_call | solution.py:238
  1608.0 18.1 %collective-permute-done.49 = bf16[1024,768]{1,0:T(8,128)(2,1)} collective-permute-done((bf16[1024,768]{1,0:T(8,128)(2,1)}, bf16[1024,768]{1,0:T(8,128)(2,1)}, u32[]{:S(2)}, u32[]{:S(2)}) %collective-permute-start.49) | collective-permute-done | bytes 1572896 | tf_op jit(solution)/shard_map/ppermute | solution.py:462
  1632.3 31.6 %reduce-scatter.9.cloned.1.call-done.rest_1_ = bf16[4,96,2048]{2,1,0:T(8,128)(2,1)} async-done(((bf16[4,768,2048]{2,1,0:T(8,128)(2,1)}), bf16[4,96,2048]{2,1,0:T(8,128)(2,1)}) %reduce-scatter.9.cloned.1.call-update) | async-done | bytes 1572880 | tf_op jit(solution)/shard_map/reduce_scatter | solution.py:1163
  1684.2 5.8 all-to-all-start.1
  1692.0 53.4 %all-to-all-done.1 = bf16[8,96,3200]{2,1,0:T(8,128)(2,1)} async-done(((bf16[8,96,3200]{2,1,0:T(8,128)(2,1)}), bf16[8,96,3200]{2,1,0:T(8,128)(2,1)}, u32[]{:S(2)}, u32[]{:S(2)}) %all-to-all-start.1) | async-done | bytes 4915232 | tf_op jit(solution)/shard_map/all_to_all | solution.py:1193
  1755.5 9.0 collective-permute-done.50
  1770.3 23.5 %collective-permute-done.51 = bf16[96,3200]{1,0:T(8,128)(2,1)S(1)} collective-permute-done((bf16[96,3200]{1,0:T(8,128)(2,1)S(1)}, bf16[96,3200]{1,0:T(8,128)(2,1)S(1)}, u32[]{:S(2)}, u32[]{:S(2)}) %collective-permute-start.51) | collective-permute-done | bytes 614432 | tf_op jit(solution)/shard_map/ppermute | solution.py:1203
  (851 shorter events, 358.2 us)
Async XLA Ops:
  7.2 77.7 %all-gather.9.cloned.1.call-start = ((), (), s32[]{:S(2)}) async-start(), calls=%async_computation.6 | async-start | bytes 5529600 | tf_op jit(solution)/shard_map/all_gather | solution.py:970
  15.6 233.4 %all-gather.17.cloned.1.call-start = ((), (), s32[]{:S(2)}) async-start(), calls=%async_computation.15 | async-start | bytes 7077888 | tf_op jit(solution)/shard_map/all_gather | solution.py:973
  17.0 232.1 %all-gather.11.cloned.1.call-start = ((), (), s32[]{:S(2)}) async-start(), calls=%async_computation.7 | async-start | bytes 14155776 | tf_op jit(solution)/shard_map/all_gather | solution.py:972
  21.7 370.3 %all-gather.13.cloned.1.call-start = ((), (), s32[]{:S(2)}) async-start(), calls=%async_computation.8 | async-start | bytes 5529600 | tf_op jit(solution)/shard_map/all_gather | solution.py:970
  23.4 577.4 %all-gather.19.cloned.1.call-start = ((), (), s32[]{:S(2)}) async-start(), calls=%async_computation.16 | async-start | bytes 7077888 | tf_op jit(solution)/shard_map/all_gather | solution.py:973
  24.0 576.8 %all-gather.15.cloned.1.call-start = ((), (), s32[]{:S(2)}) async-start(), calls=%async_computation.9 | async-start | bytes 14155776 | tf_op jit(solution)/shard_map/all_gather | solution.py:972
  27.1 1153.4 %reduce-scatter.5.cloned.1.call-start = ((), (), s32[]{:S(2)}) async-start(), calls=%async_computation.10 | async-start | bytes 14155776 | tf_op jit(solution)/shard_map/reduce_scatter | solution.py:1163
  31.1 52.0 %collective-permute-start = (bf16[1024,768]{1,0:T(8,128)(2,1)}, bf16[1024,768]{1,0:T(8,128)(2,1)}, u32[]{:S(2)}, u32[]{:S(2)}) collective-permute-start(bf16[1024,768]{1,0:T(8,128)(2,1)} %get-tuple-element.408), channel_id=1, source_target_pairs={{0,4},{1,5},{2,6},{3,7},{8,12},{9,13},{10,14},{11,15},{16,20},{17,... | collective-permute-start | bytes 4718600 | tf_op jit(solution)/shard_map/ppermute | solution.py:462
  47.8 103.4 %collective-permute-start.1 = (bf16[512,768]{1,0:T(8,128)(2,1)}, bf16[512,768]{1,0:T(8,128)(2,1)}, u32[]{:S(2)}, u32[]{:S(2)}) collective-permute-start(bf16[512,768]{1,0:T(8,128)(2,1)} %get-tuple-element.179), channel_id=1, source_target_pairs={{0,8},{8,16},{16,24},{24,0},{1,9},{9,17},{17,25},{25,1},{2,10},{10... | collective-permute-start | bytes 2359304 | tf_op jit(solution)/shard_map/ppermute | solution.py:493
  49.4 101.8 %collective-permute-start.2 = (bf16[512,768]{1,0:T(8,128)(2,1)}, bf16[512,768]{1,0:T(8,128)(2,1)}, u32[]{:S(2)}, u32[]{:S(2)}) collective-permute-start(bf16[512,768]{1,0:T(8,128)(2,1)} %get-tuple-element.180), channel_id=1, source_target_pairs={{0,16},{8,24},{16,0},{24,8},{1,17},{9,25},{17,1},{25,9},{2,18},{10... | collective-permute-start | bytes 2359304 | tf_op jit(solution)/shard_map/ppermute | solution.py:493
  52.0 99.3 %collective-permute-start.3 = (bf16[512,768]{1,0:T(8,128)(2,1)}, bf16[512,768]{1,0:T(8,128)(2,1)}, u32[]{:S(2)}, u32[]{:S(2)}) collective-permute-start(bf16[512,768]{1,0:T(8,128)(2,1)} %get-tuple-element.181), channel_id=1, source_target_pairs={{0,24},{8,0},{16,8},{24,16},{1,25},{9,1},{17,9},{25,17},{2,26},{10... | collective-permute-start | bytes 2359304 | tf_op jit(solution)/shard_map/ppermute | solution.py:493
  129.6 64.7 %collective-permute-start.7 = (bf16[1024,768]{1,0:T(8,128)(2,1)}, bf16[1024,768]{1,0:T(8,128)(2,1)S(1)}, u32[]{:S(2)}, u32[]{:S(2)}) collective-permute-start(bf16[1024,768]{1,0:T(8,128)(2,1)} %held.5), channel_id=1, source_target_pairs={{0,4},{1,5},{2,6},{3,7},{8,12},{9,13},{10,14},{11,15},{16,20},{17,... | collective-permute-start | bytes 4718600 | tf_op jit(solution)/shard_map/ppermute | solution.py:462
  155.8 91.8 %collective-permute-start.4 = (bf16[512,768]{1,0:T(8,128)(2,1)}, bf16[512,768]{1,0:T(8,128)(2,1)}, u32[]{:S(2)}, u32[]{:S(2)}) collective-permute-start(bf16[512,768]{1,0:T(8,128)(2,1)} %get-tuple-element.183), channel_id=1, source_target_pairs={{0,8},{8,16},{16,24},{24,0},{1,9},{9,17},{17,25},{25,1},{2,10},{10... | collective-permute-start | bytes 2359304 | tf_op jit(solution)/shard_map/ppermute | solution.py:493
  157.6 91.4 %collective-permute-start.5 = (bf16[512,768]{1,0:T(8,128)(2,1)}, bf16[512,768]{1,0:T(8,128)(2,1)}, u32[]{:S(2)}, u32[]{:S(2)}) collective-permute-start(bf16[512,768]{1,0:T(8,128)(2,1)} %get-tuple-element.184), channel_id=1, source_target_pairs={{0,16},{8,24},{16,0},{24,8},{1,17},{9,25},{17,1},{25,9},{2,18},{10... | collective-permute-start | bytes 2359304 | tf_op jit(solution)/shard_map/ppermute | solution.py:493
  160.5 88.5 %collective-permute-start.6 = (bf16[512,768]{1,0:T(8,128)(2,1)}, bf16[512,768]{1,0:T(8,128)(2,1)}, u32[]{:S(2)}, u32[]{:S(2)}) collective-permute-start(bf16[512,768]{1,0:T(8,128)(2,1)} %get-tuple-element.185.rest_0_), channel_id=1, source_target_pairs={{0,24},{8,0},{16,8},{24,16},{1,25},{9,1},{17,9},{25,17},{2,26},{10... | collective-permute-start | bytes 2359304 | tf_op jit(solution)/shard_map/ppermute | solution.py:493
  243.5 38.6 %collective-permute-start.11 = (bf16[512,768]{1,0:T(8,128)(2,1)}, bf16[512,768]{1,0:T(8,128)(2,1)S(1)}, u32[]{:S(2)}, u32[]{:S(2)}) collective-permute-start(bf16[512,768]{1,0:T(8,128)(2,1)} %get-tuple-element.198), channel_id=1, source_target_pairs={{0,8},{8,16},{16,24},{24,0},{1,9},{9,17},{17,25},{25,1},{2,10},{10... | collective-permute-start | bytes 2359304 | tf_op jit(solution)/shard_map/ppermute | solution.py:493
  245.1 55.4 %collective-permute-start.12 = (bf16[512,768]{1,0:T(8,128)(2,1)}, bf16[512,768]{1,0:T(8,128)(2,1)S(1)}, u32[]{:S(2)}, u32[]{:S(2)}) collective-permute-start(bf16[512,768]{1,0:T(8,128)(2,1)} %get-tuple-element.199), channel_id=1, source_target_pairs={{0,16},{8,24},{16,0},{24,8},{1,17},{9,25},{17,1},{25,9},{2,18},{10... | collective-permute-start | bytes 2359304 | tf_op jit(solution)/shard_map/ppermute | solution.py:493
  247.6 52.9 %collective-permute-start.13 = (bf16[512,768]{1,0:T(8,128)(2,1)}, bf16[512,768]{1,0:T(8,128)(2,1)}, u32[]{:S(2)}, u32[]{:S(2)}) collective-permute-start(bf16[512,768]{1,0:T(8,128)(2,1)} %get-tuple-element.189.refs_7_), channel_id=1, source_target_pairs={{0,24},{8,0},{16,8},{24,16},{1,25},{9,1},{17,9},{25,17},{2,26},{10... | collective-permute-start | bytes 2359304 | tf_op jit(solution)/shard_map/ppermute | solution.py:493
  278.3 111.4 %collective-permute-start.10 = (bf16[1,512,768]{2,1,0:T(8,128)(2,1)S(1)}, bf16[1,512,768]{2,1,0:T(8,128)(2,1)S(1)}, u32[]{:S(2)}, u32[]{:S(2)}) collective-permute-start(bf16[1,512,768]{2,1,0:T(8,128)(2,1)S(1)} %get-tuple-element.193.refs_7_), channel_id=1, source_target_pairs={{0,8},{8,16},{16,24},{24,0},{1,9},{9,17},{17,25},{25,1},{2,10},{10... | collective-permute-start | bytes 2359304 | tf_op jit(solution)/shard_map/ppermute | solution.py:493
  278.9 114.4 %collective-permute-start.8 = (bf16[1,512,768]{2,1,0:T(8,128)(2,1)}, bf16[1,512,768]{2,1,0:T(8,128)(2,1)}, u32[]{:S(2)}, u32[]{:S(2)}) collective-permute-start(bf16[1,512,768]{2,1,0:T(8,128)(2,1)} %get-tuple-element.191), channel_id=1, source_target_pairs={{0,24},{8,0},{16,8},{24,16},{1,25},{9,1},{17,9},{25,17},{2,26},{10... | collective-permute-start | bytes 2359304 | tf_op jit(solution)/shard_map/ppermute | solution.py:493
  282.1 114.6 %collective-permute-start.9 = (bf16[1,512,768]{2,1,0:T(8,128)(2,1)}, bf16[1,512,768]{2,1,0:T(8,128)(2,1)}, u32[]{:S(2)}, u32[]{:S(2)}) collective-permute-start(bf16[1,512,768]{2,1,0:T(8,128)(2,1)} %get-tuple-element.192), channel_id=1, source_target_pairs={{0,16},{8,24},{16,0},{24,8},{1,17},{9,25},{17,1},{25,9},{2,18},{10... | collective-permute-start | bytes 2359304 | tf_op jit(solution)/shard_map/ppermute | solution.py:493
  329.8 87.6 %collective-permute-start.15 = (bf16[1,512,768]{2,1,0:T(8,128)(2,1)}, bf16[1,512,768]{2,1,0:T(8,128)(2,1)S(1)}, u32[]{:S(2)}, u32[]{:S(2)}) collective-permute-start(bf16[1,512,768]{2,1,0:T(8,128)(2,1)} %get-tuple-element.204), channel_id=1, source_target_pairs={{0,24},{8,0},{16,8},{24,16},{1,25},{9,1},{17,9},{25,17},{2,26},{10... | collective-permute-start | bytes 2359304 | tf_op jit(solution)/shard_map/ppermute | solution.py:493
  389.6 57.5 %collective-permute-start.16 = (bf16[1,512,768]{2,1,0:T(8,128)(2,1)}, bf16[1,512,768]{2,1,0:T(8,128)(2,1)S(1)}, u32[]{:S(2)}, u32[]{:S(2)}) collective-permute-start(bf16[1,512,768]{2,1,0:T(8,128)(2,1)} %get-tuple-element.205), channel_id=1, source_target_pairs={{0,16},{8,24},{16,0},{24,8},{1,17},{9,25},{17,1},{25,9},{2,18},{10... | collective-permute-start | bytes 2359304 | tf_op jit(solution)/shard_map/ppermute | solution.py:493
  390.5 57.5 %collective-permute-start.17 = (bf16[1,512,768]{2,1,0:T(8,128)(2,1)}, bf16[1,512,768]{2,1,0:T(8,128)(2,1)}, u32[]{:S(2)}, u32[]{:S(2)}) collective-permute-start(bf16[1,512,768]{2,1,0:T(8,128)(2,1)} %get-tuple-element.200.refs_9_), channel_id=1, source_target_pairs={{0,8},{8,16},{16,24},{24,0},{1,9},{9,17},{17,25},{25,1},{2,10},{10... | collective-permute-start | bytes 2359304 | tf_op jit(solution)/shard_map/ppermute | solution.py:493
  412.9 71.8 %collective-permute-start.14 = (bf16[1024,768]{1,0:T(8,128)(2,1)S(1)}, bf16[1024,768]{1,0:T(8,128)(2,1)S(1)}, u32[]{:S(2)}, u32[]{:S(2)}) collective-permute-start(bf16[1024,768]{1,0:T(8,128)(2,1)S(1)} %get-tuple-element.202), channel_id=1, source_target_pairs={{0,4},{1,5},{2,6},{3,7},{8,12},{9,13},{10,14},{11,15},{16,20},{17,... | collective-permute-start | bytes 4718600 | tf_op jit(solution)/shard_map/ppermute | solution.py:462
  465.4 64.5 %collective-permute-start.18 = (bf16[512,768]{1,0:T(8,128)(2,1)}, bf16[512,768]{1,0:T(8,128)(2,1)}, u32[]{:S(2)}, u32[]{:S(2)}) collective-permute-start(bf16[512,768]{1,0:T(8,128)(2,1)} %get-tuple-element.213), channel_id=1, source_target_pairs={{0,8},{8,16},{16,24},{24,0},{1,9},{9,17},{17,25},{25,1},{2,10},{10... | collective-permute-start | bytes 2359304 | tf_op jit(solution)/shard_map/ppermute | solution.py:493
  465.4 64.5 %collective-permute-start.19 = (bf16[512,768]{1,0:T(8,128)(2,1)}, bf16[512,768]{1,0:T(8,128)(2,1)}, u32[]{:S(2)}, u32[]{:S(2)}) collective-permute-start(bf16[512,768]{1,0:T(8,128)(2,1)} %get-tuple-element.214), channel_id=1, source_target_pairs={{0,16},{8,24},{16,0},{24,8},{1,17},{9,25},{17,1},{25,9},{2,18},{10... | collective-permute-start | bytes 2359304 | tf_op jit(solution)/shard_map/ppermute | solution.py:493
  465.5 64.5 %collective-permute-start.20 = (bf16[512,768]{1,0:T(8,128)(2,1)}, bf16[512,768]{1,0:T(8,128)(2,1)}, u32[]{:S(2)}, u32[]{:S(2)}) collective-permute-start(bf16[512,768]{1,0:T(8,128)(2,1)} %get-tuple-element.215), channel_id=1, source_target_pairs={{0,24},{8,0},{16,8},{24,16},{1,25},{9,1},{17,9},{25,17},{2,26},{10... | collective-permute-start | bytes 2359304 | tf_op jit(solution)/shard_map/ppermute | solution.py:493
  469.3 76.8 %collective-permute-start.24 = (bf16[1024,768]{1,0:T(8,128)(2,1)S(1)}, bf16[1024,768]{1,0:T(8,128)(2,1)}, u32[]{:S(2)}, u32[]{:S(2)}) collective-permute-start(bf16[1024,768]{1,0:T(8,128)(2,1)S(1)} %get-tuple-element.221), channel_id=1, source_target_pairs={{0,4},{1,5},{2,6},{3,7},{8,12},{9,13},{10,14},{11,15},{16,20},{17,... | collective-permute-start | bytes 4718600 | tf_op jit(solution)/shard_map/ppermute | solution.py:462
  536.3 63.3 %collective-permute-start.21 = (bf16[512,896]{1,0:T(8,128)(2,1)S(1)}, bf16[512,896]{1,0:T(8,128)(2,1)}, u32[]{:S(2)}, u32[]{:S(2)}) collective-permute-start(bf16[512,896]{1,0:T(8,128)(2,1)S(1)} %get-tuple-element.217), channel_id=1, source_target_pairs={{0,8},{8,16},{16,24},{24,0},{1,9},{9,17},{17,25},{25,1},{2,10},{10... | collective-permute-start | bytes 2752520 | tf_op jit(solution)/shard_map/ppermute | solution.py:493
  543.6 96.3 %collective-permute-start.22 = (bf16[512,896]{1,0:T(8,128)(2,1)}, bf16[512,896]{1,0:T(8,128)(2,1)}, u32[]{:S(2)}, u32[]{:S(2)}) collective-permute-start(bf16[512,896]{1,0:T(8,128)(2,1)} %get-tuple-element.218), channel_id=1, source_target_pairs={{0,16},{8,24},{16,0},{24,8},{1,17},{9,25},{17,1},{25,9},{2,18},{10... | collective-permute-start | bytes 2752520 | tf_op jit(solution)/shard_map/ppermute | solution.py:493
  543.6 96.3 %collective-permute-start.23 = (bf16[512,896]{1,0:T(8,128)(2,1)}, bf16[512,896]{1,0:T(8,128)(2,1)}, u32[]{:S(2)}, u32[]{:S(2)}) collective-permute-start(bf16[512,896]{1,0:T(8,128)(2,1)} %get-tuple-element.219.rest_0_), channel_id=1, source_target_pairs={{0,24},{8,0},{16,8},{24,16},{1,25},{9,1},{17,9},{25,17},{2,26},{10... | collective-permute-start | bytes 2752520 | tf_op jit(solution)/shard_map/ppermute | solution.py:493
  597.0 142.8 %collective-permute-start.28 = (bf16[512,896]{1,0:T(8,128)(2,1)}, bf16[512,896]{1,0:T(8,128)(2,1)}, u32[]{:S(2)}, u32[]{:S(2)}) collective-permute-start(bf16[512,896]{1,0:T(8,128)(2,1)} %get-tuple-element.234), channel_id=1, source_target_pairs={{0,8},{8,16},{16,24},{24,0},{1,9},{9,17},{17,25},{25,1},{2,10},{10... | collective-permute-start | bytes 2752520 | tf_op jit(solution)/shard_map/ppermute | solution.py:493
  597.0 143.4 %collective-permute-start.29 = (bf16[512,896]{1,0:T(8,128)(2,1)}, bf16[512,896]{1,0:T(8,128)(2,1)}, u32[]{:S(2)}, u32[]{:S(2)}) collective-permute-start(bf16[512,896]{1,0:T(8,128)(2,1)} %get-tuple-element.235), channel_id=1, source_target_pairs={{0,16},{8,24},{16,0},{24,8},{1,17},{9,25},{17,1},{25,9},{2,18},{10... | collective-permute-start | bytes 2752520 | tf_op jit(solution)/shard_map/ppermute | solution.py:493
  599.6 140.8 %collective-permute-start.30 = (bf16[512,896]{1,0:T(8,128)(2,1)}, bf16[512,896]{1,0:T(8,128)(2,1)}, u32[]{:S(2)}, u32[]{:S(2)}) collective-permute-start(bf16[512,896]{1,0:T(8,128)(2,1)} %get-tuple-element.226.refs_15_), channel_id=1, source_target_pairs={{0,24},{8,0},{16,8},{24,16},{1,25},{9,1},{17,9},{25,17},{2,26},{10... | collective-permute-start | bytes 2752520 | tf_op jit(solution)/shard_map/ppermute | solution.py:493
  713.9 101.1 %collective-permute-start.25 = (bf16[2,512,768]{2,1,0:T(8,128)(2,1)}, bf16[2,512,768]{2,1,0:T(8,128)(2,1)S(1)}, u32[]{:S(2)}, u32[]{:S(2)}) collective-permute-start(bf16[2,512,768]{2,1,0:T(8,128)(2,1)} %get-tuple-element.228), channel_id=1, source_target_pairs={{0,24},{8,0},{16,8},{24,16},{1,25},{9,1},{17,9},{25,17},{2,26},{10... | collective-permute-start | bytes 4718600 | tf_op jit(solution)/shard_map/ppermute | solution.py:493
  739.8 132.7 %collective-permute-start.26 = (bf16[2,512,768]{2,1,0:T(8,128)(2,1)}, bf16[2,512,768]{2,1,0:T(8,128)(2,1)S(1)}, u32[]{:S(2)}, u32[]{:S(2)}) collective-permute-start(bf16[2,512,768]{2,1,0:T(8,128)(2,1)} %get-tuple-element.229), channel_id=1, source_target_pairs={{0,16},{8,24},{16,0},{24,8},{1,17},{9,25},{17,1},{25,9},{2,18},{10... | collective-permute-start | bytes 4718600 | tf_op jit(solution)/shard_map/ppermute | solution.py:493
  739.8 132.7 %collective-permute-start.27 = (bf16[2,512,768]{2,1,0:T(8,128)(2,1)}, bf16[2,512,768]{2,1,0:T(8,128)(2,1)}, u32[]{:S(2)}, u32[]{:S(2)}) collective-permute-start(bf16[2,512,768]{2,1,0:T(8,128)(2,1)} %get-tuple-element.230.refs_17_), channel_id=1, source_target_pairs={{0,8},{8,16},{16,24},{24,0},{1,9},{9,17},{17,25},{25,1},{2,10},{10... | collective-permute-start | bytes 4718600 | tf_op jit(solution)/shard_map/ppermute | solution.py:493
  873.7 420.3 %reduce-scatter.7.cloned.1.call-start = ((), (), s32[]{:S(2)}) async-start(), calls=%async_computation.11 | async-start | bytes 7077888 | tf_op jit(solution)/shard_map/reduce_scatter | solution.py:1164
  876.4 155.7 %collective-permute-start.31 = (bf16[2,512,768]{2,1,0:T(8,128)(2,1)}, bf16[2,512,768]{2,1,0:T(8,128)(2,1)}, u32[]{:S(2)}, u32[]{:S(2)}) collective-permute-start(bf16[2,512,768]{2,1,0:T(8,128)(2,1)} %get-tuple-element.242), channel_id=1, source_target_pairs={{0,24},{8,0},{16,8},{24,16},{1,25},{9,1},{17,9},{25,17},{2,26},{10... | collective-permute-start | bytes 4718600 | tf_op jit(solution)/shard_map/ppermute | solution.py:493
  876.4 155.7 %collective-permute-start.32 = (bf16[2,512,768]{2,1,0:T(8,128)(2,1)}, bf16[2,512,768]{2,1,0:T(8,128)(2,1)}, u32[]{:S(2)}, u32[]{:S(2)}) collective-permute-start(bf16[2,512,768]{2,1,0:T(8,128)(2,1)} %get-tuple-element.243), channel_id=1, source_target_pairs={{0,16},{8,24},{16,0},{24,8},{1,17},{9,25},{17,1},{25,9},{2,18},{10... | collective-permute-start | bytes 4718600 | tf_op jit(solution)/shard_map/ppermute | solution.py:493
  876.4 155.7 %collective-permute-start.33 = (bf16[2,512,768]{2,1,0:T(8,128)(2,1)}, bf16[2,512,768]{2,1,0:T(8,128)(2,1)}, u32[]{:S(2)}, u32[]{:S(2)}) collective-permute-start(bf16[2,512,768]{2,1,0:T(8,128)(2,1)} %get-tuple-element.239.refs_9_), channel_id=1, source_target_pairs={{0,8},{8,16},{16,24},{24,0},{1,9},{9,17},{17,25},{25,1},{2,10},{10... | collective-permute-start | bytes 4718600 | tf_op jit(solution)/shard_map/ppermute | solution.py:493
  982.3 41.0 %collective-permute-start.34 = (bf16[1024,768]{1,0:T(8,128)(2,1)}, bf16[1024,768]{1,0:T(8,128)(2,1)}, u32[]{:S(2)}, u32[]{:S(2)}) collective-permute-start(bf16[1024,768]{1,0:T(8,128)(2,1)} %add_convert_fusion.3), channel_id=1, source_target_pairs={{4,0},{5,1},{6,2},{7,3},{12,8},{13,9},{14,10},{15,11},{20,16},{21,... | collective-permute-start | bytes 4718600 | tf_op jit(solution)/shard_map/ppermute | solution.py:462
  1031.8 148.7 %collective-permute-start.37 = (bf16[512,768]{1,0:T(8,128)(2,1)S(1)}, bf16[512,768]{1,0:T(8,128)(2,1)}, u32[]{:S(2)}, u32[]{:S(2)}) collective-permute-start(bf16[512,768]{1,0:T(8,128)(2,1)S(1)} %get-tuple-element.255.refs_9_), channel_id=1, source_target_pairs={{0,24},{8,0},{16,8},{24,16},{1,25},{9,1},{17,9},{25,17},{2,26},{10... | collective-permute-start | bytes 2359304 | tf_op jit(solution)/shard_map/ppermute | solution.py:493
  1128.3 34.0 %collective-permute-start.38 = (bf16[1024,768]{1,0:T(8,128)(2,1)}, bf16[1024,768]{1,0:T(8,128)(2,1)S(1)}, u32[]{:S(2)}, u32[]{:S(2)}) collective-permute-start(bf16[1024,768]{1,0:T(8,128)(2,1)} %add_convert_fusion.2), channel_id=1, source_target_pairs={{4,0},{5,1},{6,2},{7,3},{12,8},{13,9},{14,10},{15,11},{20,16},{21,... | collective-permute-start | bytes 4718600 | tf_op jit(solution)/shard_map/ppermute | solution.py:462
  1129.6 40.9 %collective-permute-start.35 = (bf16[512,768]{1,0:T(8,128)(2,1)S(1)}, bf16[512,768]{1,0:T(8,128)(2,1)}, u32[]{:S(2)}, u32[]{:S(2)}) collective-permute-start(bf16[512,768]{1,0:T(8,128)(2,1)S(1)} %copy-done.162), channel_id=1, source_target_pairs={{0,8},{8,16},{16,24},{24,0},{1,9},{9,17},{17,25},{25,1},{2,10},{10... | collective-permute-start | bytes 2359304 | tf_op jit(solution)/shard_map/ppermute | solution.py:493
  1131.5 49.0 %collective-permute-start.36 = (bf16[512,768]{1,0:T(8,128)(2,1)S(1)}, bf16[512,768]{1,0:T(8,128)(2,1)}, u32[]{:S(2)}, u32[]{:S(2)}) collective-permute-start(bf16[512,768]{1,0:T(8,128)(2,1)S(1)} %copy-done.160), channel_id=1, source_target_pairs={{0,16},{8,24},{16,0},{24,8},{1,17},{9,25},{17,1},{25,9},{2,18},{10... | collective-permute-start | bytes 2359304 | tf_op jit(solution)/shard_map/ppermute | solution.py:493
  1232.6 114.3 %all-to-all-start = ((bf16[8,96,3200]{2,1,0:T(8,128)(2,1)}), bf16[8,96,3200]{2,1,0:T(8,128)(2,1)}, u32[]{:S(2)}, u32[]{:S(2)}) async-start(bf16[8,96,3200]{2,1,0:T(8,128)(2,1)} %bitcast.227), calls=%async_computation.4 | async-start | bytes 9830400 | tf_op jit(solution)/shard_map/all_to_all | solution.py:1193
  1237.8 391.8 %all-reduce.10.cloned.1.call-start = ((), (), s32[]{:S(2)}) async-start(), calls=%async_computation.14 | async-start | bytes 1228800 | tf_op jit(solution)/shard_map/psum | solution.py:1197
  1237.8 22.3 %collective-permute-start.42 = (bf16[512,768]{1,0:T(8,128)(2,1)S(1)}, bf16[512,768]{1,0:T(8,128)(2,1)S(1)}, u32[]{:S(2)}, u32[]{:S(2)}) collective-permute-start(bf16[512,768]{1,0:T(8,128)(2,1)S(1)} %get-tuple-element.283), channel_id=1, source_target_pairs={{0,8},{8,16},{16,24},{24,0},{1,9},{9,17},{17,25},{25,1},{2,10},{10... | collective-permute-start | bytes 2359304 | tf_op jit(solution)/shard_map/ppermute | solution.py:493
  1237.8 56.2 %collective-permute-start.43 = (bf16[512,768]{1,0:T(8,128)(2,1)}, bf16[512,768]{1,0:T(8,128)(2,1)}, u32[]{:S(2)}, u32[]{:S(2)}) collective-permute-start(bf16[512,768]{1,0:T(8,128)(2,1)} %get-tuple-element.284), channel_id=1, source_target_pairs={{0,16},{8,24},{16,0},{24,8},{1,17},{9,25},{17,1},{25,9},{2,18},{10... | collective-permute-start | bytes 2359304 | tf_op jit(solution)/shard_map/ppermute | solution.py:493
  1239.8 54.2 %collective-permute-start.44 = (bf16[512,768]{1,0:T(8,128)(2,1)}, bf16[512,768]{1,0:T(8,128)(2,1)}, u32[]{:S(2)}, u32[]{:S(2)}) collective-permute-start(bf16[512,768]{1,0:T(8,128)(2,1)} %get-tuple-element.271.refs_13_), channel_id=1, source_target_pairs={{0,24},{8,0},{16,8},{24,16},{1,25},{9,1},{17,9},{25,17},{2,26},{10... | collective-permute-start | bytes 2359304 | tf_op jit(solution)/shard_map/ppermute | solution.py:493
  1241.6 135.0 %collective-permute-start.41 = (bf16[1,512,768]{2,1,0:T(8,128)(2,1)}, bf16[1,512,768]{2,1,0:T(8,128)(2,1)}, u32[]{:S(2)}, u32[]{:S(2)}) collective-permute-start(bf16[1,512,768]{2,1,0:T(8,128)(2,1)} %get-tuple-element.278.refs_15_.refs_1_), channel_id=1, source_target_pairs={{0,8},{8,16},{16,24},{24,0},{1,9},{9,17},{17,25},{25,1},{2,10},{10... | collective-permute-start | bytes 2359304 | tf_op jit(solution)/shard_map/ppermute | solution.py:493
  1242.2 108.8 %collective-permute-start.39 = (bf16[1,512,768]{2,1,0:T(8,128)(2,1)}, bf16[1,512,768]{2,1,0:T(8,128)(2,1)S(1)}, u32[]{:S(2)}, u32[]{:S(2)}) collective-permute-start(bf16[1,512,768]{2,1,0:T(8,128)(2,1)} %get-tuple-element.276), channel_id=1, source_target_pairs={{0,24},{8,0},{16,8},{24,16},{1,25},{9,1},{17,9},{25,17},{2,26},{10... | collective-permute-start | bytes 2359304 | tf_op jit(solution)/shard_map/ppermute | solution.py:493
  1261.0 115.6 %collective-permute-start.40 = (bf16[1,512,768]{2,1,0:T(8,128)(2,1)}, bf16[1,512,768]{2,1,0:T(8,128)(2,1)S(1)}, u32[]{:S(2)}, u32[]{:S(2)}) collective-permute-start(bf16[1,512,768]{2,1,0:T(8,128)(2,1)} %get-tuple-element.277), channel_id=1, source_target_pairs={{0,16},{8,24},{16,0},{24,8},{1,17},{9,25},{17,1},{25,9},{2,18},{10... | collective-permute-start | bytes 2359304 | tf_op jit(solution)/shard_map/ppermute | solution.py:493
  1351.0 281.3 %reduce-scatter.11.cloned.1.call-start = ((), (), s32[]{:S(2)}) async-start(), calls=%async_computation.13 | async-start | bytes 7077888 | tf_op jit(solution)/shard_map/reduce_scatter | solution.py:1164
  1377.5 286.4 %reduce-scatter.9.cloned.1.call-start = ((), (), s32[]{:S(2)}) async-start(), calls=%async_computation.12 | async-start | bytes 14155776 | tf_op jit(solution)/shard_map/reduce_scatter | solution.py:1163
  1381.7 92.6 %collective-permute-start.48 = (bf16[1,512,768]{2,1,0:T(8,128)(2,1)}, bf16[1,512,768]{2,1,0:T(8,128)(2,1)}, u32[]{:S(2)}, u32[]{:S(2)}) collective-permute-start(bf16[1,512,768]{2,1,0:T(8,128)(2,1)} %get-tuple-element.290.refs_19_.refs_1_), channel_id=1, source_target_pairs={{0,8},{8,16},{16,24},{24,0},{1,9},{9,17},{17,25},{25,1},{2,10},{10... | collective-permute-start | bytes 2359304 | tf_op jit(solution)/shard_map/ppermute | solution.py:493
  1390.6 83.6 %collective-permute-start.46 = (bf16[1,512,768]{2,1,0:T(8,128)(2,1)}, bf16[1,512,768]{2,1,0:T(8,128)(2,1)}, u32[]{:S(2)}, u32[]{:S(2)}) collective-permute-start(bf16[1,512,768]{2,1,0:T(8,128)(2,1)} %get-tuple-element.309), channel_id=1, source_target_pairs={{0,24},{8,0},{16,8},{24,16},{1,25},{9,1},{17,9},{25,17},{2,26},{10... | collective-permute-start | bytes 2359304 | tf_op jit(solution)/shard_map/ppermute | solution.py:493
  1390.6 83.6 %collective-permute-start.47 = (bf16[1,512,768]{2,1,0:T(8,128)(2,1)}, bf16[1,512,768]{2,1,0:T(8,128)(2,1)}, u32[]{:S(2)}, u32[]{:S(2)}) collective-permute-start(bf16[1,512,768]{2,1,0:T(8,128)(2,1)} %get-tuple-element.310), channel_id=1, source_target_pairs={{0,16},{8,24},{16,0},{24,8},{1,17},{9,25},{17,1},{25,9},{2,18},{10... | collective-permute-start | bytes 2359304 | tf_op jit(solution)/shard_map/ppermute | solution.py:493
  1506.9 97.5 %collective-permute-start.45 = (bf16[1024,768]{1,0:T(8,128)(2,1)}, bf16[1024,768]{1,0:T(8,128)(2,1)}, u32[]{:S(2)}, u32[]{:S(2)}) collective-permute-start(bf16[1024,768]{1,0:T(8,128)(2,1)} %add_convert_fusion.1), channel_id=1, source_target_pairs={{4,0},{5,1},{6,2},{7,3},{12,8},{13,9},{14,10},{15,11},{20,16},{21,... | collective-permute-start | bytes 4718600 | tf_op jit(solution)/shard_map/ppermute | solution.py:462
  1562.9 63.3 %collective-permute-start.49 = (bf16[1024,768]{1,0:T(8,128)(2,1)}, bf16[1024,768]{1,0:T(8,128)(2,1)}, u32[]{:S(2)}, u32[]{:S(2)}) collective-permute-start(bf16[1024,768]{1,0:T(8,128)(2,1)} %add_convert_fusion), channel_id=1, source_target_pairs={{4,0},{5,1},{6,2},{7,3},{12,8},{13,9},{14,10},{15,11},{20,16},{21,... | collective-permute-start | bytes 4718600 | tf_op jit(solution)/shard_map/ppermute | solution.py:462
  1684.2 61.2 %all-to-all-start.1 = ((bf16[8,96,3200]{2,1,0:T(8,128)(2,1)}), bf16[8,96,3200]{2,1,0:T(8,128)(2,1)}, u32[]{:S(2)}, u32[]{:S(2)}) async-start(bf16[8,96,3200]{2,1,0:T(8,128)(2,1)} %bitcast.228), calls=%async_computation.5 | async-start | bytes 9830400 | tf_op jit(solution)/shard_map/all_to_all | solution.py:1193
  1764.7 29.1 %collective-permute-start.51 = (bf16[96,3200]{1,0:T(8,128)(2,1)S(1)}, bf16[96,3200]{1,0:T(8,128)(2,1)S(1)}, u32[]{:S(2)}, u32[]{:S(2)}) collective-permute-start(bf16[96,3200]{1,0:T(8,128)(2,1)S(1)} %add_convert_fusion.12), channel_id=1, source_target_pairs={{0,16},{8,24},{16,0},{24,8},{1,17},{9,25},{17,1},{25,9},{2,18},{10... | collective-permute-start | bytes 1843208 | tf_op jit(solution)/shard_map/ppermute | solution.py:1203
  (282 other events, 4790.8 us)
Sparse Core Ops, SparseCore 0:
  15.8 50.6 all-gather.8
  68.4 50.1 all-gather.16
  121.0 94.0 all-gather.10
  216.9 43.8 all-gather.12
  262.5 45.5 all-gather.18
  309.8 72.1 all-gather.14
  873.8 91.4 reduce-scatter.4
  989.7 65.1 reduce-scatter.6
  1351.1 107.7 all-reduce.9
  1462.5 81.2 reduce-scatter.10
  1547.3 116.5 reduce-scatter.8
